TPU v7x, 32 devices: a whole 2x2x4 slice. The times are simulated.
32 devices in a mesh: ctx: 2 (over core), exp: 4 (over z), tp: 4 (over y, x).
Axes of the slice: x: 2, y: 2, z: 4, core: 2. Of those that a mesh axis runs over, the one named last changes fastest.
Arguments:
- conv_in: bfloat16 [4, 256, 4096], P('exp', 'ctx', 'tp'), may hold values from -6 to 6
- gate_in: bfloat16 [4, 256, 4096], P('exp', 'ctx', 'tp'), may hold values from -6 to 6
- residual: bfloat16 [4, 256, 2048], P('exp', 'ctx'), may hold values from -6 to 6
- conv_weight: float32 [4, 4096], P(None, 'tp'), may hold values from -3 to 3
- conv_bias: float32 [4096], P('tp'), may hold values from -3 to 3
- proj_weight: bfloat16 [4096, 288], P('tp'), may hold values from -0.09375 to 0.09375
- step_weight: bfloat16 [256, 4096], P(None, 'tp'), may hold values from -0.375 to 0.375
- step_bias: float32 [4096], P('tp'), may hold values from -6 to -2
- decay_log: float32 [16, 4096], P(None, 'tp'), may hold values from -3 to 2
- skip_gain: float32 [4096], P('tp'), may hold values from 0.5 to 1.5
- out_weight: bfloat16 [4096, 2048], P('tp'), may hold values from -0.09375 to 0.09375
- norm_gain: float32 [2048], replicated, may hold values from 0.5 to 1.5
- expert_ids: int32 [4, 256, 2], P('exp', 'ctx'), may hold values from 0 to 3, all different within a row; in each aligned block of 128 rows (0 to 127, 128 to 255, ..., all dimensions but the last counted through in order) at most 64 rows name the same one
- route_gates: float32 [4, 256, 2], P('exp', 'ctx'), may hold values from 0.2 to 1
- expert_weight: bfloat16 [4, 3, 2048, 14336], P('exp', None, None, ('ctx', 'tp')), may hold values from -0.125 to 0.125
Outputs:
- layer_out: bfloat16 [4, 256, 2048], P('exp', 'ctx', 'tp')
Inputs may be any that keep to these rules, and one draw needn't show every extreme that they name: `expert_ids`: the 2 picks of a token differ. Among the picks of the 128 tokens of one sequence block, no expert is named more than 64 times, and in some block one expert is named exactly 64 times.
All inputs are finite; a program needn't handle non-finite values.
Results may differ from a plain program's by a relative error of at most 0.015.
Values may be sent and summed in bfloat16 or wider, within the bound.
No kernel may reach another device: no remote copies, remote signals or barrier semaphores. Data moves between devices by JAX's collectives and lax.ppermute only.
A program may use at most 128 MiB of HBM per device.

v0:
```python
import math

import jax
import jax.numpy as jnp
from jax import lax
from jax.sharding import PartitionSpec as P

D = 2048
STATE = 16
DT_RANK = 256
TOP = 2
CAP = 64


def from_behind(block, axis, distance):
    devices = range(lax.axis_size(axis))
    route = [(i - distance, i) for i in devices if i - distance in devices]
    return lax.ppermute(block, axis, route)


def prefix(value, axis, join, neutral):
    count, mine = (lax.axis_size(axis), lax.axis_index(axis))
    pieces = jax.tree.map(lambda part: lax.all_gather(part, axis), value)
    running = jax.tree.map(
        lambda part, zero: jnp.full_like(part, 0) + jnp.asarray(zero, part.dtype), value, neutral
    )

    def hop(position, running):
        longer = join(running, jax.tree.map(lambda part: part[position], pieces))
        return jax.tree.map(lambda new, old: jnp.where(position < mine, new, old), longer, running)

    return lax.fori_loop(0, count - 1, hop, running)


def chain_pair(earlier, later):
    return (earlier[0] * later[0], later[0] * earlier[1] + later[1])


def body(
    conv_in,
    gate_in,
    residual,
    conv_weight,
    conv_bias,
    proj_weight,
    step_weight,
    step_bias,
    decay_log,
    skip_gain,
    out_weight,
    norm_gain,
    expert_ids,
    route_gates,
    expert_weight,
):
    highest = lax.Precision.HIGHEST
    local_x = conv_in[0]
    token_rows = local_x.shape[0]
    channels = local_x.shape[1]
    tap_count = conv_weight.shape[0]
    before = from_behind(local_x[token_rows - tap_count + 1 :], "ctx", 1)
    extended = jnp.concatenate([before, local_x], axis=0).astype(jnp.float32)
    convolved = conv_bias[None, :] + sum(
        (conv_weight[k][None, :] * extended[k : k + token_rows] for k in range(tap_count))
    )
    xconv = jax.nn.silu(convolved).astype(jnp.bfloat16)
    projected = lax.psum(jnp.dot(xconv, proj_weight, preferred_element_type=jnp.float32), "tp")
    rank_part = projected[:, :DT_RANK].astype(jnp.bfloat16)
    input_map = projected[:, DT_RANK : DT_RANK + STATE]
    output_map = projected[:, DT_RANK + STATE :]
    step_sizes = jax.nn.softplus(
        jnp.dot(rank_part, step_weight, preferred_element_type=jnp.float32) + step_bias
    )
    decay_rates = -jnp.exp(decay_log)
    xfloat = xconv.astype(jnp.float32)
    driven = step_sizes * xfloat
    span = math.gcd(token_rows, 16)
    block_total = token_rows // span

    def run_block(state, pieces):
        steps_here, driven_here, in_here, out_here = pieces
        emitted = []
        for inner_step in range(span):
            state = (
                jnp.exp(steps_here[inner_step][None, :] * decay_rates) * state
                + driven_here[inner_step][None, :] * in_here[inner_step][:, None]
            )
            emitted.append(jnp.sum(out_here[inner_step][:, None] * state, axis=0))
        return (state, jnp.stack(emitted))

    pieces = (
        step_sizes.reshape(block_total, span, channels),
        driven.reshape(block_total, span, channels),
        input_map.reshape(block_total, span, STATE),
        output_map.reshape(block_total, span, STATE),
    )
    last_state, local_out = lax.scan(run_block, jnp.zeros((STATE, channels), jnp.float32), pieces)
    local_out = local_out.reshape(token_rows, channels)
    elapsed = jnp.cumsum(step_sizes, axis=0)
    last_decay = jnp.exp(elapsed[token_rows - 1][None, :] * decay_rates)
    incoming = prefix(
        (last_decay, last_state),
        "ctx",
        chain_pair,
        (jnp.ones_like(last_decay), jnp.zeros_like(last_state)),
    )[1]
    carried = jnp.sum(
        output_map[:, :, None] * jnp.exp(elapsed[:, None, :] * decay_rates[None]) * incoming[None],
        axis=1,
    )
    scanned = local_out + carried + skip_gain * xfloat
    gated = (scanned * jax.nn.silu(gate_in[0].astype(jnp.float32))).astype(jnp.bfloat16)
    partial_out = jnp.dot(gated, out_weight, preferred_element_type=jnp.float32)
    quarter = D // lax.axis_size("tp")
    lane_start = lax.axis_index("tp") * quarter
    expert_count = lax.axis_size("exp")
    picks = expert_ids[0]
    onehot = (picks[:, :, None] == jnp.arange(expert_count, dtype=jnp.int32)).astype(jnp.int32)
    flat_hot = onehot.reshape(token_rows * TOP, expert_count)
    ranks = jnp.cumsum(flat_hot, axis=0) - 1
    within = jnp.sum(ranks * flat_hot, axis=1).reshape(token_rows, TOP)
    places = picks * CAP + within
    table = (places[:, :, None] == jnp.arange(expert_count * CAP, dtype=jnp.int32)).astype(
        jnp.float32
    )
    chooser = jnp.sum(table, axis=1).astype(jnp.bfloat16)
    blender = jnp.sum(table * route_gates[0][:, :, None], axis=1)
    mixed = lax.psum(partial_out, "tp")
    stream = (residual[0].astype(jnp.float32) + mixed).astype(jnp.bfloat16)
    sfloat = stream.astype(jnp.float32)
    meansq = jnp.mean(sfloat * sfloat, axis=1, keepdims=True)
    normed = (sfloat * lax.rsqrt(meansq + 1e-06) * norm_gain).astype(jnp.bfloat16)
    picked = lax.dot_general(
        chooser, normed, (((0,), (0,)), ((), ())), preferred_element_type=jnp.float32
    )
    arrived = lax.all_to_all(
        picked.astype(jnp.bfloat16).reshape(expert_count, CAP, normed.shape[1]),
        "exp",
        split_axis=0,
        concat_axis=0,
        tiled=True,
    )
    own_stream = lax.dynamic_slice_in_dim(sfloat, lane_start, quarter, 1)
    slot_rows = arrived.reshape(-1, D)
    local_weights = expert_weight[0]
    piece = lax.all_gather(local_weights, "ctx", axis=2, tiled=True)
    gate_part = jnp.dot(slot_rows, piece[0], preferred_element_type=jnp.float32)
    up_part = jnp.dot(slot_rows, piece[1], preferred_element_type=jnp.float32)
    hidden = (jax.nn.silu(gate_part) * up_part).astype(jnp.bfloat16)
    summed = jnp.zeros((slot_rows.shape[0], D), jnp.float32) + lax.dot_general(
        hidden, piece[2], (((1,), (1,)), ((), ())), preferred_element_type=jnp.float32
    )
    expert_out = (
        lax.psum_scatter(summed, "tp", scatter_dimension=1, tiled=True)
        .astype(jnp.bfloat16)
        .reshape(expert_count, CAP, quarter)
    )
    returned = lax.all_to_all(expert_out, "exp", split_axis=0, concat_axis=0, tiled=True)
    moe = jnp.dot(
        blender,
        returned.reshape(expert_count * CAP, quarter).astype(jnp.float32),
        precision=highest,
        preferred_element_type=jnp.float32,
    )
    final = (own_stream + moe).astype(jnp.bfloat16)
    return final[None]


def solution(mesh):
    placed = (
        P("exp", "ctx", "tp"),
        P("exp", "ctx", "tp"),
        P("exp", "ctx", None),
        P(None, "tp"),
        P("tp"),
        P("tp", None),
        P(None, "tp"),
        P("tp"),
        P(None, "tp"),
        P("tp"),
        P("tp", None),
        P(),
        P("exp", "ctx", None),
        P("exp", "ctx", None),
        P("exp", None, None, ("ctx", "tp")),
    )
    return jax.shard_map(
        body, mesh=mesh, in_specs=placed, out_specs=P("exp", "ctx", "tp"), check_vma=False
    )
```

profile of v0, /device:TPU:0, one launch (start us, length us, event | category | flops | bytes accessed | tf_op | source)
XLA Modules:
  0.0 252.3 jit_solution(14301232931244328043)
XLA Ops:
  8.2 2.3 collective-permute-start
  10.5 0.9 fusion.64
  11.4 1.0 maximum_convert_fusion
  12.4 1.0 multiply_convert_fusion.2
  13.5 1.0 fusion.65
  14.6 44.3 %all-reduce.3.cloned.1.call-done = f32[128,288]{0,1:T(8,128)} async-done(((f32[128,288]{0,1:T(8,128)}), f32[128,288]{0,1:T(8,128)}) %all-reduce.3.cloned.1.call-update) | async-done | bytes 147472 | tf_op jit(solution)/shard_map/psum | solution.py:67
  59.8 1.6 convert_multiply_fusion.2
  61.8 0.9 multiply_exponential_fusion
  62.7 11.5 %while.3 = (s32[]{:T(128)}, f32[16,1024]{1,0:T(8,128)S(1)}, f32[8,16,1024]{2,1,0:T(8,128)S(1)}, f32[8,16,1024]{2,1,0:T(8,128)S(1)}, f32[16,1024]{1,0:T(8,128)S(1...) while((s32[]{:T(128)}, f32[16,1024]{1,0:T(8,128)S(1)}, ...), condition=%wide.region_18.19_spmd.clone, body=%wide.region_1.18_spmd.clone.sunk | while | flops 2310162 | bytes 1998056 | solution.py:97
  74.2 2.0 all-gather
  76.3 1.9 all-gather.1
  78.2 2.6 %multiply_reduce_fusion.16 = f32[128,1024]{1,0:T(8,128)S(1)} fusion(f32[16,1024]{1,0:T(8,128)S(1)} %fusion.57, f32[16,1024]{1,0:T(8,128)S(1)} %get-tuple-element.564, f32[128,1024]{1,0:T(8,128)S(1)} %reduce_window_sum.24, f32[128,16]{1,0:T(8,128)S(1)} %bitcast.364), kind=kLoop, calls=%fused_computation.136 | loop fusion | flops 8257536 | bytes 1187840 | tf_op jit(solution)/shard_map/reduce_sum | solution.py:107
  81.3 1.7 fusion.66
  84.1 1.2 reduce-window.6
  86.1 49.7 %all-reduce.5.cloned.1.call-done = f32[128,2048]{1,0:T(8,128)} async-done(((f32[128,2048]{1,0:T(8,128)}), f32[128,2048]{1,0:T(8,128)}) %all-reduce.5.cloned.1.call-update) | async-done | bytes 1048592 | tf_op jit(solution)/shard_map/psum | solution.py:128
  135.9 1.5 multiply_reduce_fusion.17
  137.9 30.1 %all_to_all.10 = bf16[4,64,2048]{2,1,0:T(8,128)(2,1)S(1)} all-to-all(bf16[4,64,2048]{2,1,0:T(8,128)(2,1)S(1)} %bitcast.286), channel_id=1, replica_groups=mesh['ctx'=2,'exp'=4,'tp'=4] {'exp'}, dimensions={0} | all-to-all | bytes 2097152 | tf_op jit(solution)/shard_map/all_to_all | solution.py:136
  168.0 11.0 %fusion.35 = f32[256,3584]{1,0:T(8,128)} fusion(bf16[256,2048]{1,0:T(8,128)(2,1)S(1)} %bitcast.289, bf16[1,3,2048,3584]{3,2,1,0:T(8,128)(2,1)} %all-gather.5.cloned.1.call-done), kind=kOutput, calls=%fused_computation.135 | convolution fusion | flops 3758096384 | bytes 19398656 | tf_op jit(solution)/shard_map/dot_general | solution.py:147
  179.0 16.3 %fusion.33 = f32[256,2048]{1,0:T(8,128)} fusion(bf16[1,3,2048,3584]{3,2,1,0:T(8,128)(2,1)} %all-gather.5.cloned.1.call-done, bf16[256,2048]{1,0:T(8,128)(2,1)S(1)} %bitcast.290, f32[256,3584]{1,0:T(8,128)} %fusion.35), kind=kOutput, calls=%fused_computation.131 | convolution fusion | flops 7521697792 | bytes 36175872 | tf_op jit(solution)/shard_map/dot_general | solution.py:150
  195.4 33.5 %reduce-scatter.2.cloned.1.call-done = f32[256,512]{1,0:T(8,128)} async-done(((f32[256,2048]{1,0:T(8,128)}), f32[256,512]{1,0:T(8,128)}) %reduce-scatter.2.cloned.1.call-update) | async-done | bytes 524304 | tf_op jit(solution)/shard_map/reduce_scatter | solution.py:154
  228.9 1.8 convert_element_type.75
  230.7 4.6 %all-to-all-start.1 = ((bf16[4,64,512]{2,1,0:T(8,128)(2,1)}), bf16[4,64,512]{2,1,0:T(8,128)(2,1)S(1)}, u32[]{:S(2)}, u32[]{:S(2)}) async-start(bf16[4,64,512]{2,1,0:T(8,128)(2,1)} %bitcast.24), calls=%async_computation.2 | async-start | bytes 524288 | tf_op jit(solution)/shard_map/all_to_all | solution.py:158
  235.3 8.9 %all-to-all-done.1 = bf16[4,64,512]{2,1,0:T(8,128)(2,1)S(1)} async-done(((bf16[4,64,512]{2,1,0:T(8,128)(2,1)}), bf16[4,64,512]{2,1,0:T(8,128)(2,1)S(1)}, u32[]{:S(2)}, u32[]{:S(2)}) %all-to-all-start.1) | async-done | bytes 262176 | tf_op jit(solution)/shard_map/all_to_all | solution.py:158
  244.2 0.9 fusion.42
  (137 shorter events, 16.1 us)
Async XLA Ops:
  7.4 6.1 %copy-start = (bf16[1024,288]{0,1:T(8,128)(2,1)S(1)}, bf16[1024,288]{0,1:T(8,128)(2,1)}, u32[]{:S(2)}) copy-start(bf16[1024,288]{0,1:T(8,128)(2,1)} %param.22) | copy-start | bytes 1769476
  7.4 51.5 %all-reduce.3.cloned.1.call-start = ((), (), s32[]{:S(2)}) async-start(), calls=%async_computation.3 | async-start | bytes 294912 | tf_op jit(solution)/shard_map/psum | solution.py:67
  8.2 3.2 %collective-permute-start = (bf16[3,1024]{1,0:T(4,128)(2,1)S(1)}, bf16[3,1024]{1,0:T(4,128)(2,1)S(1)}, u32[]{:S(2)}, u32[]{:S(2)}) collective-permute-start(bf16[3,1024]{1,0:T(4,128)(2,1)S(1)} %slice_bitcast_fusion.12), channel_id=1, source_target_pairs={{0,16},{1,17},{2,18},{3,19},{4,20},{5,21},{6,22},{7,23},{8,24},{9,... | collective-permute-start | bytes 18440 | tf_op jit(solution)/shard_map/ppermute | solution.py:18
  14.5 121.4 %all-reduce.5.cloned.1.call-start = ((), (), s32[]{:S(2)}) async-start(), calls=%async_computation.4 | async-start | bytes 2097152 | tf_op jit(solution)/shard_map/psum | solution.py:128
  62.7 18.0 %copy-start.4 = (bf16[1,128,1024]{2,1,0:T(8,128)(2,1)S(1)}, bf16[1,128,1024]{2,1,0:T(8,128)(2,1)}, u32[]{:S(2)}) copy-start(bf16[1,128,1024]{2,1,0:T(8,128)(2,1)} %param.18) | copy-start | bytes 786436
  62.7 18.0 %copy-start.5 = (f32[1024]{0:T(1024)S(1)}, f32[1024]{0:T(1024)}, u32[]{:S(2)}) copy-start(f32[1024]{0:T(1024)} %param.21) | copy-start | bytes 12292
  62.7 18.0 %copy-start.7 = (f32[1024]{0:T(1024)S(1)}, f32[1024]{0:T(1024)}, u32[]{:S(2)}) copy-start(f32[1024]{0:T(1024)} %param.26) | copy-start | bytes 12292
  74.2 7.1 %copy-start.2 = (bf16[1024,2048]{1,0:T(8,128)(2,1)S(1)}, bf16[1024,2048]{1,0:T(8,128)(2,1)}, u32[]{:S(2)}) copy-start(bf16[1024,2048]{1,0:T(8,128)(2,1)} %param.27) | copy-start | bytes 12582916
  83.0 0.7 copy-start.8
  83.0 3.0 %copy-start.9 = (f32[1,128,2]{1,2,0:T(2,128)S(1)}, f32[1,128,2]{1,2,0:T(2,128)}, u32[]{:S(2)}) copy-start(f32[1,128,2]{1,2,0:T(2,128)} %param.30) | copy-start | bytes 3076
  83.0 52.8 %copy-start.3 = (bf16[1,128,2048]{2,1,0:T(8,128)(2,1)S(1)}, bf16[1,128,2048]{2,1,0:T(8,128)(2,1)}, u32[]{:S(2)}) copy-start(bf16[1,128,2048]{2,1,0:T(8,128)(2,1)} %param.19) | copy-start | bytes 1572868
  83.0 54.3 %copy-start.6 = (f32[2048]{0:T(1024)S(1)}, f32[2048]{0:T(1024)}, u32[]{:S(2)}) copy-start(f32[2048]{0:T(1024)} %param.28) | copy-start | bytes 24580
  83.0 84.9 %all-gather.5.cloned.1.call-start = ((), (), s32[]{:S(2)}) async-start(), calls=%async_computation.6 | async-start | bytes 66060288 | tf_op jit(solution)/shard_map/all_gather | solution.py:146
  83.6 145.3 %reduce-scatter.2.cloned.1.call-start = ((), (), s32[]{:S(2)}) async-start(), calls=%async_computation.5 | async-start | bytes 2621440 | tf_op jit(solution)/shard_map/reduce_scatter | solution.py:154
  179.0 66.1 %copy-start.1 = (bf16[1024,288]{0,1:T(8,128)(2,1)S(1)}, bf16[1024,288]{0,1:T(8,128)(2,1)}, u32[]{:S(2)}) copy-start(bf16[1024,288]{0,1:T(8,128)(2,1)} %param.22) | copy-start | bytes 1769476
  230.7 13.5 %all-to-all-start.1 = ((bf16[4,64,512]{2,1,0:T(8,128)(2,1)}), bf16[4,64,512]{2,1,0:T(8,128)(2,1)S(1)}, u32[]{:S(2)}, u32[]{:S(2)}) async-start(bf16[4,64,512]{2,1,0:T(8,128)(2,1)} %bitcast.24), calls=%async_computation.2 | async-start | bytes 524288 | tf_op jit(solution)/shard_map/all_to_all | solution.py:158
Sparse Core Ops, SparseCore 0:
  14.6 44.1 all-reduce.2
  83.1 52.7 all-reduce.4
  195.5 33.3 reduce-scatter.1
Sparse Core Ops, SparseCore 1:
  85.2 66.7 all-gather.4
where the time goes:
time: 253 us; the launch traced here: 252 us
  waiting for transfers between devices  137 us (54%)
  blocking collectives  34 us (13%)
  matrix products  33.1 us (13%)
  other arithmetic  17.9 us (7%)
  between operations  14.8 us (6%)
  local copies, waits for them, and re-layouts  7.89 us (3%)
  starting transfers between devices  7.05 us (3%)
    psum x1, waiting for transfers between devices, body(): mixed = lax.psum(partial_out, 'tp')  49.7 us
    psum x1, waiting for transfers between devices, body(): lax.psum(jnp.dot(xconv, proj_weight, preferred_element_type=jnp.float32),...  44.3 us
    reduce_scatter x1, waiting for transfers between devices, body(): lax.psum_scatter(summed, 'tp', scatter_dimension=1, tiled=True)  33.5 us
    all_to_all x1, blocking collectives, body(): lax.all_to_all(picked.astype(jnp.bfloat16).reshape(expert_count, CAP, nor...  30.1 us
    dot_general x1, matrix products, body(): lax.dot_general(hidden, piece[2], (((1,), (1,)), ((), ())), preferred_ele...  16.3 us
    dot_general x1, matrix products, body(): gate_part = jnp.dot(slot_rows, piece[0], preferred_element_type=jnp.float32)  11 us
    all_to_all x1, waiting for transfers between devices, body(): lax.all_to_all(expert_out, 'exp', split_axis=0, concat_axis=0, tiled=True)  8.92 us
    reduce_sum x40, other arithmetic, run_block(): emitted.append(jnp.sum(out_here[inner_step][:, None] * state, axis=0))  6.58 us
  transfers between devices with their start and end apart: 6, of which 4 were waited for; matrix products, arithmetic and copies ran while one was open for 2% of the time, Pallas kernels for 0%

commit v1 on v0

v1 whole, which is shorter than its diff:
```python
import functools
import math

import jax
import jax.numpy as jnp
from jax import lax
from jax.experimental import pallas as pl
from jax.experimental.pallas import tpu as pltpu
from jax.sharding import PartitionSpec as P

STATE = 16
DT_RANK = 256
CAP = 64
LOG2E = math.log2(math.e)
VMEM_LIMIT = 50 * 1024 * 1024
F32 = jnp.float32
BF16 = jnp.bfloat16


def params():
    return pltpu.CompilerParams(vmem_limit_bytes=VMEM_LIMIT)


def whole():
    return pl.BlockSpec(memory_space=pltpu.VMEM)


def shaped(shape, dtype):
    return jax.ShapeDtypeStruct(shape, dtype)


def swap(block, axis, k):
    return lax.ppermute(block, axis, [(i, i ^ k) for i in range(lax.axis_size(axis))])


def sigmoid(x):
    return 1.0 / (1.0 + jnp.exp2(x * -LOG2E))


def route_kernel(ids_ref, first_ref, second_ref, chooser_ref):
    rows, slots = first_ref.shape
    own = lax.axis_index("exp")
    ids = ids_ref[...]
    lanes = lax.broadcasted_iota(jnp.int32, (rows, 128), 1)
    hot = [(ids[:, i : i + 1] == lanes).astype(F32) for i in range(2)]
    earlier = lax.broadcasted_iota(jnp.int32, (rows, rows), 1) < lax.broadcasted_iota(
        jnp.int32, (rows, rows), 0
    )
    ranks = jnp.dot(
        earlier.astype(F32).astype(BF16), (hot[0] + hot[1]).astype(BF16), preferred_element_type=F32
    )
    places = lax.broadcasted_iota(jnp.int32, (rows, slots), 1)
    tables = []
    for i in range(2):
        slot = jnp.sum(ranks * hot[i], axis=1, keepdims=True).astype(jnp.int32)
        place = jnp.bitwise_xor(ids[:, i : i + 1], own) * CAP + slot
        tables.append((place == places).astype(F32))
    first_ref[...] = tables[0].astype(BF16)
    second_ref[...] = tables[1].astype(BF16)
    chooser_ref[...] = jnp.transpose(tables[0] + tables[1]).astype(BF16)


def route(ids, expert_count):
    rows, slots = ids.shape[0], expert_count * CAP
    return pl.pallas_call(
        route_kernel,
        out_shape=(
            shaped((rows, slots), BF16),
            shaped((rows, slots), BF16),
            shaped((slots, rows), BF16),
        ),
        in_specs=[whole()],
        out_specs=[whole()] * 3,
        compiler_params=params(),
        name="route",
    )(ids)


def conv_kernel(halo_ref, x_ref, taps_ref, bias_ref, weight_ref, xconv_ref, part_ref, ext_ref):
    rows = x_ref.shape[0]
    halo = halo_ref.shape[0]
    count = taps_ref.shape[0]
    ext_ref[:halo, :] = halo_ref[...].astype(F32)
    ext_ref[halo:, :] = x_ref[...].astype(F32)
    total = bias_ref[...] + taps_ref[count - 1 : count, :] * ext_ref[halo:, :]
    for k in range(count - 1):
        start = halo - (count - 1) + k
        total = total + taps_ref[k : k + 1, :] * ext_ref[start : start + rows, :]
    xconv = (total * sigmoid(total)).astype(BF16)
    xconv_ref[...] = xconv
    part_ref[...] = jnp.dot(xconv, weight_ref[...], preferred_element_type=F32).astype(BF16)


def conv(halo, x, taps, bias, weight):
    rows, channels = x.shape
    return pl.pallas_call(
        conv_kernel,
        out_shape=(shaped((rows, channels), BF16), shaped((rows, weight.shape[1]), BF16)),
        in_specs=[whole()] * 5,
        out_specs=[whole()] * 2,
        scratch_shapes=[pltpu.VMEM((halo.shape[0] + rows, channels), F32)],
        compiler_params=params(),
        name="conv",
    )(halo, x, taps, bias, weight)


def scan_kernel(parts, *refs):
    part_refs = refs[:parts]
    xconv_ref, weight_ref, bias_ref, decay_ref, skip_ref = refs[parts : parts + 5]
    y_ref, elapsed_ref, rates_ref, maps_ref, state_ref = refs[parts + 5 : parts + 10]
    steps_ref, x_ref, tall_ref, scalars, sem = refs[parts + 10 :]
    rows, channels = xconv_ref.shape
    tiles = channels // 128
    proj = part_refs[0][...].astype(F32)
    for ref in part_refs[1:]:
        proj = proj + ref[...].astype(F32)
    maps_ref[...] = proj[:, DT_RANK:]
    copy = pltpu.make_async_copy(maps_ref, scalars, sem)
    copy.start()
    rank = proj[:, :DT_RANK].astype(BF16)
    raw = jnp.dot(rank, weight_ref[...], preferred_element_type=F32) + bias_ref[...]
    steps = jnp.maximum(raw, 0.0) + jnp.log1p(jnp.exp(-jnp.abs(raw)))
    xfloat = xconv_ref[...].astype(F32)
    rates = -LOG2E * jnp.exp(decay_ref[...])
    skip = skip_ref[...]
    for j in range(tiles):
        cut = slice(j * 128, (j + 1) * 128)
        steps_ref[:, j, :] = steps[:, cut]
        x_ref[:, j, :] = xfloat[:, cut]
        rates_ref[:, j, :] = rates[:, cut]
        tall_ref[j : j + 1, :] = skip[:, cut]
    copy.wait()
    gain = tall_ref[...]

    def step(t, carry):
        elapsed, states = carry
        now = steps_ref[t]
        x = x_ref[t]
        driven = now * x
        sums = [gain * x, None]
        new = []
        for n in range(STATE):
            state = jnp.exp2(now * rates_ref[n]) * states[n] + driven * scalars[t, n]
            new.append(state)
            term = state * scalars[t, STATE + n]
            sums[n % 2] = term if sums[n % 2] is None else sums[n % 2] + term
        elapsed = elapsed + now
        y_ref[t] = sums[0] + sums[1]
        elapsed_ref[t] = elapsed
        return elapsed, tuple(new)

    zero = jnp.zeros((tiles, 128), F32)
    _, states = lax.fori_loop(0, rows, step, (zero, (zero,) * STATE), unroll=4)
    for n in range(STATE):
        state_ref[n] = states[n]


def scan(pieces, xconv, weight, bias, decay_log, skip):
    rows, channels = xconv.shape
    tiles = channels // 128
    return pl.pallas_call(
        functools.partial(scan_kernel, len(pieces)),
        out_shape=(
            shaped((rows, tiles, 128), F32),
            shaped((rows, tiles, 128), F32),
            shaped((STATE, tiles, 128), F32),
            shaped((rows, 2 * STATE), F32),
            shaped((STATE, tiles, 128), F32),
        ),
        in_specs=[whole()] * (len(pieces) + 5),
        out_specs=[whole()] * 5,
        scratch_shapes=[
            pltpu.VMEM((rows, tiles, 128), F32),
            pltpu.VMEM((rows, tiles, 128), F32),
            pltpu.VMEM((tiles, 128), F32),
            pltpu.SMEM((rows, 2 * STATE), F32),
            pltpu.SemaphoreType.DMA,
        ],
        compiler_params=params(),
        name="scan",
    )(*pieces, xconv, weight, bias, decay_log, skip)


def mix_kernel(parts, *refs):
    maps, y_ref, elapsed_ref, rates_ref, state_ref, gate_ref, residual_ref, weight_hbm = refs[:8]
    own_ref, sent = refs[8], refs[9 : 8 + parts]
    sum_ref, gated_ref, weight_ref, sem = refs[8 + parts :]
    copy = pltpu.make_async_copy(weight_hbm, weight_ref, sem)
    copy.start()
    rows, tiles, _ = y_ref.shape

    def step(t, carry):
        elapsed = elapsed_ref[t]
        sums = [y_ref[t], None]
        for n in range(STATE):
            term = jnp.exp2(elapsed * rates_ref[n]) * state_ref[n] * maps[t, STATE + n]
            sums[n % 2] = term if sums[n % 2] is None else sums[n % 2] + term
        sum_ref[t] = sums[0] + sums[1]
        return carry

    lax.fori_loop(0, rows, step, 0, unroll=4)
    for j in range(tiles):
        cut = slice(j * 128, (j + 1) * 128)
        gate = gate_ref[:, cut].astype(F32)
        gated_ref[:, cut] = (sum_ref[:, j, :] * (gate * sigmoid(gate))).astype(BF16)
    copy.wait()
    own = lax.axis_index("tp")
    width = own_ref.shape[1]
    for k in range(parts):
        start = pl.multiple_of(jnp.bitwise_xor(own, k) * width, 128)
        product = jnp.dot(
            gated_ref[...], weight_ref[:, pl.ds(start, width)], preferred_element_type=F32
        )
        if k == 0:
            own_ref[...] = product + residual_ref[:, pl.ds(start, width)].astype(F32)
        else:
            sent[k - 1][...] = product.astype(BF16)


def mix(parts, maps, y, elapsed, rates, state, gate, residual, weight):
    rows, tiles, _ = y.shape
    width = weight.shape[1] // parts
    return pl.pallas_call(
        functools.partial(mix_kernel, parts),
        out_shape=[shaped((rows, width), F32)] + [shaped((rows, width), BF16)] * (parts - 1),
        in_specs=[pl.BlockSpec(memory_space=pltpu.SMEM)]
        + [whole()] * 6
        + [pl.BlockSpec(memory_space=pl.ANY)],
        out_specs=[whole()] * parts,
        scratch_shapes=[
            pltpu.VMEM((rows, tiles, 128), F32),
            pltpu.VMEM((rows, tiles * 128), BF16),
            pltpu.VMEM(weight.shape, BF16),
            pltpu.SemaphoreType.DMA,
        ],
        compiler_params=params(),
        name="mix",
    )(maps, y, elapsed, rates, state, gate, residual, weight)


def pick_kernel(parts, *refs):
    own_ref, arrived, chooser_ref = refs[0], refs[1:parts], refs[parts]
    stream_ref, out_refs = refs[parts + 1], refs[parts + 2 :]
    total = own_ref[...]
    for ref in arrived:
        total = total + ref[...].astype(F32)
    stream = total.astype(BF16)
    stream_ref[...] = stream
    picked = jnp.dot(chooser_ref[...], stream, preferred_element_type=F32).astype(BF16)
    for j, ref in enumerate(out_refs):
        ref[...] = picked[j * CAP : (j + 1) * CAP, :]


def pick(own, arrived, chooser):
    rows, width = own.shape
    experts = chooser.shape[0] // CAP
    return pl.pallas_call(
        functools.partial(pick_kernel, 1 + len(arrived)),
        out_shape=[shaped((rows, width), BF16)] + [shaped((CAP, width), BF16)] * experts,
        in_specs=[whole()] * (2 + len(arrived)),
        out_specs=[whole()] * (1 + experts),
        compiler_params=params(),
        name="pick",
    )(own, *arrived, chooser)


def expert_kernel(parts, *refs):
    x_refs = refs[: 2 * parts]
    gain_ref, gate_ref, up_ref, down_ref = refs[2 * parts : 2 * parts + 4]
    own_refs = refs[2 * parts + 4 : 3 * parts + 4]
    other_refs = refs[3 * parts + 4 : 4 * parts + 4]
    x_ref, acc_ref = refs[4 * parts + 4 :]
    half, width = x_refs[0].shape
    own = lax.axis_index("tp")
    block = pl.program_id(0)
    starts = [pl.multiple_of(jnp.bitwise_xor(own, k) * width, 128) for k in range(parts)]

    @pl.when(block == 0)
    def _():
        for core in range(2):
            pieces = [ref[...].astype(F32) for ref in x_refs[core * parts : (core + 1) * parts]]
            total = sum(jnp.sum(piece * piece, axis=1, keepdims=True) for piece in pieces)
            scale = lax.rsqrt(total / (width * parts) + 1e-6)
            for piece, start in zip(pieces, starts):
                gain = gain_ref[:, pl.ds(start, width)]
                x_ref[core * half : (core + 1) * half, pl.ds(start, width)] = (
                    piece * scale * gain
                ).astype(BF16)

    x = x_ref[...]
    gate = jnp.dot(x, gate_ref[0, 0], preferred_element_type=F32)
    up = jnp.dot(x, up_ref[0, 0], preferred_element_type=F32)
    hidden = (gate * sigmoid(gate) * up).astype(BF16)
    product = lax.dot_general(
        hidden, down_ref[0, 0], (((1,), (1,)), ((), ())), preferred_element_type=F32
    )

    @pl.when(block == 0)
    def _():
        acc_ref[...] = product

    @pl.when(block > 0)
    def _():
        acc_ref[...] += product

    @pl.when(block == pl.num_programs(0) - 1)
    def _():
        for k, start in enumerate(starts):
            own_refs[k][...] = acc_ref[:half, pl.ds(start, width)].astype(own_refs[k].dtype)
            other_refs[k][...] = acc_ref[half:, pl.ds(start, width)].astype(BF16)


def expert(own_rows, other_rows, gain, weights):
    parts = len(own_rows)
    half, width = own_rows[0].shape
    model, hidden = weights.shape[2:]
    size = 256 if hidden % 256 == 0 else hidden
    fixed = pl.BlockSpec((half, width), lambda b: (0, 0))

    def weight_spec(which):
        return pl.BlockSpec((1, 1, model, size), lambda b: (0, which, 0, b))

    return pl.pallas_call(
        functools.partial(expert_kernel, parts),
        grid=(hidden // size,),
        out_shape=[shaped((half, width), F32)] * parts + [shaped((half, width), BF16)] * parts,
        in_specs=[fixed] * (2 * parts)
        + [pl.BlockSpec((1, model), lambda b: (0, 0))]
        + [weight_spec(i) for i in range(3)],
        out_specs=[fixed] * (2 * parts),
        scratch_shapes=[pltpu.VMEM((2 * half, model), BF16), pltpu.VMEM((2 * half, model), F32)],
        compiler_params=params(),
        name="expert",
    )(*own_rows, *other_rows, gain, weights, weights, weights)


def total_kernel(parts, *refs):
    total = refs[0][...].astype(F32)
    for ref in refs[1:parts]:
        total = total + ref[...].astype(F32)
    total = total.astype(BF16)
    for j, ref in enumerate(refs[parts:]):
        ref[...] = total[j * CAP : (j + 1) * CAP, :]


def totals(pieces):
    rows, width = pieces[0].shape
    experts = rows // CAP
    return pl.pallas_call(
        functools.partial(total_kernel, len(pieces)),
        out_shape=[shaped((CAP, width), BF16)] * experts,
        in_specs=[whole()] * len(pieces),
        out_specs=[whole()] * experts,
        compiler_params=params(),
        name="totals",
    )(*pieces)


def blend_kernel(experts, *refs):
    back = refs[:experts]
    stream_ref, first_ref, second_ref, gates_ref, out_ref, rows_ref = refs[experts:]
    for j, ref in enumerate(back):
        rows_ref[j * CAP : (j + 1) * CAP, :] = ref[...]
    rows = rows_ref[...]
    gates = gates_ref[...]
    moe = gates[:, 0:1] * jnp.dot(first_ref[...], rows, preferred_element_type=F32)
    moe = moe + gates[:, 1:2] * jnp.dot(second_ref[...], rows, preferred_element_type=F32)
    out_ref[...] = (stream_ref[...].astype(F32) + moe).astype(BF16)


def blend(back, stream, first, second, gates):
    experts, width = len(back), stream.shape[1]
    return pl.pallas_call(
        functools.partial(blend_kernel, experts),
        out_shape=shaped(stream.shape, BF16),
        in_specs=[whole()] * (experts + 4),
        out_specs=whole(),
        scratch_shapes=[pltpu.VMEM((experts * CAP, width), BF16)],
        compiler_params=params(),
        name="blend",
    )(*back, stream, first, second, gates)


def body(
    conv_in,
    gate_in,
    residual,
    conv_weight,
    conv_bias,
    proj_weight,
    step_weight,
    step_bias,
    decay_log,
    skip_gain,
    out_weight,
    norm_gain,
    expert_ids,
    route_gates,
    expert_weight,
):
    tp, experts = lax.axis_size("tp"), lax.axis_size("exp")
    local = conv_in[0]
    halo = lax.ppermute(local[-16:], "ctx", [(0, 1)])
    first, second, chooser = route(expert_ids[0], experts)
    xconv, part = conv(halo, local, conv_weight, conv_bias[None], proj_weight)
    parts = [part] + [swap(part, "tp", k) for k in range(1, tp)]
    y, elapsed, rates, maps, state = scan(
        parts, xconv, step_weight, step_bias[None], decay_log, skip_gain[None]
    )
    before = lax.ppermute(state, "ctx", [(0, 1)])
    own, *sent = mix(tp, maps, y, elapsed, rates, before, gate_in[0], residual[0], out_weight)
    arrived = [swap(piece, "tp", k) for k, piece in enumerate(sent, 1)]
    stream, *picked = pick(own, arrived, chooser)
    rows = jnp.concatenate(
        [picked[0]] + [swap(picked[j], "exp", j) for j in range(1, experts)], axis=0
    )
    own_rows = [rows] + [swap(rows, "tp", k) for k in range(1, tp)]
    other_rows = [swap(piece, "ctx", 1) for piece in own_rows]
    made = expert(own_rows, other_rows, norm_gain[None], expert_weight)
    summed = []
    for k in range(tp):
        piece = made[k] + swap(made[tp + k], "ctx", 1).astype(F32)
        summed.append(piece if k == 0 else swap(piece.astype(BF16), "tp", k))
    results = totals(summed)
    back = [results[0]] + [swap(results[j], "exp", j) for j in range(1, experts)]
    return blend(back, stream, first, second, route_gates[0])[None]


def solution(mesh):
    placed = (
        P("exp", "ctx", "tp"),
        P("exp", "ctx", "tp"),
        P("exp", "ctx", None),
        P(None, "tp"),
        P("tp"),
        P("tp", None),
        P(None, "tp"),
        P("tp"),
        P(None, "tp"),
        P("tp"),
        P("tp", None),
        P(),
        P("exp", "ctx", None),
        P("exp", "ctx", None),
        P("exp", None, None, ("ctx", "tp")),
    )
    return jax.shard_map(
        body, mesh=mesh, in_specs=placed, out_specs=P("exp", "ctx", "tp"), check_vma=False
    )
```

time: 253 us -> 117 us (0.46)
  waiting for transfers between devices: 137 us -> 40.4 us
  blocking collectives: 34 us -> 0 us
  matrix products: 33.1 us -> 0 us
  Pallas kernels: 0 us -> 31.9 us
  starting transfers between devices: 7.05 us -> 28.7 us
  between operations: 14.8 us -> 0.16 us
  other arithmetic: 17.9 us -> 3.41 us
  local copies, waits for them, and re-layouts: 7.89 us -> 11.4 us
    psum x2 -> x0, waiting for transfers between devices: 94 us -> none  [the longest x1 49.7 us: body(): mixed = lax.psum(partial_out, 'tp')]
    ppermute x1 -> x28, waiting for transfers between devices: 0.01 us -> 40.4 us  [the longest x26 39.6 us: swap(): lax.ppermute(block, axis, [(i, i ^ k) for i in range(lax.axis_size(axis))])]
    reduce_scatter x1 -> x0, waiting for transfers between devices: 33.5 us -> none  [body(): lax.psum_scatter(summed, 'tp', scatter_dimension=1, tiled=True)]
    dot_general x7 -> x0, matrix products: 33.1 us -> none  [the longest x1 16.3 us: body(): lax.dot_general(hidden, piece[2], (((1,), (1,)), ((), ())), preferred_ele...]
    pallas_call x0 -> x8, Pallas kernels: none -> 31.9 us  [the longest x1 19.7 us: expert(): pl.pallas_call(functools.partial(expert_kernel, parts), grid=(hidden // s...]
    all_to_all x1 -> x0, blocking collectives: 30.1 us -> none  [body(): lax.all_to_all(picked.astype(jnp.bfloat16).reshape(expert_count, CAP, nor...]
    ppermute x1 -> x28, starting transfers between devices: 2.34 us -> 28.7 us  [the longest x26 25.1 us: swap(): lax.ppermute(block, axis, [(i, i ^ k) for i in range(lax.axis_size(axis))])]
    reduce_sum x44 -> x0, other arithmetic: 10.8 us -> none  [the longest x40 6.58 us: run_block(): emitted.append(jnp.sum(out_here[inner_step][:, None] * state, axis=0))]
  transfers between devices with their start and end apart: 6 -> 28, of which waited for: 4 -> 18; matrix products, arithmetic and copies ran while one was open for 2% -> 5% of each run, Pallas kernels for 0% -> 0%
where the time goes in v1:
time: 117 us; the launch traced here: 116 us
  waiting for transfers between devices  40.4 us (35%)
  Pallas kernels  31.9 us (27%)
  starting transfers between devices  28.7 us (25%)
  local copies, waits for them, and re-layouts  11.4 us (10%)
  other arithmetic  3.41 us (3%)
    ppermute x26, waiting for transfers between devices, swap(): lax.ppermute(block, axis, [(i, i ^ k) for i in range(lax.axis_size(axis))])  39.6 us
    ppermute x26, starting transfers between devices, swap(): lax.ppermute(block, axis, [(i, i ^ k) for i in range(lax.axis_size(axis))])  25.1 us
    pallas_call x1, Pallas kernels, expert(): pl.pallas_call(functools.partial(expert_kernel, parts), grid=(hidden // s...  19.7 us
    unnamed x28, local copies, waits for them, and re-layouts  10.6 us
    pallas_call x1, Pallas kernels, scan(): pl.pallas_call(functools.partial(scan_kernel, len(pieces)), out_shape=(sh...  5.14 us
    pallas_call x1, Pallas kernels, mix(): pl.pallas_call(functools.partial(mix_kernel, parts), out_shape=[shaped((r...  4.77 us
    convert_element_type x3, other arithmetic, body(): summed.append(piece if k == 0 else swap(piece.astype(BF16), 'tp', k))  3.33 us
    ppermute x1, starting transfers between devices, body(): halo = lax.ppermute(local[-16:], 'ctx', [(0, 1)])  2.35 us
  transfers between devices with their start and end apart: 28, of which 18 were waited for; matrix products, arithmetic and copies ran while one was open for 5% of the time, Pallas kernels for 0%

profile of v1, /device:TPU:0, one launch (start us, length us, event | category | flops | bytes accessed | tf_op | source)
XLA Modules:
  0.0 116.0 jit_solution(5476796421759475339)
XLA Ops:
  0.8 2.3 %collective-permute-start = (bf16[16,1024]{1,0:T(8,128)(2,1)S(1)}, bf16[16,1024]{1,0:T(8,128)(2,1)S(1)}, u32[]{:S(2)}, u32[]{:S(2)}) collective-permute-start(bf16[16,1024]{1,0:T(8,128)(2,1)S(1)} %slice_bitcast_fusion), channel_id=1, source_target_pairs={{0,16},{1,17},{2,18},{3,19},{4,20},{5,21},{6,22},{7,23},{8,24},{9,... | collective-permute-start | bytes 98312 | tf_op jit(solution)/shard_map/ppermute | solution.py:403
  3.1 1.4 %copy.16.weight_ref = bf16[1024,288]{1,0:T(8,128)(2,1)S(1)} copy(bf16[1024,288]{0,1:T(8,128)(2,1)} %param.20) | data formatting | bytes 1179648 | tf_op args[5]
  7.4 2.4 %collective-permute-start.1 = (bf16[128,288]{1,0:T(8,128)(2,1)S(1)}, bf16[128,288]{1,0:T(8,128)(2,1)S(1)}, u32[]{:S(2)}, u32[]{:S(2)}) collective-permute-start(bf16[128,288]{1,0:T(8,128)(2,1)S(1)} %get-tuple-element.36.refs_0_), channel_id=1, source_target_pairs={{0,1},{1,0},{2,3},{3,2},{4,5},{5,4},{6,7},{7,6},{8,9},{9,8},{10,11... | collective-permute-start | bytes 221192 | tf_op jit(solution)/shard_map/ppermute | solution.py:33
  9.8 1.5 %collective-permute-start.2 = (bf16[128,288]{1,0:T(8,128)(2,1)S(1)}, bf16[128,288]{1,0:T(8,128)(2,1)S(1)}, u32[]{:S(2)}, u32[]{:S(2)}) collective-permute-start(bf16[128,288]{1,0:T(8,128)(2,1)S(1)} %get-tuple-element.36.refs_0_), channel_id=1, source_target_pairs={{0,2},{1,3},{2,0},{3,1},{4,6},{5,7},{6,4},{7,5},{8,10},{9,11},{10,... | collective-permute-start | bytes 221192 | tf_op jit(solution)/shard_map/ppermute | solution.py:33
  11.4 1.6 %collective-permute-done.1.refs_1_ = bf16[128,288]{1,0:T(8,128)(2,1)S(1)} collective-permute-done((bf16[128,288]{1,0:T(8,128)(2,1)S(1)}, bf16[128,288]{1,0:T(8,128)(2,1)S(1)}, u32[]{:S(2)}, u32[]{:S(2)}) %collective-permute-start.1) | collective-permute-done | bytes 73760 | tf_op jit(solution)/shard_map/ppermute | solution.py:33
  13.0 2.5 %collective-permute-done.2.refs_2_ = bf16[128,288]{1,0:T(8,128)(2,1)S(1)} collective-permute-done((bf16[128,288]{1,0:T(8,128)(2,1)S(1)}, bf16[128,288]{1,0:T(8,128)(2,1)S(1)}, u32[]{:S(2)}, u32[]{:S(2)}) %collective-permute-start.2) | collective-permute-done | bytes 73760 | tf_op jit(solution)/shard_map/ppermute | solution.py:33
  20.1 5.1 %scan.1 = (f32[128,8,128]{2,1,0:T(8,128)S(1)}, f32[128,8,128]{2,1,0:T(8,128)S(1)}, f32[16,8,128]{2,1,0:T(8,128)S(1)}, f32[128,32]{1,0:T(8,128)S(1)}, f32[16,8,128]{2,1,0:T(8,128)S(1)}) custom-call(bf16[128,288]{1,0:T(8,128)(2,1)S(1)} %get-tuple-element.36.refs_0_, bf16[128,288]{1,0:T(8,128)(2,1)S(1)} %collective-permute-done.1.refs_1_, ...), custom_call_target="tpu_custom_call" | custom-call | tf_op jit(solution)/shard_map/scan/pallas_call | solution.py:161
  29.4 4.8 %mix.1 = (f32[128,512]{1,0:T(8,128)S(1)}, bf16[128,512]{1,0:T(8,128)(2,1)S(1)}, bf16[128,512]{1,0:T(8,128)(2,1)S(1)}, bf16[128,512]{1,0:T(8,128)(2,1)S(1)}) custom-call(f32[128,32]{1,0:T(8,128)S(1)} %get-tuple-element.38.refs_0_, f32[128,8,128]{2,1,0:T(8,128)S(1)} %get-tuple-element.39.refs_1_, f32[128,8,128]{2,1,0:T(8,128)S(1)} %get-tuple-element.40.refs_2_, ...), custom_call_target="tpu_custom_call" | custom-call | tf_op jit(solution)/shard_map/mix/pallas_call | solution.py:223
  35.7 2.0 %collective-permute-start.7 = (bf16[128,512]{1,0:T(8,128)(2,1)S(1)}, bf16[128,512]{1,0:T(8,128)(2,1)S(1)}, u32[]{:S(2)}, u32[]{:S(2)}) collective-permute-start(bf16[128,512]{1,0:T(8,128)(2,1)S(1)} %get-tuple-element.46), channel_id=1, source_target_pairs={{0,3},{1,2},{2,1},{3,0},{4,7},{5,6},{6,5},{7,4},{8,11},{9,10},{10,... | collective-permute-start | bytes 393224 | tf_op jit(solution)/shard_map/ppermute | solution.py:33
  39.1 1.5 %collective-permute-done.5.refs_1_ = bf16[128,512]{1,0:T(8,128)(2,1)S(1)} collective-permute-done((bf16[128,512]{1,0:T(8,128)(2,1)S(1)}, bf16[128,512]{1,0:T(8,128)(2,1)S(1)}, u32[]{:S(2)}, u32[]{:S(2)}) %collective-permute-start.5) | collective-permute-done | bytes 131104 | tf_op jit(solution)/shard_map/ppermute | solution.py:33
  41.0 2.2 %collective-permute-done.7.refs_3_ = bf16[128,512]{1,0:T(8,128)(2,1)S(1)} collective-permute-done((bf16[128,512]{1,0:T(8,128)(2,1)S(1)}, bf16[128,512]{1,0:T(8,128)(2,1)S(1)}, u32[]{:S(2)}, u32[]{:S(2)}) %collective-permute-start.7) | collective-permute-done | bytes 131104 | tf_op jit(solution)/shard_map/ppermute | solution.py:33
  43.5 1.6 %collective-permute-start.8 = (bf16[64,512]{1,0:T(8,128)(2,1)S(1)}, bf16[64,512]{1,0:T(8,128)(2,1)S(1)}, u32[]{:S(2)}, u32[]{:S(2)}) collective-permute-start(bf16[64,512]{1,0:T(8,128)(2,1)S(1)} %get-tuple-element.49), channel_id=1, source_target_pairs={{0,4},{4,0},{8,12},{12,8},{1,5},{5,1},{9,13},{13,9},{2,6},{6,2},{1... | collective-permute-start | bytes 196616 | tf_op jit(solution)/shard_map/ppermute | solution.py:33
  45.1 2.6 %collective-permute-start.9 = (bf16[64,512]{1,0:T(8,128)(2,1)S(1)}, bf16[64,512]{1,0:T(8,128)(2,1)S(1)}, u32[]{:S(2)}, u32[]{:S(2)}) collective-permute-start(bf16[64,512]{1,0:T(8,128)(2,1)S(1)} %get-tuple-element.50), channel_id=1, source_target_pairs={{0,8},{4,12},{8,0},{12,4},{1,9},{5,13},{9,1},{13,5},{2,10},{6,14},... | collective-permute-start | bytes 196616 | tf_op jit(solution)/shard_map/ppermute | solution.py:33
  48.0 4.1 %collective-permute-done.9 = bf16[64,512]{1,0:T(8,128)(2,1)S(1)} collective-permute-done((bf16[64,512]{1,0:T(8,128)(2,1)S(1)}, bf16[64,512]{1,0:T(8,128)(2,1)S(1)}, u32[]{:S(2)}, u32[]{:S(2)}) %collective-permute-start.9) | collective-permute-done | bytes 65568 | tf_op jit(solution)/shard_map/ppermute | solution.py:33
  52.0 1.7 %collective-permute-done.10 = bf16[64,512]{1,0:T(8,128)(2,1)S(1)} collective-permute-done((bf16[64,512]{1,0:T(8,128)(2,1)S(1)}, bf16[64,512]{1,0:T(8,128)(2,1)S(1)}, u32[]{:S(2)}, u32[]{:S(2)}) %collective-permute-start.10) | collective-permute-done | bytes 65568 | tf_op jit(solution)/shard_map/ppermute | solution.py:33
  57.3 5.3 %collective-permute-done.11.refs_1_ = bf16[256,512]{1,0:T(8,128)(2,1)S(1)} collective-permute-done((bf16[256,512]{1,0:T(8,128)(2,1)S(1)}, bf16[256,512]{1,0:T(8,128)(2,1)S(1)}, u32[]{:S(2)}, u32[]{:S(2)}) %collective-permute-start.11) | collective-permute-done | bytes 262176 | tf_op jit(solution)/shard_map/ppermute | solution.py:33
  62.6 3.9 %collective-permute-done.12.refs_2_ = bf16[256,512]{1,0:T(8,128)(2,1)S(1)} collective-permute-done((bf16[256,512]{1,0:T(8,128)(2,1)S(1)}, bf16[256,512]{1,0:T(8,128)(2,1)S(1)}, u32[]{:S(2)}, u32[]{:S(2)}) %collective-permute-start.12) | collective-permute-done | bytes 262176 | tf_op jit(solution)/shard_map/ppermute | solution.py:33
  69.1 19.7 %expert.1 = (f32[256,512]{1,0:T(8,128)S(1)}, f32[256,512]{1,0:T(8,128)}, f32[256,512]{1,0:T(8,128)}, f32[256,512]{1,0:T(8,128)}, bf16[256,512]{1,0:T(8,128)(2,1)...) custom-call(bf16[256,512]{1,0:T(8,128)(2,1)S(1)} %constant_dynamic-update-slice_fusio, ...), custom_call_target="tpu_custom_call" | custom-call | tf_op jit(solution)/shard_map/expert/pallas_call | solution.py:323
  95.9 1.4 %collective-permute-start.20 = (bf16[256,512]{1,0:T(8,128)(2,1)S(1)}, bf16[256,512]{1,0:T(8,128)(2,1)S(1)}, u32[]{:S(2)}, u32[]{:S(2)}) collective-permute-start(bf16[256,512]{1,0:T(8,128)(2,1)S(1)} %add_convert_fusion.2), channel_id=1, source_target_pairs={{0,1},{1,0},{2,3},{3,2},{4,5},{5,4},{6,7},{7,6},{8,9},{9,8},{10,11... | collective-permute-start | bytes 786440 | tf_op jit(solution)/shard_map/ppermute | solution.py:33
  97.4 4.2 %collective-permute-done.24.refs_3_ = bf16[256,512]{1,0:T(8,128)(2,1)S(1)} collective-permute-done((bf16[256,512]{1,0:T(8,128)(2,1)S(1)}, bf16[256,512]{1,0:T(8,128)(2,1)S(1)}, u32[]{:S(2)}, u32[]{:S(2)}) %collective-permute-start.24) | collective-permute-done | bytes 262176 | tf_op jit(solution)/shard_map/ppermute | solution.py:33
  101.6 4.8 %collective-permute-done.22.refs_2_ = bf16[256,512]{1,0:T(8,128)(2,1)S(1)} collective-permute-done((bf16[256,512]{1,0:T(8,128)(2,1)S(1)}, bf16[256,512]{1,0:T(8,128)(2,1)S(1)}, u32[]{:S(2)}, u32[]{:S(2)}) %collective-permute-start.22) | collective-permute-done | bytes 262176 | tf_op jit(solution)/shard_map/ppermute | solution.py:33
  106.6 1.5 %collective-permute-start.26 = (bf16[64,512]{1,0:T(8,128)(2,1)S(1)}, bf16[64,512]{1,0:T(8,128)(2,1)S(1)}, u32[]{:S(2)}, u32[]{:S(2)}) collective-permute-start(bf16[64,512]{1,0:T(8,128)(2,1)S(1)} %get-tuple-element.62), channel_id=1, source_target_pairs={{0,8},{4,12},{8,0},{12,4},{1,9},{5,13},{9,1},{13,5},{2,10},{6,14},... | collective-permute-start | bytes 196616 | tf_op jit(solution)/shard_map/ppermute | solution.py:33
  108.1 2.9 %collective-permute-start.27 = (bf16[64,512]{1,0:T(8,128)(2,1)S(1)}, bf16[64,512]{1,0:T(8,128)(2,1)S(1)}, u32[]{:S(2)}, u32[]{:S(2)}) collective-permute-start(bf16[64,512]{1,0:T(8,128)(2,1)S(1)} %get-tuple-element.63), channel_id=1, source_target_pairs={{0,12},{4,8},{8,4},{12,0},{1,13},{5,9},{9,5},{13,1},{2,14},{6,10},... | collective-permute-start | bytes 196616 | tf_op jit(solution)/shard_map/ppermute | solution.py:33
  111.8 3.3 %collective-permute-done.26.refs_2_ = bf16[64,512]{1,0:T(8,128)(2,1)S(1)} collective-permute-done((bf16[64,512]{1,0:T(8,128)(2,1)S(1)}, bf16[64,512]{1,0:T(8,128)(2,1)S(1)}, u32[]{:S(2)}, u32[]{:S(2)}) %collective-permute-start.26) | collective-permute-done | bytes 65568 | tf_op jit(solution)/shard_map/ppermute | solution.py:33
  (74 shorter events, 31.4 us)
Async XLA Ops:
  0.8 3.8 %collective-permute-start = (bf16[16,1024]{1,0:T(8,128)(2,1)S(1)}, bf16[16,1024]{1,0:T(8,128)(2,1)S(1)}, u32[]{:S(2)}, u32[]{:S(2)}) collective-permute-start(bf16[16,1024]{1,0:T(8,128)(2,1)S(1)} %slice_bitcast_fusion), channel_id=1, source_target_pairs={{0,16},{1,17},{2,18},{3,19},{4,20},{5,21},{6,22},{7,23},{8,24},{9,... | collective-permute-start | bytes 98312 | tf_op jit(solution)/shard_map/ppermute | solution.py:403
  7.4 5.5 %collective-permute-start.1 = (bf16[128,288]{1,0:T(8,128)(2,1)S(1)}, bf16[128,288]{1,0:T(8,128)(2,1)S(1)}, u32[]{:S(2)}, u32[]{:S(2)}) collective-permute-start(bf16[128,288]{1,0:T(8,128)(2,1)S(1)} %get-tuple-element.36.refs_0_), channel_id=1, source_target_pairs={{0,1},{1,0},{2,3},{3,2},{4,5},{5,4},{6,7},{7,6},{8,9},{9,8},{10,11... | collective-permute-start | bytes 221192 | tf_op jit(solution)/shard_map/ppermute | solution.py:33
  9.8 5.7 %collective-permute-start.2 = (bf16[128,288]{1,0:T(8,128)(2,1)S(1)}, bf16[128,288]{1,0:T(8,128)(2,1)S(1)}, u32[]{:S(2)}, u32[]{:S(2)}) collective-permute-start(bf16[128,288]{1,0:T(8,128)(2,1)S(1)} %get-tuple-element.36.refs_0_), channel_id=1, source_target_pairs={{0,2},{1,3},{2,0},{3,1},{4,6},{5,7},{6,4},{7,5},{8,10},{9,11},{10,... | collective-permute-start | bytes 221192 | tf_op jit(solution)/shard_map/ppermute | solution.py:33
  11.3 5.5 %collective-permute-start.3 = (bf16[128,288]{1,0:T(8,128)(2,1)S(1)}, bf16[128,288]{1,0:T(8,128)(2,1)S(1)}, u32[]{:S(2)}, u32[]{:S(2)}) collective-permute-start(bf16[128,288]{1,0:T(8,128)(2,1)S(1)} %get-tuple-element.36.refs_0_), channel_id=1, source_target_pairs={{0,3},{1,2},{2,1},{3,0},{4,7},{5,6},{6,5},{7,4},{8,11},{9,10},{10,... | collective-permute-start | bytes 221192 | tf_op jit(solution)/shard_map/ppermute | solution.py:33
  34.2 6.4 %collective-permute-start.5 = (bf16[128,512]{1,0:T(8,128)(2,1)S(1)}, bf16[128,512]{1,0:T(8,128)(2,1)S(1)}, u32[]{:S(2)}, u32[]{:S(2)}) collective-permute-start(bf16[128,512]{1,0:T(8,128)(2,1)S(1)} %get-tuple-element.44), channel_id=1, source_target_pairs={{0,1},{1,0},{2,3},{3,2},{4,5},{5,4},{6,7},{7,6},{8,9},{9,8},{10,11... | collective-permute-start | bytes 393224 | tf_op jit(solution)/shard_map/ppermute | solution.py:33
  34.9 6.0 %collective-permute-start.6 = (bf16[128,512]{1,0:T(8,128)(2,1)S(1)}, bf16[128,512]{1,0:T(8,128)(2,1)S(1)}, u32[]{:S(2)}, u32[]{:S(2)}) collective-permute-start(bf16[128,512]{1,0:T(8,128)(2,1)S(1)} %get-tuple-element.45), channel_id=1, source_target_pairs={{0,2},{1,3},{2,0},{3,1},{4,6},{5,7},{6,4},{7,5},{8,10},{9,11},{10,... | collective-permute-start | bytes 393224 | tf_op jit(solution)/shard_map/ppermute | solution.py:33
  35.7 7.5 %collective-permute-start.7 = (bf16[128,512]{1,0:T(8,128)(2,1)S(1)}, bf16[128,512]{1,0:T(8,128)(2,1)S(1)}, u32[]{:S(2)}, u32[]{:S(2)}) collective-permute-start(bf16[128,512]{1,0:T(8,128)(2,1)S(1)} %get-tuple-element.46), channel_id=1, source_target_pairs={{0,3},{1,2},{2,1},{3,0},{4,7},{5,6},{6,5},{7,4},{8,11},{9,10},{10,... | collective-permute-start | bytes 393224 | tf_op jit(solution)/shard_map/ppermute | solution.py:33
  43.5 4.5 %collective-permute-start.8 = (bf16[64,512]{1,0:T(8,128)(2,1)S(1)}, bf16[64,512]{1,0:T(8,128)(2,1)S(1)}, u32[]{:S(2)}, u32[]{:S(2)}) collective-permute-start(bf16[64,512]{1,0:T(8,128)(2,1)S(1)} %get-tuple-element.49), channel_id=1, source_target_pairs={{0,4},{4,0},{8,12},{12,8},{1,5},{5,1},{9,13},{13,9},{2,6},{6,2},{1... | collective-permute-start | bytes 196616 | tf_op jit(solution)/shard_map/ppermute | solution.py:33
  45.1 6.9 %collective-permute-start.9 = (bf16[64,512]{1,0:T(8,128)(2,1)S(1)}, bf16[64,512]{1,0:T(8,128)(2,1)S(1)}, u32[]{:S(2)}, u32[]{:S(2)}) collective-permute-start(bf16[64,512]{1,0:T(8,128)(2,1)S(1)} %get-tuple-element.50), channel_id=1, source_target_pairs={{0,8},{4,12},{8,0},{12,4},{1,9},{5,13},{9,1},{13,5},{2,10},{6,14},... | collective-permute-start | bytes 196616 | tf_op jit(solution)/shard_map/ppermute | solution.py:33
  47.7 6.1 %collective-permute-start.10 = (bf16[64,512]{1,0:T(8,128)(2,1)S(1)}, bf16[64,512]{1,0:T(8,128)(2,1)S(1)}, u32[]{:S(2)}, u32[]{:S(2)}) collective-permute-start(bf16[64,512]{1,0:T(8,128)(2,1)S(1)} %get-tuple-element.51), channel_id=1, source_target_pairs={{0,12},{4,8},{8,4},{12,0},{1,13},{5,9},{9,5},{13,1},{2,14},{6,10},... | collective-permute-start | bytes 196616 | tf_op jit(solution)/shard_map/ppermute | solution.py:33
  53.8 8.8 %collective-permute-start.11 = (bf16[256,512]{1,0:T(8,128)(2,1)S(1)}, bf16[256,512]{1,0:T(8,128)(2,1)S(1)}, u32[]{:S(2)}, u32[]{:S(2)}) collective-permute-start(bf16[256,512]{1,0:T(8,128)(2,1)S(1)} %constant_dynamic-update-slice_fusion.refs_0_), channel_id=1, source_target_pairs={{0,1},{1,0},{2,3},{3,2},{4,5},{5,4},{6,7},{7,6},{8,9},{9,8},{10,11... | collective-permute-start | bytes 786440 | tf_op jit(solution)/shard_map/ppermute | solution.py:33
  55.2 11.3 %collective-permute-start.12 = (bf16[256,512]{1,0:T(8,128)(2,1)S(1)}, bf16[256,512]{1,0:T(8,128)(2,1)S(1)}, u32[]{:S(2)}, u32[]{:S(2)}) collective-permute-start(bf16[256,512]{1,0:T(8,128)(2,1)S(1)} %constant_dynamic-update-slice_fusion.refs_0_), channel_id=1, source_target_pairs={{0,2},{1,3},{2,0},{3,1},{4,6},{5,7},{6,4},{7,5},{8,10},{9,11},{10,... | collective-permute-start | bytes 786440 | tf_op jit(solution)/shard_map/ppermute | solution.py:33
  56.0 10.5 %collective-permute-start.13 = (bf16[256,512]{1,0:T(8,128)(2,1)S(1)}, bf16[256,512]{1,0:T(8,128)(2,1)S(1)}, u32[]{:S(2)}, u32[]{:S(2)}) collective-permute-start(bf16[256,512]{1,0:T(8,128)(2,1)S(1)} %constant_dynamic-update-slice_fusion.refs_0_), channel_id=1, source_target_pairs={{0,3},{1,2},{2,1},{3,0},{4,7},{5,6},{6,5},{7,4},{8,11},{9,10},{10,... | collective-permute-start | bytes 786440 | tf_op jit(solution)/shard_map/ppermute | solution.py:33
  57.3 9.7 %collective-permute-start.14 = (bf16[256,512]{1,0:T(8,128)(2,1)S(1)}, bf16[256,512]{1,0:T(8,128)(2,1)S(1)}, u32[]{:S(2)}, u32[]{:S(2)}) collective-permute-start(bf16[256,512]{1,0:T(8,128)(2,1)S(1)} %constant_dynamic-update-slice_fusion.refs_0_), channel_id=1, source_target_pairs={{0,16},{16,0},{1,17},{17,1},{2,18},{18,2},{3,19},{19,3},{4,20},{20... | collective-permute-start | bytes 786440 | tf_op jit(solution)/shard_map/ppermute | solution.py:33
  62.6 4.4 %collective-permute-start.15 = (bf16[256,512]{1,0:T(8,128)(2,1)S(1)}, bf16[256,512]{1,0:T(8,128)(2,1)S(1)}, u32[]{:S(2)}, u32[]{:S(2)}) collective-permute-start(bf16[256,512]{1,0:T(8,128)(2,1)S(1)} %collective-permute-done.11.refs_1_), channel_id=1, source_target_pairs={{0,16},{16,0},{1,17},{17,1},{2,18},{18,2},{3,19},{19,3},{4,20},{20... | collective-permute-start | bytes 786440 | tf_op jit(solution)/shard_map/ppermute | solution.py:33
  88.9 3.9 %collective-permute-start.21 = (bf16[256,512]{1,0:T(8,128)(2,1)S(1)}, bf16[256,512]{1,0:T(8,128)(2,1)S(1)}, u32[]{:S(2)}, u32[]{:S(2)}) collective-permute-start(bf16[256,512]{1,0:T(8,128)(2,1)S(1)} %get-tuple-element.57), channel_id=1, source_target_pairs={{0,16},{16,0},{1,17},{17,1},{2,18},{18,2},{3,19},{19,3},{4,20},{20... | collective-permute-start | bytes 786440 | tf_op jit(solution)/shard_map/ppermute | solution.py:33
  89.3 5.5 %collective-permute-start.19 = (bf16[256,512]{1,0:T(8,128)(2,1)S(1)}, bf16[256,512]{1,0:T(8,128)(2,1)S(1)}, u32[]{:S(2)}, u32[]{:S(2)}) collective-permute-start(bf16[256,512]{1,0:T(8,128)(2,1)S(1)} %get-tuple-element.55), channel_id=1, source_target_pairs={{0,16},{16,0},{1,17},{17,1},{2,18},{18,2},{3,19},{19,3},{4,20},{20... | collective-permute-start | bytes 786440 | tf_op jit(solution)/shard_map/ppermute | solution.py:33
  89.4 7.9 %collective-permute-start.18 = (bf16[256,512]{1,0:T(8,128)(2,1)S(1)}, bf16[256,512]{1,0:T(8,128)(2,1)S(1)}, u32[]{:S(2)}, u32[]{:S(2)}) collective-permute-start(bf16[256,512]{1,0:T(8,128)(2,1)S(1)} %get-tuple-element.53), channel_id=1, source_target_pairs={{0,16},{16,0},{1,17},{17,1},{2,18},{18,2},{3,19},{19,3},{4,20},{20... | collective-permute-start | bytes 786440 | tf_op jit(solution)/shard_map/ppermute | solution.py:33
  91.4 10.2 %collective-permute-start.24 = (bf16[256,512]{1,0:T(8,128)(2,1)S(1)}, bf16[256,512]{1,0:T(8,128)(2,1)S(1)}, u32[]{:S(2)}, u32[]{:S(2)}) collective-permute-start(bf16[256,512]{1,0:T(8,128)(2,1)S(1)} %add_convert_fusion), channel_id=1, source_target_pairs={{0,3},{1,2},{2,1},{3,0},{4,7},{5,6},{6,5},{7,4},{8,11},{9,10},{10,... | collective-permute-start | bytes 786440 | tf_op jit(solution)/shard_map/ppermute | solution.py:33
  94.0 12.4 %collective-permute-start.22 = (bf16[256,512]{1,0:T(8,128)(2,1)S(1)}, bf16[256,512]{1,0:T(8,128)(2,1)S(1)}, u32[]{:S(2)}, u32[]{:S(2)}) collective-permute-start(bf16[256,512]{1,0:T(8,128)(2,1)S(1)} %add_convert_fusion.1), channel_id=1, source_target_pairs={{0,2},{1,3},{2,0},{3,1},{4,6},{5,7},{6,4},{7,5},{8,10},{9,11},{10,... | collective-permute-start | bytes 786440 | tf_op jit(solution)/shard_map/ppermute | solution.py:33
  95.9 10.5 %collective-permute-start.20 = (bf16[256,512]{1,0:T(8,128)(2,1)S(1)}, bf16[256,512]{1,0:T(8,128)(2,1)S(1)}, u32[]{:S(2)}, u32[]{:S(2)}) collective-permute-start(bf16[256,512]{1,0:T(8,128)(2,1)S(1)} %add_convert_fusion.2), channel_id=1, source_target_pairs={{0,1},{1,0},{2,3},{3,2},{4,5},{5,4},{6,7},{7,6},{8,9},{9,8},{10,11... | collective-permute-start | bytes 786440 | tf_op jit(solution)/shard_map/ppermute | solution.py:33
  106.5 5.3 %collective-permute-start.25 = (bf16[64,512]{1,0:T(8,128)(2,1)S(1)}, bf16[64,512]{1,0:T(8,128)(2,1)S(1)}, u32[]{:S(2)}, u32[]{:S(2)}) collective-permute-start(bf16[64,512]{1,0:T(8,128)(2,1)S(1)} %get-tuple-element.61), channel_id=1, source_target_pairs={{0,4},{4,0},{8,12},{12,8},{1,5},{5,1},{9,13},{13,9},{2,6},{6,2},{1... | collective-permute-start | bytes 196616 | tf_op jit(solution)/shard_map/ppermute | solution.py:33
  106.6 8.6 %collective-permute-start.26 = (bf16[64,512]{1,0:T(8,128)(2,1)S(1)}, bf16[64,512]{1,0:T(8,128)(2,1)S(1)}, u32[]{:S(2)}, u32[]{:S(2)}) collective-permute-start(bf16[64,512]{1,0:T(8,128)(2,1)S(1)} %get-tuple-element.62), channel_id=1, source_target_pairs={{0,8},{4,12},{8,0},{12,4},{1,9},{5,13},{9,1},{13,5},{2,10},{6,14},... | collective-permute-start | bytes 196616 | tf_op jit(solution)/shard_map/ppermute | solution.py:33
  108.1 7.1 %collective-permute-start.27 = (bf16[64,512]{1,0:T(8,128)(2,1)S(1)}, bf16[64,512]{1,0:T(8,128)(2,1)S(1)}, u32[]{:S(2)}, u32[]{:S(2)}) collective-permute-start(bf16[64,512]{1,0:T(8,128)(2,1)S(1)} %get-tuple-element.63), channel_id=1, source_target_pairs={{0,12},{4,8},{8,4},{12,0},{1,13},{5,9},{9,5},{13,1},{2,14},{6,10},... | collective-permute-start | bytes 196616 | tf_op jit(solution)/shard_map/ppermute | solution.py:33
  (15 other events, 57.3 us)

commit v2 on v1

v2 whole, which is shorter than its diff:
```python
import functools
import math

import jax
import jax.numpy as jnp
from jax import lax
from jax.experimental import pallas as pl
from jax.experimental.pallas import tpu as pltpu
from jax.sharding import PartitionSpec as P

STATE = 16
DT_RANK = 256
CAP = 64
LOG2E = math.log2(math.e)
VMEM_LIMIT = 20 * 1024 * 1024
F32 = jnp.float32
BF16 = jnp.bfloat16


def params():
    return pltpu.CompilerParams(vmem_limit_bytes=VMEM_LIMIT)


def whole():
    return pl.BlockSpec(memory_space=pltpu.VMEM)


def shaped(shape, dtype):
    return jax.ShapeDtypeStruct(shape, dtype)


def swap(block, axis, k):
    return lax.ppermute(block, axis, [(i, i ^ k) for i in range(lax.axis_size(axis))])


def sigmoid(x):
    return 1.0 / (1.0 + jnp.exp2(x * -LOG2E))


def stay(array):
    return pltpu.with_memory_space_constraint(array, pltpu.HBM)


def hbm():
    return pl.BlockSpec(memory_space=pltpu.HBM)


def unread(arrays):
    return [pl.BlockSpec(memory_space=pl.ANY)] * len(arrays)


def stack_kernel(count, *refs):
    for j, ref in enumerate(refs[:count]):
        rows = ref.shape[0]
        refs[-1][j * rows : (j + 1) * rows, :] = ref[...]


def stack(pieces, after):
    rows, width = pieces[0].shape
    return pl.pallas_call(
        functools.partial(stack_kernel, len(pieces)),
        out_shape=shaped((rows * len(pieces), width), pieces[0].dtype),
        in_specs=[whole()] * len(pieces) + unread(after),
        out_specs=whole(),
        compiler_params=params(),
        cost_estimate=cost(1e6, 0),
        name="stack",
    )(*pieces, *after)


def order_kernel(*refs):
    refs[-1][...] = jnp.zeros_like(refs[-1])


def order(after):
    return pl.pallas_call(
        order_kernel,
        out_shape=shaped((8, 128), F32),
        in_specs=unread(after),
        out_specs=whole(),
        compiler_params=params(),
        cost_estimate=cost(2e10, 0),
        name="order",
    )(*after)


def cost(flops, loaded=0):
    return pl.CostEstimate(flops=int(flops), bytes_accessed=int(loaded), transcendentals=0)


def route_kernel(ids_ref, first_ref, second_ref, chooser_ref):
    rows, slots = first_ref.shape
    own = lax.axis_index("exp")
    ids = jnp.transpose(ids_ref[...].astype(F32)).astype(jnp.int32)
    lanes = lax.broadcasted_iota(jnp.int32, (rows, 128), 1)
    hot = [(ids[:, i : i + 1] == lanes).astype(F32) for i in range(2)]
    earlier = lax.broadcasted_iota(jnp.int32, (rows, rows), 1) < lax.broadcasted_iota(
        jnp.int32, (rows, rows), 0
    )
    ranks = jnp.dot(
        earlier.astype(F32).astype(BF16), (hot[0] + hot[1]).astype(BF16), preferred_element_type=F32
    )
    places = lax.broadcasted_iota(jnp.int32, (rows, slots), 1)
    tables = []
    for i in range(2):
        slot = jnp.sum(ranks * hot[i], axis=1, keepdims=True).astype(jnp.int32)
        place = jnp.bitwise_xor(ids[:, i : i + 1], own) * CAP + slot
        tables.append((place == places).astype(F32))
    first_ref[...] = tables[0].astype(BF16)
    second_ref[...] = tables[1].astype(BF16)
    chooser_ref[...] = jnp.transpose(tables[0] + tables[1]).astype(BF16)


def route(ids, expert_count):
    rows, slots = ids.shape[1], expert_count * CAP
    return pl.pallas_call(
        route_kernel,
        out_shape=(
            shaped((rows, slots), BF16),
            shaped((rows, slots), BF16),
            shaped((slots, rows), BF16),
        ),
        in_specs=[whole()],
        out_specs=[whole()] * 3,
        compiler_params=params(),
        cost_estimate=cost(1e6, 1e6),
        name="route",
    )(ids)


def conv_kernel(
    halo_hbm, x_hbm, taps_hbm, bias_hbm, weight_hbm, xconv_ref, part_ref,
    ext_ref, halo_ref, x_ref, taps_ref, bias_ref, weight_ref, sems,
):
    rows = x_ref.shape[0]
    halo = halo_ref.shape[0]
    count = taps_ref.shape[0]
    copies = [
        pltpu.make_async_copy(source, target, sems.at[i])
        for i, (source, target) in enumerate(
            (
                (halo_hbm.at[rows - halo :], halo_ref),
                (x_hbm, x_ref),
                (taps_hbm, taps_ref),
                (bias_hbm, bias_ref),
                (weight_hbm, weight_ref),
            )
        )
    ]
    for copy in copies:
        copy.start()
    for copy in copies[:4]:
        copy.wait()
    ext_ref[:halo, :] = halo_ref[...].astype(F32)
    ext_ref[halo:, :] = x_ref[...].astype(F32)
    total = bias_ref[...] + taps_ref[count - 1 : count, :] * ext_ref[halo:, :]
    for k in range(count - 1):
        start = halo - (count - 1) + k
        total = total + taps_ref[k : k + 1, :] * ext_ref[start : start + rows, :]
    xconv = (total * sigmoid(total)).astype(BF16)
    xconv_ref[...] = xconv
    copies[4].wait()
    part_ref[...] = lax.dot_general(
        xconv, weight_ref[...], (((1,), (1,)), ((), ())), preferred_element_type=F32
    ).astype(BF16)


def conv(before, x, taps, bias, weight):
    rows, channels = x.shape
    return pl.pallas_call(
        conv_kernel,
        out_shape=(shaped((rows, channels), BF16), shaped((rows, weight.shape[0]), BF16)),
        in_specs=[hbm()] * 5,
        out_specs=[whole()] * 2,
        scratch_shapes=[
            pltpu.VMEM((16 + rows, channels), F32),
            pltpu.VMEM((16, channels), BF16),
            pltpu.VMEM((rows, channels), BF16),
            pltpu.VMEM(taps.shape, F32),
            pltpu.VMEM(bias.shape, F32),
            pltpu.VMEM(weight.shape, BF16),
            pltpu.SemaphoreType.DMA((5,)),
        ],
        compiler_params=params(),
        name="conv",
    )(before, x, taps, bias, weight)


def prepare_kernel(
    xconv_ref, gate_hbm, decay_hbm, skip_hbm, bias_hbm, step_hbm, out_hbm, residual_hbm, gain_hbm, expert_hbm,
    x_ref, silu_ref, rates_ref, skip_ref, bias_ref, step_ref, out_ref, quarter_ref, gain_ref, first_ref,
    gate_ref, decay_ref, flat_ref, residual_ref, sems,
):
    copies = [
        pltpu.make_async_copy(source, target, sems.at[i])
        for i, (source, target) in enumerate(
            (
                (gate_hbm, gate_ref),
                (decay_hbm, decay_ref),
                (skip_hbm, flat_ref),
                (residual_hbm, residual_ref),
                (bias_hbm, bias_ref),
                (gain_hbm, gain_ref),
                (step_hbm, step_ref),
                (out_hbm, out_ref),
                (expert_hbm.at[0, 0], first_ref),
            )
        )
    ]
    for copy in copies:
        copy.start()
    tiles = x_ref.shape[1]
    xfloat = xconv_ref[...].astype(F32)
    for j in range(tiles):
        x_ref[:, j, :] = xfloat[:, j * 128 : (j + 1) * 128]
    for copy in copies[:4]:
        copy.wait()
    gate = gate_ref[...].astype(F32)
    silu_ref[...] = gate * sigmoid(gate)
    rates = -LOG2E * jnp.exp(decay_ref[...])
    for j in range(tiles):
        cut = slice(j * 128, (j + 1) * 128)
        rates_ref[:, j, :] = rates[:, cut]
        skip_ref[j : j + 1, :] = flat_ref[:, cut]
    width = quarter_ref.shape[1]
    start = pl.multiple_of(lax.axis_index("tp") * width, 128)
    quarter_ref[...] = residual_ref[:, pl.ds(start, width)].astype(F32)
    for copy in copies[4:]:
        copy.wait()


def prepare(parts, xconv, gate, decay_log, skip, bias, step_weight, out_weight, residual, gain, experts):
    rows, channels = xconv.shape
    tiles = channels // 128
    return pl.pallas_call(
        prepare_kernel,
        out_shape=(
            shaped((rows, tiles, 128), F32),
            shaped((rows, channels), F32),
            shaped((STATE, tiles, 128), F32),
            shaped((tiles, 128), F32),
            shaped(bias.shape, F32),
            shaped(step_weight.shape, BF16),
            shaped(out_weight.shape, BF16),
            shaped((rows, residual.shape[1] // parts), F32),
            shaped(gain.shape, F32),
            shaped(experts.shape[2:], BF16),
        ),
        in_specs=[whole()] + [hbm()] * 9,
        out_specs=[whole()] * 10,
        scratch_shapes=[
            pltpu.VMEM((rows, channels), BF16),
            pltpu.VMEM(decay_log.shape, F32),
            pltpu.VMEM(skip.shape, F32),
            pltpu.VMEM(residual.shape, BF16),
            pltpu.SemaphoreType.DMA((9,)),
        ],
        compiler_params=params(),
        cost_estimate=cost(1e6, 14e6),
        name="prepare",
    )(xconv, gate, decay_log, skip, bias, step_weight, out_weight, residual, gain, experts)


def scan_kernel(parts, *refs):
    part_refs = refs[:parts]
    x_ref, rates_ref, gain_ref, bias_ref, weight_ref, expert_hbm = refs[parts : parts + 6]
    y_ref, elapsed_ref, maps_ref, state_ref, second_ref = refs[parts + 6 : parts + 11]
    steps_ref, scalars, sem, expert_sem = refs[parts + 11 :]
    rows, tiles, _ = x_ref.shape
    expert_copy = pltpu.make_async_copy(expert_hbm.at[0, 1], second_ref, expert_sem)
    expert_copy.start()
    proj = part_refs[0][...].astype(F32)
    for ref in part_refs[1:]:
        proj = proj + ref[...].astype(F32)
    maps_ref[...] = proj[:, DT_RANK:]
    copy = pltpu.make_async_copy(maps_ref, scalars, sem)
    copy.start()
    rank = proj[:, :DT_RANK].astype(BF16)
    raw = jnp.dot(rank, weight_ref[...], preferred_element_type=F32) + bias_ref[...]
    steps = jnp.maximum(raw, 0.0) + jnp.log1p(jnp.exp(-jnp.abs(raw)))
    for j in range(tiles):
        steps_ref[:, j, :] = steps[:, j * 128 : (j + 1) * 128]
    copy.wait()
    gain = gain_ref[...]

    def step(t, carry):
        elapsed, states = carry
        now = steps_ref[t]
        x = x_ref[t]
        driven = now * x
        sums = [gain * x, None]
        new = []
        for n in range(STATE):
            state = jnp.exp2(now * rates_ref[n]) * states[n] + driven * scalars[t, n]
            new.append(state)
            term = state * scalars[t, STATE + n]
            sums[n % 2] = term if sums[n % 2] is None else sums[n % 2] + term
        elapsed = elapsed + now
        y_ref[t] = sums[0] + sums[1]
        elapsed_ref[t] = elapsed
        return elapsed, tuple(new)

    zero = jnp.zeros((tiles, 128), F32)
    _, states = lax.fori_loop(0, rows, step, (zero, (zero,) * STATE), unroll=4)
    for n in range(STATE):
        state_ref[n] = states[n]
    expert_copy.wait()


def scan(pieces, x, rates, gain, bias, weight, experts):
    rows, tiles, _ = x.shape
    return pl.pallas_call(
        functools.partial(scan_kernel, len(pieces)),
        out_shape=(
            shaped((rows, tiles, 128), F32),
            shaped((rows, tiles, 128), F32),
            shaped((rows, 2 * STATE), F32),
            shaped((STATE, tiles, 128), F32),
            shaped(experts.shape[2:], BF16),
        ),
        in_specs=[whole()] * (len(pieces) + 5) + [hbm()],
        out_specs=[whole()] * 5,
        scratch_shapes=[
            pltpu.VMEM((rows, tiles, 128), F32),
            pltpu.SMEM((rows, 2 * STATE), F32),
            pltpu.SemaphoreType.DMA,
            pltpu.SemaphoreType.DMA,
        ],
        compiler_params=params(),
        cost_estimate=cost(1e6, 14e6),
        name="scan",
    )(*pieces, x, rates, gain, bias, weight, experts)


def mix_kernel(parts, *refs):
    maps_ref, y_ref, elapsed_ref, rates_ref, state_ref, silu_ref, quarter_ref, weight_ref, expert_hbm = refs[:9]
    own_ref, sent, third_ref = refs[9], refs[10 : 9 + parts], refs[9 + parts]
    sum_ref, gated_ref, scalars, sem, expert_sem = refs[10 + parts :]
    copy = pltpu.make_async_copy(maps_ref, scalars, sem)
    copy.start()
    expert_copy = pltpu.make_async_copy(expert_hbm.at[0, 2], third_ref, expert_sem)
    expert_copy.start()
    rows, tiles, _ = y_ref.shape
    copy.wait()

    def step(t, carry):
        elapsed = elapsed_ref[t]
        sums = [y_ref[t], None]
        for n in range(STATE):
            term = jnp.exp2(elapsed * rates_ref[n]) * state_ref[n] * scalars[t, STATE + n]
            sums[n % 2] = term if sums[n % 2] is None else sums[n % 2] + term
        sum_ref[t] = sums[0] + sums[1]
        return carry

    lax.fori_loop(0, rows, step, 0, unroll=4)
    for j in range(tiles):
        cut = slice(j * 128, (j + 1) * 128)
        gated_ref[:, cut] = (sum_ref[:, j, :] * silu_ref[:, cut]).astype(BF16)
    own = lax.axis_index("tp")
    width = own_ref.shape[1]
    for k in range(parts):
        start = pl.multiple_of(jnp.bitwise_xor(own, k) * width, 128)
        product = jnp.dot(
            gated_ref[...], weight_ref[:, pl.ds(start, width)], preferred_element_type=F32
        )
        if k == 0:
            own_ref[...] = product + quarter_ref[...]
        else:
            sent[k - 1][...] = product.astype(BF16)
    expert_copy.wait()


def mix(parts, maps, y, elapsed, rates, state, silu, quarter, weight, experts):
    rows, tiles, _ = y.shape
    width = weight.shape[1] // parts
    return pl.pallas_call(
        functools.partial(mix_kernel, parts),
        out_shape=[shaped((rows, width), F32)]
        + [shaped((rows, width), BF16)] * (parts - 1)
        + [shaped(experts.shape[2:], BF16)],
        in_specs=[whole()] * 8 + [hbm()],
        out_specs=[whole()] * (parts + 1),
        scratch_shapes=[
            pltpu.VMEM((rows, tiles, 128), F32),
            pltpu.VMEM((rows, tiles * 128), BF16),
            pltpu.SMEM(maps.shape, F32),
            pltpu.SemaphoreType.DMA,
            pltpu.SemaphoreType.DMA,
        ],
        compiler_params=params(),
        cost_estimate=cost(1e6, 12e6),
        name="mix",
    )(maps, y, elapsed, rates, state, silu, quarter, weight, experts)


def pick_kernel(parts, *refs):
    own_ref, arrived, chooser_ref = refs[0], refs[1:parts], refs[parts]
    stream_ref, out_refs = refs[parts + 1], refs[parts + 2 :]
    total = own_ref[...]
    for ref in arrived:
        total = total + ref[...].astype(F32)
    stream = total.astype(BF16)
    stream_ref[...] = stream
    picked = jnp.dot(chooser_ref[...], stream, preferred_element_type=F32).astype(BF16)
    for j, ref in enumerate(out_refs):
        ref[...] = picked[j * CAP : (j + 1) * CAP, :]


def pick(own, arrived, chooser):
    rows, width = own.shape
    experts = chooser.shape[0] // CAP
    return pl.pallas_call(
        functools.partial(pick_kernel, 1 + len(arrived)),
        out_shape=[shaped((rows, width), BF16)] + [shaped((CAP, width), BF16)] * experts,
        in_specs=[whole()] * (2 + len(arrived)),
        out_specs=[whole()] * (1 + experts),
        compiler_params=params(),
        cost_estimate=cost(1e6, 1e6),
        name="pick",
    )(own, *arrived, chooser)


def norm_kernel(parts, *refs):
    x_refs, gain_ref, out_ref = refs[:parts], refs[parts], refs[-1]
    width = x_refs[0].shape[1]
    own = lax.axis_index("tp")
    pieces = [ref[...].astype(F32) for ref in x_refs]
    total = sum(jnp.sum(piece * piece, axis=1, keepdims=True) for piece in pieces)
    scale = lax.rsqrt(total / (width * parts) + 1e-6)
    for k, piece in enumerate(pieces):
        start = pl.multiple_of(jnp.bitwise_xor(own, k) * width, 128)
        out_ref[:, pl.ds(start, width)] = (
            piece * scale * gain_ref[:, pl.ds(start, width)]
        ).astype(BF16)


def norm(pieces, gain, after):
    rows, width = pieces[0].shape
    return pl.pallas_call(
        functools.partial(norm_kernel, len(pieces)),
        out_shape=shaped((rows, width * len(pieces)), BF16),
        in_specs=[whole()] * (len(pieces) + 1) + unread(after),
        out_specs=whole(),
        compiler_params=params(),
        cost_estimate=cost(1e6, 1e6),
        name="norm",
    )(*pieces, gain, *after)


def hidden_kernel(x_ref, gate_ref, up_ref, *refs):
    hidden_ref = refs[-1]
    width = gate_ref.shape[1]
    size = 256 if width % 256 == 0 else width
    for i in range(width // size):
        cut = slice(i * size, (i + 1) * size)
        gate = jnp.dot(x_ref[...], gate_ref[:, cut], preferred_element_type=F32)
        up = jnp.dot(x_ref[...], up_ref[:, cut], preferred_element_type=F32)
        hidden_ref[:, cut] = (gate * sigmoid(gate) * up).astype(BF16)


def hidden_units(x, gate, up, after):
    rows, width = x.shape[0], gate.shape[1]
    return pl.pallas_call(
        hidden_kernel,
        out_shape=shaped((rows, width), BF16),
        in_specs=[whole()] * 3 + unread(after),
        out_specs=whole(),
        compiler_params=params(),
        cost_estimate=cost(1e6, 0),
        name="hidden",
    )(x, gate, up, *after)


def down_kernel(hidden_own_ref, hidden_other_ref, down_ref, *refs):
    own_ref, other_ref, hidden_ref = refs[-3:]
    rows = hidden_own_ref.shape[0]
    hidden_ref[:rows, :] = hidden_own_ref[...]
    hidden_ref[rows:, :] = hidden_other_ref[...]
    size = 256
    for i in range(down_ref.shape[0] // size):
        cut = slice(i * size, (i + 1) * size)
        product = lax.dot_general(
            hidden_ref[...], down_ref[cut, :], (((1,), (1,)), ((), ())), preferred_element_type=F32
        )
        own_ref[:, cut] = product[:rows]
        other_ref[:, cut] = product[rows:].astype(BF16)


def down_sums(hidden_own, hidden_other, down, after):
    rows, width = hidden_own.shape
    model = down.shape[0]
    return pl.pallas_call(
        down_kernel,
        out_shape=(shaped((rows, model), F32), shaped((rows, model), BF16)),
        in_specs=[whole()] * 3 + unread(after),
        out_specs=[whole()] * 2,
        scratch_shapes=[pltpu.VMEM((2 * rows, width), BF16)],
        compiler_params=params(),
        cost_estimate=cost(1e6, 0),
        name="down",
    )(hidden_own, hidden_other, down, *after)


def join_kernel(parts, own_ref, other_ref, *refs):
    out_refs = refs[-parts:]
    width = out_refs[0].shape[1]
    own = lax.axis_index("tp")
    for k, ref in enumerate(out_refs):
        cut = pl.ds(pl.multiple_of(jnp.bitwise_xor(own, k) * width, 128), width)
        ref[...] = (own_ref[:, cut] + other_ref[:, cut].astype(F32)).astype(ref.dtype)


def join(parts, own, other, after):
    rows, model = own.shape
    return pl.pallas_call(
        functools.partial(join_kernel, parts),
        out_shape=[shaped((rows, model // parts), BF16 if k else F32) for k in range(parts)],
        in_specs=[whole()] * 2 + unread(after),
        out_specs=[whole()] * parts,
        compiler_params=params(),
        cost_estimate=cost(1e6, 1e6),
        name="join",
    )(own, other, *after)


def total_kernel(parts, *refs):
    total = refs[0][...].astype(F32)
    for ref in refs[1:parts]:
        total = total + ref[...].astype(F32)
    total = total.astype(BF16)
    for j, ref in enumerate(refs[parts:]):
        ref[...] = total[j * CAP : (j + 1) * CAP, :]


def totals(pieces):
    rows, width = pieces[0].shape
    count = rows // CAP
    return pl.pallas_call(
        functools.partial(total_kernel, len(pieces)),
        out_shape=[shaped((CAP, width), BF16)] * count,
        in_specs=[whole()] * len(pieces),
        out_specs=[whole()] * count,
        compiler_params=params(),
        cost_estimate=cost(1e6, 1e6),
        name="totals",
    )(*pieces)


def blend_kernel(experts, *refs):
    back = refs[:experts]
    stream_ref, first_ref, second_ref, gates_ref, out_ref, rows_ref = refs[experts:]
    for j, ref in enumerate(back):
        rows_ref[j * CAP : (j + 1) * CAP, :] = ref[...]
    rows = rows_ref[...]
    gates = jnp.transpose(gates_ref[...])
    moe = gates[:, 0:1] * jnp.dot(first_ref[...], rows, preferred_element_type=F32)
    moe = moe + gates[:, 1:2] * jnp.dot(second_ref[...], rows, preferred_element_type=F32)
    out_ref[...] = (stream_ref[...].astype(F32) + moe).astype(BF16)


def blend(back, stream, first, second, gates):
    experts, width = len(back), stream.shape[1]
    return pl.pallas_call(
        functools.partial(blend_kernel, experts),
        out_shape=shaped(stream.shape, BF16),
        in_specs=[whole()] * (experts + 4),
        out_specs=whole(),
        scratch_shapes=[pltpu.VMEM((experts * CAP, width), BF16)],
        compiler_params=params(),
        name="blend",
    )(*back, stream, first, second, gates)


def expert(tp, x_own, gate, up, down, after_start, after_sums):
    x_other = swap(x_own, "ctx", 1)
    hidden_own = hidden_units(x_own, gate, up, after_start)
    hidden_other = hidden_units(x_other, gate, up, [hidden_own])
    sum_own, sum_other = down_sums(hidden_own, hidden_other, down, [])
    after_sums = [order([sum_other, *after_sums])] if after_sums else []
    joined = join(tp, sum_own, swap(sum_other, "ctx", 1), after_sums)
    return sum_own, joined


def body(
    conv_in,
    gate_in,
    residual,
    conv_weight,
    conv_bias,
    proj_weight,
    step_weight,
    step_bias,
    decay_log,
    skip_gain,
    out_weight,
    norm_gain,
    expert_ids,
    route_gates,
    expert_weight,
):
    tp, experts = lax.axis_size("tp"), lax.axis_size("exp")
    local = conv_in[0]
    before = lax.ppermute(local, "ctx", [(0, 1)])
    expert_weight = stay(expert_weight)
    xconv, part = conv(
        stay(before), stay(local), stay(conv_weight), stay(conv_bias[None]), stay(proj_weight.T)
    )
    parts = [part] + [swap(part, "tp", k) for k in range(1, tp)]
    x, silu, rates, skip, bias, step_w, out_w, quarter, gain, gate_w = prepare(
        tp, xconv, stay(gate_in[0]), stay(decay_log), stay(skip_gain[None]), stay(step_bias[None]),
        stay(step_weight), stay(out_weight), stay(residual[0]), stay(norm_gain[None]), expert_weight,
    )
    y, elapsed, maps, state, up_w = scan(parts, x, rates, skip, bias, step_w, expert_weight)
    before = lax.ppermute(state, "ctx", [(0, 1)])
    own, *sent, down_w = mix(
        tp, maps, y, elapsed, rates, before, silu, quarter, out_w, expert_weight
    )
    arrived = [swap(piece, "tp", k) for k, piece in enumerate(sent, 1)]
    first, second, chooser = route(expert_ids[0].T, experts)
    stream, *picked = pick(own, arrived, chooser)
    rows = [picked[0]] + [swap(picked[j], "exp", j) for j in range(1, experts)]
    piece_a = stack(rows[: experts // 2], [])
    piece_b = stack(rows[experts // 2 :], [piece_a])
    rows_a, rows_b = [piece_a], [piece_b]
    both = order([piece_a, piece_b])
    for k in range(1, tp):
        top = 1 << (k.bit_length() - 1)
        passed = rows_a[k ^ top]
        rows_a.append(swap(passed if k == top else stack([passed], [both]), "tp", top))
        rows_b.append(swap(piece_b, "tp", k))
    x_a = norm(rows_a, gain, [piece_b])
    own_a, joined_a = expert(tp, x_a, gate_w, up_w, down_w, [], [])
    summed_a = [joined_a[0]] + [swap(joined_a[k], "tp", k) for k in range(1, tp)]
    back = totals(summed_a)
    x_b = norm(rows_b, gain, [own_a])
    _, joined_b = expert(tp, x_b, gate_w, up_w, down_w, [joined_a[0]], [back[0]])
    back += totals([joined_b[0]] + [swap(joined_b[k], "tp", k) for k in range(1, tp)])
    back = [back[0]] + [swap(back[j], "exp", j) for j in range(1, experts)]
    return blend(back, stream, first, second, route_gates[0].T)[None]


def solution(mesh):
    placed = (
        P("exp", "ctx", "tp"),
        P("exp", "ctx", "tp"),
        P("exp", "ctx", None),
        P(None, "tp"),
        P("tp"),
        P("tp", None),
        P(None, "tp"),
        P("tp"),
        P(None, "tp"),
        P("tp"),
        P("tp", None),
        P(),
        P("exp", "ctx", None),
        P("exp", "ctx", None),
        P("exp", None, None, ("ctx", "tp")),
    )
    return jax.shard_map(
        body, mesh=mesh, in_specs=placed, out_specs=P("exp", "ctx", "tp"), check_vma=False
    )
```

time: 117 us -> 96.6 us (0.83)
  waiting for transfers between devices: 40.4 us -> 28.1 us
  local copies, waits for them, and re-layouts: 11.4 us -> 0.7 us
  starting transfers between devices: 28.7 us -> 35 us
  other arithmetic: 3.41 us -> 0 us
    ppermute x26 -> x28, waiting for transfers between devices: 39.6 us -> 25.9 us  [swap(): lax.ppermute(block, axis, [(i, i ^ k) for i in range(lax.axis_size(axis))])]
    unnamed x28 -> x6, local copies, waits for them, and re-layouts: 10.6 us -> 0.7 us
    ppermute x26 -> x28, starting transfers between devices: 25.1 us -> 31.3 us  [swap(): lax.ppermute(block, axis, [(i, i ^ k) for i in range(lax.axis_size(axis))])]
    convert_element_type x3 -> x0, other arithmetic: 3.33 us -> none  [body(): summed.append(piece if k == 0 else swap(piece.astype(BF16), 'tp', k))]
    pallas_call x1, Pallas kernels: 0.52 us -> 2.03 us  [conv(): pl.pallas_call(conv_kernel, out_shape=(shaped((rows, channels), BF16), sh...]
    ppermute x1, waiting for transfers between devices: 0.01 us -> 1.34 us  [body(): before = lax.ppermute(local, 'ctx', [(0, 1)])]
    pallas_call x1 -> x16, Pallas kernels: 19.7 us -> 18.4 us  [the longest x4 8.59 us: hidden_units(): pl.pallas_call(hidden_kernel, out_shape=shaped((rows, width), BF16), in_s...]
  transfers between devices with their start and end apart: 28 -> 30, of which waited for: 18 -> 15; matrix products, arithmetic and copies ran while one was open for 5% -> 0% of each run, Pallas kernels for 0% -> 19%
where the time goes in v2:
time: 96.6 us; the launch traced here: 96.5 us
  starting transfers between devices  35 us (36%)
  Pallas kernels  32.4 us (34%)
  waiting for transfers between devices  28.1 us (29%)
    ppermute x28, starting transfers between devices, swap(): lax.ppermute(block, axis, [(i, i ^ k) for i in range(lax.axis_size(axis))])  31.3 us
    ppermute x28, waiting for transfers between devices, swap(): lax.ppermute(block, axis, [(i, i ^ k) for i in range(lax.axis_size(axis))])  25.9 us
    pallas_call x4, Pallas kernels, hidden_units(): pl.pallas_call(hidden_kernel, out_shape=shaped((rows, width), BF16), in_s...  8.59 us
    pallas_call x1, Pallas kernels, scan(): pl.pallas_call(functools.partial(scan_kernel, len(pieces)), out_shape=(sh...  5.15 us
    pallas_call x1, Pallas kernels, prepare(): pl.pallas_call(prepare_kernel, out_shape=(shaped((rows, tiles, 128), F32)...  4.9 us
    pallas_call x1, Pallas kernels, mix(): pl.pallas_call(functools.partial(mix_kernel, parts), out_shape=[shaped((r...  4.84 us
    pallas_call x2, Pallas kernels, down_sums(): pl.pallas_call(down_kernel, out_shape=(shaped((rows, model), F32), shaped...  4.17 us
    ppermute x1, starting transfers between devices, body(): before = lax.ppermute(local, 'ctx', [(0, 1)])  2.36 us
  transfers between devices with their start and end apart: 30, of which 15 were waited for; matrix products, arithmetic and copies ran while one was open for 0% of the time, Pallas kernels for 19%

profile of v2, /device:TPU:0, one launch (start us, length us, event | category | flops | bytes accessed | tf_op | source)
XLA Modules:
  0.0 96.5 jit_solution(819626430774693589)
XLA Ops:
  0.0 2.4 %collective-permute-start = (bf16[128,1024]{1,0:T(8,128)(2,1)}, bf16[128,1024]{1,0:T(8,128)(2,1)S(1)}, u32[]{:S(2)}, u32[]{:S(2)}) collective-permute-start(bf16[128,1024]{1,0:T(8,128)(2,1)} %bitcast.20), channel_id=1, source_target_pairs={{0,16},{1,17},{2,18},{3,19},{4,20},{5,21},{6,22},{7,23},{8,24},{9,... | collective-permute-start | bytes 786440 | tf_op jit(solution)/shard_map/ppermute | solution.py:603
  4.4 2.0 %conv.1 = (bf16[128,1024]{1,0:T(8,128)(2,1)S(1)}, bf16[128,288]{1,0:T(8,128)(2,1)S(1)}) custom-call(bf16[128,1024]{1,0:T(8,128)(2,1)} %copy-done.2, bf16[128,1024]{1,0:T(8,128)(2,1)} %bitcast.21, f32[4,1024]{1,0:T(4,128)} %taps_hbm.1, f32[1,1024]{1,0:T(1,128)} %bitcast.23, bf16[288,1024]{1,0:T(8,128)(2,1)} %bitcast.17), custom_call_target="tpu_custom_call" | custom-call | tf_op jit(solution)/shard_map/conv/pallas_call | solution.py:170
  6.4 2.4 %collective-permute-start.1 = (bf16[128,288]{1,0:T(8,128)(2,1)S(1)}, bf16[128,288]{1,0:T(8,128)(2,1)S(1)}, u32[]{:S(2)}, u32[]{:S(2)}) collective-permute-start(bf16[128,288]{1,0:T(8,128)(2,1)S(1)} %get-tuple-element.51.refs_0_), channel_id=1, source_target_pairs={{0,1},{1,0},{2,3},{3,2},{4,5},{5,4},{6,7},{7,6},{8,9},{9,8},{10,11... | collective-permute-start | bytes 221192 | tf_op jit(solution)/shard_map/ppermute | solution.py:33
  10.4 4.9 %prepare.1 = (f32[128,8,128]{2,1,0:T(8,128)S(1)}, f32[128,1024]{1,0:T(8,128)S(1)}, f32[16,8,128]{2,1,0:T(8,128)S(1)}, f32[8,128]{1,0:T(8,128)S(1)}, f32[1,1024]{...) custom-call(bf16[128,1024]{1,0:T(8,128)(2,1)S(1)} %get-tuple-element, ...), custom_call_target="tpu_custom_call" | custom-call | flops 1000000 | bytes 14000000 | tf_op jit(solution)/shard_map/prepare/pallas_call | solution.py:235
  15.9 5.2 %scan.1 = (f32[128,8,128]{2,1,0:T(8,128)S(1)}, f32[128,8,128]{2,1,0:T(8,128)S(1)}, f32[128,32]{1,0:T(8,128)S(1)}, f32[16,8,128]{2,1,0:T(8,128)S(1)}, bf16[2048,1792]{1,0:T(8,128)(2,1)S(1)}) custom-call(bf16[128,288]{1,0:T(8,128)(2,1)S(1)} %get-tuple-element.51.refs_0_, bf16[128,288]{1,0:T(8,128)(2,1)S(1)} %collective-permute-done.1.refs_1_, ...), custom_call_target="tpu_custom_call" | custom-call | flops 1000000 | bytes 14000000 | tf_op jit(solution)/shard_map/scan/pallas_call | solution.py:312
  23.2 4.8 %mix.1 = (f32[128,512]{1,0:T(8,128)S(1)}, bf16[128,512]{1,0:T(8,128)(2,1)S(1)}, bf16[128,512]{1,0:T(8,128)(2,1)S(1)}, bf16[128,512]{1,0:T(8,128)(2,1)S(1)}, bf16[2048,1792]{1,0:T(8,128)(2,1)S(1)}) custom-call(f32[128,32]{1,0:T(8,128)S(1)} %get-tuple-element.58.refs_0_, f32[128,8,128]{2,1,0:T(8,128)S(1)} %get-tuple-element.59.refs_1_, ...), custom_call_target="tpu_custom_call" | custom-call | flops 1000000 | bytes 12000000 | tf_op jit(solution)/shard_map/mix/pallas_call | solution.py:376
  28.1 1.6 %collective-permute-start.5 = (bf16[128,512]{1,0:T(8,128)(2,1)S(1)}, bf16[128,512]{1,0:T(8,128)(2,1)S(1)}, u32[]{:S(2)}, u32[]{:S(2)}) collective-permute-start(bf16[128,512]{1,0:T(8,128)(2,1)S(1)} %get-tuple-element.66), channel_id=1, source_target_pairs={{0,1},{1,0},{2,3},{3,2},{4,5},{5,4},{6,7},{7,6},{8,9},{9,8},{10,11... | collective-permute-start | bytes 393224 | tf_op jit(solution)/shard_map/ppermute | solution.py:33
  32.2 1.9 %collective-permute-done.5.refs_1_ = bf16[128,512]{1,0:T(8,128)(2,1)S(1)} collective-permute-done((bf16[128,512]{1,0:T(8,128)(2,1)S(1)}, bf16[128,512]{1,0:T(8,128)(2,1)S(1)}, u32[]{:S(2)}, u32[]{:S(2)}) %collective-permute-start.5) | collective-permute-done | bytes 131104 | tf_op jit(solution)/shard_map/ppermute | solution.py:33
  34.2 3.8 %collective-permute-done.6.refs_2_ = bf16[128,512]{1,0:T(8,128)(2,1)S(1)} collective-permute-done((bf16[128,512]{1,0:T(8,128)(2,1)S(1)}, bf16[128,512]{1,0:T(8,128)(2,1)S(1)}, u32[]{:S(2)}, u32[]{:S(2)}) %collective-permute-start.6) | collective-permute-done | bytes 131104 | tf_op jit(solution)/shard_map/ppermute | solution.py:33
  38.3 1.6 %collective-permute-start.8 = (bf16[64,512]{1,0:T(8,128)(2,1)S(1)}, bf16[64,512]{1,0:T(8,128)(2,1)S(1)}, u32[]{:S(2)}, u32[]{:S(2)}) collective-permute-start(bf16[64,512]{1,0:T(8,128)(2,1)S(1)} %get-tuple-element.71), channel_id=1, source_target_pairs={{0,4},{4,0},{8,12},{12,8},{1,5},{5,1},{9,13},{13,9},{2,6},{6,2},{1... | collective-permute-start | bytes 196616 | tf_op jit(solution)/shard_map/ppermute | solution.py:33
  39.9 2.6 %collective-permute-start.11 = (bf16[64,512]{1,0:T(8,128)(2,1)S(1)}, bf16[64,512]{1,0:T(8,128)(2,1)S(1)}, u32[]{:S(2)}, u32[]{:S(2)}) collective-permute-start(bf16[64,512]{1,0:T(8,128)(2,1)S(1)} %get-tuple-element.72), channel_id=1, source_target_pairs={{0,8},{4,12},{8,0},{12,4},{1,9},{5,13},{9,1},{13,5},{2,10},{6,14},... | collective-permute-start | bytes 196616 | tf_op jit(solution)/shard_map/ppermute | solution.py:33
  46.5 2.1 %collective-permute-done.12.refs_1_ = bf16[64,512]{1,0:T(8,128)(2,1)S(1)} collective-permute-done((bf16[64,512]{1,0:T(8,128)(2,1)S(1)}, bf16[64,512]{1,0:T(8,128)(2,1)S(1)}, u32[]{:S(2)}, u32[]{:S(2)}) %collective-permute-start.12) | collective-permute-done | bytes 65568 | tf_op jit(solution)/shard_map/ppermute | solution.py:33
  50.2 3.4 %collective-permute-done.13.refs_3_ = bf16[128,512]{1,0:T(8,128)(2,1)S(1)} collective-permute-done((bf16[128,512]{1,0:T(8,128)(2,1)S(1)}, bf16[128,512]{1,0:T(8,128)(2,1)S(1)}, u32[]{:S(2)}, u32[]{:S(2)}) %collective-permute-start.13) | collective-permute-done | bytes 131104 | tf_op jit(solution)/shard_map/ppermute | solution.py:33
  57.5 2.1 %hidden.4.refs_0_.hidden_own_ref = bf16[128,1792]{1,0:T(8,128)(2,1)S(1)} custom-call(bf16[128,2048]{1,0:T(8,128)(2,1)S(1)} %norm.2.x_ref, bf16[2048,1792]{1,0:T(8,128)(2,1)S(1)} %get-tuple-element.75.gate_ref, bf16[2048,1792]{1,0:T(8,128)(2,1)S(1)} %get-tuple-element.76.up_ref), custom_call_target="tpu_custom_call" | custom-call | flops 1000000 | tf_op jit(solution)/shard_map/hidden/pallas_call | solution.py:463
  59.6 2.1 %hidden.5.hidden_other_ref = bf16[128,1792]{1,0:T(8,128)(2,1)S(1)} custom-call(bf16[128,2048]{1,0:T(8,128)(2,1)S(1)} %collective-permute-done.14.x_ref, bf16[2048,1792]{1,0:T(8,128)(2,1)S(1)} %get-tuple-element.75.gate_ref, bf16[2048,1792]{1,0:T(8,128)(2,1)S(1)} %get-tuple-element.76.up_ref, bf16[128,1792]{1,0:T(8,128)(2,1)S(1)} %hidden.4.refs_0_.hidden_own_ref), custom_call_target="tpu_custom_call" | custom-call | flops 1000000 | tf_op jit(solution)/shard_map/hidden/pallas_call | solution.py:463
  61.7 2.1 %down.2 = (f32[128,2048]{1,0:T(8,128)S(1)}, bf16[128,2048]{1,0:T(8,128)(2,1)S(1)}) custom-call(bf16[128,1792]{1,0:T(8,128)(2,1)S(1)} %hidden.4.refs_0_.hidden_own_ref, bf16[128,1792]{1,0:T(8,128)(2,1)S(1)} %hidden.5.hidden_other_ref, bf16[2048,1792]{1,0:T(8,128)(2,1)S(1)} %get-tuple-element.77.down_ref), custom_call_target="tpu_custom_call" | custom-call | flops 1000000 | tf_op jit(solution)/shard_map/down/pallas_call | solution.py:492
  69.4 2.1 %hidden.6.refs_0_.hidden_own_ref = bf16[128,1792]{1,0:T(8,128)(2,1)S(1)} custom-call(bf16[128,2048]{1,0:T(8,128)(2,1)S(1)} %norm.3.x_ref, bf16[2048,1792]{1,0:T(8,128)(2,1)S(1)} %get-tuple-element.75.gate_ref, bf16[2048,1792]{1,0:T(8,128)(2,1)S(1)} %get-tuple-element.76.up_ref, f32[128,512]{1,0:T(8,128)S(1)} %get-tuple-element.80.refs_0_), custom_call_target="tpu_custom_call" | custom-call | flops 1000000 | tf_op jit(solution)/shard_map/hidden/pallas_call | solution.py:463
  71.6 2.3 %hidden.7.hidden_other_ref = bf16[128,1792]{1,0:T(8,128)(2,1)S(1)} custom-call(bf16[128,2048]{1,0:T(8,128)(2,1)S(1)} %collective-permute-done.23.x_ref, bf16[2048,1792]{1,0:T(8,128)(2,1)S(1)} %get-tuple-element.75.gate_ref, bf16[2048,1792]{1,0:T(8,128)(2,1)S(1)} %get-tuple-element.76.up_ref, bf16[128,1792]{1,0:T(8,128)(2,1)S(1)} %hidden.6.refs_0_.hidden_own_ref), custom_call_target="tpu_custom_call" | custom-call | flops 1000000 | tf_op jit(solution)/shard_map/hidden/pallas_call | solution.py:463
  73.9 2.1 %down.3 = (f32[128,2048]{1,0:T(8,128)S(1)}, bf16[128,2048]{1,0:T(8,128)(2,1)S(1)}) custom-call(bf16[128,1792]{1,0:T(8,128)(2,1)S(1)} %hidden.6.refs_0_.hidden_own_ref, bf16[128,1792]{1,0:T(8,128)(2,1)S(1)} %hidden.7.hidden_other_ref, bf16[2048,1792]{1,0:T(8,128)(2,1)S(1)} %get-tuple-element.77.down_ref), custom_call_target="tpu_custom_call" | custom-call | flops 1000000 | tf_op jit(solution)/shard_map/down/pallas_call | solution.py:492
  76.2 1.8 %collective-permute-done.24.other_ref = bf16[128,2048]{1,0:T(8,128)(2,1)S(1)} collective-permute-done((bf16[128,2048]{1,0:T(8,128)(2,1)S(1)}, bf16[128,2048]{1,0:T(8,128)(2,1)S(1)}, u32[]{:S(2)}, u32[]{:S(2)}) %collective-permute-start.24) | collective-permute-done | bytes 524320 | tf_op jit(solution)/shard_map/ppermute | solution.py:33
  82.7 1.7 %collective-permute-done.25.refs_1_ = bf16[128,512]{1,0:T(8,128)(2,1)S(1)} collective-permute-done((bf16[128,512]{1,0:T(8,128)(2,1)S(1)}, bf16[128,512]{1,0:T(8,128)(2,1)S(1)}, u32[]{:S(2)}, u32[]{:S(2)}) %collective-permute-start.25) | collective-permute-done | bytes 131104 | tf_op jit(solution)/shard_map/ppermute | solution.py:33
  85.8 1.7 %collective-permute-done.27.refs_3_ = bf16[128,512]{1,0:T(8,128)(2,1)S(1)} collective-permute-done((bf16[128,512]{1,0:T(8,128)(2,1)S(1)}, bf16[128,512]{1,0:T(8,128)(2,1)S(1)}, u32[]{:S(2)}, u32[]{:S(2)}) %collective-permute-start.27) | collective-permute-done | bytes 131104 | tf_op jit(solution)/shard_map/ppermute | solution.py:33
  87.5 1.7 %collective-permute-start.28 = (bf16[64,512]{1,0:T(8,128)(2,1)S(1)}, bf16[64,512]{1,0:T(8,128)(2,1)S(1)}, u32[]{:S(2)}, u32[]{:S(2)}) collective-permute-start(bf16[64,512]{1,0:T(8,128)(2,1)S(1)} %get-tuple-element.92), channel_id=1, source_target_pairs={{0,8},{4,12},{8,0},{12,4},{1,9},{5,13},{9,1},{13,5},{2,10},{6,14},... | collective-permute-start | bytes 196616 | tf_op jit(solution)/shard_map/ppermute | solution.py:33
  90.8 4.8 %collective-permute-done.28.refs_2_ = bf16[64,512]{1,0:T(8,128)(2,1)S(1)} collective-permute-done((bf16[64,512]{1,0:T(8,128)(2,1)S(1)}, bf16[64,512]{1,0:T(8,128)(2,1)S(1)}, u32[]{:S(2)}, u32[]{:S(2)}) %collective-permute-start.28) | collective-permute-done | bytes 65568 | tf_op jit(solution)/shard_map/ppermute | solution.py:33
  (66 shorter events, 33.0 us)
Async XLA Ops:
  6.4 8.9 %collective-permute-start.1 = (bf16[128,288]{1,0:T(8,128)(2,1)S(1)}, bf16[128,288]{1,0:T(8,128)(2,1)S(1)}, u32[]{:S(2)}, u32[]{:S(2)}) collective-permute-start(bf16[128,288]{1,0:T(8,128)(2,1)S(1)} %get-tuple-element.51.refs_0_), channel_id=1, source_target_pairs={{0,1},{1,0},{2,3},{3,2},{4,5},{5,4},{6,7},{7,6},{8,9},{9,8},{10,11... | collective-permute-start | bytes 221192 | tf_op jit(solution)/shard_map/ppermute | solution.py:33
  8.8 6.5 %collective-permute-start.2 = (bf16[128,288]{1,0:T(8,128)(2,1)S(1)}, bf16[128,288]{1,0:T(8,128)(2,1)S(1)}, u32[]{:S(2)}, u32[]{:S(2)}) collective-permute-start(bf16[128,288]{1,0:T(8,128)(2,1)S(1)} %get-tuple-element.51.refs_0_), channel_id=1, source_target_pairs={{0,2},{1,3},{2,0},{3,1},{4,6},{5,7},{6,4},{7,5},{8,10},{9,11},{10,... | collective-permute-start | bytes 221192 | tf_op jit(solution)/shard_map/ppermute | solution.py:33
  10.4 5.5 %collective-permute-start.3 = (bf16[128,288]{1,0:T(8,128)(2,1)S(1)}, bf16[128,288]{1,0:T(8,128)(2,1)S(1)}, u32[]{:S(2)}, u32[]{:S(2)}) collective-permute-start(bf16[128,288]{1,0:T(8,128)(2,1)S(1)} %get-tuple-element.51.refs_0_), channel_id=1, source_target_pairs={{0,3},{1,2},{2,1},{3,0},{4,7},{5,6},{6,5},{7,4},{8,11},{9,10},{10,... | collective-permute-start | bytes 221192 | tf_op jit(solution)/shard_map/ppermute | solution.py:33
  28.1 6.1 %collective-permute-start.5 = (bf16[128,512]{1,0:T(8,128)(2,1)S(1)}, bf16[128,512]{1,0:T(8,128)(2,1)S(1)}, u32[]{:S(2)}, u32[]{:S(2)}) collective-permute-start(bf16[128,512]{1,0:T(8,128)(2,1)S(1)} %get-tuple-element.66), channel_id=1, source_target_pairs={{0,1},{1,0},{2,3},{3,2},{4,5},{5,4},{6,7},{7,6},{8,9},{9,8},{10,11... | collective-permute-start | bytes 393224 | tf_op jit(solution)/shard_map/ppermute | solution.py:33
  29.7 8.3 %collective-permute-start.6 = (bf16[128,512]{1,0:T(8,128)(2,1)S(1)}, bf16[128,512]{1,0:T(8,128)(2,1)S(1)}, u32[]{:S(2)}, u32[]{:S(2)}) collective-permute-start(bf16[128,512]{1,0:T(8,128)(2,1)S(1)} %get-tuple-element.67), channel_id=1, source_target_pairs={{0,2},{1,3},{2,0},{3,1},{4,6},{5,7},{6,4},{7,5},{8,10},{9,11},{10,... | collective-permute-start | bytes 393224 | tf_op jit(solution)/shard_map/ppermute | solution.py:33
  31.2 6.8 %collective-permute-start.7 = (bf16[128,512]{1,0:T(8,128)(2,1)S(1)}, bf16[128,512]{1,0:T(8,128)(2,1)S(1)}, u32[]{:S(2)}, u32[]{:S(2)}) collective-permute-start(bf16[128,512]{1,0:T(8,128)(2,1)S(1)} %get-tuple-element.68), channel_id=1, source_target_pairs={{0,3},{1,2},{2,1},{3,0},{4,7},{5,6},{6,5},{7,4},{8,11},{9,10},{10,... | collective-permute-start | bytes 393224 | tf_op jit(solution)/shard_map/ppermute | solution.py:33
  39.9 6.6 %collective-permute-start.11 = (bf16[64,512]{1,0:T(8,128)(2,1)S(1)}, bf16[64,512]{1,0:T(8,128)(2,1)S(1)}, u32[]{:S(2)}, u32[]{:S(2)}) collective-permute-start(bf16[64,512]{1,0:T(8,128)(2,1)S(1)} %get-tuple-element.72), channel_id=1, source_target_pairs={{0,8},{4,12},{8,0},{12,4},{1,9},{5,13},{9,1},{13,5},{2,10},{6,14},... | collective-permute-start | bytes 196616 | tf_op jit(solution)/shard_map/ppermute | solution.py:33
  42.5 6.1 %collective-permute-start.12 = (bf16[64,512]{1,0:T(8,128)(2,1)S(1)}, bf16[64,512]{1,0:T(8,128)(2,1)S(1)}, u32[]{:S(2)}, u32[]{:S(2)}) collective-permute-start(bf16[64,512]{1,0:T(8,128)(2,1)S(1)} %get-tuple-element.73), channel_id=1, source_target_pairs={{0,12},{4,8},{8,4},{12,0},{1,13},{5,9},{9,5},{13,1},{2,14},{6,10},... | collective-permute-start | bytes 196616 | tf_op jit(solution)/shard_map/ppermute | solution.py:33
  43.2 5.4 %collective-permute-start.9 = (bf16[128,512]{1,0:T(8,128)(2,1)S(1)}, bf16[128,512]{1,0:T(8,128)(2,1)S(1)}, u32[]{:S(2)}, u32[]{:S(2)}) collective-permute-start(bf16[128,512]{1,0:T(8,128)(2,1)S(1)} %stack.3.refs_2_.refs_0_), channel_id=1, source_target_pairs={{0,1},{1,0},{2,3},{3,2},{4,5},{5,4},{6,7},{7,6},{8,9},{9,8},{10,11... | collective-permute-start | bytes 393224 | tf_op jit(solution)/shard_map/ppermute | solution.py:33
  44.0 6.2 %collective-permute-start.10 = (bf16[128,512]{1,0:T(8,128)(2,1)S(1)}, bf16[128,512]{1,0:T(8,128)(2,1)S(1)}, u32[]{:S(2)}, u32[]{:S(2)}) collective-permute-start(bf16[128,512]{1,0:T(8,128)(2,1)S(1)} %stack.3.refs_2_.refs_0_), channel_id=1, source_target_pairs={{0,2},{1,3},{2,0},{3,1},{4,6},{5,7},{6,4},{7,5},{8,10},{9,11},{10,... | collective-permute-start | bytes 393224 | tf_op jit(solution)/shard_map/ppermute | solution.py:33
  53.9 5.7 %collective-permute-start.14 = (bf16[128,2048]{1,0:T(8,128)(2,1)S(1)}, bf16[128,2048]{1,0:T(8,128)(2,1)S(1)}, u32[]{:S(2)}, u32[]{:S(2)}) collective-permute-start(bf16[128,2048]{1,0:T(8,128)(2,1)S(1)} %norm.2.x_ref), channel_id=1, source_target_pairs={{0,16},{16,0},{1,17},{17,1},{2,18},{18,2},{3,19},{19,3},{4,20},{20... | collective-permute-start | bytes 1572872 | tf_op jit(solution)/shard_map/ppermute | solution.py:33
  54.0 9.9 %collective-permute-start.20 = (bf16[128,512]{1,0:T(8,128)(2,1)S(1)}, bf16[128,512]{1,0:T(8,128)(2,1)S(1)}, u32[]{:S(2)}, u32[]{:S(2)}) collective-permute-start(bf16[128,512]{1,0:T(8,128)(2,1)S(1)} %stack.4.refs_1_.refs_5_.refs_0_), channel_id=1, source_target_pairs={{0,1},{1,0},{2,3},{3,2},{4,5},{5,4},{6,7},{7,6},{8,9},{9,8},{10,11... | collective-permute-start | bytes 393224 | tf_op jit(solution)/shard_map/ppermute | solution.py:33
  55.3 8.6 %collective-permute-start.21 = (bf16[128,512]{1,0:T(8,128)(2,1)S(1)}, bf16[128,512]{1,0:T(8,128)(2,1)S(1)}, u32[]{:S(2)}, u32[]{:S(2)}) collective-permute-start(bf16[128,512]{1,0:T(8,128)(2,1)S(1)} %stack.4.refs_1_.refs_5_.refs_0_), channel_id=1, source_target_pairs={{0,2},{1,3},{2,0},{3,1},{4,6},{5,7},{6,4},{7,5},{8,10},{9,11},{10,... | collective-permute-start | bytes 393224 | tf_op jit(solution)/shard_map/ppermute | solution.py:33
  56.1 7.9 %collective-permute-start.22 = (bf16[128,512]{1,0:T(8,128)(2,1)S(1)}, bf16[128,512]{1,0:T(8,128)(2,1)S(1)}, u32[]{:S(2)}, u32[]{:S(2)}) collective-permute-start(bf16[128,512]{1,0:T(8,128)(2,1)S(1)} %stack.4.refs_1_.refs_5_.refs_0_), channel_id=1, source_target_pairs={{0,3},{1,2},{2,1},{3,0},{4,7},{5,6},{6,5},{7,4},{8,11},{9,10},{10,... | collective-permute-start | bytes 393224 | tf_op jit(solution)/shard_map/ppermute | solution.py:33
  64.2 7.4 %collective-permute-start.23 = (bf16[128,2048]{1,0:T(8,128)(2,1)S(1)}, bf16[128,2048]{1,0:T(8,128)(2,1)S(1)}, u32[]{:S(2)}, u32[]{:S(2)}) collective-permute-start(bf16[128,2048]{1,0:T(8,128)(2,1)S(1)} %norm.3.x_ref), channel_id=1, source_target_pairs={{0,16},{16,0},{1,17},{17,1},{2,18},{18,2},{3,19},{19,3},{4,20},{20... | collective-permute-start | bytes 1572872 | tf_op jit(solution)/shard_map/ppermute | solution.py:33
  65.9 10.2 %collective-permute-start.16 = (bf16[128,512]{1,0:T(8,128)(2,1)S(1)}, bf16[128,512]{1,0:T(8,128)(2,1)S(1)}, u32[]{:S(2)}, u32[]{:S(2)}) collective-permute-start(bf16[128,512]{1,0:T(8,128)(2,1)S(1)} %get-tuple-element.81), channel_id=1, source_target_pairs={{0,1},{1,0},{2,3},{3,2},{4,5},{5,4},{6,7},{7,6},{8,9},{9,8},{10,11... | collective-permute-start | bytes 393224 | tf_op jit(solution)/shard_map/ppermute | solution.py:33
  67.2 8.9 %collective-permute-start.17 = (bf16[128,512]{1,0:T(8,128)(2,1)S(1)}, bf16[128,512]{1,0:T(8,128)(2,1)S(1)}, u32[]{:S(2)}, u32[]{:S(2)}) collective-permute-start(bf16[128,512]{1,0:T(8,128)(2,1)S(1)} %get-tuple-element.82), channel_id=1, source_target_pairs={{0,2},{1,3},{2,0},{3,1},{4,6},{5,7},{6,4},{7,5},{8,10},{9,11},{10,... | collective-permute-start | bytes 393224 | tf_op jit(solution)/shard_map/ppermute | solution.py:33
  68.0 8.1 %collective-permute-start.18 = (bf16[128,512]{1,0:T(8,128)(2,1)S(1)}, bf16[128,512]{1,0:T(8,128)(2,1)S(1)}, u32[]{:S(2)}, u32[]{:S(2)}) collective-permute-start(bf16[128,512]{1,0:T(8,128)(2,1)S(1)} %get-tuple-element.83), channel_id=1, source_target_pairs={{0,3},{1,2},{2,1},{3,0},{4,7},{5,6},{6,5},{7,4},{8,11},{9,10},{10,... | collective-permute-start | bytes 393224 | tf_op jit(solution)/shard_map/ppermute | solution.py:33
  78.1 6.2 %collective-permute-start.25 = (bf16[128,512]{1,0:T(8,128)(2,1)S(1)}, bf16[128,512]{1,0:T(8,128)(2,1)S(1)}, u32[]{:S(2)}, u32[]{:S(2)}) collective-permute-start(bf16[128,512]{1,0:T(8,128)(2,1)S(1)} %get-tuple-element.89), channel_id=1, source_target_pairs={{0,1},{1,0},{2,3},{3,2},{4,5},{5,4},{6,7},{7,6},{8,9},{9,8},{10,11... | collective-permute-start | bytes 393224 | tf_op jit(solution)/shard_map/ppermute | solution.py:33
  79.4 6.4 %collective-permute-start.26 = (bf16[128,512]{1,0:T(8,128)(2,1)S(1)}, bf16[128,512]{1,0:T(8,128)(2,1)S(1)}, u32[]{:S(2)}, u32[]{:S(2)}) collective-permute-start(bf16[128,512]{1,0:T(8,128)(2,1)S(1)} %get-tuple-element.90), channel_id=1, source_target_pairs={{0,2},{1,3},{2,0},{3,1},{4,6},{5,7},{6,4},{7,5},{8,10},{9,11},{10,... | collective-permute-start | bytes 393224 | tf_op jit(solution)/shard_map/ppermute | solution.py:33
  80.2 7.3 %collective-permute-start.27 = (bf16[128,512]{1,0:T(8,128)(2,1)S(1)}, bf16[128,512]{1,0:T(8,128)(2,1)S(1)}, u32[]{:S(2)}, u32[]{:S(2)}) collective-permute-start(bf16[128,512]{1,0:T(8,128)(2,1)S(1)} %get-tuple-element.91), channel_id=1, source_target_pairs={{0,3},{1,2},{2,1},{3,0},{4,7},{5,6},{6,5},{7,4},{8,11},{9,10},{10,... | collective-permute-start | bytes 393224 | tf_op jit(solution)/shard_map/ppermute | solution.py:33
  81.6 9.1 %collective-permute-start.19 = (bf16[64,512]{1,0:T(8,128)(2,1)S(1)}, bf16[64,512]{1,0:T(8,128)(2,1)S(1)}, u32[]{:S(2)}, u32[]{:S(2)}) collective-permute-start(bf16[64,512]{1,0:T(8,128)(2,1)S(1)} %get-tuple-element.85), channel_id=1, source_target_pairs={{0,4},{4,0},{8,12},{12,8},{1,5},{5,1},{9,13},{13,9},{2,6},{6,2},{1... | collective-permute-start | bytes 196616 | tf_op jit(solution)/shard_map/ppermute | solution.py:33
  87.5 8.0 %collective-permute-start.28 = (bf16[64,512]{1,0:T(8,128)(2,1)S(1)}, bf16[64,512]{1,0:T(8,128)(2,1)S(1)}, u32[]{:S(2)}, u32[]{:S(2)}) collective-permute-start(bf16[64,512]{1,0:T(8,128)(2,1)S(1)} %get-tuple-element.92), channel_id=1, source_target_pairs={{0,8},{4,12},{8,0},{12,4},{1,9},{5,13},{9,1},{13,5},{2,10},{6,14},... | collective-permute-start | bytes 196616 | tf_op jit(solution)/shard_map/ppermute | solution.py:33
  89.2 6.3 %collective-permute-start.29 = (bf16[64,512]{1,0:T(8,128)(2,1)S(1)}, bf16[64,512]{1,0:T(8,128)(2,1)S(1)}, u32[]{:S(2)}, u32[]{:S(2)}) collective-permute-start(bf16[64,512]{1,0:T(8,128)(2,1)S(1)} %get-tuple-element.93), channel_id=1, source_target_pairs={{0,12},{4,8},{8,4},{12,0},{1,13},{5,9},{9,5},{13,1},{2,14},{6,10},... | collective-permute-start | bytes 196616 | tf_op jit(solution)/shard_map/ppermute | solution.py:33
  (9 other events, 48.3 us)

commit v3 on v2

--- a/solution.py
+++ b/solution.py
@@ -88,7 +88,9 @@
     return pl.CostEstimate(flops=int(flops), bytes_accessed=int(loaded), transcendentals=0)
 
 
-def route_kernel(ids_ref, first_ref, second_ref, chooser_ref):
+def route_kernel(ids_ref, expert_hbm, first_ref, second_ref, chooser_ref, weight_ref, sem):
+    copy = pltpu.make_async_copy(expert_hbm.at[0, 0], weight_ref, sem)
+    copy.start()
     rows, slots = first_ref.shape
     own = lax.axis_index("exp")
     ids = jnp.transpose(ids_ref[...].astype(F32)).astype(jnp.int32)
@@ -109,9 +111,10 @@
     first_ref[...] = tables[0].astype(BF16)
     second_ref[...] = tables[1].astype(BF16)
     chooser_ref[...] = jnp.transpose(tables[0] + tables[1]).astype(BF16)
-
-
-def route(ids, expert_count):
+    copy.wait()
+
+
+def route(ids, expert_count, experts):
     rows, slots = ids.shape[1], expert_count * CAP
     return pl.pallas_call(
         route_kernel,
@@ -119,27 +122,28 @@
             shaped((rows, slots), BF16),
             shaped((rows, slots), BF16),
             shaped((slots, rows), BF16),
+            shaped(experts.shape[2:], BF16),
         ),
-        in_specs=[whole()],
-        out_specs=[whole()] * 3,
-        compiler_params=params(),
-        cost_estimate=cost(1e6, 1e6),
+        in_specs=[whole(), hbm()],
+        out_specs=[whole()] * 4,
+        scratch_shapes=[pltpu.SemaphoreType.DMA],
+        compiler_params=params(),
+        cost_estimate=cost(1e6, 8e6),
         name="route",
-    )(ids)
+    )(ids, experts)
 
 
 def conv_kernel(
-    halo_hbm, x_hbm, taps_hbm, bias_hbm, weight_hbm, xconv_ref, part_ref,
-    ext_ref, halo_ref, x_ref, taps_ref, bias_ref, weight_ref, sems,
+    before_ref, x_hbm, taps_hbm, bias_hbm, weight_hbm, xconv_ref, part_ref,
+    ext_ref, x_ref, taps_ref, bias_ref, weight_ref, sems,
 ):
     rows = x_ref.shape[0]
-    halo = halo_ref.shape[0]
+    halo = 16
     count = taps_ref.shape[0]
     copies = [
         pltpu.make_async_copy(source, target, sems.at[i])
         for i, (source, target) in enumerate(
             (
-                (halo_hbm.at[rows - halo :], halo_ref),
                 (x_hbm, x_ref),
                 (taps_hbm, taps_ref),
                 (bias_hbm, bias_ref),
@@ -149,9 +153,9 @@
     ]
     for copy in copies:
         copy.start()
-    for copy in copies[:4]:
+    for copy in copies[:3]:
         copy.wait()
-    ext_ref[:halo, :] = halo_ref[...].astype(F32)
+    ext_ref[:halo, :] = before_ref[rows - halo :, :].astype(F32)
     ext_ref[halo:, :] = x_ref[...].astype(F32)
     total = bias_ref[...] + taps_ref[count - 1 : count, :] * ext_ref[halo:, :]
     for k in range(count - 1):
@@ -159,27 +163,32 @@
         total = total + taps_ref[k : k + 1, :] * ext_ref[start : start + rows, :]
     xconv = (total * sigmoid(total)).astype(BF16)
     xconv_ref[...] = xconv
-    copies[4].wait()
-    part_ref[...] = lax.dot_general(
-        xconv, weight_ref[...], (((1,), (1,)), ((), ())), preferred_element_type=F32
+    copies[3].wait()
+    across = (((1,), (1,)), ((), ()))
+    part_ref[:rows, :] = lax.dot_general(
+        xconv, weight_ref[:DT_RANK, :], across, preferred_element_type=F32
     ).astype(BF16)
+    maps = lax.dot_general(
+        weight_ref[DT_RANK:, :], xconv, across, preferred_element_type=F32
+    ).astype(BF16)
+    part_ref[rows:, :rows] = maps[:STATE]
+    part_ref[rows:, rows:] = maps[STATE:]
 
 
 def conv(before, x, taps, bias, weight):
     rows, channels = x.shape
     return pl.pallas_call(
         conv_kernel,
-        out_shape=(shaped((rows, channels), BF16), shaped((rows, weight.shape[0]), BF16)),
-        in_specs=[hbm()] * 5,
+        out_shape=(shaped((rows, channels), BF16), shaped((rows + STATE, DT_RANK), BF16)),
+        in_specs=[whole()] + [hbm()] * 4,
         out_specs=[whole()] * 2,
         scratch_shapes=[
             pltpu.VMEM((16 + rows, channels), F32),
-            pltpu.VMEM((16, channels), BF16),
             pltpu.VMEM((rows, channels), BF16),
             pltpu.VMEM(taps.shape, F32),
             pltpu.VMEM(bias.shape, F32),
             pltpu.VMEM(weight.shape, BF16),
-            pltpu.SemaphoreType.DMA((5,)),
+            pltpu.SemaphoreType.DMA((4,)),
         ],
         compiler_params=params(),
         name="conv",
@@ -187,9 +196,9 @@
 
 
 def prepare_kernel(
-    xconv_ref, gate_hbm, decay_hbm, skip_hbm, bias_hbm, step_hbm, out_hbm, residual_hbm, gain_hbm, expert_hbm,
-    x_ref, silu_ref, rates_ref, skip_ref, bias_ref, step_ref, out_ref, quarter_ref, gain_ref, first_ref,
-    gate_ref, decay_ref, flat_ref, residual_ref, sems,
+    gate_hbm, decay_hbm, residual_hbm, skip_hbm, bias_hbm, step_hbm, out_hbm, gain_hbm,
+    silu_ref, rates_ref, skip_ref, bias_ref, step_ref, out_ref, quarter_ref, gain_ref,
+    gate_ref, decay_ref, residual_ref, sems,
 ):
     copies = [
         pltpu.make_async_copy(source, target, sems.at[i])
@@ -197,165 +206,155 @@
             (
                 (gate_hbm, gate_ref),
                 (decay_hbm, decay_ref),
-                (skip_hbm, flat_ref),
                 (residual_hbm, residual_ref),
+                (skip_hbm, skip_ref),
                 (bias_hbm, bias_ref),
                 (gain_hbm, gain_ref),
                 (step_hbm, step_ref),
                 (out_hbm, out_ref),
-                (expert_hbm.at[0, 0], first_ref),
             )
         )
     ]
     for copy in copies:
         copy.start()
-    tiles = x_ref.shape[1]
-    xfloat = xconv_ref[...].astype(F32)
-    for j in range(tiles):
-        x_ref[:, j, :] = xfloat[:, j * 128 : (j + 1) * 128]
-    for copy in copies[:4]:
+    for copy in copies[:3]:
         copy.wait()
     gate = gate_ref[...].astype(F32)
     silu_ref[...] = gate * sigmoid(gate)
-    rates = -LOG2E * jnp.exp(decay_ref[...])
-    for j in range(tiles):
-        cut = slice(j * 128, (j + 1) * 128)
-        rates_ref[:, j, :] = rates[:, cut]
-        skip_ref[j : j + 1, :] = flat_ref[:, cut]
+    rates_ref[...] = -LOG2E * jnp.exp(decay_ref[...])
     width = quarter_ref.shape[1]
     start = pl.multiple_of(lax.axis_index("tp") * width, 128)
     quarter_ref[...] = residual_ref[:, pl.ds(start, width)].astype(F32)
-    for copy in copies[4:]:
+    for copy in copies[3:]:
         copy.wait()
 
 
-def prepare(parts, xconv, gate, decay_log, skip, bias, step_weight, out_weight, residual, gain, experts):
-    rows, channels = xconv.shape
-    tiles = channels // 128
+def prepare(parts, gate, decay_log, residual, skip, bias, step_weight, out_weight, gain):
+    rows, channels = gate.shape
     return pl.pallas_call(
         prepare_kernel,
         out_shape=(
-            shaped((rows, tiles, 128), F32),
             shaped((rows, channels), F32),
-            shaped((STATE, tiles, 128), F32),
-            shaped((tiles, 128), F32),
+            shaped(decay_log.shape, F32),
+            shaped(skip.shape, F32),
             shaped(bias.shape, F32),
             shaped(step_weight.shape, BF16),
             shaped(out_weight.shape, BF16),
             shaped((rows, residual.shape[1] // parts), F32),
             shaped(gain.shape, F32),
-            shaped(experts.shape[2:], BF16),
         ),
-        in_specs=[whole()] + [hbm()] * 9,
-        out_specs=[whole()] * 10,
+        in_specs=[hbm()] * 8,
+        out_specs=[whole()] * 8,
         scratch_shapes=[
             pltpu.VMEM((rows, channels), BF16),
             pltpu.VMEM(decay_log.shape, F32),
-            pltpu.VMEM(skip.shape, F32),
             pltpu.VMEM(residual.shape, BF16),
-            pltpu.SemaphoreType.DMA((9,)),
+            pltpu.SemaphoreType.DMA((8,)),
         ],
         compiler_params=params(),
-        cost_estimate=cost(1e6, 14e6),
+        cost_estimate=cost(1e6, 6e6),
         name="prepare",
-    )(xconv, gate, decay_log, skip, bias, step_weight, out_weight, residual, gain, experts)
+    )(gate, decay_log, residual, skip, bias, step_weight, out_weight, gain)
+
+
+def over_states(sum_ref):
+    total = sum_ref[:, 0, :]
+    for i in range(1, 8):
+        total = total + sum_ref[:, i, :]
+    return total
 
 
 def scan_kernel(parts, *refs):
     part_refs = refs[:parts]
-    x_ref, rates_ref, gain_ref, bias_ref, weight_ref, expert_hbm = refs[parts : parts + 6]
+    xconv_ref, rates_ref, gain_ref, bias_ref, weight_ref, expert_hbm = refs[parts : parts + 6]
     y_ref, elapsed_ref, maps_ref, state_ref, second_ref = refs[parts + 6 : parts + 11]
-    steps_ref, scalars, sem, expert_sem = refs[parts + 11 :]
-    rows, tiles, _ = x_ref.shape
+    steps_ref, driven_ref, sum_ref, expert_sem = refs[parts + 11 :]
+    rows, channels = xconv_ref.shape
     expert_copy = pltpu.make_async_copy(expert_hbm.at[0, 1], second_ref, expert_sem)
     expert_copy.start()
     proj = part_refs[0][...].astype(F32)
     for ref in part_refs[1:]:
         proj = proj + ref[...].astype(F32)
-    maps_ref[...] = proj[:, DT_RANK:]
-    copy = pltpu.make_async_copy(maps_ref, scalars, sem)
-    copy.start()
-    rank = proj[:, :DT_RANK].astype(BF16)
+    maps = proj[rows:]
+    maps_ref[...] = maps
+    rank = proj[:rows].astype(BF16)
     raw = jnp.dot(rank, weight_ref[...], preferred_element_type=F32) + bias_ref[...]
     steps = jnp.maximum(raw, 0.0) + jnp.log1p(jnp.exp(-jnp.abs(raw)))
-    for j in range(tiles):
-        steps_ref[:, j, :] = steps[:, j * 128 : (j + 1) * 128]
-    copy.wait()
-    gain = gain_ref[...]
-
-    def step(t, carry):
-        elapsed, states = carry
-        now = steps_ref[t]
-        x = x_ref[t]
-        driven = now * x
-        sums = [gain * x, None]
-        new = []
-        for n in range(STATE):
-            state = jnp.exp2(now * rates_ref[n]) * states[n] + driven * scalars[t, n]
-            new.append(state)
-            term = state * scalars[t, STATE + n]
-            sums[n % 2] = term if sums[n % 2] is None else sums[n % 2] + term
-        elapsed = elapsed + now
-        y_ref[t] = sums[0] + sums[1]
-        elapsed_ref[t] = elapsed
-        return elapsed, tuple(new)
-
-    zero = jnp.zeros((tiles, 128), F32)
-    _, states = lax.fori_loop(0, rows, step, (zero, (zero,) * STATE), unroll=4)
-    for n in range(STATE):
-        state_ref[n] = states[n]
+    xfloat = xconv_ref[...].astype(F32)
+    steps_ref[...] = steps
+    driven_ref[...] = steps * xfloat
+    y_ref[...] = gain_ref[...] * xfloat
+    high = steps.astype(BF16)
+    low = (steps - high.astype(F32)).astype(BF16)
+    until = lax.broadcasted_iota(jnp.int32, (rows, rows), 1) <= lax.broadcasted_iota(
+        jnp.int32, (rows, rows), 0
+    )
+    until = until.astype(F32).astype(BF16)
+    elapsed_ref[...] = jnp.dot(until, high, preferred_element_type=F32) + jnp.dot(
+        until, low, preferred_element_type=F32
+    )
+
+    def block(i, carry):
+        state, into, out = carry
+        begin = pl.multiple_of(i * 8, 8)
+        for r in range(8):
+            now = steps_ref[pl.ds(begin + r, 1), :]
+            driven = driven_ref[pl.ds(begin + r, 1), :]
+            state = jnp.exp2(now * rates_ref[...]) * state + driven * into[:, r : r + 1]
+            seen = state * out[:, r : r + 1]
+            sum_ref[r] = seen[:8] + seen[8:]
+        y_ref[pl.ds(begin, 8), :] += over_states(sum_ref)
+        return state, pltpu.roll(into, rows - 8, 1), pltpu.roll(out, rows - 8, 1)
+
+    start = jnp.zeros((STATE, channels), F32)
+    state_ref[...] = lax.fori_loop(0, rows // 8, block, (start, maps[:, :rows], maps[:, rows:]))[0]
     expert_copy.wait()
 
 
-def scan(pieces, x, rates, gain, bias, weight, experts):
-    rows, tiles, _ = x.shape
+def scan(pieces, xconv, rates, gain, bias, weight, experts):
+    rows, channels = xconv.shape
     return pl.pallas_call(
         functools.partial(scan_kernel, len(pieces)),
         out_shape=(
-            shaped((rows, tiles, 128), F32),
-            shaped((rows, tiles, 128), F32),
-            shaped((rows, 2 * STATE), F32),
-            shaped((STATE, tiles, 128), F32),
+            shaped((rows, channels), F32),
+            shaped((rows, channels), F32),
+            shaped((STATE, DT_RANK), F32),
+            shaped((STATE, channels), F32),
             shaped(experts.shape[2:], BF16),
         ),
         in_specs=[whole()] * (len(pieces) + 5) + [hbm()],
         out_specs=[whole()] * 5,
         scratch_shapes=[
-            pltpu.VMEM((rows, tiles, 128), F32),
-            pltpu.SMEM((rows, 2 * STATE), F32),
-            pltpu.SemaphoreType.DMA,
+            pltpu.VMEM((rows, channels), F32),
+            pltpu.VMEM((rows, channels), F32),
+            pltpu.VMEM((8, 8, channels), F32),
             pltpu.SemaphoreType.DMA,
         ],
         compiler_params=params(),
         cost_estimate=cost(1e6, 14e6),
         name="scan",
-    )(*pieces, x, rates, gain, bias, weight, experts)
+    )(*pieces, xconv, rates, gain, bias, weight, experts)
 
 
 def mix_kernel(parts, *refs):
     maps_ref, y_ref, elapsed_ref, rates_ref, state_ref, silu_ref, quarter_ref, weight_ref, expert_hbm = refs[:9]
     own_ref, sent, third_ref = refs[9], refs[10 : 9 + parts], refs[9 + parts]
-    sum_ref, gated_ref, scalars, sem, expert_sem = refs[10 + parts :]
-    copy = pltpu.make_async_copy(maps_ref, scalars, sem)
-    copy.start()
+    sum_ref, gated_ref, expert_sem = refs[10 + parts :]
     expert_copy = pltpu.make_async_copy(expert_hbm.at[0, 2], third_ref, expert_sem)
     expert_copy.start()
-    rows, tiles, _ = y_ref.shape
-    copy.wait()
-
-    def step(t, carry):
-        elapsed = elapsed_ref[t]
-        sums = [y_ref[t], None]
-        for n in range(STATE):
-            term = jnp.exp2(elapsed * rates_ref[n]) * state_ref[n] * scalars[t, STATE + n]
-            sums[n % 2] = term if sums[n % 2] is None else sums[n % 2] + term
-        sum_ref[t] = sums[0] + sums[1]
-        return carry
-
-    lax.fori_loop(0, rows, step, 0, unroll=4)
-    for j in range(tiles):
-        cut = slice(j * 128, (j + 1) * 128)
-        gated_ref[:, cut] = (sum_ref[:, j, :] * silu_ref[:, cut]).astype(BF16)
+    rows = y_ref.shape[0]
+
+    def block(i, out):
+        begin = pl.multiple_of(i * 16, 16)
+        for r in range(16):
+            decay = jnp.exp2(elapsed_ref[pl.ds(begin + r, 1), :] * rates_ref[...])
+            seen = decay * (state_ref[...] * out[:, r : r + 1])
+            sum_ref[r] = seen[:8] + seen[8:]
+        cut = pl.ds(begin, 16)
+        gated_ref[cut, :] = ((y_ref[cut, :] + over_states(sum_ref)) * silu_ref[cut, :]).astype(BF16)
+        return pltpu.roll(out, rows - 16, 1)
+
+    lax.fori_loop(0, rows // 16, block, maps_ref[:, rows:])
     own = lax.axis_index("tp")
     width = own_ref.shape[1]
     for k in range(parts):
@@ -371,7 +370,7 @@
 
 
 def mix(parts, maps, y, elapsed, rates, state, silu, quarter, weight, experts):
-    rows, tiles, _ = y.shape
+    rows, channels = y.shape
     width = weight.shape[1] // parts
     return pl.pallas_call(
         functools.partial(mix_kernel, parts),
@@ -381,10 +380,8 @@
         in_specs=[whole()] * 8 + [hbm()],
         out_specs=[whole()] * (parts + 1),
         scratch_shapes=[
-            pltpu.VMEM((rows, tiles, 128), F32),
-            pltpu.VMEM((rows, tiles * 128), BF16),
-            pltpu.SMEM(maps.shape, F32),
-            pltpu.SemaphoreType.DMA,
+            pltpu.VMEM((16, 8, channels), F32),
+            pltpu.VMEM((rows, channels), BF16),
             pltpu.SemaphoreType.DMA,
         ],
         compiler_params=params(),
@@ -420,31 +417,35 @@
     )(own, *arrived, chooser)
 
 
-def norm_kernel(parts, *refs):
-    x_refs, gain_ref, out_ref = refs[:parts], refs[parts], refs[-1]
-    width = x_refs[0].shape[1]
+def norm_kernel(parts, count, *refs):
+    gain_ref, out_ref = refs[parts * count], refs[-1]
     own = lax.axis_index("tp")
-    pieces = [ref[...].astype(F32) for ref in x_refs]
-    total = sum(jnp.sum(piece * piece, axis=1, keepdims=True) for piece in pieces)
-    scale = lax.rsqrt(total / (width * parts) + 1e-6)
-    for k, piece in enumerate(pieces):
-        start = pl.multiple_of(jnp.bitwise_xor(own, k) * width, 128)
-        out_ref[:, pl.ds(start, width)] = (
-            piece * scale * gain_ref[:, pl.ds(start, width)]
-        ).astype(BF16)
-
-
-def norm(pieces, gain, after):
-    rows, width = pieces[0].shape
-    return pl.pallas_call(
-        functools.partial(norm_kernel, len(pieces)),
-        out_shape=shaped((rows, width * len(pieces)), BF16),
-        in_specs=[whole()] * (len(pieces) + 1) + unread(after),
+    begin = 0
+    for i in range(count):
+        pieces = [ref[...].astype(F32) for ref in refs[i * parts : (i + 1) * parts]]
+        rows, width = pieces[0].shape
+        total = sum(jnp.sum(piece * piece, axis=1, keepdims=True) for piece in pieces)
+        scale = lax.rsqrt(total / (width * parts) + 1e-6)
+        for k, piece in enumerate(pieces):
+            start = pl.multiple_of(jnp.bitwise_xor(own, k) * width, 128)
+            out_ref[begin : begin + rows, pl.ds(start, width)] = (
+                piece * scale * gain_ref[:, pl.ds(start, width)]
+            ).astype(BF16)
+        begin += rows
+
+
+def norm(sets, gain, after):
+    parts = len(sets[0])
+    rows, width = sum(pieces[0].shape[0] for pieces in sets), sets[0][0].shape[1]
+    return pl.pallas_call(
+        functools.partial(norm_kernel, parts, len(sets)),
+        out_shape=shaped((rows, width * parts), BF16),
+        in_specs=[whole()] * (parts * len(sets) + 1) + unread(after),
         out_specs=whole(),
         compiler_params=params(),
         cost_estimate=cost(1e6, 1e6),
         name="norm",
-    )(*pieces, gain, *after)
+    )(*sum(sets, []), gain, *after)
 
 
 def hidden_kernel(x_ref, gate_ref, up_ref, *refs):
@@ -603,36 +604,35 @@
     before = lax.ppermute(local, "ctx", [(0, 1)])
     expert_weight = stay(expert_weight)
     xconv, part = conv(
-        stay(before), stay(local), stay(conv_weight), stay(conv_bias[None]), stay(proj_weight.T)
+        before, stay(local), stay(conv_weight), stay(conv_bias[None]), stay(proj_weight.T)
     )
     parts = [part] + [swap(part, "tp", k) for k in range(1, tp)]
-    x, silu, rates, skip, bias, step_w, out_w, quarter, gain, gate_w = prepare(
-        tp, xconv, stay(gate_in[0]), stay(decay_log), stay(skip_gain[None]), stay(step_bias[None]),
-        stay(step_weight), stay(out_weight), stay(residual[0]), stay(norm_gain[None]), expert_weight,
-    )
-    y, elapsed, maps, state, up_w = scan(parts, x, rates, skip, bias, step_w, expert_weight)
+    silu, rates, skip, bias, step_w, out_w, quarter, gain = prepare(
+        tp, stay(gate_in[0]), stay(decay_log), stay(residual[0]), stay(skip_gain[None]),
+        stay(step_bias[None]), stay(step_weight), stay(out_weight), stay(norm_gain[None]),
+    )
+    y, elapsed, maps, state, up_w = scan(parts, xconv, rates, skip, bias, step_w, expert_weight)
     before = lax.ppermute(state, "ctx", [(0, 1)])
     own, *sent, down_w = mix(
         tp, maps, y, elapsed, rates, before, silu, quarter, out_w, expert_weight
     )
     arrived = [swap(piece, "tp", k) for k, piece in enumerate(sent, 1)]
-    first, second, chooser = route(expert_ids[0].T, experts)
+    first, second, chooser, gate_w = route(expert_ids[0].T, experts, expert_weight)
     stream, *picked = pick(own, arrived, chooser)
     rows = [picked[0]] + [swap(picked[j], "exp", j) for j in range(1, experts)]
-    piece_a = stack(rows[: experts // 2], [])
-    piece_b = stack(rows[experts // 2 :], [piece_a])
-    rows_a, rows_b = [piece_a], [piece_b]
-    both = order([piece_a, piece_b])
-    for k in range(1, tp):
-        top = 1 << (k.bit_length() - 1)
-        passed = rows_a[k ^ top]
-        rows_a.append(swap(passed if k == top else stack([passed], [both]), "tp", top))
-        rows_b.append(swap(piece_b, "tp", k))
-    x_a = norm(rows_a, gain, [piece_b])
+    half = experts // 2
+    piece_a = rows[1] if half == 2 else stack(rows[1:half], [])
+    piece_b = stack(rows[half:], [rows[1]])
+    both = order([rows[1], piece_b])
+    sets = [
+        [piece] + [swap(piece, "tp", k) for k in range(1, tp)]
+        for piece in (rows[0], piece_a, piece_b)
+    ]
+    x_a = norm(sets[:2], gain, [both])
     own_a, joined_a = expert(tp, x_a, gate_w, up_w, down_w, [], [])
     summed_a = [joined_a[0]] + [swap(joined_a[k], "tp", k) for k in range(1, tp)]
     back = totals(summed_a)
-    x_b = norm(rows_b, gain, [own_a])
+    x_b = norm(sets[2:], gain, [own_a])
     _, joined_b = expert(tp, x_b, gate_w, up_w, down_w, [joined_a[0]], [back[0]])
     back += totals([joined_b[0]] + [swap(joined_b[k], "tp", k) for k in range(1, tp)])
     back = [back[0]] + [swap(back[j], "exp", j) for j in range(1, experts)]

time: 96.6 us -> 93.1 us (0.964)
  waiting for transfers between devices: 28.1 us -> 24.6 us
  starting transfers between devices: 35 us -> 37.5 us
  Pallas kernels: 32.4 us -> 30.4 us
    ppermute x28 -> x31, waiting for transfers between devices: 25.9 us -> 22.4 us  [swap(): lax.ppermute(block, axis, [(i, i ^ k) for i in range(lax.axis_size(axis))])]
    ppermute x28 -> x31, starting transfers between devices: 31.3 us -> 33.8 us  [swap(): lax.ppermute(block, axis, [(i, i ^ k) for i in range(lax.axis_size(axis))])]
    pallas_call x1, Pallas kernels: 0.6 us -> 3.09 us  [route(): pl.pallas_call(route_kernel, out_shape=(shaped((rows, slots), BF16), shap...]
    pallas_call x3, Pallas kernels: 5.39 us -> 3.23 us  [the longest x1 2.76 us: prepare(): pl.pallas_call(prepare_kernel, out_shape=(shaped((rows, channels), F32),...]
    pallas_call x1, Pallas kernels: 4.84 us -> 3.39 us  [mix(): pl.pallas_call(functools.partial(mix_kernel, parts), out_shape=[shaped((r...]
  transfers between devices with their start and end apart: 30 -> 33, of which waited for: 15 -> 13; matrix products, arithmetic and copies ran while one was open for 0% -> 0% of each run, Pallas kernels for 19% -> 21%
where the time goes in v3:
time: 93.1 us; the launch traced here: 92.9 us
  starting transfers between devices  37.5 us (40%)
  Pallas kernels  30.4 us (33%)
  waiting for transfers between devices  24.6 us (26%)
    ppermute x31, starting transfers between devices, swap(): lax.ppermute(block, axis, [(i, i ^ k) for i in range(lax.axis_size(axis))])  33.8 us
    ppermute x31, waiting for transfers between devices, swap(): lax.ppermute(block, axis, [(i, i ^ k) for i in range(lax.axis_size(axis))])  22.4 us
    pallas_call x4, Pallas kernels, hidden_units(): pl.pallas_call(hidden_kernel, out_shape=shaped((rows, width), BF16), in_s...  8.59 us
    pallas_call x1, Pallas kernels, scan(): pl.pallas_call(functools.partial(scan_kernel, len(pieces)), out_shape=(sh...  4.38 us
    pallas_call x2, Pallas kernels, down_sums(): pl.pallas_call(down_kernel, out_shape=(shaped((rows, model), F32), shaped...  4.18 us
    pallas_call x1, Pallas kernels, mix(): pl.pallas_call(functools.partial(mix_kernel, parts), out_shape=[shaped((r...  3.39 us
    pallas_call x1, Pallas kernels, route(): pl.pallas_call(route_kernel, out_shape=(shaped((rows, slots), BF16), shap...  3.09 us
    pallas_call x1, Pallas kernels, prepare(): pl.pallas_call(prepare_kernel, out_shape=(shaped((rows, channels), F32),...  2.76 us
  transfers between devices with their start and end apart: 33, of which 13 were waited for; matrix products, arithmetic and copies ran while one was open for 0% of the time, Pallas kernels for 21%

profile of v3, /device:TPU:0, one launch (start us, length us, event | category | flops | bytes accessed | tf_op | source)
XLA Modules:
  0.0 92.9 jit_solution(4193626051349633949)
XLA Ops:
  0.0 2.4 %collective-permute-start = (bf16[128,1024]{1,0:T(8,128)(2,1)}, bf16[128,1024]{1,0:T(8,128)(2,1)S(1)}, u32[]{:S(2)}, u32[]{:S(2)}) collective-permute-start(bf16[128,1024]{1,0:T(8,128)(2,1)} %bitcast.19), channel_id=1, source_target_pairs={{0,16},{1,17},{2,18},{3,19},{4,20},{5,21},{6,22},{7,23},{8,24},{9,... | collective-permute-start | bytes 786440 | tf_op jit(solution)/shard_map/ppermute | solution.py:604
  3.7 2.0 %conv.1 = (bf16[128,1024]{1,0:T(8,128)(2,1)S(1)}, bf16[144,256]{1,0:T(8,128)(2,1)S(1)}) custom-call(bf16[128,1024]{1,0:T(8,128)(2,1)S(1)} %collective-permute-done.before_ref, bf16[128,1024]{1,0:T(8,128)(2,1)} %bitcast.20, f32[4,1024]{1,0:T(4,128)} %taps_hbm.1, f32[1,1024]{1,0:T(1,128)} %bitcast.23, bf16[288,1024]{1,0:T(8,128)(2,1)} %bitcast.17), custom_call_target="tpu_custom_call" | custom-call | tf_op jit(solution)/shard_map/conv/pallas_call | solution.py:180
  5.7 2.4 %collective-permute-start.1 = (bf16[144,256]{1,0:T(8,128)(2,1)S(1)}, bf16[144,256]{1,0:T(8,128)(2,1)S(1)}, u32[]{:S(2)}, u32[]{:S(2)}) collective-permute-start(bf16[144,256]{1,0:T(8,128)(2,1)S(1)} %get-tuple-element.50.refs_0_), channel_id=1, source_target_pairs={{0,1},{1,0},{2,3},{3,2},{4,5},{5,4},{6,7},{7,6},{8,9},{9,8},{10,11... | collective-permute-start | bytes 221192 | tf_op jit(solution)/shard_map/ppermute | solution.py:33
  9.7 2.8 %prepare.1 = (f32[128,1024]{1,0:T(8,128)S(1)}, f32[16,1024]{1,0:T(8,128)S(1)}, f32[1,1024]{1,0:T(1,128)S(1)}, f32[1,1024]{1,0:T(1,128)S(1)}, bf16[256,1024]{1,0:...) custom-call(bf16[128,1024]{1,0:T(8,128)(2,1)} %bitcast.21, ...), custom_call_target="tpu_custom_call" | custom-call | flops 1000000 | bytes 6000000 | tf_op jit(solution)/shard_map/prepare/pallas_call | solution.py:234
  12.5 2.4 %collective-permute-done.3.refs_3_ = bf16[144,256]{1,0:T(8,128)(2,1)S(1)} collective-permute-done((bf16[144,256]{1,0:T(8,128)(2,1)S(1)}, bf16[144,256]{1,0:T(8,128)(2,1)S(1)}, u32[]{:S(2)}, u32[]{:S(2)}) %collective-permute-start.3) | collective-permute-done | bytes 73760 | tf_op jit(solution)/shard_map/ppermute | solution.py:33
  14.9 4.4 %scan.1 = (f32[128,1024]{1,0:T(8,128)S(1)}, f32[128,1024]{1,0:T(8,128)S(1)}, f32[16,256]{1,0:T(8,128)S(1)}, f32[16,1024]{1,0:T(8,128)S(1)}, bf16[2048,1792]{1,0:T(8,128)(2,1)S(1)}) custom-call(bf16[144,256]{1,0:T(8,128)(2,1)S(1)} %get-tuple-element.50.refs_0_, bf16[144,256]{1,0:T(8,128)(2,1)S(1)} %collective-permute-done.1.refs_1_, ...), custom_call_target="tpu_custom_call" | custom-call | flops 1000000 | bytes 14000000 | tf_op jit(solution)/shard_map/scan/pallas_call | solution.py:316
  21.5 3.4 %mix.1 = (f32[128,512]{1,0:T(8,128)S(1)}, bf16[128,512]{1,0:T(8,128)(2,1)S(1)}, bf16[128,512]{1,0:T(8,128)(2,1)S(1)}, bf16[128,512]{1,0:T(8,128)(2,1)S(1)}, bf16[2048,1792]{1,0:T(8,128)(2,1)S(1)}) custom-call(f32[16,256]{1,0:T(8,128)S(1)} %get-tuple-element.56.refs_0_, f32[128,1024]{1,0:T(8,128)S(1)} %get-tuple-element.57.refs_1_, ...), custom_call_target="tpu_custom_call" | custom-call | flops 1000000 | bytes 12000000 | tf_op jit(solution)/shard_map/mix/pallas_call | solution.py:375
  26.2 2.3 %collective-permute-start.7 = (bf16[128,512]{1,0:T(8,128)(2,1)S(1)}, bf16[128,512]{1,0:T(8,128)(2,1)S(1)}, u32[]{:S(2)}, u32[]{:S(2)}) collective-permute-start(bf16[128,512]{1,0:T(8,128)(2,1)S(1)} %get-tuple-element.66), channel_id=1, source_target_pairs={{0,3},{1,2},{2,1},{3,0},{4,7},{5,6},{6,5},{7,4},{8,11},{9,10},{10,... | collective-permute-start | bytes 393224 | tf_op jit(solution)/shard_map/ppermute | solution.py:33
  28.4 3.1 %route.1 = (bf16[128,256]{1,0:T(8,128)(2,1)S(1)}, bf16[128,256]{1,0:T(8,128)(2,1)S(1)}, bf16[256,128]{1,0:T(8,128)(2,1)S(1)}, bf16[2048,1792]{1,0:T(8,128)(2,1)S(1)}) custom-call(s32[2,128]{1,0:T(2,128)S(1)} %bitcast.15, bf16[1,3,2048,1792]{3,2,1,0:T(8,128)(2,1)} %expert_hbm.1), custom_call_target="tpu_custom_call" | custom-call | flops 1000000 | bytes 8000000 | tf_op jit(solution)/shard_map/route/pallas_call | solution.py:119
  31.5 2.2 %collective-permute-done.6.refs_2_ = bf16[128,512]{1,0:T(8,128)(2,1)S(1)} collective-permute-done((bf16[128,512]{1,0:T(8,128)(2,1)S(1)}, bf16[128,512]{1,0:T(8,128)(2,1)S(1)}, u32[]{:S(2)}, u32[]{:S(2)}) %collective-permute-start.6) | collective-permute-done | bytes 131104 | tf_op jit(solution)/shard_map/ppermute | solution.py:33
  35.7 2.6 %collective-permute-start.15 = (bf16[64,512]{1,0:T(8,128)(2,1)S(1)}, bf16[64,512]{1,0:T(8,128)(2,1)S(1)}, u32[]{:S(2)}, u32[]{:S(2)}) collective-permute-start(bf16[64,512]{1,0:T(8,128)(2,1)S(1)} %get-tuple-element.71), channel_id=1, source_target_pairs={{0,8},{4,12},{8,0},{12,4},{1,9},{5,13},{9,1},{13,5},{2,10},{6,14},... | collective-permute-start | bytes 196616 | tf_op jit(solution)/shard_map/ppermute | solution.py:33
  45.5 1.8 %collective-permute-start.14 = (bf16[64,512]{1,0:T(8,128)(2,1)S(1)}, bf16[64,512]{1,0:T(8,128)(2,1)S(1)}, u32[]{:S(2)}, u32[]{:S(2)}) collective-permute-start(bf16[64,512]{1,0:T(8,128)(2,1)S(1)} %collective-permute-done.11.refs_2_.refs_0_.refs_4_), channel_id=1, source_target_pairs={{0,3},{1,2},{2,1},{3,0},{4,7},{5,6},{6,5},{7,4},{8,11},{9,10},{10,... | collective-permute-start | bytes 196616 | tf_op jit(solution)/shard_map/ppermute | solution.py:33
  48.6 2.2 %collective-permute-done.14.refs_7_ = bf16[64,512]{1,0:T(8,128)(2,1)S(1)} collective-permute-done((bf16[64,512]{1,0:T(8,128)(2,1)S(1)}, bf16[64,512]{1,0:T(8,128)(2,1)S(1)}, u32[]{:S(2)}, u32[]{:S(2)}) %collective-permute-start.14) | collective-permute-done | bytes 65568 | tf_op jit(solution)/shard_map/ppermute | solution.py:33
  54.6 2.1 %hidden.4.refs_0_.hidden_own_ref = bf16[128,1792]{1,0:T(8,128)(2,1)S(1)} custom-call(bf16[128,2048]{1,0:T(8,128)(2,1)S(1)} %norm.2.x_ref, bf16[2048,1792]{1,0:T(8,128)(2,1)S(1)} %get-tuple-element.73.gate_ref, bf16[2048,1792]{1,0:T(8,128)(2,1)S(1)} %get-tuple-element.74.up_ref), custom_call_target="tpu_custom_call" | custom-call | flops 1000000 | tf_op jit(solution)/shard_map/hidden/pallas_call | solution.py:464
  56.7 2.1 %hidden.5.hidden_other_ref = bf16[128,1792]{1,0:T(8,128)(2,1)S(1)} custom-call(bf16[128,2048]{1,0:T(8,128)(2,1)S(1)} %collective-permute-done.17.x_ref, bf16[2048,1792]{1,0:T(8,128)(2,1)S(1)} %get-tuple-element.73.gate_ref, bf16[2048,1792]{1,0:T(8,128)(2,1)S(1)} %get-tuple-element.74.up_ref, bf16[128,1792]{1,0:T(8,128)(2,1)S(1)} %hidden.4.refs_0_.hidden_own_ref), custom_call_target="tpu_custom_call" | custom-call | flops 1000000 | tf_op jit(solution)/shard_map/hidden/pallas_call | solution.py:464
  58.8 2.1 %down.2 = (f32[128,2048]{1,0:T(8,128)S(1)}, bf16[128,2048]{1,0:T(8,128)(2,1)S(1)}) custom-call(bf16[128,1792]{1,0:T(8,128)(2,1)S(1)} %hidden.4.refs_0_.hidden_own_ref, bf16[128,1792]{1,0:T(8,128)(2,1)S(1)} %hidden.5.hidden_other_ref, bf16[2048,1792]{1,0:T(8,128)(2,1)S(1)} %get-tuple-element.75.down_ref), custom_call_target="tpu_custom_call" | custom-call | flops 1000000 | tf_op jit(solution)/shard_map/down/pallas_call | solution.py:493
  66.6 2.1 %hidden.6.refs_0_.hidden_own_ref = bf16[128,1792]{1,0:T(8,128)(2,1)S(1)} custom-call(bf16[128,2048]{1,0:T(8,128)(2,1)S(1)} %norm.3.x_ref, bf16[2048,1792]{1,0:T(8,128)(2,1)S(1)} %get-tuple-element.73.gate_ref, bf16[2048,1792]{1,0:T(8,128)(2,1)S(1)} %get-tuple-element.74.up_ref, f32[128,512]{1,0:T(8,128)S(1)} %get-tuple-element.78.refs_0_), custom_call_target="tpu_custom_call" | custom-call | flops 1000000 | tf_op jit(solution)/shard_map/hidden/pallas_call | solution.py:464
  68.7 2.3 %hidden.7.hidden_other_ref = bf16[128,1792]{1,0:T(8,128)(2,1)S(1)} custom-call(bf16[128,2048]{1,0:T(8,128)(2,1)S(1)} %collective-permute-done.26.x_ref, bf16[2048,1792]{1,0:T(8,128)(2,1)S(1)} %get-tuple-element.73.gate_ref, bf16[2048,1792]{1,0:T(8,128)(2,1)S(1)} %get-tuple-element.74.up_ref, bf16[128,1792]{1,0:T(8,128)(2,1)S(1)} %hidden.6.refs_0_.hidden_own_ref), custom_call_target="tpu_custom_call" | custom-call | flops 1000000 | tf_op jit(solution)/shard_map/hidden/pallas_call | solution.py:464
  71.0 2.1 %down.3 = (f32[128,2048]{1,0:T(8,128)S(1)}, bf16[128,2048]{1,0:T(8,128)(2,1)S(1)}) custom-call(bf16[128,1792]{1,0:T(8,128)(2,1)S(1)} %hidden.6.refs_0_.hidden_own_ref, bf16[128,1792]{1,0:T(8,128)(2,1)S(1)} %hidden.7.hidden_other_ref, bf16[2048,1792]{1,0:T(8,128)(2,1)S(1)} %get-tuple-element.75.down_ref), custom_call_target="tpu_custom_call" | custom-call | flops 1000000 | tf_op jit(solution)/shard_map/down/pallas_call | solution.py:493
  73.3 1.8 %collective-permute-done.27.other_ref = bf16[128,2048]{1,0:T(8,128)(2,1)S(1)} collective-permute-done((bf16[128,2048]{1,0:T(8,128)(2,1)S(1)}, bf16[128,2048]{1,0:T(8,128)(2,1)S(1)}, u32[]{:S(2)}, u32[]{:S(2)}) %collective-permute-start.27) | collective-permute-done | bytes 524320 | tf_op jit(solution)/shard_map/ppermute | solution.py:33
  78.8 2.8 %collective-permute-done.28.refs_1_ = bf16[128,512]{1,0:T(8,128)(2,1)S(1)} collective-permute-done((bf16[128,512]{1,0:T(8,128)(2,1)S(1)}, bf16[128,512]{1,0:T(8,128)(2,1)S(1)}, u32[]{:S(2)}, u32[]{:S(2)}) %collective-permute-start.28) | collective-permute-done | bytes 131104 | tf_op jit(solution)/shard_map/ppermute | solution.py:33
  81.6 2.7 %collective-permute-done.29.refs_2_ = bf16[128,512]{1,0:T(8,128)(2,1)S(1)} collective-permute-done((bf16[128,512]{1,0:T(8,128)(2,1)S(1)}, bf16[128,512]{1,0:T(8,128)(2,1)S(1)}, u32[]{:S(2)}, u32[]{:S(2)}) %collective-permute-start.29) | collective-permute-done | bytes 131104 | tf_op jit(solution)/shard_map/ppermute | solution.py:33
  85.2 1.9 %collective-permute-start.32 = (bf16[64,512]{1,0:T(8,128)(2,1)S(1)}, bf16[64,512]{1,0:T(8,128)(2,1)S(1)}, u32[]{:S(2)}, u32[]{:S(2)}) collective-permute-start(bf16[64,512]{1,0:T(8,128)(2,1)S(1)} %get-tuple-element.91), channel_id=1, source_target_pairs={{0,12},{4,8},{8,4},{12,0},{1,13},{5,9},{9,5},{13,1},{2,14},{6,10},... | collective-permute-start | bytes 196616 | tf_op jit(solution)/shard_map/ppermute | solution.py:33
  87.1 4.8 %collective-permute-done.31.refs_2_ = bf16[64,512]{1,0:T(8,128)(2,1)S(1)} collective-permute-done((bf16[64,512]{1,0:T(8,128)(2,1)S(1)}, bf16[64,512]{1,0:T(8,128)(2,1)S(1)}, u32[]{:S(2)}, u32[]{:S(2)}) %collective-permute-start.31) | collective-permute-done | bytes 65568 | tf_op jit(solution)/shard_map/ppermute | solution.py:33
  (68 shorter events, 31.9 us)
Async XLA Ops:
  5.7 6.7 %collective-permute-start.1 = (bf16[144,256]{1,0:T(8,128)(2,1)S(1)}, bf16[144,256]{1,0:T(8,128)(2,1)S(1)}, u32[]{:S(2)}, u32[]{:S(2)}) collective-permute-start(bf16[144,256]{1,0:T(8,128)(2,1)S(1)} %get-tuple-element.50.refs_0_), channel_id=1, source_target_pairs={{0,1},{1,0},{2,3},{3,2},{4,5},{5,4},{6,7},{7,6},{8,9},{9,8},{10,11... | collective-permute-start | bytes 221192 | tf_op jit(solution)/shard_map/ppermute | solution.py:33
  24.9 6.7 %collective-permute-start.5 = (bf16[128,512]{1,0:T(8,128)(2,1)S(1)}, bf16[128,512]{1,0:T(8,128)(2,1)S(1)}, u32[]{:S(2)}, u32[]{:S(2)}) collective-permute-start(bf16[128,512]{1,0:T(8,128)(2,1)S(1)} %get-tuple-element.64), channel_id=1, source_target_pairs={{0,1},{1,0},{2,3},{3,2},{4,5},{5,4},{6,7},{7,6},{8,9},{9,8},{10,11... | collective-permute-start | bytes 393224 | tf_op jit(solution)/shard_map/ppermute | solution.py:33
  25.5 8.3 %collective-permute-start.6 = (bf16[128,512]{1,0:T(8,128)(2,1)S(1)}, bf16[128,512]{1,0:T(8,128)(2,1)S(1)}, u32[]{:S(2)}, u32[]{:S(2)}) collective-permute-start(bf16[128,512]{1,0:T(8,128)(2,1)S(1)} %get-tuple-element.65), channel_id=1, source_target_pairs={{0,2},{1,3},{2,0},{3,1},{4,6},{5,7},{6,4},{7,5},{8,10},{9,11},{10,... | collective-permute-start | bytes 393224 | tf_op jit(solution)/shard_map/ppermute | solution.py:33
  26.2 7.6 %collective-permute-start.7 = (bf16[128,512]{1,0:T(8,128)(2,1)S(1)}, bf16[128,512]{1,0:T(8,128)(2,1)S(1)}, u32[]{:S(2)}, u32[]{:S(2)}) collective-permute-start(bf16[128,512]{1,0:T(8,128)(2,1)S(1)} %get-tuple-element.66), channel_id=1, source_target_pairs={{0,3},{1,2},{2,1},{3,0},{4,7},{5,6},{6,5},{7,4},{8,11},{9,10},{10,... | collective-permute-start | bytes 393224 | tf_op jit(solution)/shard_map/ppermute | solution.py:33
  34.0 6.6 %collective-permute-start.11 = (bf16[64,512]{1,0:T(8,128)(2,1)S(1)}, bf16[64,512]{1,0:T(8,128)(2,1)S(1)}, u32[]{:S(2)}, u32[]{:S(2)}) collective-permute-start(bf16[64,512]{1,0:T(8,128)(2,1)S(1)} %get-tuple-element.69), channel_id=1, source_target_pairs={{0,4},{4,0},{8,12},{12,8},{1,5},{5,1},{9,13},{13,9},{2,6},{6,2},{1... | collective-permute-start | bytes 196616 | tf_op jit(solution)/shard_map/ppermute | solution.py:33
  35.7 6.9 %collective-permute-start.15 = (bf16[64,512]{1,0:T(8,128)(2,1)S(1)}, bf16[64,512]{1,0:T(8,128)(2,1)S(1)}, u32[]{:S(2)}, u32[]{:S(2)}) collective-permute-start(bf16[64,512]{1,0:T(8,128)(2,1)S(1)} %get-tuple-element.71), channel_id=1, source_target_pairs={{0,8},{4,12},{8,0},{12,4},{1,9},{5,13},{9,1},{13,5},{2,10},{6,14},... | collective-permute-start | bytes 196616 | tf_op jit(solution)/shard_map/ppermute | solution.py:33
  38.3 6.1 %collective-permute-start.16 = (bf16[64,512]{1,0:T(8,128)(2,1)S(1)}, bf16[64,512]{1,0:T(8,128)(2,1)S(1)}, u32[]{:S(2)}, u32[]{:S(2)}) collective-permute-start(bf16[64,512]{1,0:T(8,128)(2,1)S(1)} %get-tuple-element.72), channel_id=1, source_target_pairs={{0,12},{4,8},{8,4},{12,0},{1,13},{5,9},{9,5},{13,1},{2,14},{6,10},... | collective-permute-start | bytes 196616 | tf_op jit(solution)/shard_map/ppermute | solution.py:33
  38.5 7.1 %collective-permute-start.8 = (bf16[64,512]{1,0:T(8,128)(2,1)S(1)}, bf16[64,512]{1,0:T(8,128)(2,1)S(1)}, u32[]{:S(2)}, u32[]{:S(2)}) collective-permute-start(bf16[64,512]{1,0:T(8,128)(2,1)S(1)} %get-tuple-element.68.refs_0_), channel_id=1, source_target_pairs={{0,1},{1,0},{2,3},{3,2},{4,5},{5,4},{6,7},{7,6},{8,9},{9,8},{10,11... | collective-permute-start | bytes 196616 | tf_op jit(solution)/shard_map/ppermute | solution.py:33
  40.0 7.4 %collective-permute-start.9 = (bf16[64,512]{1,0:T(8,128)(2,1)S(1)}, bf16[64,512]{1,0:T(8,128)(2,1)S(1)}, u32[]{:S(2)}, u32[]{:S(2)}) collective-permute-start(bf16[64,512]{1,0:T(8,128)(2,1)S(1)} %get-tuple-element.68.refs_0_), channel_id=1, source_target_pairs={{0,2},{1,3},{2,0},{3,1},{4,6},{5,7},{6,4},{7,5},{8,10},{9,11},{10,... | collective-permute-start | bytes 196616 | tf_op jit(solution)/shard_map/ppermute | solution.py:33
  40.7 6.7 %collective-permute-start.10 = (bf16[64,512]{1,0:T(8,128)(2,1)S(1)}, bf16[64,512]{1,0:T(8,128)(2,1)S(1)}, u32[]{:S(2)}, u32[]{:S(2)}) collective-permute-start(bf16[64,512]{1,0:T(8,128)(2,1)S(1)} %get-tuple-element.68.refs_0_), channel_id=1, source_target_pairs={{0,3},{1,2},{2,1},{3,0},{4,7},{5,6},{6,5},{7,4},{8,11},{9,10},{10,... | collective-permute-start | bytes 196616 | tf_op jit(solution)/shard_map/ppermute | solution.py:33
  51.0 5.7 %collective-permute-start.17 = (bf16[128,2048]{1,0:T(8,128)(2,1)S(1)}, bf16[128,2048]{1,0:T(8,128)(2,1)S(1)}, u32[]{:S(2)}, u32[]{:S(2)}) collective-permute-start(bf16[128,2048]{1,0:T(8,128)(2,1)S(1)} %norm.2.x_ref), channel_id=1, source_target_pairs={{0,16},{16,0},{1,17},{17,1},{2,18},{18,2},{3,19},{19,3},{4,20},{20... | collective-permute-start | bytes 1572872 | tf_op jit(solution)/shard_map/ppermute | solution.py:33
  51.1 9.9 %collective-permute-start.23 = (bf16[128,512]{1,0:T(8,128)(2,1)S(1)}, bf16[128,512]{1,0:T(8,128)(2,1)S(1)}, u32[]{:S(2)}, u32[]{:S(2)}) collective-permute-start(bf16[128,512]{1,0:T(8,128)(2,1)S(1)} %stack.1.refs_1_.refs_0_), channel_id=1, source_target_pairs={{0,1},{1,0},{2,3},{3,2},{4,5},{5,4},{6,7},{7,6},{8,9},{9,8},{10,11... | collective-permute-start | bytes 393224 | tf_op jit(solution)/shard_map/ppermute | solution.py:33
  52.1 8.9 %collective-permute-start.24 = (bf16[128,512]{1,0:T(8,128)(2,1)S(1)}, bf16[128,512]{1,0:T(8,128)(2,1)S(1)}, u32[]{:S(2)}, u32[]{:S(2)}) collective-permute-start(bf16[128,512]{1,0:T(8,128)(2,1)S(1)} %stack.1.refs_1_.refs_0_), channel_id=1, source_target_pairs={{0,2},{1,3},{2,0},{3,1},{4,6},{5,7},{6,4},{7,5},{8,10},{9,11},{10,... | collective-permute-start | bytes 393224 | tf_op jit(solution)/shard_map/ppermute | solution.py:33
  53.5 7.6 %collective-permute-start.25 = (bf16[128,512]{1,0:T(8,128)(2,1)S(1)}, bf16[128,512]{1,0:T(8,128)(2,1)S(1)}, u32[]{:S(2)}, u32[]{:S(2)}) collective-permute-start(bf16[128,512]{1,0:T(8,128)(2,1)S(1)} %stack.1.refs_1_.refs_0_), channel_id=1, source_target_pairs={{0,3},{1,2},{2,1},{3,0},{4,7},{5,6},{6,5},{7,4},{8,11},{9,10},{10,... | collective-permute-start | bytes 393224 | tf_op jit(solution)/shard_map/ppermute | solution.py:33
  61.3 7.4 %collective-permute-start.26 = (bf16[128,2048]{1,0:T(8,128)(2,1)S(1)}, bf16[128,2048]{1,0:T(8,128)(2,1)S(1)}, u32[]{:S(2)}, u32[]{:S(2)}) collective-permute-start(bf16[128,2048]{1,0:T(8,128)(2,1)S(1)} %norm.3.x_ref), channel_id=1, source_target_pairs={{0,16},{16,0},{1,17},{17,1},{2,18},{18,2},{3,19},{19,3},{4,20},{20... | collective-permute-start | bytes 1572872 | tf_op jit(solution)/shard_map/ppermute | solution.py:33
  63.0 10.2 %collective-permute-start.19 = (bf16[128,512]{1,0:T(8,128)(2,1)S(1)}, bf16[128,512]{1,0:T(8,128)(2,1)S(1)}, u32[]{:S(2)}, u32[]{:S(2)}) collective-permute-start(bf16[128,512]{1,0:T(8,128)(2,1)S(1)} %get-tuple-element.79), channel_id=1, source_target_pairs={{0,1},{1,0},{2,3},{3,2},{4,5},{5,4},{6,7},{7,6},{8,9},{9,8},{10,11... | collective-permute-start | bytes 393224 | tf_op jit(solution)/shard_map/ppermute | solution.py:33
  64.1 9.1 %collective-permute-start.20 = (bf16[128,512]{1,0:T(8,128)(2,1)S(1)}, bf16[128,512]{1,0:T(8,128)(2,1)S(1)}, u32[]{:S(2)}, u32[]{:S(2)}) collective-permute-start(bf16[128,512]{1,0:T(8,128)(2,1)S(1)} %get-tuple-element.80), channel_id=1, source_target_pairs={{0,2},{1,3},{2,0},{3,1},{4,6},{5,7},{6,4},{7,5},{8,10},{9,11},{10,... | collective-permute-start | bytes 393224 | tf_op jit(solution)/shard_map/ppermute | solution.py:33
  65.4 7.8 %collective-permute-start.21 = (bf16[128,512]{1,0:T(8,128)(2,1)S(1)}, bf16[128,512]{1,0:T(8,128)(2,1)S(1)}, u32[]{:S(2)}, u32[]{:S(2)}) collective-permute-start(bf16[128,512]{1,0:T(8,128)(2,1)S(1)} %get-tuple-element.81), channel_id=1, source_target_pairs={{0,3},{1,2},{2,1},{3,0},{4,7},{5,6},{6,5},{7,4},{8,11},{9,10},{10,... | collective-permute-start | bytes 393224 | tf_op jit(solution)/shard_map/ppermute | solution.py:33
  75.2 6.4 %collective-permute-start.28 = (bf16[128,512]{1,0:T(8,128)(2,1)S(1)}, bf16[128,512]{1,0:T(8,128)(2,1)S(1)}, u32[]{:S(2)}, u32[]{:S(2)}) collective-permute-start(bf16[128,512]{1,0:T(8,128)(2,1)S(1)} %get-tuple-element.87), channel_id=1, source_target_pairs={{0,1},{1,0},{2,3},{3,2},{4,5},{5,4},{6,7},{7,6},{8,9},{9,8},{10,11... | collective-permute-start | bytes 393224 | tf_op jit(solution)/shard_map/ppermute | solution.py:33
  76.3 8.1 %collective-permute-start.29 = (bf16[128,512]{1,0:T(8,128)(2,1)S(1)}, bf16[128,512]{1,0:T(8,128)(2,1)S(1)}, u32[]{:S(2)}, u32[]{:S(2)}) collective-permute-start(bf16[128,512]{1,0:T(8,128)(2,1)S(1)} %get-tuple-element.88), channel_id=1, source_target_pairs={{0,2},{1,3},{2,0},{3,1},{4,6},{5,7},{6,4},{7,5},{8,10},{9,11},{10,... | collective-permute-start | bytes 393224 | tf_op jit(solution)/shard_map/ppermute | solution.py:33
  77.6 6.7 %collective-permute-start.30 = (bf16[128,512]{1,0:T(8,128)(2,1)S(1)}, bf16[128,512]{1,0:T(8,128)(2,1)S(1)}, u32[]{:S(2)}, u32[]{:S(2)}) collective-permute-start(bf16[128,512]{1,0:T(8,128)(2,1)S(1)} %get-tuple-element.89), channel_id=1, source_target_pairs={{0,3},{1,2},{2,1},{3,0},{4,7},{5,6},{6,5},{7,4},{8,11},{9,10},{10,... | collective-permute-start | bytes 393224 | tf_op jit(solution)/shard_map/ppermute | solution.py:33
  78.8 8.3 %collective-permute-start.22 = (bf16[64,512]{1,0:T(8,128)(2,1)S(1)}, bf16[64,512]{1,0:T(8,128)(2,1)S(1)}, u32[]{:S(2)}, u32[]{:S(2)}) collective-permute-start(bf16[64,512]{1,0:T(8,128)(2,1)S(1)} %get-tuple-element.83), channel_id=1, source_target_pairs={{0,4},{4,0},{8,12},{12,8},{1,5},{5,1},{9,13},{13,9},{2,6},{6,2},{1... | collective-permute-start | bytes 196616 | tf_op jit(solution)/shard_map/ppermute | solution.py:33
  84.4 7.6 %collective-permute-start.31 = (bf16[64,512]{1,0:T(8,128)(2,1)S(1)}, bf16[64,512]{1,0:T(8,128)(2,1)S(1)}, u32[]{:S(2)}, u32[]{:S(2)}) collective-permute-start(bf16[64,512]{1,0:T(8,128)(2,1)S(1)} %get-tuple-element.90), channel_id=1, source_target_pairs={{0,8},{4,12},{8,0},{12,4},{1,9},{5,13},{9,1},{13,5},{2,10},{6,14},... | collective-permute-start | bytes 196616 | tf_op jit(solution)/shard_map/ppermute | solution.py:33
  85.2 6.7 %collective-permute-start.32 = (bf16[64,512]{1,0:T(8,128)(2,1)S(1)}, bf16[64,512]{1,0:T(8,128)(2,1)S(1)}, u32[]{:S(2)}, u32[]{:S(2)}) collective-permute-start(bf16[64,512]{1,0:T(8,128)(2,1)S(1)} %get-tuple-element.91), channel_id=1, source_target_pairs={{0,12},{4,8},{8,4},{12,0},{1,13},{5,9},{9,5},{13,1},{2,14},{6,10},... | collective-permute-start | bytes 196616 | tf_op jit(solution)/shard_map/ppermute | solution.py:33
  (11 other events, 59.4 us)

commit v4 on v3

--- a/solution.py
+++ b/solution.py
@@ -31,6 +31,11 @@
 
 def swap(block, axis, k):
     return lax.ppermute(block, axis, [(i, i ^ k) for i in range(lax.axis_size(axis))])
+
+
+def swaps(blocks):
+    got = {k: swap(blocks[k - 1], "tp", k) for k in range(len(blocks), 0, -1)}
+    return [got[k] for k in sorted(got)]
 
 
 def sigmoid(x):
@@ -133,28 +138,10 @@
     )(ids, experts)
 
 
-def conv_kernel(
-    before_ref, x_hbm, taps_hbm, bias_hbm, weight_hbm, xconv_ref, part_ref,
-    ext_ref, x_ref, taps_ref, bias_ref, weight_ref, sems,
-):
+def conv_kernel(before_ref, x_ref, taps_ref, bias_ref, weight_ref, xconv_ref, part_ref, ext_ref):
     rows = x_ref.shape[0]
     halo = 16
     count = taps_ref.shape[0]
-    copies = [
-        pltpu.make_async_copy(source, target, sems.at[i])
-        for i, (source, target) in enumerate(
-            (
-                (x_hbm, x_ref),
-                (taps_hbm, taps_ref),
-                (bias_hbm, bias_ref),
-                (weight_hbm, weight_ref),
-            )
-        )
-    ]
-    for copy in copies:
-        copy.start()
-    for copy in copies[:3]:
-        copy.wait()
     ext_ref[:halo, :] = before_ref[rows - halo :, :].astype(F32)
     ext_ref[halo:, :] = x_ref[...].astype(F32)
     total = bias_ref[...] + taps_ref[count - 1 : count, :] * ext_ref[halo:, :]
@@ -163,7 +150,6 @@
         total = total + taps_ref[k : k + 1, :] * ext_ref[start : start + rows, :]
     xconv = (total * sigmoid(total)).astype(BF16)
     xconv_ref[...] = xconv
-    copies[3].wait()
     across = (((1,), (1,)), ((), ()))
     part_ref[:rows, :] = lax.dot_general(
         xconv, weight_ref[:DT_RANK, :], across, preferred_element_type=F32
@@ -180,19 +166,37 @@
     return pl.pallas_call(
         conv_kernel,
         out_shape=(shaped((rows, channels), BF16), shaped((rows + STATE, DT_RANK), BF16)),
-        in_specs=[whole()] + [hbm()] * 4,
+        in_specs=[whole()] * 5,
         out_specs=[whole()] * 2,
-        scratch_shapes=[
-            pltpu.VMEM((16 + rows, channels), F32),
-            pltpu.VMEM((rows, channels), BF16),
-            pltpu.VMEM(taps.shape, F32),
-            pltpu.VMEM(bias.shape, F32),
-            pltpu.VMEM(weight.shape, BF16),
-            pltpu.SemaphoreType.DMA((4,)),
-        ],
-        compiler_params=params(),
+        scratch_shapes=[pltpu.VMEM((16 + rows, channels), F32)],
+        compiler_params=params(),
+        cost_estimate=cost(1e6, 1e6),
         name="conv",
     )(before, x, taps, bias, weight)
+
+
+def load_kernel(count, *refs):
+    copies = [
+        pltpu.make_async_copy(refs[i], refs[count + i], refs[-1].at[i]) for i in range(count)
+    ]
+    for copy in copies:
+        copy.start()
+    for copy in copies:
+        copy.wait()
+
+
+def load(*arrays):
+    count = len(arrays)
+    return pl.pallas_call(
+        functools.partial(load_kernel, count),
+        out_shape=[shaped(array.shape, array.dtype) for array in arrays],
+        in_specs=[hbm()] * count,
+        out_specs=[whole()] * count,
+        scratch_shapes=[pltpu.SemaphoreType.DMA((count,))],
+        compiler_params=params(),
+        cost_estimate=cost(1e6, 2e6),
+        name="load",
+    )(*arrays)
 
 
 def prepare_kernel(
@@ -547,29 +551,31 @@
     )(*pieces)
 
 
-def blend_kernel(experts, *refs):
-    back = refs[:experts]
-    stream_ref, first_ref, second_ref, gates_ref, out_ref, rows_ref = refs[experts:]
+def blend_kernel(begin, count, *refs):
+    back = refs[:count]
+    base_ref, first_ref, second_ref, gates_ref, out_ref, rows_ref = refs[count:]
     for j, ref in enumerate(back):
         rows_ref[j * CAP : (j + 1) * CAP, :] = ref[...]
     rows = rows_ref[...]
     gates = jnp.transpose(gates_ref[...])
-    moe = gates[:, 0:1] * jnp.dot(first_ref[...], rows, preferred_element_type=F32)
-    moe = moe + gates[:, 1:2] * jnp.dot(second_ref[...], rows, preferred_element_type=F32)
-    out_ref[...] = (stream_ref[...].astype(F32) + moe).astype(BF16)
-
-
-def blend(back, stream, first, second, gates):
-    experts, width = len(back), stream.shape[1]
-    return pl.pallas_call(
-        functools.partial(blend_kernel, experts),
-        out_shape=shaped(stream.shape, BF16),
-        in_specs=[whole()] * (experts + 4),
+    cut = slice(begin, begin + count * CAP)
+    moe = gates[:, 0:1] * jnp.dot(first_ref[:, cut], rows, preferred_element_type=F32)
+    moe = moe + gates[:, 1:2] * jnp.dot(second_ref[:, cut], rows, preferred_element_type=F32)
+    out_ref[...] = (base_ref[...].astype(F32) + moe).astype(out_ref.dtype)
+
+
+def blend(begin, back, base, first, second, gates, dtype):
+    count, width = len(back), base.shape[1]
+    return pl.pallas_call(
+        functools.partial(blend_kernel, begin, count),
+        out_shape=shaped(base.shape, dtype),
+        in_specs=[whole()] * (count + 4),
         out_specs=whole(),
-        scratch_shapes=[pltpu.VMEM((experts * CAP, width), BF16)],
-        compiler_params=params(),
+        scratch_shapes=[pltpu.VMEM((count * CAP, width), BF16)],
+        compiler_params=params(),
+        cost_estimate=cost(1e6, 1e6),
         name="blend",
-    )(*back, stream, first, second, gates)
+    )(*back, base, first, second, gates)
 
 
 def expert(tp, x_own, gate, up, down, after_start, after_sums):
@@ -603,10 +609,9 @@
     local = conv_in[0]
     before = lax.ppermute(local, "ctx", [(0, 1)])
     expert_weight = stay(expert_weight)
-    xconv, part = conv(
-        before, stay(local), stay(conv_weight), stay(conv_bias[None]), stay(proj_weight.T)
-    )
-    parts = [part] + [swap(part, "tp", k) for k in range(1, tp)]
+    near = load(stay(local), stay(conv_weight), stay(conv_bias[None]), stay(proj_weight.T))
+    xconv, part = conv(before, *near)
+    parts = [part] + swaps([part] * (tp - 1))
     silu, rates, skip, bias, step_w, out_w, quarter, gain = prepare(
         tp, stay(gate_in[0]), stay(decay_log), stay(residual[0]), stay(skip_gain[None]),
         stay(step_bias[None]), stay(step_weight), stay(out_weight), stay(norm_gain[None]),
@@ -616,27 +621,27 @@
     own, *sent, down_w = mix(
         tp, maps, y, elapsed, rates, before, silu, quarter, out_w, expert_weight
     )
-    arrived = [swap(piece, "tp", k) for k, piece in enumerate(sent, 1)]
+    arrived = swaps(sent)
     first, second, chooser, gate_w = route(expert_ids[0].T, experts, expert_weight)
     stream, *picked = pick(own, arrived, chooser)
-    rows = [picked[0]] + [swap(picked[j], "exp", j) for j in range(1, experts)]
     half = experts // 2
-    piece_a = rows[1] if half == 2 else stack(rows[1:half], [])
-    piece_b = stack(rows[half:], [rows[1]])
-    both = order([rows[1], piece_b])
-    sets = [
-        [piece] + [swap(piece, "tp", k) for k in range(1, tp)]
-        for piece in (rows[0], piece_a, piece_b)
-    ]
-    x_a = norm(sets[:2], gain, [both])
+    rows = {j: swap(picked[j], "exp", j) for j in range(experts - 1, 0, -1)}
+    piece_a = stack([rows[j] for j in range(half, experts)], [])
+    piece_b = stack([picked[0]] + [rows[j] for j in range(1, half)], [piece_a])
+    both = order([piece_a, piece_b])
+    rows_a = [piece_a] + swaps([piece_a] * (tp - 1))
+    rows_b = [piece_b] + swaps([piece_b] * (tp - 1))
+    x_a = norm([rows_a], gain, [both])
     own_a, joined_a = expert(tp, x_a, gate_w, up_w, down_w, [], [])
-    summed_a = [joined_a[0]] + [swap(joined_a[k], "tp", k) for k in range(1, tp)]
-    back = totals(summed_a)
-    x_b = norm(sets[2:], gain, [own_a])
-    _, joined_b = expert(tp, x_b, gate_w, up_w, down_w, [joined_a[0]], [back[0]])
-    back += totals([joined_b[0]] + [swap(joined_b[k], "tp", k) for k in range(1, tp)])
-    back = [back[0]] + [swap(back[j], "exp", j) for j in range(1, experts)]
-    return blend(back, stream, first, second, route_gates[0].T)[None]
+    made_a = totals([joined_a[0]] + swaps(joined_a[1:]))
+    x_b = norm([rows_b], gain, [own_a])
+    _, joined_b = expert(tp, x_b, gate_w, up_w, down_w, [joined_a[0]], [made_a[0]])
+    made_b = totals([joined_b[0]] + swaps(joined_b[1:]))
+    back_a = [swap(piece, "exp", j) for j, piece in enumerate(made_a, half)]
+    back_b = [made_b[0]] + [swap(made_b[j], "exp", j) for j in range(1, half)]
+    gates = route_gates[0].T
+    partial = blend(half * CAP, back_a, stream, first, second, gates, F32)
+    return blend(0, back_b, partial, first, second, gates, BF16)[None]
 
 
 def solution(mesh):

time: 93.1 us -> 89.5 us (0.961)
  starting transfers between devices: 37.5 us -> 32.4 us
  waiting for transfers between devices: 24.6 us -> 26.1 us
    ppermute x31 -> x28, starting transfers between devices: 33.8 us -> 28.8 us  [swap(): lax.ppermute(block, axis, [(i, i ^ k) for i in range(lax.axis_size(axis))])]
    ppermute x31 -> x28, waiting for transfers between devices: 22.4 us -> 25.1 us  [swap(): lax.ppermute(block, axis, [(i, i ^ k) for i in range(lax.axis_size(axis))])]
    pallas_call x1, Pallas kernels: 2.02 us -> 0.56 us  [conv(): pl.pallas_call(conv_kernel, out_shape=(shaped((rows, channels), BF16), sh...]
    pallas_call x1 -> x3, Pallas kernels: 0.94 us -> 2.39 us  [the longest x1 1.22 us: load(): pl.pallas_call(functools.partial(load_kernel, count), out_shape=[shaped(a...]
    ppermute x1, waiting for transfers between devices: 1.34 us -> 0.11 us  [body(): before = lax.ppermute(local, 'ctx', [(0, 1)])]
  transfers between devices with their start and end apart: 33 -> 30, of which waited for: 13 -> 14; matrix products, arithmetic and copies ran while one was open for 0% -> 0% of each run, Pallas kernels for 21% -> 23%
where the time goes in v4:
time: 89.5 us; the launch traced here: 89.3 us
  starting transfers between devices  32.4 us (36%)
  Pallas kernels  30.4 us (34%)
  waiting for transfers between devices  26.1 us (29%)
    ppermute x28, starting transfers between devices, swap(): lax.ppermute(block, axis, [(i, i ^ k) for i in range(lax.axis_size(axis))])  28.8 us
    ppermute x28, waiting for transfers between devices, swap(): lax.ppermute(block, axis, [(i, i ^ k) for i in range(lax.axis_size(axis))])  25.1 us
    pallas_call x4, Pallas kernels, hidden_units(): pl.pallas_call(hidden_kernel, out_shape=shaped((rows, width), BF16), in_s...  8.6 us
    pallas_call x1, Pallas kernels, scan(): pl.pallas_call(functools.partial(scan_kernel, len(pieces)), out_shape=(sh...  4.38 us
    pallas_call x2, Pallas kernels, down_sums(): pl.pallas_call(down_kernel, out_shape=(shaped((rows, model), F32), shaped...  4.18 us
    pallas_call x1, Pallas kernels, mix(): pl.pallas_call(functools.partial(mix_kernel, parts), out_shape=[shaped((r...  3.37 us
    pallas_call x1, Pallas kernels, route(): pl.pallas_call(route_kernel, out_shape=(shaped((rows, slots), BF16), shap...  3.09 us
    pallas_call x1, Pallas kernels, prepare(): pl.pallas_call(prepare_kernel, out_shape=(shaped((rows, channels), F32),...  2.76 us
  transfers between devices with their start and end apart: 30, of which 14 were waited for; matrix products, arithmetic and copies ran while one was open for 0% of the time, Pallas kernels for 23%

profile of v4, /device:TPU:0, one launch (start us, length us, event | category | flops | bytes accessed | tf_op | source)
XLA Modules:
  0.0 89.3 jit_solution(10168924564977147482)
XLA Ops:
  0.0 2.4 %collective-permute-start = (bf16[128,1024]{1,0:T(8,128)(2,1)}, bf16[128,1024]{1,0:T(8,128)(2,1)S(1)}, u32[]{:S(2)}, u32[]{:S(2)}) collective-permute-start(bf16[128,1024]{1,0:T(8,128)(2,1)} %bitcast.21), channel_id=1, source_target_pairs={{0,16},{1,17},{2,18},{3,19},{4,20},{5,21},{6,22},{7,23},{8,24},{9,... | collective-permute-start | bytes 786440 | tf_op jit(solution)/shard_map/ppermute | solution.py:610
  4.3 2.4 %collective-permute-start.1 = (bf16[144,256]{1,0:T(8,128)(2,1)S(1)}, bf16[144,256]{1,0:T(8,128)(2,1)S(1)}, u32[]{:S(2)}, u32[]{:S(2)}) collective-permute-start(bf16[144,256]{1,0:T(8,128)(2,1)S(1)} %get-tuple-element.58.refs_0_), channel_id=1, source_target_pairs={{0,1},{1,0},{2,3},{3,2},{4,5},{5,4},{6,7},{7,6},{8,9},{9,8},{10,11... | collective-permute-start | bytes 221192 | tf_op jit(solution)/shard_map/ppermute | solution.py:33
  8.2 2.8 %prepare.1 = (f32[128,1024]{1,0:T(8,128)S(1)}, f32[16,1024]{1,0:T(8,128)S(1)}, f32[1,1024]{1,0:T(1,128)S(1)}, f32[1,1024]{1,0:T(1,128)S(1)}, bf16[256,1024]{1,0:...) custom-call(bf16[128,1024]{1,0:T(8,128)(2,1)} %bitcast.20, ...), custom_call_target="tpu_custom_call" | custom-call | flops 1000000 | bytes 6000000 | tf_op jit(solution)/shard_map/prepare/pallas_call | solution.py:238
  11.0 2.4 %collective-permute-done.3.refs_3_ = bf16[144,256]{1,0:T(8,128)(2,1)S(1)} collective-permute-done((bf16[144,256]{1,0:T(8,128)(2,1)S(1)}, bf16[144,256]{1,0:T(8,128)(2,1)S(1)}, u32[]{:S(2)}, u32[]{:S(2)}) %collective-permute-start.3) | collective-permute-done | bytes 73760 | tf_op jit(solution)/shard_map/ppermute | solution.py:33
  13.5 4.4 %scan.1 = (f32[128,1024]{1,0:T(8,128)S(1)}, f32[128,1024]{1,0:T(8,128)S(1)}, f32[16,256]{1,0:T(8,128)S(1)}, f32[16,1024]{1,0:T(8,128)S(1)}, bf16[2048,1792]{1,0:T(8,128)(2,1)S(1)}) custom-call(bf16[144,256]{1,0:T(8,128)(2,1)S(1)} %get-tuple-element.58.refs_0_, bf16[144,256]{1,0:T(8,128)(2,1)S(1)} %collective-permute-done.1.refs_1_, ...), custom_call_target="tpu_custom_call" | custom-call | flops 1000000 | bytes 14000000 | tf_op jit(solution)/shard_map/scan/pallas_call | solution.py:320
  20.0 3.4 %mix.1 = (f32[128,512]{1,0:T(8,128)S(1)}, bf16[128,512]{1,0:T(8,128)(2,1)S(1)}, bf16[128,512]{1,0:T(8,128)(2,1)S(1)}, bf16[128,512]{1,0:T(8,128)(2,1)S(1)}, bf16[2048,1792]{1,0:T(8,128)(2,1)S(1)}) custom-call(f32[16,256]{1,0:T(8,128)S(1)} %get-tuple-element.64.refs_0_, f32[128,1024]{1,0:T(8,128)S(1)} %get-tuple-element.65.refs_1_, ...), custom_call_target="tpu_custom_call" | custom-call | flops 1000000 | bytes 12000000 | tf_op jit(solution)/shard_map/mix/pallas_call | solution.py:379
  24.7 2.3 %collective-permute-start.7 = (bf16[128,512]{1,0:T(8,128)(2,1)S(1)}, bf16[128,512]{1,0:T(8,128)(2,1)S(1)}, u32[]{:S(2)}, u32[]{:S(2)}) collective-permute-start(bf16[128,512]{1,0:T(8,128)(2,1)S(1)} %get-tuple-element.74), channel_id=1, source_target_pairs={{0,3},{1,2},{2,1},{3,0},{4,7},{5,6},{6,5},{7,4},{8,11},{9,10},{10,... | collective-permute-start | bytes 393224 | tf_op jit(solution)/shard_map/ppermute | solution.py:33
  27.0 3.1 %route.1 = (bf16[128,256]{1,0:T(8,128)(2,1)S(1)}, bf16[128,256]{1,0:T(8,128)(2,1)S(1)}, bf16[256,128]{1,0:T(8,128)(2,1)S(1)}, bf16[2048,1792]{1,0:T(8,128)(2,1)S(1)}) custom-call(s32[2,128]{1,0:T(2,128)S(1)} %bitcast.17, bf16[1,3,2048,1792]{3,2,1,0:T(8,128)(2,1)} %expert_hbm.1), custom_call_target="tpu_custom_call" | custom-call | flops 1000000 | bytes 8000000 | tf_op jit(solution)/shard_map/route/pallas_call | solution.py:124
  30.1 2.2 %collective-permute-done.6.refs_2_ = bf16[128,512]{1,0:T(8,128)(2,1)S(1)} collective-permute-done((bf16[128,512]{1,0:T(8,128)(2,1)S(1)}, bf16[128,512]{1,0:T(8,128)(2,1)S(1)}, u32[]{:S(2)}, u32[]{:S(2)}) %collective-permute-start.6) | collective-permute-done | bytes 131104 | tf_op jit(solution)/shard_map/ppermute | solution.py:33
  32.6 3.7 %collective-permute-start.10 = (bf16[64,512]{1,0:T(8,128)(2,1)S(1)}, bf16[64,512]{1,0:T(8,128)(2,1)S(1)}, u32[]{:S(2)}, u32[]{:S(2)}) collective-permute-start(bf16[64,512]{1,0:T(8,128)(2,1)S(1)} %get-tuple-element.79), channel_id=1, source_target_pairs={{0,12},{4,8},{8,4},{12,0},{1,13},{5,9},{9,5},{13,1},{2,14},{6,10},... | collective-permute-start | bytes 196616 | tf_op jit(solution)/shard_map/ppermute | solution.py:33
  37.0 2.4 %collective-permute-done.10.refs_1_ = bf16[64,512]{1,0:T(8,128)(2,1)S(1)} collective-permute-done((bf16[64,512]{1,0:T(8,128)(2,1)S(1)}, bf16[64,512]{1,0:T(8,128)(2,1)S(1)}, u32[]{:S(2)}, u32[]{:S(2)}) %collective-permute-start.10) | collective-permute-done | bytes 65568 | tf_op jit(solution)/shard_map/ppermute | solution.py:33
  39.4 2.1 %collective-permute-done.9.refs_0_ = bf16[64,512]{1,0:T(8,128)(2,1)S(1)} collective-permute-done((bf16[64,512]{1,0:T(8,128)(2,1)S(1)}, bf16[64,512]{1,0:T(8,128)(2,1)S(1)}, u32[]{:S(2)}, u32[]{:S(2)}) %collective-permute-start.9) | collective-permute-done | bytes 65568 | tf_op jit(solution)/shard_map/ppermute | solution.py:33
  45.1 2.6 %collective-permute-done.14.refs_1_ = bf16[128,512]{1,0:T(8,128)(2,1)S(1)} collective-permute-done((bf16[128,512]{1,0:T(8,128)(2,1)S(1)}, bf16[128,512]{1,0:T(8,128)(2,1)S(1)}, u32[]{:S(2)}, u32[]{:S(2)}) %collective-permute-start.14) | collective-permute-done | bytes 131104 | tf_op jit(solution)/shard_map/ppermute | solution.py:33
  47.7 2.6 %collective-permute-done.15.refs_2_ = bf16[128,512]{1,0:T(8,128)(2,1)S(1)} collective-permute-done((bf16[128,512]{1,0:T(8,128)(2,1)S(1)}, bf16[128,512]{1,0:T(8,128)(2,1)S(1)}, u32[]{:S(2)}, u32[]{:S(2)}) %collective-permute-start.15) | collective-permute-done | bytes 131104 | tf_op jit(solution)/shard_map/ppermute | solution.py:33
  54.2 2.1 %hidden.4.refs_0_.hidden_own_ref = bf16[128,1792]{1,0:T(8,128)(2,1)S(1)} custom-call(bf16[128,2048]{1,0:T(8,128)(2,1)S(1)} %norm.2.x_ref, bf16[2048,1792]{1,0:T(8,128)(2,1)S(1)} %get-tuple-element.81.gate_ref, bf16[2048,1792]{1,0:T(8,128)(2,1)S(1)} %get-tuple-element.82.up_ref), custom_call_target="tpu_custom_call" | custom-call | flops 1000000 | tf_op jit(solution)/shard_map/hidden/pallas_call | solution.py:468
  56.3 2.1 %hidden.5.hidden_other_ref = bf16[128,1792]{1,0:T(8,128)(2,1)S(1)} custom-call(bf16[128,2048]{1,0:T(8,128)(2,1)S(1)} %collective-permute-done.17.x_ref, bf16[2048,1792]{1,0:T(8,128)(2,1)S(1)} %get-tuple-element.81.gate_ref, bf16[2048,1792]{1,0:T(8,128)(2,1)S(1)} %get-tuple-element.82.up_ref, bf16[128,1792]{1,0:T(8,128)(2,1)S(1)} %hidden.4.refs_0_.hidden_own_ref), custom_call_target="tpu_custom_call" | custom-call | flops 1000000 | tf_op jit(solution)/shard_map/hidden/pallas_call | solution.py:468
  58.4 2.1 %down.2 = (f32[128,2048]{1,0:T(8,128)S(1)}, bf16[128,2048]{1,0:T(8,128)(2,1)S(1)}) custom-call(bf16[128,1792]{1,0:T(8,128)(2,1)S(1)} %hidden.4.refs_0_.hidden_own_ref, bf16[128,1792]{1,0:T(8,128)(2,1)S(1)} %hidden.5.hidden_other_ref, bf16[2048,1792]{1,0:T(8,128)(2,1)S(1)} %get-tuple-element.83.down_ref), custom_call_target="tpu_custom_call" | custom-call | flops 1000000 | tf_op jit(solution)/shard_map/down/pallas_call | solution.py:497
  66.1 2.1 %hidden.6.refs_0_.hidden_own_ref = bf16[128,1792]{1,0:T(8,128)(2,1)S(1)} custom-call(bf16[128,2048]{1,0:T(8,128)(2,1)S(1)} %norm.3.x_ref, bf16[2048,1792]{1,0:T(8,128)(2,1)S(1)} %get-tuple-element.81.gate_ref, bf16[2048,1792]{1,0:T(8,128)(2,1)S(1)} %get-tuple-element.82.up_ref, f32[128,512]{1,0:T(8,128)S(1)} %get-tuple-element.86.refs_0_), custom_call_target="tpu_custom_call" | custom-call | flops 1000000 | tf_op jit(solution)/shard_map/hidden/pallas_call | solution.py:468
  68.2 2.3 %hidden.7.hidden_other_ref = bf16[128,1792]{1,0:T(8,128)(2,1)S(1)} custom-call(bf16[128,2048]{1,0:T(8,128)(2,1)S(1)} %collective-permute-done.19.x_ref, bf16[2048,1792]{1,0:T(8,128)(2,1)S(1)} %get-tuple-element.81.gate_ref, bf16[2048,1792]{1,0:T(8,128)(2,1)S(1)} %get-tuple-element.82.up_ref, bf16[128,1792]{1,0:T(8,128)(2,1)S(1)} %hidden.6.refs_0_.hidden_own_ref), custom_call_target="tpu_custom_call" | custom-call | flops 1000000 | tf_op jit(solution)/shard_map/hidden/pallas_call | solution.py:468
  70.6 2.1 %down.3 = (f32[128,2048]{1,0:T(8,128)S(1)}, bf16[128,2048]{1,0:T(8,128)(2,1)S(1)}) custom-call(bf16[128,1792]{1,0:T(8,128)(2,1)S(1)} %hidden.6.refs_0_.hidden_own_ref, bf16[128,1792]{1,0:T(8,128)(2,1)S(1)} %hidden.7.hidden_other_ref, bf16[2048,1792]{1,0:T(8,128)(2,1)S(1)} %get-tuple-element.83.down_ref), custom_call_target="tpu_custom_call" | custom-call | flops 1000000 | tf_op jit(solution)/shard_map/down/pallas_call | solution.py:497
  72.9 1.8 %collective-permute-done.20.other_ref = bf16[128,2048]{1,0:T(8,128)(2,1)S(1)} collective-permute-done((bf16[128,2048]{1,0:T(8,128)(2,1)S(1)}, bf16[128,2048]{1,0:T(8,128)(2,1)S(1)}, u32[]{:S(2)}, u32[]{:S(2)}) %collective-permute-start.20) | collective-permute-done | bytes 524320 | tf_op jit(solution)/shard_map/ppermute | solution.py:33
  78.5 1.6 %collective-permute-start.29 = (bf16[64,512]{1,0:T(8,128)(2,1)S(1)}, bf16[64,512]{1,0:T(8,128)(2,1)S(1)}, u32[]{:S(2)}, u32[]{:S(2)}) collective-permute-start(bf16[64,512]{1,0:T(8,128)(2,1)S(1)} %get-tuple-element.99), channel_id=1, source_target_pairs={{0,12},{4,8},{8,4},{12,0},{1,13},{5,9},{9,5},{13,1},{2,14},{6,10},... | collective-permute-start | bytes 196616 | tf_op jit(solution)/shard_map/ppermute | solution.py:33
  81.2 2.8 %collective-permute-done.25.refs_2_ = bf16[128,512]{1,0:T(8,128)(2,1)S(1)} collective-permute-done((bf16[128,512]{1,0:T(8,128)(2,1)S(1)}, bf16[128,512]{1,0:T(8,128)(2,1)S(1)}, u32[]{:S(2)}, u32[]{:S(2)}) %collective-permute-start.25) | collective-permute-done | bytes 131104 | tf_op jit(solution)/shard_map/ppermute | solution.py:33
  85.6 2.8 %collective-permute-done.27.refs_1_ = bf16[64,512]{1,0:T(8,128)(2,1)S(1)} collective-permute-done((bf16[64,512]{1,0:T(8,128)(2,1)S(1)}, bf16[64,512]{1,0:T(8,128)(2,1)S(1)}, u32[]{:S(2)}, u32[]{:S(2)}) %collective-permute-start.27) | collective-permute-done | bytes 65568 | tf_op jit(solution)/shard_map/ppermute | solution.py:33
  (65 shorter events, 28.5 us)
Async XLA Ops:
  4.3 6.7 %collective-permute-start.1 = (bf16[144,256]{1,0:T(8,128)(2,1)S(1)}, bf16[144,256]{1,0:T(8,128)(2,1)S(1)}, u32[]{:S(2)}, u32[]{:S(2)}) collective-permute-start(bf16[144,256]{1,0:T(8,128)(2,1)S(1)} %get-tuple-element.58.refs_0_), channel_id=1, source_target_pairs={{0,1},{1,0},{2,3},{3,2},{4,5},{5,4},{6,7},{7,6},{8,9},{9,8},{10,11... | collective-permute-start | bytes 221192 | tf_op jit(solution)/shard_map/ppermute | solution.py:33
  8.2 5.3 %collective-permute-start.3 = (bf16[144,256]{1,0:T(8,128)(2,1)S(1)}, bf16[144,256]{1,0:T(8,128)(2,1)S(1)}, u32[]{:S(2)}, u32[]{:S(2)}) collective-permute-start(bf16[144,256]{1,0:T(8,128)(2,1)S(1)} %get-tuple-element.58.refs_0_), channel_id=1, source_target_pairs={{0,3},{1,2},{2,1},{3,0},{4,7},{5,6},{6,5},{7,4},{8,11},{9,10},{10,... | collective-permute-start | bytes 221192 | tf_op jit(solution)/shard_map/ppermute | solution.py:33
  23.4 6.7 %collective-permute-start.5 = (bf16[128,512]{1,0:T(8,128)(2,1)S(1)}, bf16[128,512]{1,0:T(8,128)(2,1)S(1)}, u32[]{:S(2)}, u32[]{:S(2)}) collective-permute-start(bf16[128,512]{1,0:T(8,128)(2,1)S(1)} %get-tuple-element.72), channel_id=1, source_target_pairs={{0,1},{1,0},{2,3},{3,2},{4,5},{5,4},{6,7},{7,6},{8,9},{9,8},{10,11... | collective-permute-start | bytes 393224 | tf_op jit(solution)/shard_map/ppermute | solution.py:33
  24.0 8.3 %collective-permute-start.6 = (bf16[128,512]{1,0:T(8,128)(2,1)S(1)}, bf16[128,512]{1,0:T(8,128)(2,1)S(1)}, u32[]{:S(2)}, u32[]{:S(2)}) collective-permute-start(bf16[128,512]{1,0:T(8,128)(2,1)S(1)} %get-tuple-element.73), channel_id=1, source_target_pairs={{0,2},{1,3},{2,0},{3,1},{4,6},{5,7},{6,4},{7,5},{8,10},{9,11},{10,... | collective-permute-start | bytes 393224 | tf_op jit(solution)/shard_map/ppermute | solution.py:33
  24.7 7.6 %collective-permute-start.7 = (bf16[128,512]{1,0:T(8,128)(2,1)S(1)}, bf16[128,512]{1,0:T(8,128)(2,1)S(1)}, u32[]{:S(2)}, u32[]{:S(2)}) collective-permute-start(bf16[128,512]{1,0:T(8,128)(2,1)S(1)} %get-tuple-element.74), channel_id=1, source_target_pairs={{0,3},{1,2},{2,1},{3,0},{4,7},{5,6},{6,5},{7,4},{8,11},{9,10},{10,... | collective-permute-start | bytes 393224 | tf_op jit(solution)/shard_map/ppermute | solution.py:33
  32.6 6.8 %collective-permute-start.10 = (bf16[64,512]{1,0:T(8,128)(2,1)S(1)}, bf16[64,512]{1,0:T(8,128)(2,1)S(1)}, u32[]{:S(2)}, u32[]{:S(2)}) collective-permute-start(bf16[64,512]{1,0:T(8,128)(2,1)S(1)} %get-tuple-element.79), channel_id=1, source_target_pairs={{0,12},{4,8},{8,4},{12,0},{1,13},{5,9},{9,5},{13,1},{2,14},{6,10},... | collective-permute-start | bytes 196616 | tf_op jit(solution)/shard_map/ppermute | solution.py:33
  36.2 5.3 %collective-permute-start.9 = (bf16[64,512]{1,0:T(8,128)(2,1)S(1)}, bf16[64,512]{1,0:T(8,128)(2,1)S(1)}, u32[]{:S(2)}, u32[]{:S(2)}) collective-permute-start(bf16[64,512]{1,0:T(8,128)(2,1)S(1)} %get-tuple-element.78), channel_id=1, source_target_pairs={{0,8},{4,12},{8,0},{12,4},{1,9},{5,13},{9,1},{13,5},{2,10},{6,14},... | collective-permute-start | bytes 196616 | tf_op jit(solution)/shard_map/ppermute | solution.py:33
  36.2 8.9 %collective-permute-start.8 = (bf16[64,512]{1,0:T(8,128)(2,1)S(1)}, bf16[64,512]{1,0:T(8,128)(2,1)S(1)}, u32[]{:S(2)}, u32[]{:S(2)}) collective-permute-start(bf16[64,512]{1,0:T(8,128)(2,1)S(1)} %get-tuple-element.77), channel_id=1, source_target_pairs={{0,4},{4,0},{8,12},{12,8},{1,5},{5,1},{9,13},{13,9},{2,6},{6,2},{1... | collective-permute-start | bytes 196616 | tf_op jit(solution)/shard_map/ppermute | solution.py:33
  41.5 6.2 %collective-permute-start.14 = (bf16[128,512]{1,0:T(8,128)(2,1)S(1)}, bf16[128,512]{1,0:T(8,128)(2,1)S(1)}, u32[]{:S(2)}, u32[]{:S(2)}) collective-permute-start(bf16[128,512]{1,0:T(8,128)(2,1)S(1)} %stack.2.refs_2_.refs_0_), channel_id=1, source_target_pairs={{0,1},{1,0},{2,3},{3,2},{4,5},{5,4},{6,7},{7,6},{8,9},{9,8},{10,11... | collective-permute-start | bytes 393224 | tf_op jit(solution)/shard_map/ppermute | solution.py:33
  43.1 7.2 %collective-permute-start.15 = (bf16[128,512]{1,0:T(8,128)(2,1)S(1)}, bf16[128,512]{1,0:T(8,128)(2,1)S(1)}, u32[]{:S(2)}, u32[]{:S(2)}) collective-permute-start(bf16[128,512]{1,0:T(8,128)(2,1)S(1)} %stack.2.refs_2_.refs_0_), channel_id=1, source_target_pairs={{0,2},{1,3},{2,0},{3,1},{4,6},{5,7},{6,4},{7,5},{8,10},{9,11},{10,... | collective-permute-start | bytes 393224 | tf_op jit(solution)/shard_map/ppermute | solution.py:33
  43.8 6.5 %collective-permute-start.16 = (bf16[128,512]{1,0:T(8,128)(2,1)S(1)}, bf16[128,512]{1,0:T(8,128)(2,1)S(1)}, u32[]{:S(2)}, u32[]{:S(2)}) collective-permute-start(bf16[128,512]{1,0:T(8,128)(2,1)S(1)} %stack.2.refs_2_.refs_0_), channel_id=1, source_target_pairs={{0,3},{1,2},{2,1},{3,0},{4,7},{5,6},{6,5},{7,4},{8,11},{9,10},{10,... | collective-permute-start | bytes 393224 | tf_op jit(solution)/shard_map/ppermute | solution.py:33
  50.6 5.7 %collective-permute-start.17 = (bf16[128,2048]{1,0:T(8,128)(2,1)S(1)}, bf16[128,2048]{1,0:T(8,128)(2,1)S(1)}, u32[]{:S(2)}, u32[]{:S(2)}) collective-permute-start(bf16[128,2048]{1,0:T(8,128)(2,1)S(1)} %norm.2.x_ref), channel_id=1, source_target_pairs={{0,16},{16,0},{1,17},{17,1},{2,18},{18,2},{3,19},{19,3},{4,20},{20... | collective-permute-start | bytes 1572872 | tf_op jit(solution)/shard_map/ppermute | solution.py:33
  50.7 9.9 %collective-permute-start.11 = (bf16[128,512]{1,0:T(8,128)(2,1)S(1)}, bf16[128,512]{1,0:T(8,128)(2,1)S(1)}, u32[]{:S(2)}, u32[]{:S(2)}) collective-permute-start(bf16[128,512]{1,0:T(8,128)(2,1)S(1)} %stack.3.refs_1_.refs_0_), channel_id=1, source_target_pairs={{0,1},{1,0},{2,3},{3,2},{4,5},{5,4},{6,7},{7,6},{8,9},{9,8},{10,11... | collective-permute-start | bytes 393224 | tf_op jit(solution)/shard_map/ppermute | solution.py:33
  51.8 8.8 %collective-permute-start.12 = (bf16[128,512]{1,0:T(8,128)(2,1)S(1)}, bf16[128,512]{1,0:T(8,128)(2,1)S(1)}, u32[]{:S(2)}, u32[]{:S(2)}) collective-permute-start(bf16[128,512]{1,0:T(8,128)(2,1)S(1)} %stack.3.refs_1_.refs_0_), channel_id=1, source_target_pairs={{0,2},{1,3},{2,0},{3,1},{4,6},{5,7},{6,4},{7,5},{8,10},{9,11},{10,... | collective-permute-start | bytes 393224 | tf_op jit(solution)/shard_map/ppermute | solution.py:33
  52.7 7.9 %collective-permute-start.13 = (bf16[128,512]{1,0:T(8,128)(2,1)S(1)}, bf16[128,512]{1,0:T(8,128)(2,1)S(1)}, u32[]{:S(2)}, u32[]{:S(2)}) collective-permute-start(bf16[128,512]{1,0:T(8,128)(2,1)S(1)} %stack.3.refs_1_.refs_0_), channel_id=1, source_target_pairs={{0,3},{1,2},{2,1},{3,0},{4,7},{5,6},{6,5},{7,4},{8,11},{9,10},{10,... | collective-permute-start | bytes 393224 | tf_op jit(solution)/shard_map/ppermute | solution.py:33
  60.9 7.4 %collective-permute-start.19 = (bf16[128,2048]{1,0:T(8,128)(2,1)S(1)}, bf16[128,2048]{1,0:T(8,128)(2,1)S(1)}, u32[]{:S(2)}, u32[]{:S(2)}) collective-permute-start(bf16[128,2048]{1,0:T(8,128)(2,1)S(1)} %norm.3.x_ref), channel_id=1, source_target_pairs={{0,16},{16,0},{1,17},{17,1},{2,18},{18,2},{3,19},{19,3},{4,20},{20... | collective-permute-start | bytes 1572872 | tf_op jit(solution)/shard_map/ppermute | solution.py:33
  62.6 10.2 %collective-permute-start.21 = (bf16[128,512]{1,0:T(8,128)(2,1)S(1)}, bf16[128,512]{1,0:T(8,128)(2,1)S(1)}, u32[]{:S(2)}, u32[]{:S(2)}) collective-permute-start(bf16[128,512]{1,0:T(8,128)(2,1)S(1)} %get-tuple-element.89), channel_id=1, source_target_pairs={{0,1},{1,0},{2,3},{3,2},{4,5},{5,4},{6,7},{7,6},{8,9},{9,8},{10,11... | collective-permute-start | bytes 393224 | tf_op jit(solution)/shard_map/ppermute | solution.py:33
  63.7 9.0 %collective-permute-start.22 = (bf16[128,512]{1,0:T(8,128)(2,1)S(1)}, bf16[128,512]{1,0:T(8,128)(2,1)S(1)}, u32[]{:S(2)}, u32[]{:S(2)}) collective-permute-start(bf16[128,512]{1,0:T(8,128)(2,1)S(1)} %get-tuple-element.90), channel_id=1, source_target_pairs={{0,2},{1,3},{2,0},{3,1},{4,6},{5,7},{6,4},{7,5},{8,10},{9,11},{10,... | collective-permute-start | bytes 393224 | tf_op jit(solution)/shard_map/ppermute | solution.py:33
  64.6 8.2 %collective-permute-start.23 = (bf16[128,512]{1,0:T(8,128)(2,1)S(1)}, bf16[128,512]{1,0:T(8,128)(2,1)S(1)}, u32[]{:S(2)}, u32[]{:S(2)}) collective-permute-start(bf16[128,512]{1,0:T(8,128)(2,1)S(1)} %get-tuple-element.91), channel_id=1, source_target_pairs={{0,3},{1,2},{2,1},{3,0},{4,7},{5,6},{6,5},{7,4},{8,11},{9,10},{10,... | collective-permute-start | bytes 393224 | tf_op jit(solution)/shard_map/ppermute | solution.py:33
  74.8 6.4 %collective-permute-start.24 = (bf16[128,512]{1,0:T(8,128)(2,1)S(1)}, bf16[128,512]{1,0:T(8,128)(2,1)S(1)}, u32[]{:S(2)}, u32[]{:S(2)}) collective-permute-start(bf16[128,512]{1,0:T(8,128)(2,1)S(1)} %get-tuple-element.94), channel_id=1, source_target_pairs={{0,1},{1,0},{2,3},{3,2},{4,5},{5,4},{6,7},{7,6},{8,9},{9,8},{10,11... | collective-permute-start | bytes 393224 | tf_op jit(solution)/shard_map/ppermute | solution.py:33
  75.9 8.1 %collective-permute-start.25 = (bf16[128,512]{1,0:T(8,128)(2,1)S(1)}, bf16[128,512]{1,0:T(8,128)(2,1)S(1)}, u32[]{:S(2)}, u32[]{:S(2)}) collective-permute-start(bf16[128,512]{1,0:T(8,128)(2,1)S(1)} %get-tuple-element.95), channel_id=1, source_target_pairs={{0,2},{1,3},{2,0},{3,1},{4,6},{5,7},{6,4},{7,5},{8,10},{9,11},{10,... | collective-permute-start | bytes 393224 | tf_op jit(solution)/shard_map/ppermute | solution.py:33
  76.8 7.2 %collective-permute-start.26 = (bf16[128,512]{1,0:T(8,128)(2,1)S(1)}, bf16[128,512]{1,0:T(8,128)(2,1)S(1)}, u32[]{:S(2)}, u32[]{:S(2)}) collective-permute-start(bf16[128,512]{1,0:T(8,128)(2,1)S(1)} %get-tuple-element.96), channel_id=1, source_target_pairs={{0,3},{1,2},{2,1},{3,0},{4,7},{5,6},{6,5},{7,4},{8,11},{9,10},{10,... | collective-permute-start | bytes 393224 | tf_op jit(solution)/shard_map/ppermute | solution.py:33
  78.3 7.0 %collective-permute-start.28 = (bf16[64,512]{1,0:T(8,128)(2,1)S(1)}, bf16[64,512]{1,0:T(8,128)(2,1)S(1)}, u32[]{:S(2)}, u32[]{:S(2)}) collective-permute-start(bf16[64,512]{1,0:T(8,128)(2,1)S(1)} %get-tuple-element.92.refs_1_), channel_id=1, source_target_pairs={{0,8},{4,12},{8,0},{12,4},{1,9},{5,13},{9,1},{13,5},{2,10},{6,14},... | collective-permute-start | bytes 196616 | tf_op jit(solution)/shard_map/ppermute | solution.py:33
  78.5 6.9 %collective-permute-start.29 = (bf16[64,512]{1,0:T(8,128)(2,1)S(1)}, bf16[64,512]{1,0:T(8,128)(2,1)S(1)}, u32[]{:S(2)}, u32[]{:S(2)}) collective-permute-start(bf16[64,512]{1,0:T(8,128)(2,1)S(1)} %get-tuple-element.99), channel_id=1, source_target_pairs={{0,12},{4,8},{8,4},{12,0},{1,13},{5,9},{9,5},{13,1},{2,14},{6,10},... | collective-permute-start | bytes 196616 | tf_op jit(solution)/shard_map/ppermute | solution.py:33
  (8 other events, 37.9 us)

commit v5 on v4

--- a/solution.py
+++ b/solution.py
@@ -71,6 +71,27 @@
         cost_estimate=cost(1e6, 0),
         name="stack",
     )(*pieces, *after)
+
+
+def last_weight_kernel(expert_hbm, *refs):
+    weight_ref, token_ref, sem = refs[-3:]
+    copy = pltpu.make_async_copy(expert_hbm.at[0, 2], weight_ref, sem)
+    copy.start()
+    token_ref[...] = jnp.zeros_like(token_ref)
+    copy.wait()
+
+
+def last_weight(experts, after):
+    return pl.pallas_call(
+        last_weight_kernel,
+        out_shape=(shaped(experts.shape[2:], BF16), shaped((8, 128), F32)),
+        in_specs=[hbm()] + unread(after),
+        out_specs=[whole()] * 2,
+        scratch_shapes=[pltpu.SemaphoreType.DMA],
+        compiler_params=params(),
+        cost_estimate=cost(2e10, 0),
+        name="weight",
+    )(experts, *after)
 
 
 def order_kernel(*refs):
@@ -200,9 +221,9 @@
 
 
 def prepare_kernel(
-    gate_hbm, decay_hbm, residual_hbm, skip_hbm, bias_hbm, step_hbm, out_hbm, gain_hbm,
-    silu_ref, rates_ref, skip_ref, bias_ref, step_ref, out_ref, quarter_ref, gain_ref,
-    gate_ref, decay_ref, residual_ref, sems,
+    xconv_ref, gate_hbm, decay_hbm, residual_hbm, skip_hbm, bias_hbm, step_hbm, out_hbm, gain_hbm,
+    silu_ref, rates_ref, skipped_ref, bias_ref, step_ref, out_ref, quarter_ref, gain_ref,
+    gate_ref, decay_ref, residual_ref, skip_ref, sems,
 ):
     copies = [
         pltpu.make_async_copy(source, target, sems.at[i])
@@ -221,144 +242,153 @@
     ]
     for copy in copies:
         copy.start()
-    for copy in copies[:3]:
+    for copy in copies[:4]:
         copy.wait()
     gate = gate_ref[...].astype(F32)
     silu_ref[...] = gate * sigmoid(gate)
-    rates_ref[...] = -LOG2E * jnp.exp(decay_ref[...])
+    skipped_ref[...] = skip_ref[...] * xconv_ref[...].astype(F32)
+    rates = -LOG2E * jnp.exp(decay_ref[...])
+    for j in range(rates_ref.shape[1]):
+        rates_ref[:, j, :] = rates[:, j * 128 : (j + 1) * 128]
     width = quarter_ref.shape[1]
     start = pl.multiple_of(lax.axis_index("tp") * width, 128)
     quarter_ref[...] = residual_ref[:, pl.ds(start, width)].astype(F32)
-    for copy in copies[3:]:
+    for copy in copies[4:]:
         copy.wait()
 
 
-def prepare(parts, gate, decay_log, residual, skip, bias, step_weight, out_weight, gain):
+def prepare(parts, xconv, gate, decay_log, residual, skip, bias, step_weight, out_weight, gain):
     rows, channels = gate.shape
     return pl.pallas_call(
         prepare_kernel,
         out_shape=(
             shaped((rows, channels), F32),
-            shaped(decay_log.shape, F32),
-            shaped(skip.shape, F32),
+            shaped((STATE, channels // 128, 128), F32),
+            shaped((rows, channels), F32),
             shaped(bias.shape, F32),
             shaped(step_weight.shape, BF16),
             shaped(out_weight.shape, BF16),
             shaped((rows, residual.shape[1] // parts), F32),
             shaped(gain.shape, F32),
         ),
-        in_specs=[hbm()] * 8,
+        in_specs=[whole()] + [hbm()] * 8,
         out_specs=[whole()] * 8,
         scratch_shapes=[
             pltpu.VMEM((rows, channels), BF16),
             pltpu.VMEM(decay_log.shape, F32),
             pltpu.VMEM(residual.shape, BF16),
+            pltpu.VMEM(skip.shape, F32),
             pltpu.SemaphoreType.DMA((8,)),
         ],
         compiler_params=params(),
         cost_estimate=cost(1e6, 6e6),
         name="prepare",
-    )(gate, decay_log, residual, skip, bias, step_weight, out_weight, gain)
-
-
-def over_states(sum_ref):
-    total = sum_ref[:, 0, :]
-    for i in range(1, 8):
-        total = total + sum_ref[:, i, :]
-    return total
+    )(xconv, gate, decay_log, residual, skip, bias, step_weight, out_weight, gain)
 
 
 def scan_kernel(parts, *refs):
     part_refs = refs[:parts]
-    xconv_ref, rates_ref, gain_ref, bias_ref, weight_ref, expert_hbm = refs[parts : parts + 6]
-    y_ref, elapsed_ref, maps_ref, state_ref, second_ref = refs[parts + 6 : parts + 11]
-    steps_ref, driven_ref, sum_ref, expert_sem = refs[parts + 11 :]
-    rows, channels = xconv_ref.shape
+    xconv_ref, rates_ref, bias_ref, weight_ref, expert_hbm = refs[parts : parts + 5]
+    y_ref, elapsed_ref, seen_ref, state_ref, second_ref = refs[parts + 5 : parts + 10]
+    steps_ref, driven_ref, spread_ref, expert_sem = refs[parts + 10 :]
+    rows = xconv_ref.shape[0]
+    tiles = rates_ref.shape[1]
     expert_copy = pltpu.make_async_copy(expert_hbm.at[0, 1], second_ref, expert_sem)
     expert_copy.start()
     proj = part_refs[0][...].astype(F32)
     for ref in part_refs[1:]:
         proj = proj + ref[...].astype(F32)
     maps = proj[rows:]
-    maps_ref[...] = maps
+
+    for t in range(rows):
+        spread_ref[t] = jnp.broadcast_to(maps[:, t : t + 1], (STATE, 128))
+        seen_ref[t] = jnp.broadcast_to(maps[:, rows + t : rows + t + 1], (STATE, 128))
     rank = proj[:rows].astype(BF16)
     raw = jnp.dot(rank, weight_ref[...], preferred_element_type=F32) + bias_ref[...]
     steps = jnp.maximum(raw, 0.0) + jnp.log1p(jnp.exp(-jnp.abs(raw)))
-    xfloat = xconv_ref[...].astype(F32)
-    steps_ref[...] = steps
-    driven_ref[...] = steps * xfloat
-    y_ref[...] = gain_ref[...] * xfloat
-    high = steps.astype(BF16)
-    low = (steps - high.astype(F32)).astype(BF16)
-    until = lax.broadcasted_iota(jnp.int32, (rows, rows), 1) <= lax.broadcasted_iota(
-        jnp.int32, (rows, rows), 0
-    )
-    until = until.astype(F32).astype(BF16)
-    elapsed_ref[...] = jnp.dot(until, high, preferred_element_type=F32) + jnp.dot(
-        until, low, preferred_element_type=F32
-    )
-
-    def block(i, carry):
-        state, into, out = carry
-        begin = pl.multiple_of(i * 8, 8)
-        for r in range(8):
-            now = steps_ref[pl.ds(begin + r, 1), :]
-            driven = driven_ref[pl.ds(begin + r, 1), :]
-            state = jnp.exp2(now * rates_ref[...]) * state + driven * into[:, r : r + 1]
-            seen = state * out[:, r : r + 1]
-            sum_ref[r] = seen[:8] + seen[8:]
-        y_ref[pl.ds(begin, 8), :] += over_states(sum_ref)
-        return state, pltpu.roll(into, rows - 8, 1), pltpu.roll(out, rows - 8, 1)
-
-    start = jnp.zeros((STATE, channels), F32)
-    state_ref[...] = lax.fori_loop(0, rows // 8, block, (start, maps[:, :rows], maps[:, rows:]))[0]
+    driven = steps * xconv_ref[...].astype(F32)
+    for j in range(tiles):
+        cut = slice(j * 128, (j + 1) * 128)
+        steps_ref[:, j, :] = steps[:, cut]
+        driven_ref[:, j, :] = driven[:, cut]
+
+    def step(t, carry):
+        elapsed, states = carry
+        now, driven = steps_ref[t], driven_ref[t]
+        sums = [None, None]
+        new = []
+        for n in range(STATE):
+            state = jnp.exp2(now * rates_ref[n]) * states[n] + driven * spread_ref[t, n : n + 1, :]
+            new.append(state)
+            term = state * seen_ref[t, n : n + 1, :]
+            sums[n % 2] = term if sums[n % 2] is None else sums[n % 2] + term
+        elapsed = elapsed + now
+        y_ref[t] = sums[0] + sums[1]
+        elapsed_ref[t] = elapsed
+        return elapsed, tuple(new)
+
+    zero = jnp.zeros((tiles, 128), F32)
+    _, states = lax.fori_loop(0, rows, step, (zero, (zero,) * STATE), unroll=16)
+    for n in range(STATE):
+        state_ref[n] = states[n]
     expert_copy.wait()
 
 
-def scan(pieces, xconv, rates, gain, bias, weight, experts):
-    rows, channels = xconv.shape
+def scan(pieces, xconv, rates, bias, weight, experts):
+    rows = xconv.shape[0]
+    tall = (rows, *rates.shape[1:])
     return pl.pallas_call(
         functools.partial(scan_kernel, len(pieces)),
         out_shape=(
-            shaped((rows, channels), F32),
-            shaped((rows, channels), F32),
-            shaped((STATE, DT_RANK), F32),
-            shaped((STATE, channels), F32),
+            shaped(tall, F32),
+            shaped(tall, F32),
+            shaped((rows, STATE, 128), F32),
+            shaped(rates.shape, F32),
             shaped(experts.shape[2:], BF16),
         ),
-        in_specs=[whole()] * (len(pieces) + 5) + [hbm()],
+        in_specs=[whole()] * (len(pieces) + 4) + [hbm()],
         out_specs=[whole()] * 5,
         scratch_shapes=[
-            pltpu.VMEM((rows, channels), F32),
-            pltpu.VMEM((rows, channels), F32),
-            pltpu.VMEM((8, 8, channels), F32),
+            pltpu.VMEM(tall, F32),
+            pltpu.VMEM(tall, F32),
+            pltpu.VMEM((rows, STATE, 128), F32),
             pltpu.SemaphoreType.DMA,
         ],
         compiler_params=params(),
         cost_estimate=cost(1e6, 14e6),
         name="scan",
-    )(*pieces, xconv, rates, gain, bias, weight, experts)
+    )(*pieces, xconv, rates, bias, weight, experts)
 
 
 def mix_kernel(parts, *refs):
-    maps_ref, y_ref, elapsed_ref, rates_ref, state_ref, silu_ref, quarter_ref, weight_ref, expert_hbm = refs[:9]
-    own_ref, sent, third_ref = refs[9], refs[10 : 9 + parts], refs[9 + parts]
-    sum_ref, gated_ref, expert_sem = refs[10 + parts :]
-    expert_copy = pltpu.make_async_copy(expert_hbm.at[0, 2], third_ref, expert_sem)
-    expert_copy.start()
-    rows = y_ref.shape[0]
-
-    def block(i, out):
-        begin = pl.multiple_of(i * 16, 16)
-        for r in range(16):
-            decay = jnp.exp2(elapsed_ref[pl.ds(begin + r, 1), :] * rates_ref[...])
-            seen = decay * (state_ref[...] * out[:, r : r + 1])
-            sum_ref[r] = seen[:8] + seen[8:]
-        cut = pl.ds(begin, 16)
-        gated_ref[cut, :] = ((y_ref[cut, :] + over_states(sum_ref)) * silu_ref[cut, :]).astype(BF16)
-        return pltpu.roll(out, rows - 16, 1)
-
-    lax.fori_loop(0, rows // 16, block, maps_ref[:, rows:])
+    seen_ref, y_ref, elapsed_ref, rates_ref, state_ref, skipped_ref, silu_ref, quarter_ref, weight_ref = refs[:9]
+    own_ref, sent = refs[9], refs[10 : 9 + parts]
+    sum_ref, gated_ref = refs[9 + parts :]
+    rows, tiles, _ = y_ref.shape
+
+    def step(t, carry):
+        elapsed = elapsed_ref[t]
+        sums = [y_ref[t], None]
+        for n in range(STATE):
+            term = jnp.exp2(elapsed * rates_ref[n]) * (state_ref[n] * seen_ref[t, n : n + 1, :])
+            sums[n % 2] = term if sums[n % 2] is None else sums[n % 2] + term
+        sum_ref[t] = sums[0] + sums[1]
+        return carry
+
+    first = lax.axis_index("ctx") == 0
+
+    @pl.when(first)
+    def _():
+        sum_ref[...] = y_ref[...]
+
+    @pl.when(jnp.logical_not(first))
+    def _():
+        lax.fori_loop(0, rows, step, 0, unroll=8)
+
+    for j in range(tiles):
+        cut = slice(j * 128, (j + 1) * 128)
+        total = sum_ref[:, j, :] + skipped_ref[:, cut]
+        gated_ref[:, cut] = (total * silu_ref[:, cut]).astype(BF16)
     own = lax.axis_index("tp")
     width = own_ref.shape[1]
     for k in range(parts):
@@ -370,28 +400,25 @@
             own_ref[...] = product + quarter_ref[...]
         else:
             sent[k - 1][...] = product.astype(BF16)
-    expert_copy.wait()
-
-
-def mix(parts, maps, y, elapsed, rates, state, silu, quarter, weight, experts):
-    rows, channels = y.shape
+
+
+def mix(parts, seen, y, elapsed, rates, state, skipped, silu, quarter, weight):
+    rows, tiles, _ = y.shape
     width = weight.shape[1] // parts
     return pl.pallas_call(
         functools.partial(mix_kernel, parts),
         out_shape=[shaped((rows, width), F32)]
-        + [shaped((rows, width), BF16)] * (parts - 1)
-        + [shaped(experts.shape[2:], BF16)],
-        in_specs=[whole()] * 8 + [hbm()],
-        out_specs=[whole()] * (parts + 1),
+        + [shaped((rows, width), BF16)] * (parts - 1),
+        in_specs=[whole()] * 9,
+        out_specs=[whole()] * parts,
         scratch_shapes=[
-            pltpu.VMEM((16, 8, channels), F32),
-            pltpu.VMEM((rows, channels), BF16),
-            pltpu.SemaphoreType.DMA,
+            pltpu.VMEM((rows, tiles, 128), F32),
+            pltpu.VMEM((rows, tiles * 128), BF16),
         ],
         compiler_params=params(),
         cost_estimate=cost(1e6, 12e6),
         name="mix",
-    )(maps, y, elapsed, rates, state, silu, quarter, weight, experts)
+    )(seen, y, elapsed, rates, state, skipped, silu, quarter, weight)
 
 
 def pick_kernel(parts, *refs):
@@ -612,15 +639,13 @@
     near = load(stay(local), stay(conv_weight), stay(conv_bias[None]), stay(proj_weight.T))
     xconv, part = conv(before, *near)
     parts = [part] + swaps([part] * (tp - 1))
-    silu, rates, skip, bias, step_w, out_w, quarter, gain = prepare(
-        tp, stay(gate_in[0]), stay(decay_log), stay(residual[0]), stay(skip_gain[None]),
+    silu, rates, skipped, bias, step_w, out_w, quarter, gain = prepare(
+        tp, xconv, stay(gate_in[0]), stay(decay_log), stay(residual[0]), stay(skip_gain[None]),
         stay(step_bias[None]), stay(step_weight), stay(out_weight), stay(norm_gain[None]),
     )
-    y, elapsed, maps, state, up_w = scan(parts, xconv, rates, skip, bias, step_w, expert_weight)
+    y, elapsed, seen, state, up_w = scan(parts, xconv, rates, bias, step_w, expert_weight)
     before = lax.ppermute(state, "ctx", [(0, 1)])
-    own, *sent, down_w = mix(
-        tp, maps, y, elapsed, rates, before, silu, quarter, out_w, expert_weight
-    )
+    own, *sent = mix(tp, seen, y, elapsed, rates, before, skipped, silu, quarter, out_w)
     arrived = swaps(sent)
     first, second, chooser, gate_w = route(expert_ids[0].T, experts, expert_weight)
     stream, *picked = pick(own, arrived, chooser)
@@ -628,7 +653,7 @@
     rows = {j: swap(picked[j], "exp", j) for j in range(experts - 1, 0, -1)}
     piece_a = stack([rows[j] for j in range(half, experts)], [])
     piece_b = stack([picked[0]] + [rows[j] for j in range(1, half)], [piece_a])
-    both = order([piece_a, piece_b])
+    down_w, both = last_weight(expert_weight, [piece_a, piece_b])
     rows_a = [piece_a] + swaps([piece_a] * (tp - 1))
     rows_b = [piece_b] + swaps([piece_b] * (tp - 1))
     x_a = norm([rows_a], gain, [both])

time: 89.5 us -> 88 us (0.983)
  waiting for transfers between devices: 26.1 us -> 23.7 us
    pallas_call x0 -> x1, Pallas kernels: none -> 3.1 us  [last_weight(): pl.pallas_call(last_weight_kernel, out_shape=(shaped(experts.shape[2:], B...]
    ppermute x28, waiting for transfers between devices: 25.1 us -> 22.7 us  [swap(): lax.ppermute(block, axis, [(i, i ^ k) for i in range(lax.axis_size(axis))])]
    pallas_call x1, Pallas kernels: 3.37 us -> 1.26 us  [mix(): pl.pallas_call(functools.partial(mix_kernel, parts), out_shape=[shaped((r...]
  transfers between devices with their start and end apart: 30 -> 30, of which waited for: 14 -> 14; matrix products, arithmetic and copies ran while one was open for 0% -> 0% of each run, Pallas kernels for 23% -> 27%
where the time goes in v5:
time: 88 us; the launch traced here: 87.8 us
  starting transfers between devices  33.1 us (38%)
  Pallas kernels  30.7 us (35%)
  waiting for transfers between devices  23.7 us (27%)
    ppermute x28, starting transfers between devices, swap(): lax.ppermute(block, axis, [(i, i ^ k) for i in range(lax.axis_size(axis))])  29.4 us
    ppermute x28, waiting for transfers between devices, swap(): lax.ppermute(block, axis, [(i, i ^ k) for i in range(lax.axis_size(axis))])  22.7 us
    pallas_call x4, Pallas kernels, hidden_units(): pl.pallas_call(hidden_kernel, out_shape=shaped((rows, width), BF16), in_s...  8.59 us
    pallas_call x2, Pallas kernels, down_sums(): pl.pallas_call(down_kernel, out_shape=(shaped((rows, model), F32), shaped...  4.18 us
    pallas_call x1, Pallas kernels, scan(): pl.pallas_call(functools.partial(scan_kernel, len(pieces)), out_shape=(sh...  3.62 us
    pallas_call x1, Pallas kernels, last_weight(): pl.pallas_call(last_weight_kernel, out_shape=(shaped(experts.shape[2:], B...  3.1 us
    pallas_call x1, Pallas kernels, route(): pl.pallas_call(route_kernel, out_shape=(shaped((rows, slots), BF16), shap...  3.09 us
    pallas_call x1, Pallas kernels, prepare(): pl.pallas_call(prepare_kernel, out_shape=(shaped((rows, channels), F32),...  2.76 us
  transfers between devices with their start and end apart: 30, of which 14 were waited for; matrix products, arithmetic and copies ran while one was open for 0% of the time, Pallas kernels for 27%

profile of v5, /device:TPU:0, one launch (start us, length us, event | category | flops | bytes accessed | tf_op | source)
XLA Modules:
  0.0 87.8 jit_solution(3286975212057964241)
XLA Ops:
  0.0 2.4 %collective-permute-start = (bf16[128,1024]{1,0:T(8,128)(2,1)}, bf16[128,1024]{1,0:T(8,128)(2,1)S(1)}, u32[]{:S(2)}, u32[]{:S(2)}) collective-permute-start(bf16[128,1024]{1,0:T(8,128)(2,1)} %bitcast.21), channel_id=1, source_target_pairs={{0,16},{1,17},{2,18},{3,19},{4,20},{5,21},{6,22},{7,23},{8,24},{9,... | collective-permute-start | bytes 786440 | tf_op jit(solution)/shard_map/ppermute | solution.py:637
  4.3 2.4 %collective-permute-start.1 = (bf16[144,256]{1,0:T(8,128)(2,1)S(1)}, bf16[144,256]{1,0:T(8,128)(2,1)S(1)}, u32[]{:S(2)}, u32[]{:S(2)}) collective-permute-start(bf16[144,256]{1,0:T(8,128)(2,1)S(1)} %get-tuple-element.59.refs_0_), channel_id=1, source_target_pairs={{0,1},{1,0},{2,3},{3,2},{4,5},{5,4},{6,7},{7,6},{8,9},{9,8},{10,11... | collective-permute-start | bytes 221192 | tf_op jit(solution)/shard_map/ppermute | solution.py:33
  8.2 2.8 %prepare.1 = (f32[128,1024]{1,0:T(8,128)S(1)}, f32[16,8,128]{2,1,0:T(8,128)S(1)}, f32[128,1024]{1,0:T(8,128)S(1)}, f32[1,1024]{1,0:T(1,128)S(1)}, bf16[256,1024]...) custom-call(bf16[128,1024]{1,0:T(8,128)(2,1)S(1)} %get-tuple-element.60.xconv_, ...), custom_call_target="tpu_custom_call" | custom-call | flops 1000000 | bytes 6000000 | tf_op jit(solution)/shard_map/prepare/pallas_call | solution.py:262
  11.0 2.4 %collective-permute-done.3.refs_3_ = bf16[144,256]{1,0:T(8,128)(2,1)S(1)} collective-permute-done((bf16[144,256]{1,0:T(8,128)(2,1)S(1)}, bf16[144,256]{1,0:T(8,128)(2,1)S(1)}, u32[]{:S(2)}, u32[]{:S(2)}) %collective-permute-start.3) | collective-permute-done | bytes 73760 | tf_op jit(solution)/shard_map/ppermute | solution.py:33
  13.5 3.6 %scan.1 = (f32[128,8,128]{2,1,0:T(8,128)S(1)}, f32[128,8,128]{2,1,0:T(8,128)S(1)}, f32[128,16,128]{2,1,0:T(8,128)S(1)}, f32[16,8,128]{2,1,0:T(8,128)S(1)}, bf16[2048,1792]{1,0:T(8,128)(2,1)S(1)}) custom-call(bf16[144,256]{1,0:T(8,128)(2,1)S(1)} %get-tuple-element.59.refs_0_, bf16[144,256]{1,0:T(8,128)(2,1)S(1)} %collective-permute-done.1.refs_1_, ...), custom_call_target="tpu_custom_call" | custom-call | flops 1000000 | bytes 14000000 | tf_op jit(solution)/shard_map/scan/pallas_call | solution.py:340
  21.9 2.2 %collective-permute-start.7 = (bf16[128,512]{1,0:T(8,128)(2,1)S(1)}, bf16[128,512]{1,0:T(8,128)(2,1)S(1)}, u32[]{:S(2)}, u32[]{:S(2)}) collective-permute-start(bf16[128,512]{1,0:T(8,128)(2,1)S(1)} %get-tuple-element.75), channel_id=1, source_target_pairs={{0,3},{1,2},{2,1},{3,0},{4,7},{5,6},{6,5},{7,4},{8,11},{9,10},{10,... | collective-permute-start | bytes 393224 | tf_op jit(solution)/shard_map/ppermute | solution.py:33
  24.1 3.1 %route.1 = (bf16[128,256]{1,0:T(8,128)(2,1)S(1)}, bf16[128,256]{1,0:T(8,128)(2,1)S(1)}, bf16[256,128]{1,0:T(8,128)(2,1)S(1)}, bf16[2048,1792]{1,0:T(8,128)(2,1)S(1)}) custom-call(s32[2,128]{1,0:T(2,128)S(1)} %bitcast.17, bf16[1,3,2048,1792]{3,2,1,0:T(8,128)(2,1)} %expert_hbm.3), custom_call_target="tpu_custom_call" | custom-call | flops 1000000 | bytes 8000000 | tf_op jit(solution)/shard_map/route/pallas_call | solution.py:145
  29.5 3.7 %collective-permute-start.10 = (bf16[64,512]{1,0:T(8,128)(2,1)S(1)}, bf16[64,512]{1,0:T(8,128)(2,1)S(1)}, u32[]{:S(2)}, u32[]{:S(2)}) collective-permute-start(bf16[64,512]{1,0:T(8,128)(2,1)S(1)} %get-tuple-element.80), channel_id=1, source_target_pairs={{0,12},{4,8},{8,4},{12,0},{1,13},{5,9},{9,5},{13,1},{2,14},{6,10},... | collective-permute-start | bytes 196616 | tf_op jit(solution)/shard_map/ppermute | solution.py:33
  34.0 2.5 %collective-permute-done.10.refs_1_ = bf16[64,512]{1,0:T(8,128)(2,1)S(1)} collective-permute-done((bf16[64,512]{1,0:T(8,128)(2,1)S(1)}, bf16[64,512]{1,0:T(8,128)(2,1)S(1)}, u32[]{:S(2)}, u32[]{:S(2)}) %collective-permute-start.10) | collective-permute-done | bytes 65568 | tf_op jit(solution)/shard_map/ppermute | solution.py:33
  36.4 3.3 %collective-permute-done.9.refs_0_ = bf16[64,512]{1,0:T(8,128)(2,1)S(1)} collective-permute-done((bf16[64,512]{1,0:T(8,128)(2,1)S(1)}, bf16[64,512]{1,0:T(8,128)(2,1)S(1)}, u32[]{:S(2)}, u32[]{:S(2)}) %collective-permute-start.9) | collective-permute-done | bytes 65568 | tf_op jit(solution)/shard_map/ppermute | solution.py:33
  43.3 3.1 %weight.1 = (bf16[2048,1792]{1,0:T(8,128)(2,1)S(1)}, f32[8,128]{1,0:T(8,128)S(1)}) custom-call(bf16[1,3,2048,1792]{3,2,1,0:T(8,128)(2,1)} %expert_hbm.3, bf16[128,512]{1,0:T(8,128)(2,1)S(1)} %stack.2.refs_2_.refs_0_, bf16[128,512]{1,0:T(8,128)(2,1)S(1)} %stack.3.refs_1_.refs_0_), custom_call_target="tpu_custom_call" | custom-call | flops 20000000000 | tf_op jit(solution)/shard_map/weight/pallas_call | solution.py:85
  46.4 2.5 %collective-permute-done.15.refs_2_ = bf16[128,512]{1,0:T(8,128)(2,1)S(1)} collective-permute-done((bf16[128,512]{1,0:T(8,128)(2,1)S(1)}, bf16[128,512]{1,0:T(8,128)(2,1)S(1)}, u32[]{:S(2)}, u32[]{:S(2)}) %collective-permute-start.15) | collective-permute-done | bytes 131104 | tf_op jit(solution)/shard_map/ppermute | solution.py:33
  51.0 1.8 %collective-permute-start.13 = (bf16[128,512]{1,0:T(8,128)(2,1)S(1)}, bf16[128,512]{1,0:T(8,128)(2,1)S(1)}, u32[]{:S(2)}, u32[]{:S(2)}) collective-permute-start(bf16[128,512]{1,0:T(8,128)(2,1)S(1)} %stack.3.refs_1_.refs_0_), channel_id=1, source_target_pairs={{0,3},{1,2},{2,1},{3,0},{4,7},{5,6},{6,5},{7,4},{8,11},{9,10},{10,... | collective-permute-start | bytes 393224 | tf_op jit(solution)/shard_map/ppermute | solution.py:33
  52.9 2.1 %hidden.4.refs_0_.hidden_own_ref = bf16[128,1792]{1,0:T(8,128)(2,1)S(1)} custom-call(bf16[128,2048]{1,0:T(8,128)(2,1)S(1)} %norm.2.x_ref, bf16[2048,1792]{1,0:T(8,128)(2,1)S(1)} %get-tuple-element.83.gate_ref, bf16[2048,1792]{1,0:T(8,128)(2,1)S(1)} %get-tuple-element.84.up_ref), custom_call_target="tpu_custom_call" | custom-call | flops 1000000 | tf_op jit(solution)/shard_map/hidden/pallas_call | solution.py:495
  55.0 2.1 %hidden.5.hidden_other_ref = bf16[128,1792]{1,0:T(8,128)(2,1)S(1)} custom-call(bf16[128,2048]{1,0:T(8,128)(2,1)S(1)} %collective-permute-done.17.x_ref, bf16[2048,1792]{1,0:T(8,128)(2,1)S(1)} %get-tuple-element.83.gate_ref, bf16[2048,1792]{1,0:T(8,128)(2,1)S(1)} %get-tuple-element.84.up_ref, bf16[128,1792]{1,0:T(8,128)(2,1)S(1)} %hidden.4.refs_0_.hidden_own_ref), custom_call_target="tpu_custom_call" | custom-call | flops 1000000 | tf_op jit(solution)/shard_map/hidden/pallas_call | solution.py:495
  57.1 2.1 %down.2 = (f32[128,2048]{1,0:T(8,128)S(1)}, bf16[128,2048]{1,0:T(8,128)(2,1)S(1)}) custom-call(bf16[128,1792]{1,0:T(8,128)(2,1)S(1)} %hidden.4.refs_0_.hidden_own_ref, bf16[128,1792]{1,0:T(8,128)(2,1)S(1)} %hidden.5.hidden_other_ref, bf16[2048,1792]{1,0:T(8,128)(2,1)S(1)} %get-tuple-element.85.down_ref), custom_call_target="tpu_custom_call" | custom-call | flops 1000000 | tf_op jit(solution)/shard_map/down/pallas_call | solution.py:524
  63.0 1.8 %collective-permute-start.23 = (bf16[128,512]{1,0:T(8,128)(2,1)S(1)}, bf16[128,512]{1,0:T(8,128)(2,1)S(1)}, u32[]{:S(2)}, u32[]{:S(2)}) collective-permute-start(bf16[128,512]{1,0:T(8,128)(2,1)S(1)} %get-tuple-element.93), channel_id=1, source_target_pairs={{0,3},{1,2},{2,1},{3,0},{4,7},{5,6},{6,5},{7,4},{8,11},{9,10},{10,... | collective-permute-start | bytes 393224 | tf_op jit(solution)/shard_map/ppermute | solution.py:33
  64.8 2.1 %hidden.6.refs_0_.hidden_own_ref = bf16[128,1792]{1,0:T(8,128)(2,1)S(1)} custom-call(bf16[128,2048]{1,0:T(8,128)(2,1)S(1)} %norm.3.x_ref, bf16[2048,1792]{1,0:T(8,128)(2,1)S(1)} %get-tuple-element.83.gate_ref, bf16[2048,1792]{1,0:T(8,128)(2,1)S(1)} %get-tuple-element.84.up_ref, f32[128,512]{1,0:T(8,128)S(1)} %get-tuple-element.88.refs_0_), custom_call_target="tpu_custom_call" | custom-call | flops 1000000 | tf_op jit(solution)/shard_map/hidden/pallas_call | solution.py:495
  66.9 2.3 %hidden.7.hidden_other_ref = bf16[128,1792]{1,0:T(8,128)(2,1)S(1)} custom-call(bf16[128,2048]{1,0:T(8,128)(2,1)S(1)} %collective-permute-done.19.x_ref, bf16[2048,1792]{1,0:T(8,128)(2,1)S(1)} %get-tuple-element.83.gate_ref, bf16[2048,1792]{1,0:T(8,128)(2,1)S(1)} %get-tuple-element.84.up_ref, bf16[128,1792]{1,0:T(8,128)(2,1)S(1)} %hidden.6.refs_0_.hidden_own_ref), custom_call_target="tpu_custom_call" | custom-call | flops 1000000 | tf_op jit(solution)/shard_map/hidden/pallas_call | solution.py:495
  69.2 2.1 %down.3 = (f32[128,2048]{1,0:T(8,128)S(1)}, bf16[128,2048]{1,0:T(8,128)(2,1)S(1)}) custom-call(bf16[128,1792]{1,0:T(8,128)(2,1)S(1)} %hidden.6.refs_0_.hidden_own_ref, bf16[128,1792]{1,0:T(8,128)(2,1)S(1)} %hidden.7.hidden_other_ref, bf16[2048,1792]{1,0:T(8,128)(2,1)S(1)} %get-tuple-element.85.down_ref), custom_call_target="tpu_custom_call" | custom-call | flops 1000000 | tf_op jit(solution)/shard_map/down/pallas_call | solution.py:524
  75.1 1.8 %collective-permute-start.26 = (bf16[128,512]{1,0:T(8,128)(2,1)S(1)}, bf16[128,512]{1,0:T(8,128)(2,1)S(1)}, u32[]{:S(2)}, u32[]{:S(2)}) collective-permute-start(bf16[128,512]{1,0:T(8,128)(2,1)S(1)} %get-tuple-element.98), channel_id=1, source_target_pairs={{0,3},{1,2},{2,1},{3,0},{4,7},{5,6},{6,5},{7,4},{8,11},{9,10},{10,... | collective-permute-start | bytes 393224 | tf_op jit(solution)/shard_map/ppermute | solution.py:33
  79.8 2.6 %collective-permute-done.25.refs_2_ = bf16[128,512]{1,0:T(8,128)(2,1)S(1)} collective-permute-done((bf16[128,512]{1,0:T(8,128)(2,1)S(1)}, bf16[128,512]{1,0:T(8,128)(2,1)S(1)}, u32[]{:S(2)}, u32[]{:S(2)}) %collective-permute-start.25) | collective-permute-done | bytes 131104 | tf_op jit(solution)/shard_map/ppermute | solution.py:33
  82.6 2.0 %collective-permute-done.28.refs_0_ = bf16[64,512]{1,0:T(8,128)(2,1)S(1)} collective-permute-done((bf16[64,512]{1,0:T(8,128)(2,1)S(1)}, bf16[64,512]{1,0:T(8,128)(2,1)S(1)}, u32[]{:S(2)}, u32[]{:S(2)}) %collective-permute-start.28) | collective-permute-done | bytes 65568 | tf_op jit(solution)/shard_map/ppermute | solution.py:33
  84.9 2.0 %collective-permute-done.27.refs_1_ = bf16[64,512]{1,0:T(8,128)(2,1)S(1)} collective-permute-done((bf16[64,512]{1,0:T(8,128)(2,1)S(1)}, bf16[64,512]{1,0:T(8,128)(2,1)S(1)}, u32[]{:S(2)}, u32[]{:S(2)}) %collective-permute-start.27) | collective-permute-done | bytes 65568 | tf_op jit(solution)/shard_map/ppermute | solution.py:33
  (65 shorter events, 28.6 us)
Async XLA Ops:
  4.3 6.7 %collective-permute-start.1 = (bf16[144,256]{1,0:T(8,128)(2,1)S(1)}, bf16[144,256]{1,0:T(8,128)(2,1)S(1)}, u32[]{:S(2)}, u32[]{:S(2)}) collective-permute-start(bf16[144,256]{1,0:T(8,128)(2,1)S(1)} %get-tuple-element.59.refs_0_), channel_id=1, source_target_pairs={{0,1},{1,0},{2,3},{3,2},{4,5},{5,4},{6,7},{7,6},{8,9},{9,8},{10,11... | collective-permute-start | bytes 221192 | tf_op jit(solution)/shard_map/ppermute | solution.py:33
  8.2 5.3 %collective-permute-start.3 = (bf16[144,256]{1,0:T(8,128)(2,1)S(1)}, bf16[144,256]{1,0:T(8,128)(2,1)S(1)}, u32[]{:S(2)}, u32[]{:S(2)}) collective-permute-start(bf16[144,256]{1,0:T(8,128)(2,1)S(1)} %get-tuple-element.59.refs_0_), channel_id=1, source_target_pairs={{0,3},{1,2},{2,1},{3,0},{4,7},{5,6},{6,5},{7,4},{8,11},{9,10},{10,... | collective-permute-start | bytes 221192 | tf_op jit(solution)/shard_map/ppermute | solution.py:33
  20.5 6.7 %collective-permute-start.5 = (bf16[128,512]{1,0:T(8,128)(2,1)S(1)}, bf16[128,512]{1,0:T(8,128)(2,1)S(1)}, u32[]{:S(2)}, u32[]{:S(2)}) collective-permute-start(bf16[128,512]{1,0:T(8,128)(2,1)S(1)} %get-tuple-element.73), channel_id=1, source_target_pairs={{0,1},{1,0},{2,3},{3,2},{4,5},{5,4},{6,7},{7,6},{8,9},{9,8},{10,11... | collective-permute-start | bytes 393224 | tf_op jit(solution)/shard_map/ppermute | solution.py:33
  21.2 6.4 %collective-permute-start.6 = (bf16[128,512]{1,0:T(8,128)(2,1)S(1)}, bf16[128,512]{1,0:T(8,128)(2,1)S(1)}, u32[]{:S(2)}, u32[]{:S(2)}) collective-permute-start(bf16[128,512]{1,0:T(8,128)(2,1)S(1)} %get-tuple-element.74), channel_id=1, source_target_pairs={{0,2},{1,3},{2,0},{3,1},{4,6},{5,7},{6,4},{7,5},{8,10},{9,11},{10,... | collective-permute-start | bytes 393224 | tf_op jit(solution)/shard_map/ppermute | solution.py:33
  21.9 7.4 %collective-permute-start.7 = (bf16[128,512]{1,0:T(8,128)(2,1)S(1)}, bf16[128,512]{1,0:T(8,128)(2,1)S(1)}, u32[]{:S(2)}, u32[]{:S(2)}) collective-permute-start(bf16[128,512]{1,0:T(8,128)(2,1)S(1)} %get-tuple-element.75), channel_id=1, source_target_pairs={{0,3},{1,2},{2,1},{3,0},{4,7},{5,6},{6,5},{7,4},{8,11},{9,10},{10,... | collective-permute-start | bytes 393224 | tf_op jit(solution)/shard_map/ppermute | solution.py:33
  29.5 6.9 %collective-permute-start.10 = (bf16[64,512]{1,0:T(8,128)(2,1)S(1)}, bf16[64,512]{1,0:T(8,128)(2,1)S(1)}, u32[]{:S(2)}, u32[]{:S(2)}) collective-permute-start(bf16[64,512]{1,0:T(8,128)(2,1)S(1)} %get-tuple-element.80), channel_id=1, source_target_pairs={{0,12},{4,8},{8,4},{12,0},{1,13},{5,9},{9,5},{13,1},{2,14},{6,10},... | collective-permute-start | bytes 196616 | tf_op jit(solution)/shard_map/ppermute | solution.py:33
  33.2 6.6 %collective-permute-start.9 = (bf16[64,512]{1,0:T(8,128)(2,1)S(1)}, bf16[64,512]{1,0:T(8,128)(2,1)S(1)}, u32[]{:S(2)}, u32[]{:S(2)}) collective-permute-start(bf16[64,512]{1,0:T(8,128)(2,1)S(1)} %get-tuple-element.79), channel_id=1, source_target_pairs={{0,8},{4,12},{8,0},{12,4},{1,9},{5,13},{9,1},{13,5},{2,10},{6,14},... | collective-permute-start | bytes 196616 | tf_op jit(solution)/shard_map/ppermute | solution.py:33
  33.2 10.1 %collective-permute-start.8 = (bf16[64,512]{1,0:T(8,128)(2,1)S(1)}, bf16[64,512]{1,0:T(8,128)(2,1)S(1)}, u32[]{:S(2)}, u32[]{:S(2)}) collective-permute-start(bf16[64,512]{1,0:T(8,128)(2,1)S(1)} %get-tuple-element.78), channel_id=1, source_target_pairs={{0,4},{4,0},{8,12},{12,8},{1,5},{5,1},{9,13},{13,9},{2,6},{6,2},{1... | collective-permute-start | bytes 196616 | tf_op jit(solution)/shard_map/ppermute | solution.py:33
  39.8 6.7 %collective-permute-start.14 = (bf16[128,512]{1,0:T(8,128)(2,1)S(1)}, bf16[128,512]{1,0:T(8,128)(2,1)S(1)}, u32[]{:S(2)}, u32[]{:S(2)}) collective-permute-start(bf16[128,512]{1,0:T(8,128)(2,1)S(1)} %stack.2.refs_2_.refs_0_), channel_id=1, source_target_pairs={{0,1},{1,0},{2,3},{3,2},{4,5},{5,4},{6,7},{7,6},{8,9},{9,8},{10,11... | collective-permute-start | bytes 393224 | tf_op jit(solution)/shard_map/ppermute | solution.py:33
  41.3 7.7 %collective-permute-start.15 = (bf16[128,512]{1,0:T(8,128)(2,1)S(1)}, bf16[128,512]{1,0:T(8,128)(2,1)S(1)}, u32[]{:S(2)}, u32[]{:S(2)}) collective-permute-start(bf16[128,512]{1,0:T(8,128)(2,1)S(1)} %stack.2.refs_2_.refs_0_), channel_id=1, source_target_pairs={{0,2},{1,3},{2,0},{3,1},{4,6},{5,7},{6,4},{7,5},{8,10},{9,11},{10,... | collective-permute-start | bytes 393224 | tf_op jit(solution)/shard_map/ppermute | solution.py:33
  42.0 7.0 %collective-permute-start.16 = (bf16[128,512]{1,0:T(8,128)(2,1)S(1)}, bf16[128,512]{1,0:T(8,128)(2,1)S(1)}, u32[]{:S(2)}, u32[]{:S(2)}) collective-permute-start(bf16[128,512]{1,0:T(8,128)(2,1)S(1)} %stack.2.refs_2_.refs_0_), channel_id=1, source_target_pairs={{0,3},{1,2},{2,1},{3,0},{4,7},{5,6},{6,5},{7,4},{8,11},{9,10},{10,... | collective-permute-start | bytes 393224 | tf_op jit(solution)/shard_map/ppermute | solution.py:33
  49.2 5.7 %collective-permute-start.17 = (bf16[128,2048]{1,0:T(8,128)(2,1)S(1)}, bf16[128,2048]{1,0:T(8,128)(2,1)S(1)}, u32[]{:S(2)}, u32[]{:S(2)}) collective-permute-start(bf16[128,2048]{1,0:T(8,128)(2,1)S(1)} %norm.2.x_ref), channel_id=1, source_target_pairs={{0,16},{16,0},{1,17},{17,1},{2,18},{18,2},{3,19},{19,3},{4,20},{20... | collective-permute-start | bytes 1572872 | tf_op jit(solution)/shard_map/ppermute | solution.py:33
  49.3 9.9 %collective-permute-start.11 = (bf16[128,512]{1,0:T(8,128)(2,1)S(1)}, bf16[128,512]{1,0:T(8,128)(2,1)S(1)}, u32[]{:S(2)}, u32[]{:S(2)}) collective-permute-start(bf16[128,512]{1,0:T(8,128)(2,1)S(1)} %stack.3.refs_1_.refs_0_), channel_id=1, source_target_pairs={{0,1},{1,0},{2,3},{3,2},{4,5},{5,4},{6,7},{7,6},{8,9},{9,8},{10,11... | collective-permute-start | bytes 393224 | tf_op jit(solution)/shard_map/ppermute | solution.py:33
  50.3 9.0 %collective-permute-start.12 = (bf16[128,512]{1,0:T(8,128)(2,1)S(1)}, bf16[128,512]{1,0:T(8,128)(2,1)S(1)}, u32[]{:S(2)}, u32[]{:S(2)}) collective-permute-start(bf16[128,512]{1,0:T(8,128)(2,1)S(1)} %stack.3.refs_1_.refs_0_), channel_id=1, source_target_pairs={{0,2},{1,3},{2,0},{3,1},{4,6},{5,7},{6,4},{7,5},{8,10},{9,11},{10,... | collective-permute-start | bytes 393224 | tf_op jit(solution)/shard_map/ppermute | solution.py:33
  51.0 8.2 %collective-permute-start.13 = (bf16[128,512]{1,0:T(8,128)(2,1)S(1)}, bf16[128,512]{1,0:T(8,128)(2,1)S(1)}, u32[]{:S(2)}, u32[]{:S(2)}) collective-permute-start(bf16[128,512]{1,0:T(8,128)(2,1)S(1)} %stack.3.refs_1_.refs_0_), channel_id=1, source_target_pairs={{0,3},{1,2},{2,1},{3,0},{4,7},{5,6},{6,5},{7,4},{8,11},{9,10},{10,... | collective-permute-start | bytes 393224 | tf_op jit(solution)/shard_map/ppermute | solution.py:33
  59.5 7.4 %collective-permute-start.19 = (bf16[128,2048]{1,0:T(8,128)(2,1)S(1)}, bf16[128,2048]{1,0:T(8,128)(2,1)S(1)}, u32[]{:S(2)}, u32[]{:S(2)}) collective-permute-start(bf16[128,2048]{1,0:T(8,128)(2,1)S(1)} %norm.3.x_ref), channel_id=1, source_target_pairs={{0,16},{16,0},{1,17},{17,1},{2,18},{18,2},{3,19},{19,3},{4,20},{20... | collective-permute-start | bytes 1572872 | tf_op jit(solution)/shard_map/ppermute | solution.py:33
  61.2 10.2 %collective-permute-start.21 = (bf16[128,512]{1,0:T(8,128)(2,1)S(1)}, bf16[128,512]{1,0:T(8,128)(2,1)S(1)}, u32[]{:S(2)}, u32[]{:S(2)}) collective-permute-start(bf16[128,512]{1,0:T(8,128)(2,1)S(1)} %get-tuple-element.91), channel_id=1, source_target_pairs={{0,1},{1,0},{2,3},{3,2},{4,5},{5,4},{6,7},{7,6},{8,9},{9,8},{10,11... | collective-permute-start | bytes 393224 | tf_op jit(solution)/shard_map/ppermute | solution.py:33
  62.2 9.2 %collective-permute-start.22 = (bf16[128,512]{1,0:T(8,128)(2,1)S(1)}, bf16[128,512]{1,0:T(8,128)(2,1)S(1)}, u32[]{:S(2)}, u32[]{:S(2)}) collective-permute-start(bf16[128,512]{1,0:T(8,128)(2,1)S(1)} %get-tuple-element.92), channel_id=1, source_target_pairs={{0,2},{1,3},{2,0},{3,1},{4,6},{5,7},{6,4},{7,5},{8,10},{9,11},{10,... | collective-permute-start | bytes 393224 | tf_op jit(solution)/shard_map/ppermute | solution.py:33
  63.0 8.5 %collective-permute-start.23 = (bf16[128,512]{1,0:T(8,128)(2,1)S(1)}, bf16[128,512]{1,0:T(8,128)(2,1)S(1)}, u32[]{:S(2)}, u32[]{:S(2)}) collective-permute-start(bf16[128,512]{1,0:T(8,128)(2,1)S(1)} %get-tuple-element.93), channel_id=1, source_target_pairs={{0,3},{1,2},{2,1},{3,0},{4,7},{5,6},{6,5},{7,4},{8,11},{9,10},{10,... | collective-permute-start | bytes 393224 | tf_op jit(solution)/shard_map/ppermute | solution.py:33
  73.4 6.4 %collective-permute-start.24 = (bf16[128,512]{1,0:T(8,128)(2,1)S(1)}, bf16[128,512]{1,0:T(8,128)(2,1)S(1)}, u32[]{:S(2)}, u32[]{:S(2)}) collective-permute-start(bf16[128,512]{1,0:T(8,128)(2,1)S(1)} %get-tuple-element.96), channel_id=1, source_target_pairs={{0,1},{1,0},{2,3},{3,2},{4,5},{5,4},{6,7},{7,6},{8,9},{9,8},{10,11... | collective-permute-start | bytes 393224 | tf_op jit(solution)/shard_map/ppermute | solution.py:33
  74.4 8.1 %collective-permute-start.25 = (bf16[128,512]{1,0:T(8,128)(2,1)S(1)}, bf16[128,512]{1,0:T(8,128)(2,1)S(1)}, u32[]{:S(2)}, u32[]{:S(2)}) collective-permute-start(bf16[128,512]{1,0:T(8,128)(2,1)S(1)} %get-tuple-element.97), channel_id=1, source_target_pairs={{0,2},{1,3},{2,0},{3,1},{4,6},{5,7},{6,4},{7,5},{8,10},{9,11},{10,... | collective-permute-start | bytes 393224 | tf_op jit(solution)/shard_map/ppermute | solution.py:33
  75.1 7.3 %collective-permute-start.26 = (bf16[128,512]{1,0:T(8,128)(2,1)S(1)}, bf16[128,512]{1,0:T(8,128)(2,1)S(1)}, u32[]{:S(2)}, u32[]{:S(2)}) collective-permute-start(bf16[128,512]{1,0:T(8,128)(2,1)S(1)} %get-tuple-element.98), channel_id=1, source_target_pairs={{0,3},{1,2},{2,1},{3,0},{4,7},{5,6},{6,5},{7,4},{8,11},{9,10},{10,... | collective-permute-start | bytes 393224 | tf_op jit(solution)/shard_map/ppermute | solution.py:33
  77.0 7.6 %collective-permute-start.28 = (bf16[64,512]{1,0:T(8,128)(2,1)S(1)}, bf16[64,512]{1,0:T(8,128)(2,1)S(1)}, u32[]{:S(2)}, u32[]{:S(2)}) collective-permute-start(bf16[64,512]{1,0:T(8,128)(2,1)S(1)} %get-tuple-element.94.refs_1_), channel_id=1, source_target_pairs={{0,8},{4,12},{8,0},{12,4},{1,9},{5,13},{9,1},{13,5},{2,10},{6,14},... | collective-permute-start | bytes 196616 | tf_op jit(solution)/shard_map/ppermute | solution.py:33
  77.9 6.7 %collective-permute-start.29 = (bf16[64,512]{1,0:T(8,128)(2,1)S(1)}, bf16[64,512]{1,0:T(8,128)(2,1)S(1)}, u32[]{:S(2)}, u32[]{:S(2)}) collective-permute-start(bf16[64,512]{1,0:T(8,128)(2,1)S(1)} %get-tuple-element.101), channel_id=1, source_target_pairs={{0,12},{4,8},{8,4},{12,0},{1,13},{5,9},{9,5},{13,1},{2,14},{6,10},... | collective-permute-start | bytes 196616 | tf_op jit(solution)/shard_map/ppermute | solution.py:33
  (8 other events, 38.6 us)

commit v6 on v5

--- a/solution.py
+++ b/solution.py
@@ -71,27 +71,6 @@
         cost_estimate=cost(1e6, 0),
         name="stack",
     )(*pieces, *after)
-
-
-def last_weight_kernel(expert_hbm, *refs):
-    weight_ref, token_ref, sem = refs[-3:]
-    copy = pltpu.make_async_copy(expert_hbm.at[0, 2], weight_ref, sem)
-    copy.start()
-    token_ref[...] = jnp.zeros_like(token_ref)
-    copy.wait()
-
-
-def last_weight(experts, after):
-    return pl.pallas_call(
-        last_weight_kernel,
-        out_shape=(shaped(experts.shape[2:], BF16), shaped((8, 128), F32)),
-        in_specs=[hbm()] + unread(after),
-        out_specs=[whole()] * 2,
-        scratch_shapes=[pltpu.SemaphoreType.DMA],
-        compiler_params=params(),
-        cost_estimate=cost(2e10, 0),
-        name="weight",
-    )(experts, *after)
 
 
 def order_kernel(*refs):
@@ -479,8 +458,14 @@
     )(*sum(sets, []), gain, *after)
 
 
-def hidden_kernel(x_ref, gate_ref, up_ref, *refs):
-    hidden_ref = refs[-1]
+def hidden_kernel(part, x_ref, gate_ref, up_ref, *refs):
+    if part is None:
+        hidden_ref = refs[-1]
+    else:
+        hidden_ref, weight_ref, sem = refs[-3:]
+        count = weight_ref.shape[0]
+        copy = pltpu.make_async_copy(refs[0].at[0, 2, pl.ds(part * count, count)], weight_ref, sem)
+        copy.start()
     width = gate_ref.shape[1]
     size = 256 if width % 256 == 0 else width
     for i in range(width // size):
@@ -488,31 +473,44 @@
         gate = jnp.dot(x_ref[...], gate_ref[:, cut], preferred_element_type=F32)
         up = jnp.dot(x_ref[...], up_ref[:, cut], preferred_element_type=F32)
         hidden_ref[:, cut] = (gate * sigmoid(gate) * up).astype(BF16)
-
-
-def hidden_units(x, gate, up, after):
+    if part is not None:
+        copy.wait()
+
+
+def hidden_units(x, gate, up, after, experts=None, part=None):
     rows, width = x.shape[0], gate.shape[1]
-    return pl.pallas_call(
-        hidden_kernel,
-        out_shape=shaped((rows, width), BF16),
-        in_specs=[whole()] * 3 + unread(after),
-        out_specs=whole(),
+    made = [shaped((rows, width), BF16)]
+    extra = []
+    if part is not None:
+        made.append(shaped((gate.shape[0] // 2, width), BF16))
+        extra = [experts]
+    return pl.pallas_call(
+        functools.partial(hidden_kernel, part),
+        out_shape=made,
+        in_specs=[whole()] * 3 + [hbm()] * len(extra) + unread(after),
+        out_specs=[whole()] * len(made),
+        scratch_shapes=[pltpu.SemaphoreType.DMA] * len(extra),
         compiler_params=params(),
         cost_estimate=cost(1e6, 0),
         name="hidden",
-    )(x, gate, up, *after)
-
-
-def down_kernel(hidden_own_ref, hidden_other_ref, down_ref, *refs):
+    )(x, gate, up, *extra, *after)
+
+
+def down_kernel(hidden_own_ref, hidden_other_ref, low_ref, high_ref, *refs):
     own_ref, other_ref, hidden_ref = refs[-3:]
     rows = hidden_own_ref.shape[0]
     hidden_ref[:rows, :] = hidden_own_ref[...]
     hidden_ref[rows:, :] = hidden_other_ref[...]
     size = 256
-    for i in range(down_ref.shape[0] // size):
+    half = low_ref.shape[0]
+    for i in range(2 * half // size):
         cut = slice(i * size, (i + 1) * size)
+        down_ref, begin = (low_ref, i * size) if i * size < half else (high_ref, i * size - half)
         product = lax.dot_general(
-            hidden_ref[...], down_ref[cut, :], (((1,), (1,)), ((), ())), preferred_element_type=F32
+            hidden_ref[...],
+            down_ref[begin : begin + size, :],
+            (((1,), (1,)), ((), ())),
+            preferred_element_type=F32,
         )
         own_ref[:, cut] = product[:rows]
         other_ref[:, cut] = product[rows:].astype(BF16)
@@ -520,17 +518,17 @@
 
 def down_sums(hidden_own, hidden_other, down, after):
     rows, width = hidden_own.shape
-    model = down.shape[0]
+    model = 2 * down[0].shape[0]
     return pl.pallas_call(
         down_kernel,
         out_shape=(shaped((rows, model), F32), shaped((rows, model), BF16)),
-        in_specs=[whole()] * 3 + unread(after),
+        in_specs=[whole()] * 4 + unread(after),
         out_specs=[whole()] * 2,
         scratch_shapes=[pltpu.VMEM((2 * rows, width), BF16)],
         compiler_params=params(),
         cost_estimate=cost(1e6, 0),
         name="down",
-    )(hidden_own, hidden_other, down, *after)
+    )(hidden_own, hidden_other, *down, *after)
 
 
 def join_kernel(parts, own_ref, other_ref, *refs):
@@ -603,16 +601,6 @@
         cost_estimate=cost(1e6, 1e6),
         name="blend",
     )(*back, base, first, second, gates)
-
-
-def expert(tp, x_own, gate, up, down, after_start, after_sums):
-    x_other = swap(x_own, "ctx", 1)
-    hidden_own = hidden_units(x_own, gate, up, after_start)
-    hidden_other = hidden_units(x_other, gate, up, [hidden_own])
-    sum_own, sum_other = down_sums(hidden_own, hidden_other, down, [])
-    after_sums = [order([sum_other, *after_sums])] if after_sums else []
-    joined = join(tp, sum_own, swap(sum_other, "ctx", 1), after_sums)
-    return sum_own, joined
 
 
 def body(
@@ -650,18 +638,26 @@
     first, second, chooser, gate_w = route(expert_ids[0].T, experts, expert_weight)
     stream, *picked = pick(own, arrived, chooser)
     half = experts // 2
-    rows = {j: swap(picked[j], "exp", j) for j in range(experts - 1, 0, -1)}
-    piece_a = stack([rows[j] for j in range(half, experts)], [])
-    piece_b = stack([picked[0]] + [rows[j] for j in range(1, half)], [piece_a])
-    down_w, both = last_weight(expert_weight, [piece_a, piece_b])
-    rows_a = [piece_a] + swaps([piece_a] * (tp - 1))
-    rows_b = [piece_b] + swaps([piece_b] * (tp - 1))
-    x_a = norm([rows_a], gain, [both])
-    own_a, joined_a = expert(tp, x_a, gate_w, up_w, down_w, [], [])
+    rows = [picked[0]] + [swap(picked[j], "exp", j) for j in range(1, experts)]
+    piece_b = stack(rows[:half], [])
+    both = order([rows[half], piece_b])
+    first_a = rows[experts - 1]
+    second_a = rows[half] if half == 2 else stack(rows[half : experts - 1], [])
+    sets = [[piece] + swaps([piece] * (tp - 1)) for piece in (first_a, second_a, piece_b)]
+    x_a = norm(sets[:2], gain, [both])
+    own_a, low = hidden_units(x_a, gate_w, up_w, [], expert_weight, 0)
+    other_a, high = hidden_units(swap(x_a, "ctx", 1), gate_w, up_w, [own_a, order([x_a])], expert_weight, 1)
+    down_w = (low, high)
+    sum_a, sent_a = down_sums(own_a, other_a, down_w, [])
+    joined_a = join(tp, sum_a, swap(sent_a, "ctx", 1), [])
     made_a = totals([joined_a[0]] + swaps(joined_a[1:]))
-    x_b = norm([rows_b], gain, [own_a])
-    _, joined_b = expert(tp, x_b, gate_w, up_w, down_w, [joined_a[0]], [made_a[0]])
+    x_b = norm(sets[2:], gain, [sum_a])
+    own_b, = hidden_units(x_b, gate_w, up_w, [joined_a[0]])
+    other_b, = hidden_units(swap(x_b, "ctx", 1), gate_w, up_w, [own_b])
+    sum_b, sent_b = down_sums(own_b, other_b, down_w, [])
+    joined_b = join(tp, sum_b, swap(sent_b, "ctx", 1), [order([sent_b, made_a[0]])])
     made_b = totals([joined_b[0]] + swaps(joined_b[1:]))
+    made_a = made_a[1:] + made_a[:1]
     back_a = [swap(piece, "exp", j) for j, piece in enumerate(made_a, half)]
     back_b = [made_b[0]] + [swap(made_b[j], "exp", j) for j in range(1, half)]
     gates = route_gates[0].T

time: 88 us -> 85.2 us (0.968)
  waiting for transfers between devices: 23.7 us -> 15 us
  starting transfers between devices: 33.1 us -> 41.6 us
  Pallas kernels: 30.7 us -> 28 us
    ppermute x28 -> x31, waiting for transfers between devices: 22.7 us -> 14 us  [swap(): lax.ppermute(block, axis, [(i, i ^ k) for i in range(lax.axis_size(axis))])]
    ppermute x28 -> x31, starting transfers between devices: 29.4 us -> 38 us  [swap(): lax.ppermute(block, axis, [(i, i ^ k) for i in range(lax.axis_size(axis))])]
    pallas_call x5 -> x4, Pallas kernels: 11.7 us -> 9.05 us  [hidden_units(): pl.pallas_call(functools.partial(hidden_kernel, part), out_shape=made, in...]
  transfers between devices with their start and end apart: 30 -> 33, of which waited for: 14 -> 12; matrix products, arithmetic and copies ran while one was open for 0% -> 0% of each run, Pallas kernels for 27% -> 25%
where the time goes in v6:
time: 85.2 us; the launch traced here: 84.9 us
  starting transfers between devices  41.6 us (49%)
  Pallas kernels  28 us (33%)
  waiting for transfers between devices  15 us (18%)
    ppermute x31, starting transfers between devices, swap(): lax.ppermute(block, axis, [(i, i ^ k) for i in range(lax.axis_size(axis))])  38 us
    ppermute x31, waiting for transfers between devices, swap(): lax.ppermute(block, axis, [(i, i ^ k) for i in range(lax.axis_size(axis))])  14 us
    pallas_call x4, Pallas kernels, hidden_units(): pl.pallas_call(functools.partial(hidden_kernel, part), out_shape=made, in...  9.05 us
    pallas_call x2, Pallas kernels, down_sums(): pl.pallas_call(down_kernel, out_shape=(shaped((rows, model), F32), shaped...  4.18 us
    pallas_call x1, Pallas kernels, scan(): pl.pallas_call(functools.partial(scan_kernel, len(pieces)), out_shape=(sh...  3.62 us
    pallas_call x1, Pallas kernels, route(): pl.pallas_call(route_kernel, out_shape=(shaped((rows, slots), BF16), shap...  3.09 us
    pallas_call x1, Pallas kernels, prepare(): pl.pallas_call(prepare_kernel, out_shape=(shaped((rows, channels), F32),...  2.76 us
    ppermute x1, starting transfers between devices, body(): before = lax.ppermute(local, 'ctx', [(0, 1)])  2.36 us
  transfers between devices with their start and end apart: 33, of which 12 were waited for; matrix products, arithmetic and copies ran while one was open for 0% of the time, Pallas kernels for 25%

profile of v6, /device:TPU:0, one launch (start us, length us, event | category | flops | bytes accessed | tf_op | source)
XLA Modules:
  0.0 84.9 jit_solution(14917142709083777837)
XLA Ops:
  0.0 2.4 %collective-permute-start = (bf16[128,1024]{1,0:T(8,128)(2,1)}, bf16[128,1024]{1,0:T(8,128)(2,1)S(1)}, u32[]{:S(2)}, u32[]{:S(2)}) collective-permute-start(bf16[128,1024]{1,0:T(8,128)(2,1)} %bitcast.21), channel_id=1, source_target_pairs={{0,16},{1,17},{2,18},{3,19},{4,20},{5,21},{6,22},{7,23},{8,24},{9,... | collective-permute-start | bytes 786440 | tf_op jit(solution)/shard_map/ppermute | solution.py:625
  4.3 2.4 %collective-permute-start.1 = (bf16[144,256]{1,0:T(8,128)(2,1)S(1)}, bf16[144,256]{1,0:T(8,128)(2,1)S(1)}, u32[]{:S(2)}, u32[]{:S(2)}) collective-permute-start(bf16[144,256]{1,0:T(8,128)(2,1)S(1)} %get-tuple-element.61.refs_0_), channel_id=1, source_target_pairs={{0,1},{1,0},{2,3},{3,2},{4,5},{5,4},{6,7},{7,6},{8,9},{9,8},{10,11... | collective-permute-start | bytes 221192 | tf_op jit(solution)/shard_map/ppermute | solution.py:33
  8.2 2.8 %prepare.1 = (f32[128,1024]{1,0:T(8,128)S(1)}, f32[16,8,128]{2,1,0:T(8,128)S(1)}, f32[128,1024]{1,0:T(8,128)S(1)}, f32[1,1024]{1,0:T(1,128)S(1)}, bf16[256,1024]...) custom-call(bf16[128,1024]{1,0:T(8,128)(2,1)S(1)} %get-tuple-element.62.xconv_, ...), custom_call_target="tpu_custom_call" | custom-call | flops 1000000 | bytes 6000000 | tf_op jit(solution)/shard_map/prepare/pallas_call | solution.py:241
  11.0 2.4 %collective-permute-done.3.refs_3_ = bf16[144,256]{1,0:T(8,128)(2,1)S(1)} collective-permute-done((bf16[144,256]{1,0:T(8,128)(2,1)S(1)}, bf16[144,256]{1,0:T(8,128)(2,1)S(1)}, u32[]{:S(2)}, u32[]{:S(2)}) %collective-permute-start.3) | collective-permute-done | bytes 73760 | tf_op jit(solution)/shard_map/ppermute | solution.py:33
  13.5 3.6 %scan.1 = (f32[128,8,128]{2,1,0:T(8,128)S(1)}, f32[128,8,128]{2,1,0:T(8,128)S(1)}, f32[128,16,128]{2,1,0:T(8,128)S(1)}, f32[16,8,128]{2,1,0:T(8,128)S(1)}, bf16[2048,1792]{1,0:T(8,128)(2,1)S(1)}) custom-call(bf16[144,256]{1,0:T(8,128)(2,1)S(1)} %get-tuple-element.61.refs_0_, bf16[144,256]{1,0:T(8,128)(2,1)S(1)} %collective-permute-done.1.refs_1_, ...), custom_call_target="tpu_custom_call" | custom-call | flops 1000000 | bytes 14000000 | tf_op jit(solution)/shard_map/scan/pallas_call | solution.py:319
  21.9 2.2 %collective-permute-start.7 = (bf16[128,512]{1,0:T(8,128)(2,1)S(1)}, bf16[128,512]{1,0:T(8,128)(2,1)S(1)}, u32[]{:S(2)}, u32[]{:S(2)}) collective-permute-start(bf16[128,512]{1,0:T(8,128)(2,1)S(1)} %get-tuple-element.77), channel_id=1, source_target_pairs={{0,3},{1,2},{2,1},{3,0},{4,7},{5,6},{6,5},{7,4},{8,11},{9,10},{10,... | collective-permute-start | bytes 393224 | tf_op jit(solution)/shard_map/ppermute | solution.py:33
  24.1 3.1 %route.1 = (bf16[128,256]{1,0:T(8,128)(2,1)S(1)}, bf16[128,256]{1,0:T(8,128)(2,1)S(1)}, bf16[256,128]{1,0:T(8,128)(2,1)S(1)}, bf16[2048,1792]{1,0:T(8,128)(2,1)S(1)}) custom-call(s32[2,128]{1,0:T(2,128)S(1)} %bitcast.17, bf16[1,3,2048,1792]{3,2,1,0:T(8,128)(2,1)} %refs_0_.3), custom_call_target="tpu_custom_call" | custom-call | flops 1000000 | bytes 8000000 | tf_op jit(solution)/shard_map/route/pallas_call | solution.py:124
  27.6 1.7 %collective-permute-done.7.refs_3_ = bf16[128,512]{1,0:T(8,128)(2,1)S(1)} collective-permute-done((bf16[128,512]{1,0:T(8,128)(2,1)S(1)}, bf16[128,512]{1,0:T(8,128)(2,1)S(1)}, u32[]{:S(2)}, u32[]{:S(2)}) %collective-permute-start.7) | collective-permute-done | bytes 131104 | tf_op jit(solution)/shard_map/ppermute | solution.py:33
  29.5 3.7 %collective-permute-start.12 = (bf16[64,512]{1,0:T(8,128)(2,1)S(1)}, bf16[64,512]{1,0:T(8,128)(2,1)S(1)}, u32[]{:S(2)}, u32[]{:S(2)}) collective-permute-start(bf16[64,512]{1,0:T(8,128)(2,1)S(1)} %get-tuple-element.82), channel_id=1, source_target_pairs={{0,12},{4,8},{8,4},{12,0},{1,13},{5,9},{9,5},{13,1},{2,14},{6,10},... | collective-permute-start | bytes 196616 | tf_op jit(solution)/shard_map/ppermute | solution.py:33
  34.0 2.5 %collective-permute-done.12.refs_0_ = bf16[64,512]{1,0:T(8,128)(2,1)S(1)} collective-permute-done((bf16[64,512]{1,0:T(8,128)(2,1)S(1)}, bf16[64,512]{1,0:T(8,128)(2,1)S(1)}, u32[]{:S(2)}, u32[]{:S(2)}) %collective-permute-start.12) | collective-permute-done | bytes 65568 | tf_op jit(solution)/shard_map/ppermute | solution.py:33
  39.9 1.6 %collective-permute-start.17 = (bf16[64,512]{1,0:T(8,128)(2,1)S(1)}, bf16[64,512]{1,0:T(8,128)(2,1)S(1)}, u32[]{:S(2)}, u32[]{:S(2)}) collective-permute-start(bf16[64,512]{1,0:T(8,128)(2,1)S(1)} %collective-permute-done.16.refs_0_.refs_4_), channel_id=1, source_target_pairs={{0,1},{1,0},{2,3},{3,2},{4,5},{5,4},{6,7},{7,6},{8,9},{9,8},{10,11... | collective-permute-start | bytes 196616 | tf_op jit(solution)/shard_map/ppermute | solution.py:33
  44.6 2.0 %collective-permute-start.11 = (bf16[128,512]{1,0:T(8,128)(2,1)S(1)}, bf16[128,512]{1,0:T(8,128)(2,1)S(1)}, u32[]{:S(2)}, u32[]{:S(2)}) collective-permute-start(bf16[128,512]{1,0:T(8,128)(2,1)S(1)} %stack.1.refs_1_.refs_0_), channel_id=1, source_target_pairs={{0,3},{1,2},{2,1},{3,0},{4,7},{5,6},{6,5},{7,4},{8,11},{9,10},{10,... | collective-permute-start | bytes 393224 | tf_op jit(solution)/shard_map/ppermute | solution.py:33
  47.0 1.9 %collective-permute-done.18.refs_6_ = bf16[64,512]{1,0:T(8,128)(2,1)S(1)} collective-permute-done((bf16[64,512]{1,0:T(8,128)(2,1)S(1)}, bf16[64,512]{1,0:T(8,128)(2,1)S(1)}, u32[]{:S(2)}, u32[]{:S(2)}) %collective-permute-start.18) | collective-permute-done | bytes 65568 | tf_op jit(solution)/shard_map/ppermute | solution.py:33
  49.2 2.2 %hidden.4 = (bf16[128,1792]{1,0:T(8,128)(2,1)S(1)}, bf16[1024,1792]{1,0:T(8,128)(2,1)S(1)}) custom-call(bf16[128,2048]{1,0:T(8,128)(2,1)S(1)} %norm.2.x_ref.refs_0_, bf16[2048,1792]{1,0:T(8,128)(2,1)S(1)} %get-tuple-element.84.gate_ref, bf16[2048,1792]{1,0:T(8,128)(2,1)S(1)} %get-tuple-element.85.up_ref, bf16[1,3,2048,1792]{3,2,1,0:T(8,128)(2,1)} %refs_0_.3), custom_call_target="tpu_custom_call" | custom-call | flops 1000000 | tf_op jit(solution)/shard_map/hidden/pallas_call | solution.py:487
  51.5 2.2 %hidden.5 = (bf16[128,1792]{1,0:T(8,128)(2,1)S(1)}, bf16[1024,1792]{1,0:T(8,128)(2,1)S(1)}) custom-call(bf16[128,2048]{1,0:T(8,128)(2,1)S(1)} %collective-permute-done.20.x_ref, bf16[2048,1792]{1,0:T(8,128)(2,1)S(1)} %get-tuple-element.84.gate_ref, bf16[2048,1792]{1,0:T(8,128)(2,1)S(1)} %get-tuple-element.85.up_ref, bf16[1,3,2048,1792]{3,2,1,0:T(8,128)(2,1)} %refs_0_.3, ...), custom_call_target="tpu_custom_call" | custom-call | flops 1000000 | tf_op jit(solution)/shard_map/hidden/pallas_call | solution.py:487
  53.7 2.1 %down.2 = (f32[128,2048]{1,0:T(8,128)S(1)}, bf16[128,2048]{1,0:T(8,128)(2,1)S(1)}) custom-call(bf16[128,1792]{1,0:T(8,128)(2,1)S(1)} %get-tuple-element.86.refs_1_.hidden_own_ref, bf16[128,1792]{1,0:T(8,128)(2,1)S(1)} %get-tuple-element.87.hidden_other_ref, bf16[1024,1792]{1,0:T(8,128)(2,1)S(1)} %get-tuple-element.88.low_ref, ...), custom_call_target="tpu_custom_call" | custom-call | flops 1000000 | tf_op jit(solution)/shard_map/down/pallas_call | solution.py:522
  58.9 2.7 %collective-permute-start.26 = (bf16[128,512]{1,0:T(8,128)(2,1)S(1)}, bf16[128,512]{1,0:T(8,128)(2,1)S(1)}, u32[]{:S(2)}, u32[]{:S(2)}) collective-permute-start(bf16[128,512]{1,0:T(8,128)(2,1)S(1)} %get-tuple-element.97), channel_id=1, source_target_pairs={{0,3},{1,2},{2,1},{3,0},{4,7},{5,6},{6,5},{7,4},{8,11},{9,10},{10,... | collective-permute-start | bytes 393224 | tf_op jit(solution)/shard_map/ppermute | solution.py:33
  61.6 2.2 %hidden.6.refs_0_.hidden_own_ref = bf16[128,1792]{1,0:T(8,128)(2,1)S(1)} custom-call(bf16[128,2048]{1,0:T(8,128)(2,1)S(1)} %norm.3.x_ref, bf16[2048,1792]{1,0:T(8,128)(2,1)S(1)} %get-tuple-element.84.gate_ref, bf16[2048,1792]{1,0:T(8,128)(2,1)S(1)} %get-tuple-element.85.up_ref, f32[128,512]{1,0:T(8,128)S(1)} %get-tuple-element.92.refs_0_), custom_call_target="tpu_custom_call" | custom-call | flops 1000000 | tf_op jit(solution)/shard_map/hidden/pallas_call | solution.py:487
  63.8 2.4 %hidden.7.hidden_other_ref = bf16[128,1792]{1,0:T(8,128)(2,1)S(1)} custom-call(bf16[128,2048]{1,0:T(8,128)(2,1)S(1)} %collective-permute-done.22.x_ref, bf16[2048,1792]{1,0:T(8,128)(2,1)S(1)} %get-tuple-element.84.gate_ref, bf16[2048,1792]{1,0:T(8,128)(2,1)S(1)} %get-tuple-element.85.up_ref, bf16[128,1792]{1,0:T(8,128)(2,1)S(1)} %hidden.6.refs_0_.hidden_own_ref), custom_call_target="tpu_custom_call" | custom-call | flops 1000000 | tf_op jit(solution)/shard_map/hidden/pallas_call | solution.py:487
  66.2 2.1 %down.3 = (f32[128,2048]{1,0:T(8,128)S(1)}, bf16[128,2048]{1,0:T(8,128)(2,1)S(1)}) custom-call(bf16[128,1792]{1,0:T(8,128)(2,1)S(1)} %hidden.6.refs_0_.hidden_own_ref, bf16[128,1792]{1,0:T(8,128)(2,1)S(1)} %hidden.7.hidden_other_ref, bf16[1024,1792]{1,0:T(8,128)(2,1)S(1)} %get-tuple-element.88.low_ref, bf16[1024,1792]{1,0:T(8,128)(2,1)S(1)} %get-tuple-element.89.high_ref), custom_call_target="tpu_custom_call" | custom-call | flops 1000000 | tf_op jit(solution)/shard_map/down/pallas_call | solution.py:522
  68.5 1.8 %collective-permute-done.23.other_ref = bf16[128,2048]{1,0:T(8,128)(2,1)S(1)} collective-permute-done((bf16[128,2048]{1,0:T(8,128)(2,1)S(1)}, bf16[128,2048]{1,0:T(8,128)(2,1)S(1)}, u32[]{:S(2)}, u32[]{:S(2)}) %collective-permute-start.23) | collective-permute-done | bytes 524320 | tf_op jit(solution)/shard_map/ppermute | solution.py:33
  71.3 2.7 %collective-permute-start.29 = (bf16[128,512]{1,0:T(8,128)(2,1)S(1)}, bf16[128,512]{1,0:T(8,128)(2,1)S(1)}, u32[]{:S(2)}, u32[]{:S(2)}) collective-permute-start(bf16[128,512]{1,0:T(8,128)(2,1)S(1)} %get-tuple-element.102), channel_id=1, source_target_pairs={{0,3},{1,2},{2,1},{3,0},{4,7},{5,6},{6,5},{7,4},{8,11},{9,10},{10,... | collective-permute-start | bytes 393224 | tf_op jit(solution)/shard_map/ppermute | solution.py:33
  75.4 3.4 %collective-permute-start.32 = (bf16[64,512]{1,0:T(8,128)(2,1)S(1)}, bf16[64,512]{1,0:T(8,128)(2,1)S(1)}, u32[]{:S(2)}, u32[]{:S(2)}) collective-permute-start(bf16[64,512]{1,0:T(8,128)(2,1)S(1)} %get-tuple-element.98.refs_1_), channel_id=1, source_target_pairs={{0,12},{4,8},{8,4},{12,0},{1,13},{5,9},{9,5},{13,1},{2,14},{6,10},... | collective-permute-start | bytes 196616 | tf_op jit(solution)/shard_map/ppermute | solution.py:33
  79.0 2.8 %collective-permute-start.30 = (bf16[64,512]{1,0:T(8,128)(2,1)S(1)}, bf16[64,512]{1,0:T(8,128)(2,1)S(1)}, u32[]{:S(2)}, u32[]{:S(2)}) collective-permute-start(bf16[64,512]{1,0:T(8,128)(2,1)S(1)} %get-tuple-element.104), channel_id=1, source_target_pairs={{0,4},{4,0},{8,12},{12,8},{1,5},{5,1},{9,13},{13,9},{2,6},{6,2},{1... | collective-permute-start | bytes 196616 | tf_op jit(solution)/shard_map/ppermute | solution.py:33
  (71 shorter events, 25.9 us)
Async XLA Ops:
  4.3 6.7 %collective-permute-start.1 = (bf16[144,256]{1,0:T(8,128)(2,1)S(1)}, bf16[144,256]{1,0:T(8,128)(2,1)S(1)}, u32[]{:S(2)}, u32[]{:S(2)}) collective-permute-start(bf16[144,256]{1,0:T(8,128)(2,1)S(1)} %get-tuple-element.61.refs_0_), channel_id=1, source_target_pairs={{0,1},{1,0},{2,3},{3,2},{4,5},{5,4},{6,7},{7,6},{8,9},{9,8},{10,11... | collective-permute-start | bytes 221192 | tf_op jit(solution)/shard_map/ppermute | solution.py:33
  20.5 6.7 %collective-permute-start.5 = (bf16[128,512]{1,0:T(8,128)(2,1)S(1)}, bf16[128,512]{1,0:T(8,128)(2,1)S(1)}, u32[]{:S(2)}, u32[]{:S(2)}) collective-permute-start(bf16[128,512]{1,0:T(8,128)(2,1)S(1)} %get-tuple-element.75), channel_id=1, source_target_pairs={{0,1},{1,0},{2,3},{3,2},{4,5},{5,4},{6,7},{7,6},{8,9},{9,8},{10,11... | collective-permute-start | bytes 393224 | tf_op jit(solution)/shard_map/ppermute | solution.py:33
  21.2 6.4 %collective-permute-start.6 = (bf16[128,512]{1,0:T(8,128)(2,1)S(1)}, bf16[128,512]{1,0:T(8,128)(2,1)S(1)}, u32[]{:S(2)}, u32[]{:S(2)}) collective-permute-start(bf16[128,512]{1,0:T(8,128)(2,1)S(1)} %get-tuple-element.76), channel_id=1, source_target_pairs={{0,2},{1,3},{2,0},{3,1},{4,6},{5,7},{6,4},{7,5},{8,10},{9,11},{10,... | collective-permute-start | bytes 393224 | tf_op jit(solution)/shard_map/ppermute | solution.py:33
  21.9 7.4 %collective-permute-start.7 = (bf16[128,512]{1,0:T(8,128)(2,1)S(1)}, bf16[128,512]{1,0:T(8,128)(2,1)S(1)}, u32[]{:S(2)}, u32[]{:S(2)}) collective-permute-start(bf16[128,512]{1,0:T(8,128)(2,1)S(1)} %get-tuple-element.77), channel_id=1, source_target_pairs={{0,3},{1,2},{2,1},{3,0},{4,7},{5,6},{6,5},{7,4},{8,11},{9,10},{10,... | collective-permute-start | bytes 393224 | tf_op jit(solution)/shard_map/ppermute | solution.py:33
  29.5 6.9 %collective-permute-start.12 = (bf16[64,512]{1,0:T(8,128)(2,1)S(1)}, bf16[64,512]{1,0:T(8,128)(2,1)S(1)}, u32[]{:S(2)}, u32[]{:S(2)}) collective-permute-start(bf16[64,512]{1,0:T(8,128)(2,1)S(1)} %get-tuple-element.82), channel_id=1, source_target_pairs={{0,12},{4,8},{8,4},{12,0},{1,13},{5,9},{9,5},{13,1},{2,14},{6,10},... | collective-permute-start | bytes 196616 | tf_op jit(solution)/shard_map/ppermute | solution.py:33
  33.2 6.7 %collective-permute-start.16 = (bf16[64,512]{1,0:T(8,128)(2,1)S(1)}, bf16[64,512]{1,0:T(8,128)(2,1)S(1)}, u32[]{:S(2)}, u32[]{:S(2)}) collective-permute-start(bf16[64,512]{1,0:T(8,128)(2,1)S(1)} %get-tuple-element.83), channel_id=1, source_target_pairs={{0,8},{4,12},{8,0},{12,4},{1,9},{5,13},{9,1},{13,5},{2,10},{6,14},... | collective-permute-start | bytes 196616 | tf_op jit(solution)/shard_map/ppermute | solution.py:33
  33.2 8.3 %collective-permute-start.8 = (bf16[64,512]{1,0:T(8,128)(2,1)S(1)}, bf16[64,512]{1,0:T(8,128)(2,1)S(1)}, u32[]{:S(2)}, u32[]{:S(2)}) collective-permute-start(bf16[64,512]{1,0:T(8,128)(2,1)S(1)} %get-tuple-element.80), channel_id=1, source_target_pairs={{0,4},{4,0},{8,12},{12,8},{1,5},{5,1},{9,13},{13,9},{2,6},{6,2},{1... | collective-permute-start | bytes 196616 | tf_op jit(solution)/shard_map/ppermute | solution.py:33
  36.4 5.8 %collective-permute-start.13 = (bf16[64,512]{1,0:T(8,128)(2,1)S(1)}, bf16[64,512]{1,0:T(8,128)(2,1)S(1)}, u32[]{:S(2)}, u32[]{:S(2)}) collective-permute-start(bf16[64,512]{1,0:T(8,128)(2,1)S(1)} %collective-permute-done.12.refs_0_), channel_id=1, source_target_pairs={{0,1},{1,0},{2,3},{3,2},{4,5},{5,4},{6,7},{7,6},{8,9},{9,8},{10,11... | collective-permute-start | bytes 196616 | tf_op jit(solution)/shard_map/ppermute | solution.py:33
  38.7 5.8 %collective-permute-start.15 = (bf16[64,512]{1,0:T(8,128)(2,1)S(1)}, bf16[64,512]{1,0:T(8,128)(2,1)S(1)}, u32[]{:S(2)}, u32[]{:S(2)}) collective-permute-start(bf16[64,512]{1,0:T(8,128)(2,1)S(1)} %collective-permute-done.12.refs_0_), channel_id=1, source_target_pairs={{0,3},{1,2},{2,1},{3,0},{4,7},{5,6},{6,5},{7,4},{8,11},{9,10},{10,... | collective-permute-start | bytes 196616 | tf_op jit(solution)/shard_map/ppermute | solution.py:33
  39.9 6.7 %collective-permute-start.17 = (bf16[64,512]{1,0:T(8,128)(2,1)S(1)}, bf16[64,512]{1,0:T(8,128)(2,1)S(1)}, u32[]{:S(2)}, u32[]{:S(2)}) collective-permute-start(bf16[64,512]{1,0:T(8,128)(2,1)S(1)} %collective-permute-done.16.refs_0_.refs_4_), channel_id=1, source_target_pairs={{0,1},{1,0},{2,3},{3,2},{4,5},{5,4},{6,7},{7,6},{8,9},{9,8},{10,11... | collective-permute-start | bytes 196616 | tf_op jit(solution)/shard_map/ppermute | solution.py:33
  41.5 7.4 %collective-permute-start.18 = (bf16[64,512]{1,0:T(8,128)(2,1)S(1)}, bf16[64,512]{1,0:T(8,128)(2,1)S(1)}, u32[]{:S(2)}, u32[]{:S(2)}) collective-permute-start(bf16[64,512]{1,0:T(8,128)(2,1)S(1)} %collective-permute-done.16.refs_0_.refs_4_), channel_id=1, source_target_pairs={{0,2},{1,3},{2,0},{3,1},{4,6},{5,7},{6,4},{7,5},{8,10},{9,11},{10,... | collective-permute-start | bytes 196616 | tf_op jit(solution)/shard_map/ppermute | solution.py:33
  42.2 6.7 %collective-permute-start.19 = (bf16[64,512]{1,0:T(8,128)(2,1)S(1)}, bf16[64,512]{1,0:T(8,128)(2,1)S(1)}, u32[]{:S(2)}, u32[]{:S(2)}) collective-permute-start(bf16[64,512]{1,0:T(8,128)(2,1)S(1)} %collective-permute-done.16.refs_0_.refs_4_), channel_id=1, source_target_pairs={{0,3},{1,2},{2,1},{3,0},{4,7},{5,6},{6,5},{7,4},{8,11},{9,10},{10,... | collective-permute-start | bytes 196616 | tf_op jit(solution)/shard_map/ppermute | solution.py:33
  43.5 12.8 %collective-permute-start.10 = (bf16[128,512]{1,0:T(8,128)(2,1)S(1)}, bf16[128,512]{1,0:T(8,128)(2,1)S(1)}, u32[]{:S(2)}, u32[]{:S(2)}) collective-permute-start(bf16[128,512]{1,0:T(8,128)(2,1)S(1)} %stack.1.refs_1_.refs_0_), channel_id=1, source_target_pairs={{0,2},{1,3},{2,0},{3,1},{4,6},{5,7},{6,4},{7,5},{8,10},{9,11},{10,... | collective-permute-start | bytes 393224 | tf_op jit(solution)/shard_map/ppermute | solution.py:33
  44.6 11.8 %collective-permute-start.11 = (bf16[128,512]{1,0:T(8,128)(2,1)S(1)}, bf16[128,512]{1,0:T(8,128)(2,1)S(1)}, u32[]{:S(2)}, u32[]{:S(2)}) collective-permute-start(bf16[128,512]{1,0:T(8,128)(2,1)S(1)} %stack.1.refs_1_.refs_0_), channel_id=1, source_target_pairs={{0,3},{1,2},{2,1},{3,0},{4,7},{5,6},{6,5},{7,4},{8,11},{9,10},{10,... | collective-permute-start | bytes 393224 | tf_op jit(solution)/shard_map/ppermute | solution.py:33
  46.6 9.8 %collective-permute-start.9 = (bf16[128,512]{1,0:T(8,128)(2,1)S(1)}, bf16[128,512]{1,0:T(8,128)(2,1)S(1)}, u32[]{:S(2)}, u32[]{:S(2)}) collective-permute-start(bf16[128,512]{1,0:T(8,128)(2,1)S(1)} %stack.1.refs_1_.refs_0_), channel_id=1, source_target_pairs={{0,1},{1,0},{2,3},{3,2},{4,5},{5,4},{6,7},{7,6},{8,9},{9,8},{10,11... | collective-permute-start | bytes 393224 | tf_op jit(solution)/shard_map/ppermute | solution.py:33
  56.6 7.1 %collective-permute-start.22 = (bf16[128,2048]{1,0:T(8,128)(2,1)S(1)}, bf16[128,2048]{1,0:T(8,128)(2,1)S(1)}, u32[]{:S(2)}, u32[]{:S(2)}) collective-permute-start(bf16[128,2048]{1,0:T(8,128)(2,1)S(1)} %norm.3.x_ref), channel_id=1, source_target_pairs={{0,16},{16,0},{1,17},{17,1},{2,18},{18,2},{3,19},{19,3},{4,20},{20... | collective-permute-start | bytes 1572872 | tf_op jit(solution)/shard_map/ppermute | solution.py:33
  58.0 10.4 %collective-permute-start.24 = (bf16[128,512]{1,0:T(8,128)(2,1)S(1)}, bf16[128,512]{1,0:T(8,128)(2,1)S(1)}, u32[]{:S(2)}, u32[]{:S(2)}) collective-permute-start(bf16[128,512]{1,0:T(8,128)(2,1)S(1)} %get-tuple-element.95), channel_id=1, source_target_pairs={{0,1},{1,0},{2,3},{3,2},{4,5},{5,4},{6,7},{7,6},{8,9},{9,8},{10,11... | collective-permute-start | bytes 393224 | tf_op jit(solution)/shard_map/ppermute | solution.py:33
  58.1 10.3 %collective-permute-start.25 = (bf16[128,512]{1,0:T(8,128)(2,1)S(1)}, bf16[128,512]{1,0:T(8,128)(2,1)S(1)}, u32[]{:S(2)}, u32[]{:S(2)}) collective-permute-start(bf16[128,512]{1,0:T(8,128)(2,1)S(1)} %get-tuple-element.96), channel_id=1, source_target_pairs={{0,2},{1,3},{2,0},{3,1},{4,6},{5,7},{6,4},{7,5},{8,10},{9,11},{10,... | collective-permute-start | bytes 393224 | tf_op jit(solution)/shard_map/ppermute | solution.py:33
  58.9 9.6 %collective-permute-start.26 = (bf16[128,512]{1,0:T(8,128)(2,1)S(1)}, bf16[128,512]{1,0:T(8,128)(2,1)S(1)}, u32[]{:S(2)}, u32[]{:S(2)}) collective-permute-start(bf16[128,512]{1,0:T(8,128)(2,1)S(1)} %get-tuple-element.97), channel_id=1, source_target_pairs={{0,3},{1,2},{2,1},{3,0},{4,7},{5,6},{6,5},{7,4},{8,11},{9,10},{10,... | collective-permute-start | bytes 393224 | tf_op jit(solution)/shard_map/ppermute | solution.py:33
  70.4 8.4 %collective-permute-start.27 = (bf16[128,512]{1,0:T(8,128)(2,1)S(1)}, bf16[128,512]{1,0:T(8,128)(2,1)S(1)}, u32[]{:S(2)}, u32[]{:S(2)}) collective-permute-start(bf16[128,512]{1,0:T(8,128)(2,1)S(1)} %get-tuple-element.100), channel_id=1, source_target_pairs={{0,1},{1,0},{2,3},{3,2},{4,5},{5,4},{6,7},{7,6},{8,9},{9,8},{10,11... | collective-permute-start | bytes 393224 | tf_op jit(solution)/shard_map/ppermute | solution.py:33
  70.6 8.2 %collective-permute-start.28 = (bf16[128,512]{1,0:T(8,128)(2,1)S(1)}, bf16[128,512]{1,0:T(8,128)(2,1)S(1)}, u32[]{:S(2)}, u32[]{:S(2)}) collective-permute-start(bf16[128,512]{1,0:T(8,128)(2,1)S(1)} %get-tuple-element.101), channel_id=1, source_target_pairs={{0,2},{1,3},{2,0},{3,1},{4,6},{5,7},{6,4},{7,5},{8,10},{9,11},{10,... | collective-permute-start | bytes 393224 | tf_op jit(solution)/shard_map/ppermute | solution.py:33
  71.3 7.7 %collective-permute-start.29 = (bf16[128,512]{1,0:T(8,128)(2,1)S(1)}, bf16[128,512]{1,0:T(8,128)(2,1)S(1)}, u32[]{:S(2)}, u32[]{:S(2)}) collective-permute-start(bf16[128,512]{1,0:T(8,128)(2,1)S(1)} %get-tuple-element.102), channel_id=1, source_target_pairs={{0,3},{1,2},{2,1},{3,0},{4,7},{5,6},{6,5},{7,4},{8,11},{9,10},{10,... | collective-permute-start | bytes 393224 | tf_op jit(solution)/shard_map/ppermute | solution.py:33
  74.0 8.4 %collective-permute-start.31 = (bf16[64,512]{1,0:T(8,128)(2,1)S(1)}, bf16[64,512]{1,0:T(8,128)(2,1)S(1)}, u32[]{:S(2)}, u32[]{:S(2)}) collective-permute-start(bf16[64,512]{1,0:T(8,128)(2,1)S(1)} %get-tuple-element.105), channel_id=1, source_target_pairs={{0,8},{4,12},{8,0},{12,4},{1,9},{5,13},{9,1},{13,5},{2,10},{6,14},... | collective-permute-start | bytes 196616 | tf_op jit(solution)/shard_map/ppermute | solution.py:33
  75.4 7.0 %collective-permute-start.32 = (bf16[64,512]{1,0:T(8,128)(2,1)S(1)}, bf16[64,512]{1,0:T(8,128)(2,1)S(1)}, u32[]{:S(2)}, u32[]{:S(2)}) collective-permute-start(bf16[64,512]{1,0:T(8,128)(2,1)S(1)} %get-tuple-element.98.refs_1_), channel_id=1, source_target_pairs={{0,12},{4,8},{8,4},{12,0},{1,13},{5,9},{9,5},{13,1},{2,14},{6,10},... | collective-permute-start | bytes 196616 | tf_op jit(solution)/shard_map/ppermute | solution.py:33
  (11 other events, 53.2 us)

commit v7 on v6

--- a/solution.py
+++ b/solution.py
@@ -34,8 +34,7 @@
 
 
 def swaps(blocks):
-    got = {k: swap(blocks[k - 1], "tp", k) for k in range(len(blocks), 0, -1)}
-    return [got[k] for k in sorted(got)]
+    return [swap(block, "tp", k) for k, block in enumerate(blocks, 1)]
 
 
 def sigmoid(x):
@@ -626,7 +625,7 @@
     expert_weight = stay(expert_weight)
     near = load(stay(local), stay(conv_weight), stay(conv_bias[None]), stay(proj_weight.T))
     xconv, part = conv(before, *near)
-    parts = [part] + swaps([part] * (tp - 1))
+    parts = [part] + [swap(part, "tp", k) for k in range(tp - 1, 0, -1)]
     silu, rates, skipped, bias, step_w, out_w, quarter, gain = prepare(
         tp, xconv, stay(gate_in[0]), stay(decay_log), stay(residual[0]), stay(skip_gain[None]),
         stay(step_bias[None]), stay(step_weight), stay(out_weight), stay(norm_gain[None]),
@@ -640,24 +639,24 @@
     half = experts // 2
     rows = [picked[0]] + [swap(picked[j], "exp", j) for j in range(1, experts)]
     piece_b = stack(rows[:half], [])
-    both = order([rows[half], piece_b])
-    first_a = rows[experts - 1]
-    second_a = rows[half] if half == 2 else stack(rows[half : experts - 1], [])
+    both = order([rows[experts - 1], piece_b])
+    first_a = rows[half]
+    second_a = rows[experts - 1] if half == 2 else stack(rows[half + 1 :], [])
     sets = [[piece] + swaps([piece] * (tp - 1)) for piece in (first_a, second_a, piece_b)]
     x_a = norm(sets[:2], gain, [both])
     own_a, low = hidden_units(x_a, gate_w, up_w, [], expert_weight, 0)
     other_a, high = hidden_units(swap(x_a, "ctx", 1), gate_w, up_w, [own_a, order([x_a])], expert_weight, 1)
     down_w = (low, high)
     sum_a, sent_a = down_sums(own_a, other_a, down_w, [])
-    joined_a = join(tp, sum_a, swap(sent_a, "ctx", 1), [])
+    sent_a = swap(sent_a, "ctx", 1)
+    x_b = norm(sets[2:], gain, [sum_a])
+    own_b, = hidden_units(x_b, gate_w, up_w, [])
+    joined_a = join(tp, sum_a, sent_a, [own_b])
     made_a = totals([joined_a[0]] + swaps(joined_a[1:]))
-    x_b = norm(sets[2:], gain, [sum_a])
-    own_b, = hidden_units(x_b, gate_w, up_w, [joined_a[0]])
-    other_b, = hidden_units(swap(x_b, "ctx", 1), gate_w, up_w, [own_b])
+    other_b, = hidden_units(swap(x_b, "ctx", 1), gate_w, up_w, [joined_a[0]])
     sum_b, sent_b = down_sums(own_b, other_b, down_w, [])
     joined_b = join(tp, sum_b, swap(sent_b, "ctx", 1), [order([sent_b, made_a[0]])])
     made_b = totals([joined_b[0]] + swaps(joined_b[1:]))
-    made_a = made_a[1:] + made_a[:1]
     back_a = [swap(piece, "exp", j) for j, piece in enumerate(made_a, half)]
     back_b = [made_b[0]] + [swap(made_b[j], "exp", j) for j in range(1, half)]
     gates = route_gates[0].T

time: 85.2 us -> 84.2 us (0.988)
  starting transfers between devices: 41.6 us -> 40.6 us
    ppermute x31, starting transfers between devices: 38 us -> 36.9 us  [swap(): lax.ppermute(block, axis, [(i, i ^ k) for i in range(lax.axis_size(axis))])]
  transfers between devices with their start and end apart: 33 -> 33, of which waited for: 12 -> 13; matrix products, arithmetic and copies ran while one was open for 0% -> 0% of each run, Pallas kernels for 25% -> 25%
where the time goes in v7:
time: 84.2 us; the launch traced here: 84 us
  starting transfers between devices  40.6 us (48%)
  Pallas kernels  28 us (33%)
  waiting for transfers between devices  15.1 us (18%)
    ppermute x31, starting transfers between devices, swap(): lax.ppermute(block, axis, [(i, i ^ k) for i in range(lax.axis_size(axis))])  36.9 us
    ppermute x31, waiting for transfers between devices, swap(): lax.ppermute(block, axis, [(i, i ^ k) for i in range(lax.axis_size(axis))])  14.1 us
    pallas_call x4, Pallas kernels, hidden_units(): pl.pallas_call(functools.partial(hidden_kernel, part), out_shape=made, in...  9.06 us
    pallas_call x2, Pallas kernels, down_sums(): pl.pallas_call(down_kernel, out_shape=(shaped((rows, model), F32), shaped...  4.18 us
    pallas_call x1, Pallas kernels, scan(): pl.pallas_call(functools.partial(scan_kernel, len(pieces)), out_shape=(sh...  3.61 us
    pallas_call x1, Pallas kernels, route(): pl.pallas_call(route_kernel, out_shape=(shaped((rows, slots), BF16), shap...  3.09 us
    pallas_call x1, Pallas kernels, prepare(): pl.pallas_call(prepare_kernel, out_shape=(shaped((rows, channels), F32),...  2.76 us
    ppermute x1, starting transfers between devices, body(): before = lax.ppermute(local, 'ctx', [(0, 1)])  2.36 us
  transfers between devices with their start and end apart: 33, of which 13 were waited for; matrix products, arithmetic and copies ran while one was open for 0% of the time, Pallas kernels for 25%

profile of v7, /device:TPU:0, one launch (start us, length us, event | category | flops | bytes accessed | tf_op | source)
XLA Modules:
  0.0 84.0 jit_solution(10927739565798343837)
XLA Ops:
  0.0 2.4 %collective-permute-start = (bf16[128,1024]{1,0:T(8,128)(2,1)}, bf16[128,1024]{1,0:T(8,128)(2,1)S(1)}, u32[]{:S(2)}, u32[]{:S(2)}) collective-permute-start(bf16[128,1024]{1,0:T(8,128)(2,1)} %bitcast.21), channel_id=1, source_target_pairs={{0,16},{1,17},{2,18},{3,19},{4,20},{5,21},{6,22},{7,23},{8,24},{9,... | collective-permute-start | bytes 786440 | tf_op jit(solution)/shard_map/ppermute | solution.py:624
  4.3 2.4 %collective-permute-start.3 = (bf16[144,256]{1,0:T(8,128)(2,1)S(1)}, bf16[144,256]{1,0:T(8,128)(2,1)S(1)}, u32[]{:S(2)}, u32[]{:S(2)}) collective-permute-start(bf16[144,256]{1,0:T(8,128)(2,1)S(1)} %get-tuple-element.61.refs_0_), channel_id=1, source_target_pairs={{0,1},{1,0},{2,3},{3,2},{4,5},{5,4},{6,7},{7,6},{8,9},{9,8},{10,11... | collective-permute-start | bytes 221192 | tf_op jit(solution)/shard_map/ppermute | solution.py:33
  6.7 1.5 %collective-permute-start.2 = (bf16[144,256]{1,0:T(8,128)(2,1)S(1)}, bf16[144,256]{1,0:T(8,128)(2,1)S(1)}, u32[]{:S(2)}, u32[]{:S(2)}) collective-permute-start(bf16[144,256]{1,0:T(8,128)(2,1)S(1)} %get-tuple-element.61.refs_0_), channel_id=1, source_target_pairs={{0,2},{1,3},{2,0},{3,1},{4,6},{5,7},{6,4},{7,5},{8,10},{9,11},{10,... | collective-permute-start | bytes 221192 | tf_op jit(solution)/shard_map/ppermute | solution.py:33
  8.2 2.8 %prepare.1 = (f32[128,1024]{1,0:T(8,128)S(1)}, f32[16,8,128]{2,1,0:T(8,128)S(1)}, f32[128,1024]{1,0:T(8,128)S(1)}, f32[1,1024]{1,0:T(1,128)S(1)}, bf16[256,1024]...) custom-call(bf16[128,1024]{1,0:T(8,128)(2,1)S(1)} %get-tuple-element.62.xconv_, ...), custom_call_target="tpu_custom_call" | custom-call | flops 1000000 | bytes 6000000 | tf_op jit(solution)/shard_map/prepare/pallas_call | solution.py:240
  11.0 2.4 %collective-permute-done.1.refs_1_ = bf16[144,256]{1,0:T(8,128)(2,1)S(1)} collective-permute-done((bf16[144,256]{1,0:T(8,128)(2,1)S(1)}, bf16[144,256]{1,0:T(8,128)(2,1)S(1)}, u32[]{:S(2)}, u32[]{:S(2)}) %collective-permute-start.1) | collective-permute-done | bytes 73760 | tf_op jit(solution)/shard_map/ppermute | solution.py:33
  13.5 3.6 %scan.1 = (f32[128,8,128]{2,1,0:T(8,128)S(1)}, f32[128,8,128]{2,1,0:T(8,128)S(1)}, f32[128,16,128]{2,1,0:T(8,128)S(1)}, f32[16,8,128]{2,1,0:T(8,128)S(1)}, bf16[2048,1792]{1,0:T(8,128)(2,1)S(1)}) custom-call(bf16[144,256]{1,0:T(8,128)(2,1)S(1)} %get-tuple-element.61.refs_0_, bf16[144,256]{1,0:T(8,128)(2,1)S(1)} %collective-permute-done.1.refs_1_, ...), custom_call_target="tpu_custom_call" | custom-call | flops 1000000 | bytes 14000000 | tf_op jit(solution)/shard_map/scan/pallas_call | solution.py:318
  21.9 2.2 %collective-permute-start.7 = (bf16[128,512]{1,0:T(8,128)(2,1)S(1)}, bf16[128,512]{1,0:T(8,128)(2,1)S(1)}, u32[]{:S(2)}, u32[]{:S(2)}) collective-permute-start(bf16[128,512]{1,0:T(8,128)(2,1)S(1)} %get-tuple-element.77), channel_id=1, source_target_pairs={{0,3},{1,2},{2,1},{3,0},{4,7},{5,6},{6,5},{7,4},{8,11},{9,10},{10,... | collective-permute-start | bytes 393224 | tf_op jit(solution)/shard_map/ppermute | solution.py:33
  24.1 3.1 %route.1 = (bf16[128,256]{1,0:T(8,128)(2,1)S(1)}, bf16[128,256]{1,0:T(8,128)(2,1)S(1)}, bf16[256,128]{1,0:T(8,128)(2,1)S(1)}, bf16[2048,1792]{1,0:T(8,128)(2,1)S(1)}) custom-call(s32[2,128]{1,0:T(2,128)S(1)} %bitcast.17, bf16[1,3,2048,1792]{3,2,1,0:T(8,128)(2,1)} %refs_0_.3), custom_call_target="tpu_custom_call" | custom-call | flops 1000000 | bytes 8000000 | tf_op jit(solution)/shard_map/route/pallas_call | solution.py:123
  27.5 1.7 %collective-permute-done.7.refs_3_ = bf16[128,512]{1,0:T(8,128)(2,1)S(1)} collective-permute-done((bf16[128,512]{1,0:T(8,128)(2,1)S(1)}, bf16[128,512]{1,0:T(8,128)(2,1)S(1)}, u32[]{:S(2)}, u32[]{:S(2)}) %collective-permute-start.7) | collective-permute-done | bytes 131104 | tf_op jit(solution)/shard_map/ppermute | solution.py:33
  29.5 2.7 %collective-permute-start.12 = (bf16[64,512]{1,0:T(8,128)(2,1)S(1)}, bf16[64,512]{1,0:T(8,128)(2,1)S(1)}, u32[]{:S(2)}, u32[]{:S(2)}) collective-permute-start(bf16[64,512]{1,0:T(8,128)(2,1)S(1)} %get-tuple-element.82), channel_id=1, source_target_pairs={{0,8},{4,12},{8,0},{12,4},{1,9},{5,13},{9,1},{13,5},{2,10},{6,14},... | collective-permute-start | bytes 196616 | tf_op jit(solution)/shard_map/ppermute | solution.py:33
  33.7 3.2 %collective-permute-done.12.refs_0_ = bf16[64,512]{1,0:T(8,128)(2,1)S(1)} collective-permute-done((bf16[64,512]{1,0:T(8,128)(2,1)S(1)}, bf16[64,512]{1,0:T(8,128)(2,1)S(1)}, u32[]{:S(2)}, u32[]{:S(2)}) %collective-permute-start.12) | collective-permute-done | bytes 65568 | tf_op jit(solution)/shard_map/ppermute | solution.py:33
  36.9 1.7 %collective-permute-start.15 = (bf16[64,512]{1,0:T(8,128)(2,1)S(1)}, bf16[64,512]{1,0:T(8,128)(2,1)S(1)}, u32[]{:S(2)}, u32[]{:S(2)}) collective-permute-start(bf16[64,512]{1,0:T(8,128)(2,1)S(1)} %collective-permute-done.12.refs_0_), channel_id=1, source_target_pairs={{0,3},{1,2},{2,1},{3,0},{4,7},{5,6},{6,5},{7,4},{8,11},{9,10},{10,... | collective-permute-start | bytes 196616 | tf_op jit(solution)/shard_map/ppermute | solution.py:33
  40.4 1.7 %collective-permute-start.19 = (bf16[64,512]{1,0:T(8,128)(2,1)S(1)}, bf16[64,512]{1,0:T(8,128)(2,1)S(1)}, u32[]{:S(2)}, u32[]{:S(2)}) collective-permute-start(bf16[64,512]{1,0:T(8,128)(2,1)S(1)} %collective-permute-done.16.refs_0_.refs_4_), channel_id=1, source_target_pairs={{0,3},{1,2},{2,1},{3,0},{4,7},{5,6},{6,5},{7,4},{8,11},{9,10},{10,... | collective-permute-start | bytes 196616 | tf_op jit(solution)/shard_map/ppermute | solution.py:33
  49.1 2.2 %hidden.4 = (bf16[128,1792]{1,0:T(8,128)(2,1)S(1)}, bf16[1024,1792]{1,0:T(8,128)(2,1)S(1)}) custom-call(bf16[128,2048]{1,0:T(8,128)(2,1)S(1)} %norm.2.x_ref.refs_0_, bf16[2048,1792]{1,0:T(8,128)(2,1)S(1)} %get-tuple-element.84.gate_ref, bf16[2048,1792]{1,0:T(8,128)(2,1)S(1)} %get-tuple-element.85.up_ref, bf16[1,3,2048,1792]{3,2,1,0:T(8,128)(2,1)} %refs_0_.3), custom_call_target="tpu_custom_call" | custom-call | flops 1000000 | tf_op jit(solution)/shard_map/hidden/pallas_call | solution.py:486
  51.3 2.2 %hidden.5 = (bf16[128,1792]{1,0:T(8,128)(2,1)S(1)}, bf16[1024,1792]{1,0:T(8,128)(2,1)S(1)}) custom-call(bf16[128,2048]{1,0:T(8,128)(2,1)S(1)} %collective-permute-done.20.x_ref, bf16[2048,1792]{1,0:T(8,128)(2,1)S(1)} %get-tuple-element.84.gate_ref, bf16[2048,1792]{1,0:T(8,128)(2,1)S(1)} %get-tuple-element.85.up_ref, bf16[1,3,2048,1792]{3,2,1,0:T(8,128)(2,1)} %refs_0_.3, ...), custom_call_target="tpu_custom_call" | custom-call | flops 1000000 | tf_op jit(solution)/shard_map/hidden/pallas_call | solution.py:486
  53.5 2.1 %down.2 = (f32[128,2048]{1,0:T(8,128)S(1)}, bf16[128,2048]{1,0:T(8,128)(2,1)S(1)}) custom-call(bf16[128,1792]{1,0:T(8,128)(2,1)S(1)} %get-tuple-element.86.refs_1_.hidden_own_ref, bf16[128,1792]{1,0:T(8,128)(2,1)S(1)} %get-tuple-element.87.hidden_other_ref, bf16[1024,1792]{1,0:T(8,128)(2,1)S(1)} %get-tuple-element.88.low_ref, ...), custom_call_target="tpu_custom_call" | custom-call | flops 1000000 | tf_op jit(solution)/shard_map/down/pallas_call | solution.py:521
  56.5 2.2 %hidden.6.refs_0_.hidden_own_ref = bf16[128,1792]{1,0:T(8,128)(2,1)S(1)} custom-call(bf16[128,2048]{1,0:T(8,128)(2,1)S(1)} %norm.3.x_ref, bf16[2048,1792]{1,0:T(8,128)(2,1)S(1)} %get-tuple-element.84.gate_ref, bf16[2048,1792]{1,0:T(8,128)(2,1)S(1)} %get-tuple-element.85.up_ref), custom_call_target="tpu_custom_call" | custom-call | flops 1000000 | tf_op jit(solution)/shard_map/hidden/pallas_call | solution.py:486
  60.8 1.6 %collective-permute-start.26 = (bf16[128,512]{1,0:T(8,128)(2,1)S(1)}, bf16[128,512]{1,0:T(8,128)(2,1)S(1)}, u32[]{:S(2)}, u32[]{:S(2)}) collective-permute-start(bf16[128,512]{1,0:T(8,128)(2,1)S(1)} %get-tuple-element.97), channel_id=1, source_target_pairs={{0,3},{1,2},{2,1},{3,0},{4,7},{5,6},{6,5},{7,4},{8,11},{9,10},{10,... | collective-permute-start | bytes 393224 | tf_op jit(solution)/shard_map/ppermute | solution.py:33
  62.4 2.4 %hidden.7.hidden_other_ref = bf16[128,1792]{1,0:T(8,128)(2,1)S(1)} custom-call(bf16[128,2048]{1,0:T(8,128)(2,1)S(1)} %collective-permute-done.21.x_ref, bf16[2048,1792]{1,0:T(8,128)(2,1)S(1)} %get-tuple-element.84.gate_ref, bf16[2048,1792]{1,0:T(8,128)(2,1)S(1)} %get-tuple-element.85.up_ref, f32[128,512]{1,0:T(8,128)S(1)} %get-tuple-element.92.refs_0_), custom_call_target="tpu_custom_call" | custom-call | flops 1000000 | tf_op jit(solution)/shard_map/hidden/pallas_call | solution.py:486
  64.9 2.1 %down.3 = (f32[128,2048]{1,0:T(8,128)S(1)}, bf16[128,2048]{1,0:T(8,128)(2,1)S(1)}) custom-call(bf16[128,1792]{1,0:T(8,128)(2,1)S(1)} %hidden.6.refs_0_.hidden_own_ref, bf16[128,1792]{1,0:T(8,128)(2,1)S(1)} %hidden.7.hidden_other_ref, bf16[1024,1792]{1,0:T(8,128)(2,1)S(1)} %get-tuple-element.88.low_ref, bf16[1024,1792]{1,0:T(8,128)(2,1)S(1)} %get-tuple-element.89.high_ref), custom_call_target="tpu_custom_call" | custom-call | flops 1000000 | tf_op jit(solution)/shard_map/down/pallas_call | solution.py:521
  71.0 1.6 %collective-permute-start.29 = (bf16[128,512]{1,0:T(8,128)(2,1)S(1)}, bf16[128,512]{1,0:T(8,128)(2,1)S(1)}, u32[]{:S(2)}, u32[]{:S(2)}) collective-permute-start(bf16[128,512]{1,0:T(8,128)(2,1)S(1)} %get-tuple-element.102), channel_id=1, source_target_pairs={{0,3},{1,2},{2,1},{3,0},{4,7},{5,6},{6,5},{7,4},{8,11},{9,10},{10,... | collective-permute-start | bytes 393224 | tf_op jit(solution)/shard_map/ppermute | solution.py:33
  72.6 4.6 %collective-permute-start.32 = (bf16[64,512]{1,0:T(8,128)(2,1)S(1)}, bf16[64,512]{1,0:T(8,128)(2,1)S(1)}, u32[]{:S(2)}, u32[]{:S(2)}) collective-permute-start(bf16[64,512]{1,0:T(8,128)(2,1)S(1)} %get-tuple-element.105), channel_id=1, source_target_pairs={{0,12},{4,8},{8,4},{12,0},{1,13},{5,9},{9,5},{13,1},{2,14},{6,10},... | collective-permute-start | bytes 196616 | tf_op jit(solution)/shard_map/ppermute | solution.py:33
  78.2 2.0 %collective-permute-start.30 = (bf16[64,512]{1,0:T(8,128)(2,1)S(1)}, bf16[64,512]{1,0:T(8,128)(2,1)S(1)}, u32[]{:S(2)}, u32[]{:S(2)}) collective-permute-start(bf16[64,512]{1,0:T(8,128)(2,1)S(1)} %get-tuple-element.104), channel_id=1, source_target_pairs={{0,4},{4,0},{8,12},{12,8},{1,5},{5,1},{9,13},{13,9},{2,6},{6,2},{1... | collective-permute-start | bytes 196616 | tf_op jit(solution)/shard_map/ppermute | solution.py:33
  80.2 2.2 %collective-permute-done.31.refs_0_ = bf16[64,512]{1,0:T(8,128)(2,1)S(1)} collective-permute-done((bf16[64,512]{1,0:T(8,128)(2,1)S(1)}, bf16[64,512]{1,0:T(8,128)(2,1)S(1)}, u32[]{:S(2)}, u32[]{:S(2)}) %collective-permute-start.31) | collective-permute-done | bytes 65568 | tf_op jit(solution)/shard_map/ppermute | solution.py:33
  (71 shorter events, 27.2 us)
Async XLA Ops:
  4.3 6.7 %collective-permute-start.3 = (bf16[144,256]{1,0:T(8,128)(2,1)S(1)}, bf16[144,256]{1,0:T(8,128)(2,1)S(1)}, u32[]{:S(2)}, u32[]{:S(2)}) collective-permute-start(bf16[144,256]{1,0:T(8,128)(2,1)S(1)} %get-tuple-element.61.refs_0_), channel_id=1, source_target_pairs={{0,1},{1,0},{2,3},{3,2},{4,5},{5,4},{6,7},{7,6},{8,9},{9,8},{10,11... | collective-permute-start | bytes 221192 | tf_op jit(solution)/shard_map/ppermute | solution.py:33
  8.2 5.3 %collective-permute-start.1 = (bf16[144,256]{1,0:T(8,128)(2,1)S(1)}, bf16[144,256]{1,0:T(8,128)(2,1)S(1)}, u32[]{:S(2)}, u32[]{:S(2)}) collective-permute-start(bf16[144,256]{1,0:T(8,128)(2,1)S(1)} %get-tuple-element.61.refs_0_), channel_id=1, source_target_pairs={{0,3},{1,2},{2,1},{3,0},{4,7},{5,6},{6,5},{7,4},{8,11},{9,10},{10,... | collective-permute-start | bytes 221192 | tf_op jit(solution)/shard_map/ppermute | solution.py:33
  20.5 6.7 %collective-permute-start.5 = (bf16[128,512]{1,0:T(8,128)(2,1)S(1)}, bf16[128,512]{1,0:T(8,128)(2,1)S(1)}, u32[]{:S(2)}, u32[]{:S(2)}) collective-permute-start(bf16[128,512]{1,0:T(8,128)(2,1)S(1)} %get-tuple-element.75), channel_id=1, source_target_pairs={{0,1},{1,0},{2,3},{3,2},{4,5},{5,4},{6,7},{7,6},{8,9},{9,8},{10,11... | collective-permute-start | bytes 393224 | tf_op jit(solution)/shard_map/ppermute | solution.py:33
  21.2 6.4 %collective-permute-start.6 = (bf16[128,512]{1,0:T(8,128)(2,1)S(1)}, bf16[128,512]{1,0:T(8,128)(2,1)S(1)}, u32[]{:S(2)}, u32[]{:S(2)}) collective-permute-start(bf16[128,512]{1,0:T(8,128)(2,1)S(1)} %get-tuple-element.76), channel_id=1, source_target_pairs={{0,2},{1,3},{2,0},{3,1},{4,6},{5,7},{6,4},{7,5},{8,10},{9,11},{10,... | collective-permute-start | bytes 393224 | tf_op jit(solution)/shard_map/ppermute | solution.py:33
  21.9 7.4 %collective-permute-start.7 = (bf16[128,512]{1,0:T(8,128)(2,1)S(1)}, bf16[128,512]{1,0:T(8,128)(2,1)S(1)}, u32[]{:S(2)}, u32[]{:S(2)}) collective-permute-start(bf16[128,512]{1,0:T(8,128)(2,1)S(1)} %get-tuple-element.77), channel_id=1, source_target_pairs={{0,3},{1,2},{2,1},{3,0},{4,7},{5,6},{6,5},{7,4},{8,11},{9,10},{10,... | collective-permute-start | bytes 393224 | tf_op jit(solution)/shard_map/ppermute | solution.py:33
  29.5 7.4 %collective-permute-start.12 = (bf16[64,512]{1,0:T(8,128)(2,1)S(1)}, bf16[64,512]{1,0:T(8,128)(2,1)S(1)}, u32[]{:S(2)}, u32[]{:S(2)}) collective-permute-start(bf16[64,512]{1,0:T(8,128)(2,1)S(1)} %get-tuple-element.82), channel_id=1, source_target_pairs={{0,8},{4,12},{8,0},{12,4},{1,9},{5,13},{9,1},{13,5},{2,10},{6,14},... | collective-permute-start | bytes 196616 | tf_op jit(solution)/shard_map/ppermute | solution.py:33
  32.2 8.2 %collective-permute-start.16 = (bf16[64,512]{1,0:T(8,128)(2,1)S(1)}, bf16[64,512]{1,0:T(8,128)(2,1)S(1)}, u32[]{:S(2)}, u32[]{:S(2)}) collective-permute-start(bf16[64,512]{1,0:T(8,128)(2,1)S(1)} %get-tuple-element.83), channel_id=1, source_target_pairs={{0,12},{4,8},{8,4},{12,0},{1,13},{5,9},{9,5},{13,1},{2,14},{6,10},... | collective-permute-start | bytes 196616 | tf_op jit(solution)/shard_map/ppermute | solution.py:33
  33.5 8.6 %collective-permute-start.8 = (bf16[64,512]{1,0:T(8,128)(2,1)S(1)}, bf16[64,512]{1,0:T(8,128)(2,1)S(1)}, u32[]{:S(2)}, u32[]{:S(2)}) collective-permute-start(bf16[64,512]{1,0:T(8,128)(2,1)S(1)} %get-tuple-element.80), channel_id=1, source_target_pairs={{0,4},{4,0},{8,12},{12,8},{1,5},{5,1},{9,13},{13,9},{2,6},{6,2},{1... | collective-permute-start | bytes 196616 | tf_op jit(solution)/shard_map/ppermute | solution.py:33
  36.9 6.6 %collective-permute-start.15 = (bf16[64,512]{1,0:T(8,128)(2,1)S(1)}, bf16[64,512]{1,0:T(8,128)(2,1)S(1)}, u32[]{:S(2)}, u32[]{:S(2)}) collective-permute-start(bf16[64,512]{1,0:T(8,128)(2,1)S(1)} %collective-permute-done.12.refs_0_), channel_id=1, source_target_pairs={{0,3},{1,2},{2,1},{3,0},{4,7},{5,6},{6,5},{7,4},{8,11},{9,10},{10,... | collective-permute-start | bytes 196616 | tf_op jit(solution)/shard_map/ppermute | solution.py:33
  38.6 6.0 %collective-permute-start.14 = (bf16[64,512]{1,0:T(8,128)(2,1)S(1)}, bf16[64,512]{1,0:T(8,128)(2,1)S(1)}, u32[]{:S(2)}, u32[]{:S(2)}) collective-permute-start(bf16[64,512]{1,0:T(8,128)(2,1)S(1)} %collective-permute-done.12.refs_0_), channel_id=1, source_target_pairs={{0,2},{1,3},{2,0},{3,1},{4,6},{5,7},{6,4},{7,5},{8,10},{9,11},{10,... | collective-permute-start | bytes 196616 | tf_op jit(solution)/shard_map/ppermute | solution.py:33
  40.0 5.7 %collective-permute-start.13 = (bf16[64,512]{1,0:T(8,128)(2,1)S(1)}, bf16[64,512]{1,0:T(8,128)(2,1)S(1)}, u32[]{:S(2)}, u32[]{:S(2)}) collective-permute-start(bf16[64,512]{1,0:T(8,128)(2,1)S(1)} %collective-permute-done.12.refs_0_), channel_id=1, source_target_pairs={{0,1},{1,0},{2,3},{3,2},{4,5},{5,4},{6,7},{7,6},{8,9},{9,8},{10,11... | collective-permute-start | bytes 196616 | tf_op jit(solution)/shard_map/ppermute | solution.py:33
  40.4 6.7 %collective-permute-start.19 = (bf16[64,512]{1,0:T(8,128)(2,1)S(1)}, bf16[64,512]{1,0:T(8,128)(2,1)S(1)}, u32[]{:S(2)}, u32[]{:S(2)}) collective-permute-start(bf16[64,512]{1,0:T(8,128)(2,1)S(1)} %collective-permute-done.16.refs_0_.refs_4_), channel_id=1, source_target_pairs={{0,3},{1,2},{2,1},{3,0},{4,7},{5,6},{6,5},{7,4},{8,11},{9,10},{10,... | collective-permute-start | bytes 196616 | tf_op jit(solution)/shard_map/ppermute | solution.py:33
  42.1 6.6 %collective-permute-start.18 = (bf16[64,512]{1,0:T(8,128)(2,1)S(1)}, bf16[64,512]{1,0:T(8,128)(2,1)S(1)}, u32[]{:S(2)}, u32[]{:S(2)}) collective-permute-start(bf16[64,512]{1,0:T(8,128)(2,1)S(1)} %collective-permute-done.16.refs_0_.refs_4_), channel_id=1, source_target_pairs={{0,2},{1,3},{2,0},{3,1},{4,6},{5,7},{6,4},{7,5},{8,10},{9,11},{10,... | collective-permute-start | bytes 196616 | tf_op jit(solution)/shard_map/ppermute | solution.py:33
  44.6 11.6 %collective-permute-start.11 = (bf16[128,512]{1,0:T(8,128)(2,1)S(1)}, bf16[128,512]{1,0:T(8,128)(2,1)S(1)}, u32[]{:S(2)}, u32[]{:S(2)}) collective-permute-start(bf16[128,512]{1,0:T(8,128)(2,1)S(1)} %stack.1.refs_1_.refs_0_), channel_id=1, source_target_pairs={{0,3},{1,2},{2,1},{3,0},{4,7},{5,6},{6,5},{7,4},{8,11},{9,10},{10,... | collective-permute-start | bytes 393224 | tf_op jit(solution)/shard_map/ppermute | solution.py:33
  45.7 10.5 %collective-permute-start.10 = (bf16[128,512]{1,0:T(8,128)(2,1)S(1)}, bf16[128,512]{1,0:T(8,128)(2,1)S(1)}, u32[]{:S(2)}, u32[]{:S(2)}) collective-permute-start(bf16[128,512]{1,0:T(8,128)(2,1)S(1)} %stack.1.refs_1_.refs_0_), channel_id=1, source_target_pairs={{0,2},{1,3},{2,0},{3,1},{4,6},{5,7},{6,4},{7,5},{8,10},{9,11},{10,... | collective-permute-start | bytes 393224 | tf_op jit(solution)/shard_map/ppermute | solution.py:33
  47.1 9.1 %collective-permute-start.9 = (bf16[128,512]{1,0:T(8,128)(2,1)S(1)}, bf16[128,512]{1,0:T(8,128)(2,1)S(1)}, u32[]{:S(2)}, u32[]{:S(2)}) collective-permute-start(bf16[128,512]{1,0:T(8,128)(2,1)S(1)} %stack.1.refs_1_.refs_0_), channel_id=1, source_target_pairs={{0,1},{1,0},{2,3},{3,2},{4,5},{5,4},{6,7},{7,6},{8,9},{9,8},{10,11... | collective-permute-start | bytes 393224 | tf_op jit(solution)/shard_map/ppermute | solution.py:33
  56.4 6.0 %collective-permute-start.21 = (bf16[128,2048]{1,0:T(8,128)(2,1)S(1)}, bf16[128,2048]{1,0:T(8,128)(2,1)S(1)}, u32[]{:S(2)}, u32[]{:S(2)}) collective-permute-start(bf16[128,2048]{1,0:T(8,128)(2,1)S(1)} %norm.3.x_ref), channel_id=1, source_target_pairs={{0,16},{16,0},{1,17},{17,1},{2,18},{18,2},{3,19},{19,3},{4,20},{20... | collective-permute-start | bytes 1572872 | tf_op jit(solution)/shard_map/ppermute | solution.py:33
  58.9 8.2 %collective-permute-start.24 = (bf16[128,512]{1,0:T(8,128)(2,1)S(1)}, bf16[128,512]{1,0:T(8,128)(2,1)S(1)}, u32[]{:S(2)}, u32[]{:S(2)}) collective-permute-start(bf16[128,512]{1,0:T(8,128)(2,1)S(1)} %get-tuple-element.95), channel_id=1, source_target_pairs={{0,1},{1,0},{2,3},{3,2},{4,5},{5,4},{6,7},{7,6},{8,9},{9,8},{10,11... | collective-permute-start | bytes 393224 | tf_op jit(solution)/shard_map/ppermute | solution.py:33
  59.9 7.2 %collective-permute-start.25 = (bf16[128,512]{1,0:T(8,128)(2,1)S(1)}, bf16[128,512]{1,0:T(8,128)(2,1)S(1)}, u32[]{:S(2)}, u32[]{:S(2)}) collective-permute-start(bf16[128,512]{1,0:T(8,128)(2,1)S(1)} %get-tuple-element.96), channel_id=1, source_target_pairs={{0,2},{1,3},{2,0},{3,1},{4,6},{5,7},{6,4},{7,5},{8,10},{9,11},{10,... | collective-permute-start | bytes 393224 | tf_op jit(solution)/shard_map/ppermute | solution.py:33
  60.8 7.5 %collective-permute-start.26 = (bf16[128,512]{1,0:T(8,128)(2,1)S(1)}, bf16[128,512]{1,0:T(8,128)(2,1)S(1)}, u32[]{:S(2)}, u32[]{:S(2)}) collective-permute-start(bf16[128,512]{1,0:T(8,128)(2,1)S(1)} %get-tuple-element.97), channel_id=1, source_target_pairs={{0,3},{1,2},{2,1},{3,0},{4,7},{5,6},{6,5},{7,4},{8,11},{9,10},{10,... | collective-permute-start | bytes 393224 | tf_op jit(solution)/shard_map/ppermute | solution.py:33
  69.0 8.1 %collective-permute-start.27 = (bf16[128,512]{1,0:T(8,128)(2,1)S(1)}, bf16[128,512]{1,0:T(8,128)(2,1)S(1)}, u32[]{:S(2)}, u32[]{:S(2)}) collective-permute-start(bf16[128,512]{1,0:T(8,128)(2,1)S(1)} %get-tuple-element.100), channel_id=1, source_target_pairs={{0,1},{1,0},{2,3},{3,2},{4,5},{5,4},{6,7},{7,6},{8,9},{9,8},{10,11... | collective-permute-start | bytes 393224 | tf_op jit(solution)/shard_map/ppermute | solution.py:33
  70.1 7.1 %collective-permute-start.28 = (bf16[128,512]{1,0:T(8,128)(2,1)S(1)}, bf16[128,512]{1,0:T(8,128)(2,1)S(1)}, u32[]{:S(2)}, u32[]{:S(2)}) collective-permute-start(bf16[128,512]{1,0:T(8,128)(2,1)S(1)} %get-tuple-element.101), channel_id=1, source_target_pairs={{0,2},{1,3},{2,0},{3,1},{4,6},{5,7},{6,4},{7,5},{8,10},{9,11},{10,... | collective-permute-start | bytes 393224 | tf_op jit(solution)/shard_map/ppermute | solution.py:33
  71.0 7.1 %collective-permute-start.29 = (bf16[128,512]{1,0:T(8,128)(2,1)S(1)}, bf16[128,512]{1,0:T(8,128)(2,1)S(1)}, u32[]{:S(2)}, u32[]{:S(2)}) collective-permute-start(bf16[128,512]{1,0:T(8,128)(2,1)S(1)} %get-tuple-element.102), channel_id=1, source_target_pairs={{0,3},{1,2},{2,1},{3,0},{4,7},{5,6},{6,5},{7,4},{8,11},{9,10},{10,... | collective-permute-start | bytes 393224 | tf_op jit(solution)/shard_map/ppermute | solution.py:33
  72.6 7.6 %collective-permute-start.32 = (bf16[64,512]{1,0:T(8,128)(2,1)S(1)}, bf16[64,512]{1,0:T(8,128)(2,1)S(1)}, u32[]{:S(2)}, u32[]{:S(2)}) collective-permute-start(bf16[64,512]{1,0:T(8,128)(2,1)S(1)} %get-tuple-element.105), channel_id=1, source_target_pairs={{0,12},{4,8},{8,4},{12,0},{1,13},{5,9},{9,5},{13,1},{2,14},{6,10},... | collective-permute-start | bytes 196616 | tf_op jit(solution)/shard_map/ppermute | solution.py:33
  (11 other events, 54.0 us)

commit v8 on v7

--- a/solution.py
+++ b/solution.py
@@ -338,11 +338,35 @@
     )(*pieces, xconv, rates, bias, weight, experts)
 
 
+def project(total_ref, skipped_ref, silu_ref, quarter_ref, weight_ref, own_ref, sent, gated_ref):
+    for j in range(total_ref.shape[1]):
+        cut = slice(j * 128, (j + 1) * 128)
+        total = total_ref[:, j, :] + skipped_ref[:, cut]
+        gated_ref[:, cut] = (total * silu_ref[:, cut]).astype(BF16)
+    own = lax.axis_index("tp")
+    width = own_ref.shape[1]
+    for k in range(len(sent) + 1):
+        start = pl.multiple_of(jnp.bitwise_xor(own, k) * width, 128)
+        product = jnp.dot(
+            gated_ref[...], weight_ref[:, pl.ds(start, width)], preferred_element_type=F32
+        )
+        if k == 0:
+            own_ref[...] = product + quarter_ref[...]
+        else:
+            sent[k - 1][...] = product.astype(BF16)
+
+
+def mix_first_kernel(parts, y_ref, skipped_ref, silu_ref, quarter_ref, weight_ref, *refs):
+    @pl.when(lax.axis_index("ctx") == 0)
+    def _():
+        project(y_ref, skipped_ref, silu_ref, quarter_ref, weight_ref, refs[0], refs[1:parts], refs[parts])
+
+
 def mix_kernel(parts, *refs):
     seen_ref, y_ref, elapsed_ref, rates_ref, state_ref, skipped_ref, silu_ref, quarter_ref, weight_ref = refs[:9]
-    own_ref, sent = refs[9], refs[10 : 9 + parts]
-    sum_ref, gated_ref = refs[9 + parts :]
-    rows, tiles, _ = y_ref.shape
+    own_ref, sent = refs[9 + parts], refs[10 + parts : 9 + 2 * parts]
+    sum_ref, gated_ref = refs[9 + 2 * parts :]
+    rows = y_ref.shape[0]
 
     def step(t, carry):
         elapsed = elapsed_ref[t]
@@ -353,42 +377,32 @@
         sum_ref[t] = sums[0] + sums[1]
         return carry
 
-    first = lax.axis_index("ctx") == 0
-
-    @pl.when(first)
-    def _():
-        sum_ref[...] = y_ref[...]
-
-    @pl.when(jnp.logical_not(first))
+    @pl.when(lax.axis_index("ctx") > 0)
     def _():
         lax.fori_loop(0, rows, step, 0, unroll=8)
-
-    for j in range(tiles):
-        cut = slice(j * 128, (j + 1) * 128)
-        total = sum_ref[:, j, :] + skipped_ref[:, cut]
-        gated_ref[:, cut] = (total * silu_ref[:, cut]).astype(BF16)
-    own = lax.axis_index("tp")
-    width = own_ref.shape[1]
-    for k in range(parts):
-        start = pl.multiple_of(jnp.bitwise_xor(own, k) * width, 128)
-        product = jnp.dot(
-            gated_ref[...], weight_ref[:, pl.ds(start, width)], preferred_element_type=F32
-        )
-        if k == 0:
-            own_ref[...] = product + quarter_ref[...]
-        else:
-            sent[k - 1][...] = product.astype(BF16)
+        project(sum_ref, skipped_ref, silu_ref, quarter_ref, weight_ref, own_ref, sent, gated_ref)
 
 
 def mix(parts, seen, y, elapsed, rates, state, skipped, silu, quarter, weight):
     rows, tiles, _ = y.shape
     width = weight.shape[1] // parts
+    made = [shaped((rows, width), F32)] + [shaped((rows, width), BF16)] * (parts - 1)
+    started = pl.pallas_call(
+        functools.partial(mix_first_kernel, parts),
+        out_shape=made,
+        in_specs=[whole()] * 5,
+        out_specs=[whole()] * parts,
+        scratch_shapes=[pltpu.VMEM((rows, tiles * 128), BF16)],
+        compiler_params=params(),
+        cost_estimate=cost(3e9, 0),
+        name="mix_first",
+    )(y, skipped, silu, quarter, weight)
     return pl.pallas_call(
         functools.partial(mix_kernel, parts),
-        out_shape=[shaped((rows, width), F32)]
-        + [shaped((rows, width), BF16)] * (parts - 1),
-        in_specs=[whole()] * 9,
+        out_shape=made,
+        in_specs=[whole()] * (9 + parts),
         out_specs=[whole()] * parts,
+        input_output_aliases={9 + i: i for i in range(parts)},
         scratch_shapes=[
             pltpu.VMEM((rows, tiles, 128), F32),
             pltpu.VMEM((rows, tiles * 128), BF16),
@@ -396,7 +410,7 @@
         compiler_params=params(),
         cost_estimate=cost(1e6, 12e6),
         name="mix",
-    )(seen, y, elapsed, rates, state, skipped, silu, quarter, weight)
+    )(seen, y, elapsed, rates, state, skipped, silu, quarter, weight, *started)
 
 
 def pick_kernel(parts, *refs):

time: 84.2 us -> 82.6 us (0.981)
  waiting for transfers between devices: 15.1 us -> 14.1 us
    ppermute x1, waiting for transfers between devices: 0.88 us -> 0.01 us  [body(): before = lax.ppermute(state, 'ctx', [(0, 1)])]
  transfers between devices with their start and end apart: 33 -> 33, of which waited for: 13 -> 10; matrix products, arithmetic and copies ran while one was open for 0% -> 0% of each run, Pallas kernels for 25% -> 27%
where the time goes in v8:
time: 82.6 us; the launch traced here: 82.3 us
  starting transfers between devices  39.9 us (48%)
  Pallas kernels  28 us (34%)
  waiting for transfers between devices  14.1 us (17%)
    ppermute x31, starting transfers between devices, swap(): lax.ppermute(block, axis, [(i, i ^ k) for i in range(lax.axis_size(axis))])  36.2 us
    ppermute x31, waiting for transfers between devices, swap(): lax.ppermute(block, axis, [(i, i ^ k) for i in range(lax.axis_size(axis))])  14 us
    pallas_call x4, Pallas kernels, hidden_units(): pl.pallas_call(functools.partial(hidden_kernel, part), out_shape=made, in...  9.08 us
    pallas_call x2, Pallas kernels, down_sums(): pl.pallas_call(down_kernel, out_shape=(shaped((rows, model), F32), shaped...  4.18 us
    pallas_call x1, Pallas kernels, scan(): pl.pallas_call(functools.partial(scan_kernel, len(pieces)), out_shape=(sh...  3.61 us
    pallas_call x1, Pallas kernels, route(): pl.pallas_call(route_kernel, out_shape=(shaped((rows, slots), BF16), shap...  3.09 us
    pallas_call x1, Pallas kernels, prepare(): pl.pallas_call(prepare_kernel, out_shape=(shaped((rows, channels), F32),...  2.76 us
    ppermute x1, starting transfers between devices, body(): before = lax.ppermute(local, 'ctx', [(0, 1)])  2.36 us
  transfers between devices with their start and end apart: 33, of which 10 were waited for; matrix products, arithmetic and copies ran while one was open for 0% of the time, Pallas kernels for 27%

profile of v8, /device:TPU:0, one launch (start us, length us, event | category | flops | bytes accessed | tf_op | source)
XLA Modules:
  0.0 82.3 jit_solution(18300812005930681591)
XLA Ops:
  0.0 2.4 %collective-permute-start = (bf16[128,1024]{1,0:T(8,128)(2,1)}, bf16[128,1024]{1,0:T(8,128)(2,1)S(1)}, u32[]{:S(2)}, u32[]{:S(2)}) collective-permute-start(bf16[128,1024]{1,0:T(8,128)(2,1)} %bitcast.21), channel_id=1, source_target_pairs={{0,16},{1,17},{2,18},{3,19},{4,20},{5,21},{6,22},{7,23},{8,24},{9,... | collective-permute-start | bytes 786440 | tf_op jit(solution)/shard_map/ppermute | solution.py:638
  4.3 2.4 %collective-permute-start.3 = (bf16[144,256]{1,0:T(8,128)(2,1)S(1)}, bf16[144,256]{1,0:T(8,128)(2,1)S(1)}, u32[]{:S(2)}, u32[]{:S(2)}) collective-permute-start(bf16[144,256]{1,0:T(8,128)(2,1)S(1)} %get-tuple-element.65.refs_0_), channel_id=1, source_target_pairs={{0,1},{1,0},{2,3},{3,2},{4,5},{5,4},{6,7},{7,6},{8,9},{9,8},{10,11... | collective-permute-start | bytes 221192 | tf_op jit(solution)/shard_map/ppermute | solution.py:33
  8.2 2.8 %prepare.1 = (f32[128,1024]{1,0:T(8,128)S(1)}, f32[16,8,128]{2,1,0:T(8,128)S(1)}, f32[128,1024]{1,0:T(8,128)S(1)}, f32[1,1024]{1,0:T(1,128)S(1)}, bf16[256,1024]...) custom-call(bf16[128,1024]{1,0:T(8,128)(2,1)S(1)} %get-tuple-element.66.xconv_, ...), custom_call_target="tpu_custom_call" | custom-call | flops 1000000 | bytes 6000000 | tf_op jit(solution)/shard_map/prepare/pallas_call | solution.py:240
  11.0 2.4 %collective-permute-done.1.refs_1_ = bf16[144,256]{1,0:T(8,128)(2,1)S(1)} collective-permute-done((bf16[144,256]{1,0:T(8,128)(2,1)S(1)}, bf16[144,256]{1,0:T(8,128)(2,1)S(1)}, u32[]{:S(2)}, u32[]{:S(2)}) %collective-permute-start.1) | collective-permute-done | bytes 73760 | tf_op jit(solution)/shard_map/ppermute | solution.py:33
  13.5 3.6 %scan.1 = (f32[128,8,128]{2,1,0:T(8,128)S(1)}, f32[128,8,128]{2,1,0:T(8,128)S(1)}, f32[128,16,128]{2,1,0:T(8,128)S(1)}, f32[16,8,128]{2,1,0:T(8,128)S(1)}, bf16[2048,1792]{1,0:T(8,128)(2,1)S(1)}) custom-call(bf16[144,256]{1,0:T(8,128)(2,1)S(1)} %get-tuple-element.65.refs_0_, bf16[144,256]{1,0:T(8,128)(2,1)S(1)} %collective-permute-done.1.refs_1_, ...), custom_call_target="tpu_custom_call" | custom-call | flops 1000000 | bytes 14000000 | tf_op jit(solution)/shard_map/scan/pallas_call | solution.py:318
  21.0 2.3 %collective-permute-start.7 = (bf16[128,512]{1,0:T(8,128)(2,1)S(1)}, bf16[128,512]{1,0:T(8,128)(2,1)S(1)}, u32[]{:S(2)}, u32[]{:S(2)}) collective-permute-start(bf16[128,512]{1,0:T(8,128)(2,1)S(1)} %get-tuple-element.85), channel_id=1, source_target_pairs={{0,3},{1,2},{2,1},{3,0},{4,7},{5,6},{6,5},{7,4},{8,11},{9,10},{10,... | collective-permute-start | bytes 393224 | tf_op jit(solution)/shard_map/ppermute | solution.py:33
  23.2 3.1 %route.1 = (bf16[128,256]{1,0:T(8,128)(2,1)S(1)}, bf16[128,256]{1,0:T(8,128)(2,1)S(1)}, bf16[256,128]{1,0:T(8,128)(2,1)S(1)}, bf16[2048,1792]{1,0:T(8,128)(2,1)S(1)}) custom-call(s32[2,128]{1,0:T(2,128)S(1)} %bitcast.17, bf16[1,3,2048,1792]{3,2,1,0:T(8,128)(2,1)} %refs_0_.3), custom_call_target="tpu_custom_call" | custom-call | flops 1000000 | bytes 8000000 | tf_op jit(solution)/shard_map/route/pallas_call | solution.py:123
  26.4 2.0 %collective-permute-done.7.refs_3_ = bf16[128,512]{1,0:T(8,128)(2,1)S(1)} collective-permute-done((bf16[128,512]{1,0:T(8,128)(2,1)S(1)}, bf16[128,512]{1,0:T(8,128)(2,1)S(1)}, u32[]{:S(2)}, u32[]{:S(2)}) %collective-permute-start.7) | collective-permute-done | bytes 131104 | tf_op jit(solution)/shard_map/ppermute | solution.py:33
  28.6 2.7 %collective-permute-start.12 = (bf16[64,512]{1,0:T(8,128)(2,1)S(1)}, bf16[64,512]{1,0:T(8,128)(2,1)S(1)}, u32[]{:S(2)}, u32[]{:S(2)}) collective-permute-start(bf16[64,512]{1,0:T(8,128)(2,1)S(1)} %get-tuple-element.90), channel_id=1, source_target_pairs={{0,8},{4,12},{8,0},{12,4},{1,9},{5,13},{9,1},{13,5},{2,10},{6,14},... | collective-permute-start | bytes 196616 | tf_op jit(solution)/shard_map/ppermute | solution.py:33
  32.8 3.0 %collective-permute-done.12.refs_0_ = bf16[64,512]{1,0:T(8,128)(2,1)S(1)} collective-permute-done((bf16[64,512]{1,0:T(8,128)(2,1)S(1)}, bf16[64,512]{1,0:T(8,128)(2,1)S(1)}, u32[]{:S(2)}, u32[]{:S(2)}) %collective-permute-start.12) | collective-permute-done | bytes 65568 | tf_op jit(solution)/shard_map/ppermute | solution.py:33
  37.3 2.0 %collective-permute-start.13 = (bf16[64,512]{1,0:T(8,128)(2,1)S(1)}, bf16[64,512]{1,0:T(8,128)(2,1)S(1)}, u32[]{:S(2)}, u32[]{:S(2)}) collective-permute-start(bf16[64,512]{1,0:T(8,128)(2,1)S(1)} %collective-permute-done.12.refs_0_), channel_id=1, source_target_pairs={{0,1},{1,0},{2,3},{3,2},{4,5},{5,4},{6,7},{7,6},{8,9},{9,8},{10,11... | collective-permute-start | bytes 196616 | tf_op jit(solution)/shard_map/ppermute | solution.py:33
  41.2 1.8 %collective-permute-start.17 = (bf16[64,512]{1,0:T(8,128)(2,1)S(1)}, bf16[64,512]{1,0:T(8,128)(2,1)S(1)}, u32[]{:S(2)}, u32[]{:S(2)}) collective-permute-start(bf16[64,512]{1,0:T(8,128)(2,1)S(1)} %collective-permute-done.16.refs_0_.refs_4_), channel_id=1, source_target_pairs={{0,1},{1,0},{2,3},{3,2},{4,5},{5,4},{6,7},{7,6},{8,9},{9,8},{10,11... | collective-permute-start | bytes 196616 | tf_op jit(solution)/shard_map/ppermute | solution.py:33
  46.8 2.2 %hidden.4 = (bf16[128,1792]{1,0:T(8,128)(2,1)S(1)}, bf16[1024,1792]{1,0:T(8,128)(2,1)S(1)}) custom-call(bf16[128,2048]{1,0:T(8,128)(2,1)S(1)} %norm.2.x_ref.refs_0_, bf16[2048,1792]{1,0:T(8,128)(2,1)S(1)} %get-tuple-element.92.gate_ref, bf16[2048,1792]{1,0:T(8,128)(2,1)S(1)} %get-tuple-element.93.up_ref, bf16[1,3,2048,1792]{3,2,1,0:T(8,128)(2,1)} %refs_0_.3), custom_call_target="tpu_custom_call" | custom-call | flops 1000000 | tf_op jit(solution)/shard_map/hidden/pallas_call | solution.py:500
  49.0 2.2 %hidden.5 = (bf16[128,1792]{1,0:T(8,128)(2,1)S(1)}, bf16[1024,1792]{1,0:T(8,128)(2,1)S(1)}) custom-call(bf16[128,2048]{1,0:T(8,128)(2,1)S(1)} %collective-permute-done.20.x_ref, bf16[2048,1792]{1,0:T(8,128)(2,1)S(1)} %get-tuple-element.92.gate_ref, bf16[2048,1792]{1,0:T(8,128)(2,1)S(1)} %get-tuple-element.93.up_ref, bf16[1,3,2048,1792]{3,2,1,0:T(8,128)(2,1)} %refs_0_.3, ...), custom_call_target="tpu_custom_call" | custom-call | flops 1000000 | tf_op jit(solution)/shard_map/hidden/pallas_call | solution.py:500
  51.2 2.1 %down.2 = (f32[128,2048]{1,0:T(8,128)S(1)}, bf16[128,2048]{1,0:T(8,128)(2,1)S(1)}) custom-call(bf16[128,1792]{1,0:T(8,128)(2,1)S(1)} %get-tuple-element.94.refs_1_.hidden_own_ref, bf16[128,1792]{1,0:T(8,128)(2,1)S(1)} %get-tuple-element.95.hidden_other_ref, bf16[1024,1792]{1,0:T(8,128)(2,1)S(1)} %get-tuple-element.96.low_ref, ...), custom_call_target="tpu_custom_call" | custom-call | flops 1000000 | tf_op jit(solution)/shard_map/down/pallas_call | solution.py:535
  54.2 2.2 %hidden.6.refs_0_.hidden_own_ref = bf16[128,1792]{1,0:T(8,128)(2,1)S(1)} custom-call(bf16[128,2048]{1,0:T(8,128)(2,1)S(1)} %norm.3.x_ref, bf16[2048,1792]{1,0:T(8,128)(2,1)S(1)} %get-tuple-element.92.gate_ref, bf16[2048,1792]{1,0:T(8,128)(2,1)S(1)} %get-tuple-element.93.up_ref), custom_call_target="tpu_custom_call" | custom-call | flops 1000000 | tf_op jit(solution)/shard_map/hidden/pallas_call | solution.py:500
  56.6 1.8 %collective-permute-start.24 = (bf16[128,512]{1,0:T(8,128)(2,1)S(1)}, bf16[128,512]{1,0:T(8,128)(2,1)S(1)}, u32[]{:S(2)}, u32[]{:S(2)}) collective-permute-start(bf16[128,512]{1,0:T(8,128)(2,1)S(1)} %get-tuple-element.103), channel_id=1, source_target_pairs={{0,1},{1,0},{2,3},{3,2},{4,5},{5,4},{6,7},{7,6},{8,9},{9,8},{10,11... | collective-permute-start | bytes 393224 | tf_op jit(solution)/shard_map/ppermute | solution.py:33
  60.1 2.4 %hidden.7.hidden_other_ref = bf16[128,1792]{1,0:T(8,128)(2,1)S(1)} custom-call(bf16[128,2048]{1,0:T(8,128)(2,1)S(1)} %collective-permute-done.21.x_ref, bf16[2048,1792]{1,0:T(8,128)(2,1)S(1)} %get-tuple-element.92.gate_ref, bf16[2048,1792]{1,0:T(8,128)(2,1)S(1)} %get-tuple-element.93.up_ref, f32[128,512]{1,0:T(8,128)S(1)} %get-tuple-element.100.refs_0_), custom_call_target="tpu_custom_call" | custom-call | flops 1000000 | tf_op jit(solution)/shard_map/hidden/pallas_call | solution.py:500
  62.6 2.1 %down.3 = (f32[128,2048]{1,0:T(8,128)S(1)}, bf16[128,2048]{1,0:T(8,128)(2,1)S(1)}) custom-call(bf16[128,1792]{1,0:T(8,128)(2,1)S(1)} %hidden.6.refs_0_.hidden_own_ref, bf16[128,1792]{1,0:T(8,128)(2,1)S(1)} %hidden.7.hidden_other_ref, bf16[1024,1792]{1,0:T(8,128)(2,1)S(1)} %get-tuple-element.96.low_ref, bf16[1024,1792]{1,0:T(8,128)(2,1)S(1)} %get-tuple-element.97.high_ref), custom_call_target="tpu_custom_call" | custom-call | flops 1000000 | tf_op jit(solution)/shard_map/down/pallas_call | solution.py:535
  64.8 2.0 %collective-permute-done.25.refs_2_ = bf16[128,512]{1,0:T(8,128)(2,1)S(1)} collective-permute-done((bf16[128,512]{1,0:T(8,128)(2,1)S(1)}, bf16[128,512]{1,0:T(8,128)(2,1)S(1)}, u32[]{:S(2)}, u32[]{:S(2)}) %collective-permute-start.25) | collective-permute-done | bytes 131104 | tf_op jit(solution)/shard_map/ppermute | solution.py:33
  67.0 1.6 %collective-permute-start.27 = (bf16[128,512]{1,0:T(8,128)(2,1)S(1)}, bf16[128,512]{1,0:T(8,128)(2,1)S(1)}, u32[]{:S(2)}, u32[]{:S(2)}) collective-permute-start(bf16[128,512]{1,0:T(8,128)(2,1)S(1)} %get-tuple-element.108), channel_id=1, source_target_pairs={{0,1},{1,0},{2,3},{3,2},{4,5},{5,4},{6,7},{7,6},{8,9},{9,8},{10,11... | collective-permute-start | bytes 393224 | tf_op jit(solution)/shard_map/ppermute | solution.py:33
  70.5 4.9 %collective-permute-start.32 = (bf16[64,512]{1,0:T(8,128)(2,1)S(1)}, bf16[64,512]{1,0:T(8,128)(2,1)S(1)}, u32[]{:S(2)}, u32[]{:S(2)}) collective-permute-start(bf16[64,512]{1,0:T(8,128)(2,1)S(1)} %get-tuple-element.113), channel_id=1, source_target_pairs={{0,12},{4,8},{8,4},{12,0},{1,13},{5,9},{9,5},{13,1},{2,14},{6,10},... | collective-permute-start | bytes 196616 | tf_op jit(solution)/shard_map/ppermute | solution.py:33
  76.7 2.0 %collective-permute-start.30 = (bf16[64,512]{1,0:T(8,128)(2,1)S(1)}, bf16[64,512]{1,0:T(8,128)(2,1)S(1)}, u32[]{:S(2)}, u32[]{:S(2)}) collective-permute-start(bf16[64,512]{1,0:T(8,128)(2,1)S(1)} %get-tuple-element.112), channel_id=1, source_target_pairs={{0,4},{4,0},{8,12},{12,8},{1,5},{5,1},{9,13},{13,9},{2,6},{6,2},{1... | collective-permute-start | bytes 196616 | tf_op jit(solution)/shard_map/ppermute | solution.py:33
  78.7 1.9 %collective-permute-done.31.refs_0_ = bf16[64,512]{1,0:T(8,128)(2,1)S(1)} collective-permute-done((bf16[64,512]{1,0:T(8,128)(2,1)S(1)}, bf16[64,512]{1,0:T(8,128)(2,1)S(1)}, u32[]{:S(2)}, u32[]{:S(2)}) %collective-permute-start.31) | collective-permute-done | bytes 65568 | tf_op jit(solution)/shard_map/ppermute | solution.py:33
  (72 shorter events, 24.3 us)
Async XLA Ops:
  4.3 6.7 %collective-permute-start.3 = (bf16[144,256]{1,0:T(8,128)(2,1)S(1)}, bf16[144,256]{1,0:T(8,128)(2,1)S(1)}, u32[]{:S(2)}, u32[]{:S(2)}) collective-permute-start(bf16[144,256]{1,0:T(8,128)(2,1)S(1)} %get-tuple-element.65.refs_0_), channel_id=1, source_target_pairs={{0,1},{1,0},{2,3},{3,2},{4,5},{5,4},{6,7},{7,6},{8,9},{9,8},{10,11... | collective-permute-start | bytes 221192 | tf_op jit(solution)/shard_map/ppermute | solution.py:33
  19.7 6.7 %collective-permute-start.5 = (bf16[128,512]{1,0:T(8,128)(2,1)S(1)}, bf16[128,512]{1,0:T(8,128)(2,1)S(1)}, u32[]{:S(2)}, u32[]{:S(2)}) collective-permute-start(bf16[128,512]{1,0:T(8,128)(2,1)S(1)} %get-tuple-element.83), channel_id=1, source_target_pairs={{0,1},{1,0},{2,3},{3,2},{4,5},{5,4},{6,7},{7,6},{8,9},{9,8},{10,11... | collective-permute-start | bytes 393224 | tf_op jit(solution)/shard_map/ppermute | solution.py:33
  20.3 6.1 %collective-permute-start.6 = (bf16[128,512]{1,0:T(8,128)(2,1)S(1)}, bf16[128,512]{1,0:T(8,128)(2,1)S(1)}, u32[]{:S(2)}, u32[]{:S(2)}) collective-permute-start(bf16[128,512]{1,0:T(8,128)(2,1)S(1)} %get-tuple-element.84), channel_id=1, source_target_pairs={{0,2},{1,3},{2,0},{3,1},{4,6},{5,7},{6,4},{7,5},{8,10},{9,11},{10,... | collective-permute-start | bytes 393224 | tf_op jit(solution)/shard_map/ppermute | solution.py:33
  21.0 7.4 %collective-permute-start.7 = (bf16[128,512]{1,0:T(8,128)(2,1)S(1)}, bf16[128,512]{1,0:T(8,128)(2,1)S(1)}, u32[]{:S(2)}, u32[]{:S(2)}) collective-permute-start(bf16[128,512]{1,0:T(8,128)(2,1)S(1)} %get-tuple-element.85), channel_id=1, source_target_pairs={{0,3},{1,2},{2,1},{3,0},{4,7},{5,6},{6,5},{7,4},{8,11},{9,10},{10,... | collective-permute-start | bytes 393224 | tf_op jit(solution)/shard_map/ppermute | solution.py:33
  28.6 7.2 %collective-permute-start.12 = (bf16[64,512]{1,0:T(8,128)(2,1)S(1)}, bf16[64,512]{1,0:T(8,128)(2,1)S(1)}, u32[]{:S(2)}, u32[]{:S(2)}) collective-permute-start(bf16[64,512]{1,0:T(8,128)(2,1)S(1)} %get-tuple-element.90), channel_id=1, source_target_pairs={{0,8},{4,12},{8,0},{12,4},{1,9},{5,13},{9,1},{13,5},{2,10},{6,14},... | collective-permute-start | bytes 196616 | tf_op jit(solution)/shard_map/ppermute | solution.py:33
  31.3 8.1 %collective-permute-start.16 = (bf16[64,512]{1,0:T(8,128)(2,1)S(1)}, bf16[64,512]{1,0:T(8,128)(2,1)S(1)}, u32[]{:S(2)}, u32[]{:S(2)}) collective-permute-start(bf16[64,512]{1,0:T(8,128)(2,1)S(1)} %get-tuple-element.91), channel_id=1, source_target_pairs={{0,12},{4,8},{8,4},{12,0},{1,13},{5,9},{9,5},{13,1},{2,14},{6,10},... | collective-permute-start | bytes 196616 | tf_op jit(solution)/shard_map/ppermute | solution.py:33
  32.6 8.2 %collective-permute-start.8 = (bf16[64,512]{1,0:T(8,128)(2,1)S(1)}, bf16[64,512]{1,0:T(8,128)(2,1)S(1)}, u32[]{:S(2)}, u32[]{:S(2)}) collective-permute-start(bf16[64,512]{1,0:T(8,128)(2,1)S(1)} %get-tuple-element.88), channel_id=1, source_target_pairs={{0,4},{4,0},{8,12},{12,8},{1,5},{5,1},{9,13},{13,9},{2,6},{6,2},{1... | collective-permute-start | bytes 196616 | tf_op jit(solution)/shard_map/ppermute | solution.py:33
  35.9 5.3 %collective-permute-start.15 = (bf16[64,512]{1,0:T(8,128)(2,1)S(1)}, bf16[64,512]{1,0:T(8,128)(2,1)S(1)}, u32[]{:S(2)}, u32[]{:S(2)}) collective-permute-start(bf16[64,512]{1,0:T(8,128)(2,1)S(1)} %collective-permute-done.12.refs_0_), channel_id=1, source_target_pairs={{0,3},{1,2},{2,1},{3,0},{4,7},{5,6},{6,5},{7,4},{8,11},{9,10},{10,... | collective-permute-start | bytes 196616 | tf_op jit(solution)/shard_map/ppermute | solution.py:33
  37.3 5.6 %collective-permute-start.14 = (bf16[64,512]{1,0:T(8,128)(2,1)S(1)}, bf16[64,512]{1,0:T(8,128)(2,1)S(1)}, u32[]{:S(2)}, u32[]{:S(2)}) collective-permute-start(bf16[64,512]{1,0:T(8,128)(2,1)S(1)} %collective-permute-done.12.refs_0_), channel_id=1, source_target_pairs={{0,2},{1,3},{2,0},{3,1},{4,6},{5,7},{6,4},{7,5},{8,10},{9,11},{10,... | collective-permute-start | bytes 196616 | tf_op jit(solution)/shard_map/ppermute | solution.py:33
  37.3 7.1 %collective-permute-start.13 = (bf16[64,512]{1,0:T(8,128)(2,1)S(1)}, bf16[64,512]{1,0:T(8,128)(2,1)S(1)}, u32[]{:S(2)}, u32[]{:S(2)}) collective-permute-start(bf16[64,512]{1,0:T(8,128)(2,1)S(1)} %collective-permute-done.12.refs_0_), channel_id=1, source_target_pairs={{0,1},{1,0},{2,3},{3,2},{4,5},{5,4},{6,7},{7,6},{8,9},{9,8},{10,11... | collective-permute-start | bytes 196616 | tf_op jit(solution)/shard_map/ppermute | solution.py:33
  39.3 5.8 %collective-permute-start.19 = (bf16[64,512]{1,0:T(8,128)(2,1)S(1)}, bf16[64,512]{1,0:T(8,128)(2,1)S(1)}, u32[]{:S(2)}, u32[]{:S(2)}) collective-permute-start(bf16[64,512]{1,0:T(8,128)(2,1)S(1)} %collective-permute-done.16.refs_0_.refs_4_), channel_id=1, source_target_pairs={{0,3},{1,2},{2,1},{3,0},{4,7},{5,6},{6,5},{7,4},{8,11},{9,10},{10,... | collective-permute-start | bytes 196616 | tf_op jit(solution)/shard_map/ppermute | solution.py:33
  40.8 5.6 %collective-permute-start.18 = (bf16[64,512]{1,0:T(8,128)(2,1)S(1)}, bf16[64,512]{1,0:T(8,128)(2,1)S(1)}, u32[]{:S(2)}, u32[]{:S(2)}) collective-permute-start(bf16[64,512]{1,0:T(8,128)(2,1)S(1)} %collective-permute-done.16.refs_0_.refs_4_), channel_id=1, source_target_pairs={{0,2},{1,3},{2,0},{3,1},{4,6},{5,7},{6,4},{7,5},{8,10},{9,11},{10,... | collective-permute-start | bytes 196616 | tf_op jit(solution)/shard_map/ppermute | solution.py:33
  41.2 5.3 %collective-permute-start.17 = (bf16[64,512]{1,0:T(8,128)(2,1)S(1)}, bf16[64,512]{1,0:T(8,128)(2,1)S(1)}, u32[]{:S(2)}, u32[]{:S(2)}) collective-permute-start(bf16[64,512]{1,0:T(8,128)(2,1)S(1)} %collective-permute-done.16.refs_0_.refs_4_), channel_id=1, source_target_pairs={{0,1},{1,0},{2,3},{3,2},{4,5},{5,4},{6,7},{7,6},{8,9},{9,8},{10,11... | collective-permute-start | bytes 196616 | tf_op jit(solution)/shard_map/ppermute | solution.py:33
  42.9 10.9 %collective-permute-start.11 = (bf16[128,512]{1,0:T(8,128)(2,1)S(1)}, bf16[128,512]{1,0:T(8,128)(2,1)S(1)}, u32[]{:S(2)}, u32[]{:S(2)}) collective-permute-start(bf16[128,512]{1,0:T(8,128)(2,1)S(1)} %stack.1.refs_1_.refs_0_), channel_id=1, source_target_pairs={{0,3},{1,2},{2,1},{3,0},{4,7},{5,6},{6,5},{7,4},{8,11},{9,10},{10,... | collective-permute-start | bytes 393224 | tf_op jit(solution)/shard_map/ppermute | solution.py:33
  44.4 9.4 %collective-permute-start.10 = (bf16[128,512]{1,0:T(8,128)(2,1)S(1)}, bf16[128,512]{1,0:T(8,128)(2,1)S(1)}, u32[]{:S(2)}, u32[]{:S(2)}) collective-permute-start(bf16[128,512]{1,0:T(8,128)(2,1)S(1)} %stack.1.refs_1_.refs_0_), channel_id=1, source_target_pairs={{0,2},{1,3},{2,0},{3,1},{4,6},{5,7},{6,4},{7,5},{8,10},{9,11},{10,... | collective-permute-start | bytes 393224 | tf_op jit(solution)/shard_map/ppermute | solution.py:33
  45.2 8.7 %collective-permute-start.9 = (bf16[128,512]{1,0:T(8,128)(2,1)S(1)}, bf16[128,512]{1,0:T(8,128)(2,1)S(1)}, u32[]{:S(2)}, u32[]{:S(2)}) collective-permute-start(bf16[128,512]{1,0:T(8,128)(2,1)S(1)} %stack.1.refs_1_.refs_0_), channel_id=1, source_target_pairs={{0,1},{1,0},{2,3},{3,2},{4,5},{5,4},{6,7},{7,6},{8,9},{9,8},{10,11... | collective-permute-start | bytes 393224 | tf_op jit(solution)/shard_map/ppermute | solution.py:33
  54.1 6.0 %collective-permute-start.21 = (bf16[128,2048]{1,0:T(8,128)(2,1)S(1)}, bf16[128,2048]{1,0:T(8,128)(2,1)S(1)}, u32[]{:S(2)}, u32[]{:S(2)}) collective-permute-start(bf16[128,2048]{1,0:T(8,128)(2,1)S(1)} %norm.3.x_ref), channel_id=1, source_target_pairs={{0,16},{16,0},{1,17},{17,1},{2,18},{18,2},{3,19},{19,3},{4,20},{20... | collective-permute-start | bytes 1572872 | tf_op jit(solution)/shard_map/ppermute | solution.py:33
  56.6 8.2 %collective-permute-start.24 = (bf16[128,512]{1,0:T(8,128)(2,1)S(1)}, bf16[128,512]{1,0:T(8,128)(2,1)S(1)}, u32[]{:S(2)}, u32[]{:S(2)}) collective-permute-start(bf16[128,512]{1,0:T(8,128)(2,1)S(1)} %get-tuple-element.103), channel_id=1, source_target_pairs={{0,1},{1,0},{2,3},{3,2},{4,5},{5,4},{6,7},{7,6},{8,9},{9,8},{10,11... | collective-permute-start | bytes 393224 | tf_op jit(solution)/shard_map/ppermute | solution.py:33
  58.3 8.4 %collective-permute-start.25 = (bf16[128,512]{1,0:T(8,128)(2,1)S(1)}, bf16[128,512]{1,0:T(8,128)(2,1)S(1)}, u32[]{:S(2)}, u32[]{:S(2)}) collective-permute-start(bf16[128,512]{1,0:T(8,128)(2,1)S(1)} %get-tuple-element.104), channel_id=1, source_target_pairs={{0,2},{1,3},{2,0},{3,1},{4,6},{5,7},{6,4},{7,5},{8,10},{9,11},{10,... | collective-permute-start | bytes 393224 | tf_op jit(solution)/shard_map/ppermute | solution.py:33
  58.9 7.8 %collective-permute-start.26 = (bf16[128,512]{1,0:T(8,128)(2,1)S(1)}, bf16[128,512]{1,0:T(8,128)(2,1)S(1)}, u32[]{:S(2)}, u32[]{:S(2)}) collective-permute-start(bf16[128,512]{1,0:T(8,128)(2,1)S(1)} %get-tuple-element.105), channel_id=1, source_target_pairs={{0,3},{1,2},{2,1},{3,0},{4,7},{5,6},{6,5},{7,4},{8,11},{9,10},{10,... | collective-permute-start | bytes 393224 | tf_op jit(solution)/shard_map/ppermute | solution.py:33
  67.0 8.4 %collective-permute-start.27 = (bf16[128,512]{1,0:T(8,128)(2,1)S(1)}, bf16[128,512]{1,0:T(8,128)(2,1)S(1)}, u32[]{:S(2)}, u32[]{:S(2)}) collective-permute-start(bf16[128,512]{1,0:T(8,128)(2,1)S(1)} %get-tuple-element.108), channel_id=1, source_target_pairs={{0,1},{1,0},{2,3},{3,2},{4,5},{5,4},{6,7},{7,6},{8,9},{9,8},{10,11... | collective-permute-start | bytes 393224 | tf_op jit(solution)/shard_map/ppermute | solution.py:33
  68.5 8.1 %collective-permute-start.28 = (bf16[128,512]{1,0:T(8,128)(2,1)S(1)}, bf16[128,512]{1,0:T(8,128)(2,1)S(1)}, u32[]{:S(2)}, u32[]{:S(2)}) collective-permute-start(bf16[128,512]{1,0:T(8,128)(2,1)S(1)} %get-tuple-element.109), channel_id=1, source_target_pairs={{0,2},{1,3},{2,0},{3,1},{4,6},{5,7},{6,4},{7,5},{8,10},{9,11},{10,... | collective-permute-start | bytes 393224 | tf_op jit(solution)/shard_map/ppermute | solution.py:33
  69.1 7.5 %collective-permute-start.29 = (bf16[128,512]{1,0:T(8,128)(2,1)S(1)}, bf16[128,512]{1,0:T(8,128)(2,1)S(1)}, u32[]{:S(2)}, u32[]{:S(2)}) collective-permute-start(bf16[128,512]{1,0:T(8,128)(2,1)S(1)} %get-tuple-element.110), channel_id=1, source_target_pairs={{0,3},{1,2},{2,1},{3,0},{4,7},{5,6},{6,5},{7,4},{8,11},{9,10},{10,... | collective-permute-start | bytes 393224 | tf_op jit(solution)/shard_map/ppermute | solution.py:33
  70.5 8.2 %collective-permute-start.32 = (bf16[64,512]{1,0:T(8,128)(2,1)S(1)}, bf16[64,512]{1,0:T(8,128)(2,1)S(1)}, u32[]{:S(2)}, u32[]{:S(2)}) collective-permute-start(bf16[64,512]{1,0:T(8,128)(2,1)S(1)} %get-tuple-element.113), channel_id=1, source_target_pairs={{0,12},{4,8},{8,4},{12,0},{1,13},{5,9},{9,5},{13,1},{2,14},{6,10},... | collective-permute-start | bytes 196616 | tf_op jit(solution)/shard_map/ppermute | solution.py:33
  (11 other events, 50.9 us)

commit v9 on v8

--- a/solution.py
+++ b/solution.py
@@ -674,8 +674,7 @@
     back_a = [swap(piece, "exp", j) for j, piece in enumerate(made_a, half)]
     back_b = [made_b[0]] + [swap(made_b[j], "exp", j) for j in range(1, half)]
     gates = route_gates[0].T
-    partial = blend(half * CAP, back_a, stream, first, second, gates, F32)
-    return blend(0, back_b, partial, first, second, gates, BF16)[None]
+    return blend(0, back_b + back_a, stream, first, second, gates, BF16)[None]
 
 
 def solution(mesh):

time: 82.6 us -> 82.2 us (level)
  transfers between devices with their start and end apart: 33 -> 33, of which waited for: 10 -> 9; matrix products, arithmetic and copies ran while one was open for 0% -> 0% of each run, Pallas kernels for 27% -> 27%
where the time goes in v9:
time: 82.2 us; the launch traced here: 81.9 us
  starting transfers between devices  39.9 us (49%)
  Pallas kernels  27.8 us (34%)
  waiting for transfers between devices  14 us (17%)
    ppermute x31, starting transfers between devices, swap(): lax.ppermute(block, axis, [(i, i ^ k) for i in range(lax.axis_size(axis))])  36.2 us
    ppermute x31, waiting for transfers between devices, swap(): lax.ppermute(block, axis, [(i, i ^ k) for i in range(lax.axis_size(axis))])  13.8 us
    pallas_call x4, Pallas kernels, hidden_units(): pl.pallas_call(functools.partial(hidden_kernel, part), out_shape=made, in...  9.07 us
    pallas_call x2, Pallas kernels, down_sums(): pl.pallas_call(down_kernel, out_shape=(shaped((rows, model), F32), shaped...  4.18 us
    pallas_call x1, Pallas kernels, scan(): pl.pallas_call(functools.partial(scan_kernel, len(pieces)), out_shape=(sh...  3.61 us
    pallas_call x1, Pallas kernels, route(): pl.pallas_call(route_kernel, out_shape=(shaped((rows, slots), BF16), shap...  3.09 us
    pallas_call x1, Pallas kernels, prepare(): pl.pallas_call(prepare_kernel, out_shape=(shaped((rows, channels), F32),...  2.76 us
    ppermute x1, starting transfers between devices, body(): before = lax.ppermute(local, 'ctx', [(0, 1)])  2.36 us
  transfers between devices with their start and end apart: 33, of which 9 were waited for; matrix products, arithmetic and copies ran while one was open for 0% of the time, Pallas kernels for 27%

profile of v9, /device:TPU:0, one launch (start us, length us, event | category | flops | bytes accessed | tf_op | source)
XLA Modules:
  0.0 81.9 jit_solution(5965987340345936252)
XLA Ops:
  0.0 2.4 %collective-permute-start = (bf16[128,1024]{1,0:T(8,128)(2,1)}, bf16[128,1024]{1,0:T(8,128)(2,1)S(1)}, u32[]{:S(2)}, u32[]{:S(2)}) collective-permute-start(bf16[128,1024]{1,0:T(8,128)(2,1)} %bitcast.20), channel_id=1, source_target_pairs={{0,16},{1,17},{2,18},{3,19},{4,20},{5,21},{6,22},{7,23},{8,24},{9,... | collective-permute-start | bytes 786440 | tf_op jit(solution)/shard_map/ppermute | solution.py:638
  4.3 2.4 %collective-permute-start.3 = (bf16[144,256]{1,0:T(8,128)(2,1)S(1)}, bf16[144,256]{1,0:T(8,128)(2,1)S(1)}, u32[]{:S(2)}, u32[]{:S(2)}) collective-permute-start(bf16[144,256]{1,0:T(8,128)(2,1)S(1)} %get-tuple-element.65.refs_0_), channel_id=1, source_target_pairs={{0,1},{1,0},{2,3},{3,2},{4,5},{5,4},{6,7},{7,6},{8,9},{9,8},{10,11... | collective-permute-start | bytes 221192 | tf_op jit(solution)/shard_map/ppermute | solution.py:33
  8.2 2.8 %prepare.1 = (f32[128,1024]{1,0:T(8,128)S(1)}, f32[16,8,128]{2,1,0:T(8,128)S(1)}, f32[128,1024]{1,0:T(8,128)S(1)}, f32[1,1024]{1,0:T(1,128)S(1)}, bf16[256,1024]...) custom-call(bf16[128,1024]{1,0:T(8,128)(2,1)S(1)} %get-tuple-element.66.xconv_, ...), custom_call_target="tpu_custom_call" | custom-call | flops 1000000 | bytes 6000000 | tf_op jit(solution)/shard_map/prepare/pallas_call | solution.py:240
  11.0 2.4 %collective-permute-done.1.refs_1_ = bf16[144,256]{1,0:T(8,128)(2,1)S(1)} collective-permute-done((bf16[144,256]{1,0:T(8,128)(2,1)S(1)}, bf16[144,256]{1,0:T(8,128)(2,1)S(1)}, u32[]{:S(2)}, u32[]{:S(2)}) %collective-permute-start.1) | collective-permute-done | bytes 73760 | tf_op jit(solution)/shard_map/ppermute | solution.py:33
  13.5 3.6 %scan.1 = (f32[128,8,128]{2,1,0:T(8,128)S(1)}, f32[128,8,128]{2,1,0:T(8,128)S(1)}, f32[128,16,128]{2,1,0:T(8,128)S(1)}, f32[16,8,128]{2,1,0:T(8,128)S(1)}, bf16[2048,1792]{1,0:T(8,128)(2,1)S(1)}) custom-call(bf16[144,256]{1,0:T(8,128)(2,1)S(1)} %get-tuple-element.65.refs_0_, bf16[144,256]{1,0:T(8,128)(2,1)S(1)} %collective-permute-done.1.refs_1_, ...), custom_call_target="tpu_custom_call" | custom-call | flops 1000000 | bytes 14000000 | tf_op jit(solution)/shard_map/scan/pallas_call | solution.py:318
  21.0 2.3 %collective-permute-start.7 = (bf16[128,512]{1,0:T(8,128)(2,1)S(1)}, bf16[128,512]{1,0:T(8,128)(2,1)S(1)}, u32[]{:S(2)}, u32[]{:S(2)}) collective-permute-start(bf16[128,512]{1,0:T(8,128)(2,1)S(1)} %get-tuple-element.85), channel_id=1, source_target_pairs={{0,3},{1,2},{2,1},{3,0},{4,7},{5,6},{6,5},{7,4},{8,11},{9,10},{10,... | collective-permute-start | bytes 393224 | tf_op jit(solution)/shard_map/ppermute | solution.py:33
  23.2 3.1 %route.1 = (bf16[128,256]{1,0:T(8,128)(2,1)S(1)}, bf16[128,256]{1,0:T(8,128)(2,1)S(1)}, bf16[256,128]{1,0:T(8,128)(2,1)S(1)}, bf16[2048,1792]{1,0:T(8,128)(2,1)S(1)}) custom-call(s32[2,128]{1,0:T(2,128)S(1)} %bitcast.15, bf16[1,3,2048,1792]{3,2,1,0:T(8,128)(2,1)} %refs_0_.3), custom_call_target="tpu_custom_call" | custom-call | flops 1000000 | bytes 8000000 | tf_op jit(solution)/shard_map/route/pallas_call | solution.py:123
  26.4 2.0 %collective-permute-done.7.refs_3_ = bf16[128,512]{1,0:T(8,128)(2,1)S(1)} collective-permute-done((bf16[128,512]{1,0:T(8,128)(2,1)S(1)}, bf16[128,512]{1,0:T(8,128)(2,1)S(1)}, u32[]{:S(2)}, u32[]{:S(2)}) %collective-permute-start.7) | collective-permute-done | bytes 131104 | tf_op jit(solution)/shard_map/ppermute | solution.py:33
  28.6 2.7 %collective-permute-start.12 = (bf16[64,512]{1,0:T(8,128)(2,1)S(1)}, bf16[64,512]{1,0:T(8,128)(2,1)S(1)}, u32[]{:S(2)}, u32[]{:S(2)}) collective-permute-start(bf16[64,512]{1,0:T(8,128)(2,1)S(1)} %get-tuple-element.90), channel_id=1, source_target_pairs={{0,8},{4,12},{8,0},{12,4},{1,9},{5,13},{9,1},{13,5},{2,10},{6,14},... | collective-permute-start | bytes 196616 | tf_op jit(solution)/shard_map/ppermute | solution.py:33
  32.8 3.0 %collective-permute-done.12.refs_0_ = bf16[64,512]{1,0:T(8,128)(2,1)S(1)} collective-permute-done((bf16[64,512]{1,0:T(8,128)(2,1)S(1)}, bf16[64,512]{1,0:T(8,128)(2,1)S(1)}, u32[]{:S(2)}, u32[]{:S(2)}) %collective-permute-start.12) | collective-permute-done | bytes 65568 | tf_op jit(solution)/shard_map/ppermute | solution.py:33
  37.3 2.0 %collective-permute-start.13 = (bf16[64,512]{1,0:T(8,128)(2,1)S(1)}, bf16[64,512]{1,0:T(8,128)(2,1)S(1)}, u32[]{:S(2)}, u32[]{:S(2)}) collective-permute-start(bf16[64,512]{1,0:T(8,128)(2,1)S(1)} %collective-permute-done.12.refs_0_), channel_id=1, source_target_pairs={{0,1},{1,0},{2,3},{3,2},{4,5},{5,4},{6,7},{7,6},{8,9},{9,8},{10,11... | collective-permute-start | bytes 196616 | tf_op jit(solution)/shard_map/ppermute | solution.py:33
  41.2 1.8 %collective-permute-start.17 = (bf16[64,512]{1,0:T(8,128)(2,1)S(1)}, bf16[64,512]{1,0:T(8,128)(2,1)S(1)}, u32[]{:S(2)}, u32[]{:S(2)}) collective-permute-start(bf16[64,512]{1,0:T(8,128)(2,1)S(1)} %collective-permute-done.16.refs_0_.refs_4_), channel_id=1, source_target_pairs={{0,1},{1,0},{2,3},{3,2},{4,5},{5,4},{6,7},{7,6},{8,9},{9,8},{10,11... | collective-permute-start | bytes 196616 | tf_op jit(solution)/shard_map/ppermute | solution.py:33
  46.8 2.2 %hidden.4 = (bf16[128,1792]{1,0:T(8,128)(2,1)S(1)}, bf16[1024,1792]{1,0:T(8,128)(2,1)S(1)}) custom-call(bf16[128,2048]{1,0:T(8,128)(2,1)S(1)} %norm.2.x_ref.refs_0_, bf16[2048,1792]{1,0:T(8,128)(2,1)S(1)} %get-tuple-element.92.gate_ref, bf16[2048,1792]{1,0:T(8,128)(2,1)S(1)} %get-tuple-element.93.up_ref, bf16[1,3,2048,1792]{3,2,1,0:T(8,128)(2,1)} %refs_0_.3), custom_call_target="tpu_custom_call" | custom-call | flops 1000000 | tf_op jit(solution)/shard_map/hidden/pallas_call | solution.py:500
  49.0 2.2 %hidden.5 = (bf16[128,1792]{1,0:T(8,128)(2,1)S(1)}, bf16[1024,1792]{1,0:T(8,128)(2,1)S(1)}) custom-call(bf16[128,2048]{1,0:T(8,128)(2,1)S(1)} %collective-permute-done.20.x_ref, bf16[2048,1792]{1,0:T(8,128)(2,1)S(1)} %get-tuple-element.92.gate_ref, bf16[2048,1792]{1,0:T(8,128)(2,1)S(1)} %get-tuple-element.93.up_ref, bf16[1,3,2048,1792]{3,2,1,0:T(8,128)(2,1)} %refs_0_.3, ...), custom_call_target="tpu_custom_call" | custom-call | flops 1000000 | tf_op jit(solution)/shard_map/hidden/pallas_call | solution.py:500
  51.2 2.1 %down.2 = (f32[128,2048]{1,0:T(8,128)S(1)}, bf16[128,2048]{1,0:T(8,128)(2,1)S(1)}) custom-call(bf16[128,1792]{1,0:T(8,128)(2,1)S(1)} %get-tuple-element.94.refs_1_.hidden_own_ref, bf16[128,1792]{1,0:T(8,128)(2,1)S(1)} %get-tuple-element.95.hidden_other_ref, bf16[1024,1792]{1,0:T(8,128)(2,1)S(1)} %get-tuple-element.96.low_ref, ...), custom_call_target="tpu_custom_call" | custom-call | flops 1000000 | tf_op jit(solution)/shard_map/down/pallas_call | solution.py:535
  54.2 2.2 %hidden.6.refs_0_.hidden_own_ref = bf16[128,1792]{1,0:T(8,128)(2,1)S(1)} custom-call(bf16[128,2048]{1,0:T(8,128)(2,1)S(1)} %norm.3.x_ref, bf16[2048,1792]{1,0:T(8,128)(2,1)S(1)} %get-tuple-element.92.gate_ref, bf16[2048,1792]{1,0:T(8,128)(2,1)S(1)} %get-tuple-element.93.up_ref), custom_call_target="tpu_custom_call" | custom-call | flops 1000000 | tf_op jit(solution)/shard_map/hidden/pallas_call | solution.py:500
  56.6 1.8 %collective-permute-start.24 = (bf16[128,512]{1,0:T(8,128)(2,1)S(1)}, bf16[128,512]{1,0:T(8,128)(2,1)S(1)}, u32[]{:S(2)}, u32[]{:S(2)}) collective-permute-start(bf16[128,512]{1,0:T(8,128)(2,1)S(1)} %get-tuple-element.103), channel_id=1, source_target_pairs={{0,1},{1,0},{2,3},{3,2},{4,5},{5,4},{6,7},{7,6},{8,9},{9,8},{10,11... | collective-permute-start | bytes 393224 | tf_op jit(solution)/shard_map/ppermute | solution.py:33
  60.1 2.4 %hidden.7.hidden_other_ref = bf16[128,1792]{1,0:T(8,128)(2,1)S(1)} custom-call(bf16[128,2048]{1,0:T(8,128)(2,1)S(1)} %collective-permute-done.21.x_ref, bf16[2048,1792]{1,0:T(8,128)(2,1)S(1)} %get-tuple-element.92.gate_ref, bf16[2048,1792]{1,0:T(8,128)(2,1)S(1)} %get-tuple-element.93.up_ref, f32[128,512]{1,0:T(8,128)S(1)} %get-tuple-element.100.refs_0_), custom_call_target="tpu_custom_call" | custom-call | flops 1000000 | tf_op jit(solution)/shard_map/hidden/pallas_call | solution.py:500
  62.6 2.1 %down.3 = (f32[128,2048]{1,0:T(8,128)S(1)}, bf16[128,2048]{1,0:T(8,128)(2,1)S(1)}) custom-call(bf16[128,1792]{1,0:T(8,128)(2,1)S(1)} %hidden.6.refs_0_.hidden_own_ref, bf16[128,1792]{1,0:T(8,128)(2,1)S(1)} %hidden.7.hidden_other_ref, bf16[1024,1792]{1,0:T(8,128)(2,1)S(1)} %get-tuple-element.96.low_ref, bf16[1024,1792]{1,0:T(8,128)(2,1)S(1)} %get-tuple-element.97.high_ref), custom_call_target="tpu_custom_call" | custom-call | flops 1000000 | tf_op jit(solution)/shard_map/down/pallas_call | solution.py:535
  64.8 2.0 %collective-permute-done.25.refs_2_ = bf16[128,512]{1,0:T(8,128)(2,1)S(1)} collective-permute-done((bf16[128,512]{1,0:T(8,128)(2,1)S(1)}, bf16[128,512]{1,0:T(8,128)(2,1)S(1)}, u32[]{:S(2)}, u32[]{:S(2)}) %collective-permute-start.25) | collective-permute-done | bytes 131104 | tf_op jit(solution)/shard_map/ppermute | solution.py:33
  70.5 1.8 %collective-permute-start.31 = (bf16[64,512]{1,0:T(8,128)(2,1)S(1)}, bf16[64,512]{1,0:T(8,128)(2,1)S(1)}, u32[]{:S(2)}, u32[]{:S(2)}) collective-permute-start(bf16[64,512]{1,0:T(8,128)(2,1)S(1)} %get-tuple-element.106.refs_1_), channel_id=1, source_target_pairs={{0,8},{4,12},{8,0},{12,4},{1,9},{5,13},{9,1},{13,5},{2,10},{6,14},... | collective-permute-start | bytes 196616 | tf_op jit(solution)/shard_map/ppermute | solution.py:33
  72.3 3.1 %collective-permute-start.32 = (bf16[64,512]{1,0:T(8,128)(2,1)S(1)}, bf16[64,512]{1,0:T(8,128)(2,1)S(1)}, u32[]{:S(2)}, u32[]{:S(2)}) collective-permute-start(bf16[64,512]{1,0:T(8,128)(2,1)S(1)} %get-tuple-element.113), channel_id=1, source_target_pairs={{0,12},{4,8},{8,4},{12,0},{1,13},{5,9},{9,5},{13,1},{2,14},{6,10},... | collective-permute-start | bytes 196616 | tf_op jit(solution)/shard_map/ppermute | solution.py:33
  76.7 2.0 %collective-permute-start.30 = (bf16[64,512]{1,0:T(8,128)(2,1)S(1)}, bf16[64,512]{1,0:T(8,128)(2,1)S(1)}, u32[]{:S(2)}, u32[]{:S(2)}) collective-permute-start(bf16[64,512]{1,0:T(8,128)(2,1)S(1)} %get-tuple-element.112), channel_id=1, source_target_pairs={{0,4},{4,0},{8,12},{12,8},{1,5},{5,1},{9,13},{13,9},{2,6},{6,2},{1... | collective-permute-start | bytes 196616 | tf_op jit(solution)/shard_map/ppermute | solution.py:33
  78.7 2.3 %collective-permute-done.30.refs_1_ = bf16[64,512]{1,0:T(8,128)(2,1)S(1)} collective-permute-done((bf16[64,512]{1,0:T(8,128)(2,1)S(1)}, bf16[64,512]{1,0:T(8,128)(2,1)S(1)}, u32[]{:S(2)}, u32[]{:S(2)}) %collective-permute-start.30) | collective-permute-done | bytes 65568 | tf_op jit(solution)/shard_map/ppermute | solution.py:33
  (71 shorter events, 25.1 us)
Async XLA Ops:
  4.3 6.7 %collective-permute-start.3 = (bf16[144,256]{1,0:T(8,128)(2,1)S(1)}, bf16[144,256]{1,0:T(8,128)(2,1)S(1)}, u32[]{:S(2)}, u32[]{:S(2)}) collective-permute-start(bf16[144,256]{1,0:T(8,128)(2,1)S(1)} %get-tuple-element.65.refs_0_), channel_id=1, source_target_pairs={{0,1},{1,0},{2,3},{3,2},{4,5},{5,4},{6,7},{7,6},{8,9},{9,8},{10,11... | collective-permute-start | bytes 221192 | tf_op jit(solution)/shard_map/ppermute | solution.py:33
  19.7 6.7 %collective-permute-start.5 = (bf16[128,512]{1,0:T(8,128)(2,1)S(1)}, bf16[128,512]{1,0:T(8,128)(2,1)S(1)}, u32[]{:S(2)}, u32[]{:S(2)}) collective-permute-start(bf16[128,512]{1,0:T(8,128)(2,1)S(1)} %get-tuple-element.83), channel_id=1, source_target_pairs={{0,1},{1,0},{2,3},{3,2},{4,5},{5,4},{6,7},{7,6},{8,9},{9,8},{10,11... | collective-permute-start | bytes 393224 | tf_op jit(solution)/shard_map/ppermute | solution.py:33
  20.3 6.1 %collective-permute-start.6 = (bf16[128,512]{1,0:T(8,128)(2,1)S(1)}, bf16[128,512]{1,0:T(8,128)(2,1)S(1)}, u32[]{:S(2)}, u32[]{:S(2)}) collective-permute-start(bf16[128,512]{1,0:T(8,128)(2,1)S(1)} %get-tuple-element.84), channel_id=1, source_target_pairs={{0,2},{1,3},{2,0},{3,1},{4,6},{5,7},{6,4},{7,5},{8,10},{9,11},{10,... | collective-permute-start | bytes 393224 | tf_op jit(solution)/shard_map/ppermute | solution.py:33
  21.0 7.4 %collective-permute-start.7 = (bf16[128,512]{1,0:T(8,128)(2,1)S(1)}, bf16[128,512]{1,0:T(8,128)(2,1)S(1)}, u32[]{:S(2)}, u32[]{:S(2)}) collective-permute-start(bf16[128,512]{1,0:T(8,128)(2,1)S(1)} %get-tuple-element.85), channel_id=1, source_target_pairs={{0,3},{1,2},{2,1},{3,0},{4,7},{5,6},{6,5},{7,4},{8,11},{9,10},{10,... | collective-permute-start | bytes 393224 | tf_op jit(solution)/shard_map/ppermute | solution.py:33
  28.6 7.3 %collective-permute-start.12 = (bf16[64,512]{1,0:T(8,128)(2,1)S(1)}, bf16[64,512]{1,0:T(8,128)(2,1)S(1)}, u32[]{:S(2)}, u32[]{:S(2)}) collective-permute-start(bf16[64,512]{1,0:T(8,128)(2,1)S(1)} %get-tuple-element.90), channel_id=1, source_target_pairs={{0,8},{4,12},{8,0},{12,4},{1,9},{5,13},{9,1},{13,5},{2,10},{6,14},... | collective-permute-start | bytes 196616 | tf_op jit(solution)/shard_map/ppermute | solution.py:33
  31.3 8.1 %collective-permute-start.16 = (bf16[64,512]{1,0:T(8,128)(2,1)S(1)}, bf16[64,512]{1,0:T(8,128)(2,1)S(1)}, u32[]{:S(2)}, u32[]{:S(2)}) collective-permute-start(bf16[64,512]{1,0:T(8,128)(2,1)S(1)} %get-tuple-element.91), channel_id=1, source_target_pairs={{0,12},{4,8},{8,4},{12,0},{1,13},{5,9},{9,5},{13,1},{2,14},{6,10},... | collective-permute-start | bytes 196616 | tf_op jit(solution)/shard_map/ppermute | solution.py:33
  32.6 8.2 %collective-permute-start.8 = (bf16[64,512]{1,0:T(8,128)(2,1)S(1)}, bf16[64,512]{1,0:T(8,128)(2,1)S(1)}, u32[]{:S(2)}, u32[]{:S(2)}) collective-permute-start(bf16[64,512]{1,0:T(8,128)(2,1)S(1)} %get-tuple-element.88), channel_id=1, source_target_pairs={{0,4},{4,0},{8,12},{12,8},{1,5},{5,1},{9,13},{13,9},{2,6},{6,2},{1... | collective-permute-start | bytes 196616 | tf_op jit(solution)/shard_map/ppermute | solution.py:33
  35.9 5.3 %collective-permute-start.15 = (bf16[64,512]{1,0:T(8,128)(2,1)S(1)}, bf16[64,512]{1,0:T(8,128)(2,1)S(1)}, u32[]{:S(2)}, u32[]{:S(2)}) collective-permute-start(bf16[64,512]{1,0:T(8,128)(2,1)S(1)} %collective-permute-done.12.refs_0_), channel_id=1, source_target_pairs={{0,3},{1,2},{2,1},{3,0},{4,7},{5,6},{6,5},{7,4},{8,11},{9,10},{10,... | collective-permute-start | bytes 196616 | tf_op jit(solution)/shard_map/ppermute | solution.py:33
  37.3 5.6 %collective-permute-start.14 = (bf16[64,512]{1,0:T(8,128)(2,1)S(1)}, bf16[64,512]{1,0:T(8,128)(2,1)S(1)}, u32[]{:S(2)}, u32[]{:S(2)}) collective-permute-start(bf16[64,512]{1,0:T(8,128)(2,1)S(1)} %collective-permute-done.12.refs_0_), channel_id=1, source_target_pairs={{0,2},{1,3},{2,0},{3,1},{4,6},{5,7},{6,4},{7,5},{8,10},{9,11},{10,... | collective-permute-start | bytes 196616 | tf_op jit(solution)/shard_map/ppermute | solution.py:33
  37.3 7.1 %collective-permute-start.13 = (bf16[64,512]{1,0:T(8,128)(2,1)S(1)}, bf16[64,512]{1,0:T(8,128)(2,1)S(1)}, u32[]{:S(2)}, u32[]{:S(2)}) collective-permute-start(bf16[64,512]{1,0:T(8,128)(2,1)S(1)} %collective-permute-done.12.refs_0_), channel_id=1, source_target_pairs={{0,1},{1,0},{2,3},{3,2},{4,5},{5,4},{6,7},{7,6},{8,9},{9,8},{10,11... | collective-permute-start | bytes 196616 | tf_op jit(solution)/shard_map/ppermute | solution.py:33
  39.4 5.8 %collective-permute-start.19 = (bf16[64,512]{1,0:T(8,128)(2,1)S(1)}, bf16[64,512]{1,0:T(8,128)(2,1)S(1)}, u32[]{:S(2)}, u32[]{:S(2)}) collective-permute-start(bf16[64,512]{1,0:T(8,128)(2,1)S(1)} %collective-permute-done.16.refs_0_.refs_4_), channel_id=1, source_target_pairs={{0,3},{1,2},{2,1},{3,0},{4,7},{5,6},{6,5},{7,4},{8,11},{9,10},{10,... | collective-permute-start | bytes 196616 | tf_op jit(solution)/shard_map/ppermute | solution.py:33
  40.8 5.6 %collective-permute-start.18 = (bf16[64,512]{1,0:T(8,128)(2,1)S(1)}, bf16[64,512]{1,0:T(8,128)(2,1)S(1)}, u32[]{:S(2)}, u32[]{:S(2)}) collective-permute-start(bf16[64,512]{1,0:T(8,128)(2,1)S(1)} %collective-permute-done.16.refs_0_.refs_4_), channel_id=1, source_target_pairs={{0,2},{1,3},{2,0},{3,1},{4,6},{5,7},{6,4},{7,5},{8,10},{9,11},{10,... | collective-permute-start | bytes 196616 | tf_op jit(solution)/shard_map/ppermute | solution.py:33
  42.9 10.9 %collective-permute-start.11 = (bf16[128,512]{1,0:T(8,128)(2,1)S(1)}, bf16[128,512]{1,0:T(8,128)(2,1)S(1)}, u32[]{:S(2)}, u32[]{:S(2)}) collective-permute-start(bf16[128,512]{1,0:T(8,128)(2,1)S(1)} %stack.1.refs_1_.refs_0_), channel_id=1, source_target_pairs={{0,3},{1,2},{2,1},{3,0},{4,7},{5,6},{6,5},{7,4},{8,11},{9,10},{10,... | collective-permute-start | bytes 393224 | tf_op jit(solution)/shard_map/ppermute | solution.py:33
  44.4 9.4 %collective-permute-start.10 = (bf16[128,512]{1,0:T(8,128)(2,1)S(1)}, bf16[128,512]{1,0:T(8,128)(2,1)S(1)}, u32[]{:S(2)}, u32[]{:S(2)}) collective-permute-start(bf16[128,512]{1,0:T(8,128)(2,1)S(1)} %stack.1.refs_1_.refs_0_), channel_id=1, source_target_pairs={{0,2},{1,3},{2,0},{3,1},{4,6},{5,7},{6,4},{7,5},{8,10},{9,11},{10,... | collective-permute-start | bytes 393224 | tf_op jit(solution)/shard_map/ppermute | solution.py:33
  45.2 8.7 %collective-permute-start.9 = (bf16[128,512]{1,0:T(8,128)(2,1)S(1)}, bf16[128,512]{1,0:T(8,128)(2,1)S(1)}, u32[]{:S(2)}, u32[]{:S(2)}) collective-permute-start(bf16[128,512]{1,0:T(8,128)(2,1)S(1)} %stack.1.refs_1_.refs_0_), channel_id=1, source_target_pairs={{0,1},{1,0},{2,3},{3,2},{4,5},{5,4},{6,7},{7,6},{8,9},{9,8},{10,11... | collective-permute-start | bytes 393224 | tf_op jit(solution)/shard_map/ppermute | solution.py:33
  54.1 6.0 %collective-permute-start.21 = (bf16[128,2048]{1,0:T(8,128)(2,1)S(1)}, bf16[128,2048]{1,0:T(8,128)(2,1)S(1)}, u32[]{:S(2)}, u32[]{:S(2)}) collective-permute-start(bf16[128,2048]{1,0:T(8,128)(2,1)S(1)} %norm.3.x_ref), channel_id=1, source_target_pairs={{0,16},{16,0},{1,17},{17,1},{2,18},{18,2},{3,19},{19,3},{4,20},{20... | collective-permute-start | bytes 1572872 | tf_op jit(solution)/shard_map/ppermute | solution.py:33
  56.6 8.2 %collective-permute-start.24 = (bf16[128,512]{1,0:T(8,128)(2,1)S(1)}, bf16[128,512]{1,0:T(8,128)(2,1)S(1)}, u32[]{:S(2)}, u32[]{:S(2)}) collective-permute-start(bf16[128,512]{1,0:T(8,128)(2,1)S(1)} %get-tuple-element.103), channel_id=1, source_target_pairs={{0,1},{1,0},{2,3},{3,2},{4,5},{5,4},{6,7},{7,6},{8,9},{9,8},{10,11... | collective-permute-start | bytes 393224 | tf_op jit(solution)/shard_map/ppermute | solution.py:33
  58.3 8.4 %collective-permute-start.25 = (bf16[128,512]{1,0:T(8,128)(2,1)S(1)}, bf16[128,512]{1,0:T(8,128)(2,1)S(1)}, u32[]{:S(2)}, u32[]{:S(2)}) collective-permute-start(bf16[128,512]{1,0:T(8,128)(2,1)S(1)} %get-tuple-element.104), channel_id=1, source_target_pairs={{0,2},{1,3},{2,0},{3,1},{4,6},{5,7},{6,4},{7,5},{8,10},{9,11},{10,... | collective-permute-start | bytes 393224 | tf_op jit(solution)/shard_map/ppermute | solution.py:33
  58.9 7.8 %collective-permute-start.26 = (bf16[128,512]{1,0:T(8,128)(2,1)S(1)}, bf16[128,512]{1,0:T(8,128)(2,1)S(1)}, u32[]{:S(2)}, u32[]{:S(2)}) collective-permute-start(bf16[128,512]{1,0:T(8,128)(2,1)S(1)} %get-tuple-element.105), channel_id=1, source_target_pairs={{0,3},{1,2},{2,1},{3,0},{4,7},{5,6},{6,5},{7,4},{8,11},{9,10},{10,... | collective-permute-start | bytes 393224 | tf_op jit(solution)/shard_map/ppermute | solution.py:33
  67.0 8.4 %collective-permute-start.27 = (bf16[128,512]{1,0:T(8,128)(2,1)S(1)}, bf16[128,512]{1,0:T(8,128)(2,1)S(1)}, u32[]{:S(2)}, u32[]{:S(2)}) collective-permute-start(bf16[128,512]{1,0:T(8,128)(2,1)S(1)} %get-tuple-element.108), channel_id=1, source_target_pairs={{0,1},{1,0},{2,3},{3,2},{4,5},{5,4},{6,7},{7,6},{8,9},{9,8},{10,11... | collective-permute-start | bytes 393224 | tf_op jit(solution)/shard_map/ppermute | solution.py:33
  68.5 8.1 %collective-permute-start.28 = (bf16[128,512]{1,0:T(8,128)(2,1)S(1)}, bf16[128,512]{1,0:T(8,128)(2,1)S(1)}, u32[]{:S(2)}, u32[]{:S(2)}) collective-permute-start(bf16[128,512]{1,0:T(8,128)(2,1)S(1)} %get-tuple-element.109), channel_id=1, source_target_pairs={{0,2},{1,3},{2,0},{3,1},{4,6},{5,7},{6,4},{7,5},{8,10},{9,11},{10,... | collective-permute-start | bytes 393224 | tf_op jit(solution)/shard_map/ppermute | solution.py:33
  69.1 7.5 %collective-permute-start.29 = (bf16[128,512]{1,0:T(8,128)(2,1)S(1)}, bf16[128,512]{1,0:T(8,128)(2,1)S(1)}, u32[]{:S(2)}, u32[]{:S(2)}) collective-permute-start(bf16[128,512]{1,0:T(8,128)(2,1)S(1)} %get-tuple-element.110), channel_id=1, source_target_pairs={{0,3},{1,2},{2,1},{3,0},{4,7},{5,6},{6,5},{7,4},{8,11},{9,10},{10,... | collective-permute-start | bytes 393224 | tf_op jit(solution)/shard_map/ppermute | solution.py:33
  70.5 8.2 %collective-permute-start.31 = (bf16[64,512]{1,0:T(8,128)(2,1)S(1)}, bf16[64,512]{1,0:T(8,128)(2,1)S(1)}, u32[]{:S(2)}, u32[]{:S(2)}) collective-permute-start(bf16[64,512]{1,0:T(8,128)(2,1)S(1)} %get-tuple-element.106.refs_1_), channel_id=1, source_target_pairs={{0,8},{4,12},{8,0},{12,4},{1,9},{5,13},{9,1},{13,5},{2,10},{6,14},... | collective-permute-start | bytes 196616 | tf_op jit(solution)/shard_map/ppermute | solution.py:33
  72.3 6.4 %collective-permute-start.32 = (bf16[64,512]{1,0:T(8,128)(2,1)S(1)}, bf16[64,512]{1,0:T(8,128)(2,1)S(1)}, u32[]{:S(2)}, u32[]{:S(2)}) collective-permute-start(bf16[64,512]{1,0:T(8,128)(2,1)S(1)} %get-tuple-element.113), channel_id=1, source_target_pairs={{0,12},{4,8},{8,4},{12,0},{1,13},{5,9},{9,5},{13,1},{2,14},{6,10},... | collective-permute-start | bytes 196616 | tf_op jit(solution)/shard_map/ppermute | solution.py:33
  (11 other events, 50.9 us)

commit v10 on v9

--- a/solution.py
+++ b/solution.py
@@ -306,7 +306,7 @@
         return elapsed, tuple(new)
 
     zero = jnp.zeros((tiles, 128), F32)
-    _, states = lax.fori_loop(0, rows, step, (zero, (zero,) * STATE), unroll=16)
+    _, states = lax.fori_loop(0, rows, step, (zero, (zero,) * STATE), unroll=32)
     for n in range(STATE):
         state_ref[n] = states[n]
     expert_copy.wait()

time: 82.2 us -> 82.1 us (level)
  no operation moved by 1% of the time
where the time goes in v10:
time: 82.1 us; the launch traced here: 81.9 us
  starting transfers between devices  39.9 us (49%)
  Pallas kernels  27.8 us (34%)
  waiting for transfers between devices  13.9 us (17%)
    ppermute x31, starting transfers between devices, swap(): lax.ppermute(block, axis, [(i, i ^ k) for i in range(lax.axis_size(axis))])  36.2 us
    ppermute x31, waiting for transfers between devices, swap(): lax.ppermute(block, axis, [(i, i ^ k) for i in range(lax.axis_size(axis))])  13.8 us
    pallas_call x4, Pallas kernels, hidden_units(): pl.pallas_call(functools.partial(hidden_kernel, part), out_shape=made, in...  9.07 us
    pallas_call x2, Pallas kernels, down_sums(): pl.pallas_call(down_kernel, out_shape=(shaped((rows, model), F32), shaped...  4.18 us
    pallas_call x1, Pallas kernels, scan(): pl.pallas_call(functools.partial(scan_kernel, len(pieces)), out_shape=(sh...  3.57 us
    pallas_call x1, Pallas kernels, route(): pl.pallas_call(route_kernel, out_shape=(shaped((rows, slots), BF16), shap...  3.09 us
    pallas_call x1, Pallas kernels, prepare(): pl.pallas_call(prepare_kernel, out_shape=(shaped((rows, channels), F32),...  2.76 us
    ppermute x1, starting transfers between devices, body(): before = lax.ppermute(local, 'ctx', [(0, 1)])  2.36 us
  transfers between devices with their start and end apart: 33, of which 9 were waited for; matrix products, arithmetic and copies ran while one was open for 0% of the time, Pallas kernels for 27%

profile of v10, /device:TPU:0, one launch (start us, length us, event | category | flops | bytes accessed | tf_op | source)
XLA Modules:
  0.0 81.9 jit_solution(2344289750022184416)
XLA Ops:
  0.0 2.4 %collective-permute-start = (bf16[128,1024]{1,0:T(8,128)(2,1)}, bf16[128,1024]{1,0:T(8,128)(2,1)S(1)}, u32[]{:S(2)}, u32[]{:S(2)}) collective-permute-start(bf16[128,1024]{1,0:T(8,128)(2,1)} %bitcast.20), channel_id=1, source_target_pairs={{0,16},{1,17},{2,18},{3,19},{4,20},{5,21},{6,22},{7,23},{8,24},{9,... | collective-permute-start | bytes 786440 | tf_op jit(solution)/shard_map/ppermute | solution.py:638
  4.3 2.4 %collective-permute-start.3 = (bf16[144,256]{1,0:T(8,128)(2,1)S(1)}, bf16[144,256]{1,0:T(8,128)(2,1)S(1)}, u32[]{:S(2)}, u32[]{:S(2)}) collective-permute-start(bf16[144,256]{1,0:T(8,128)(2,1)S(1)} %get-tuple-element.65.refs_0_), channel_id=1, source_target_pairs={{0,1},{1,0},{2,3},{3,2},{4,5},{5,4},{6,7},{7,6},{8,9},{9,8},{10,11... | collective-permute-start | bytes 221192 | tf_op jit(solution)/shard_map/ppermute | solution.py:33
  8.2 2.8 %prepare.1 = (f32[128,1024]{1,0:T(8,128)S(1)}, f32[16,8,128]{2,1,0:T(8,128)S(1)}, f32[128,1024]{1,0:T(8,128)S(1)}, f32[1,1024]{1,0:T(1,128)S(1)}, bf16[256,1024]...) custom-call(bf16[128,1024]{1,0:T(8,128)(2,1)S(1)} %get-tuple-element.66.xconv_, ...), custom_call_target="tpu_custom_call" | custom-call | flops 1000000 | bytes 6000000 | tf_op jit(solution)/shard_map/prepare/pallas_call | solution.py:240
  11.0 2.4 %collective-permute-done.1.refs_1_ = bf16[144,256]{1,0:T(8,128)(2,1)S(1)} collective-permute-done((bf16[144,256]{1,0:T(8,128)(2,1)S(1)}, bf16[144,256]{1,0:T(8,128)(2,1)S(1)}, u32[]{:S(2)}, u32[]{:S(2)}) %collective-permute-start.1) | collective-permute-done | bytes 73760 | tf_op jit(solution)/shard_map/ppermute | solution.py:33
  13.5 3.6 %scan.1 = (f32[128,8,128]{2,1,0:T(8,128)S(1)}, f32[128,8,128]{2,1,0:T(8,128)S(1)}, f32[128,16,128]{2,1,0:T(8,128)S(1)}, f32[16,8,128]{2,1,0:T(8,128)S(1)}, bf16[2048,1792]{1,0:T(8,128)(2,1)S(1)}) custom-call(bf16[144,256]{1,0:T(8,128)(2,1)S(1)} %get-tuple-element.65.refs_0_, bf16[144,256]{1,0:T(8,128)(2,1)S(1)} %collective-permute-done.1.refs_1_, ...), custom_call_target="tpu_custom_call" | custom-call | flops 1000000 | bytes 14000000 | tf_op jit(solution)/shard_map/scan/pallas_call | solution.py:318
  20.9 2.3 %collective-permute-start.7 = (bf16[128,512]{1,0:T(8,128)(2,1)S(1)}, bf16[128,512]{1,0:T(8,128)(2,1)S(1)}, u32[]{:S(2)}, u32[]{:S(2)}) collective-permute-start(bf16[128,512]{1,0:T(8,128)(2,1)S(1)} %get-tuple-element.85), channel_id=1, source_target_pairs={{0,3},{1,2},{2,1},{3,0},{4,7},{5,6},{6,5},{7,4},{8,11},{9,10},{10,... | collective-permute-start | bytes 393224 | tf_op jit(solution)/shard_map/ppermute | solution.py:33
  23.2 3.1 %route.1 = (bf16[128,256]{1,0:T(8,128)(2,1)S(1)}, bf16[128,256]{1,0:T(8,128)(2,1)S(1)}, bf16[256,128]{1,0:T(8,128)(2,1)S(1)}, bf16[2048,1792]{1,0:T(8,128)(2,1)S(1)}) custom-call(s32[2,128]{1,0:T(2,128)S(1)} %bitcast.15, bf16[1,3,2048,1792]{3,2,1,0:T(8,128)(2,1)} %refs_0_.3), custom_call_target="tpu_custom_call" | custom-call | flops 1000000 | bytes 8000000 | tf_op jit(solution)/shard_map/route/pallas_call | solution.py:123
  26.3 2.0 %collective-permute-done.7.refs_3_ = bf16[128,512]{1,0:T(8,128)(2,1)S(1)} collective-permute-done((bf16[128,512]{1,0:T(8,128)(2,1)S(1)}, bf16[128,512]{1,0:T(8,128)(2,1)S(1)}, u32[]{:S(2)}, u32[]{:S(2)}) %collective-permute-start.7) | collective-permute-done | bytes 131104 | tf_op jit(solution)/shard_map/ppermute | solution.py:33
  28.6 2.6 %collective-permute-start.12 = (bf16[64,512]{1,0:T(8,128)(2,1)S(1)}, bf16[64,512]{1,0:T(8,128)(2,1)S(1)}, u32[]{:S(2)}, u32[]{:S(2)}) collective-permute-start(bf16[64,512]{1,0:T(8,128)(2,1)S(1)} %get-tuple-element.90), channel_id=1, source_target_pairs={{0,8},{4,12},{8,0},{12,4},{1,9},{5,13},{9,1},{13,5},{2,10},{6,14},... | collective-permute-start | bytes 196616 | tf_op jit(solution)/shard_map/ppermute | solution.py:33
  32.8 3.0 %collective-permute-done.12.refs_0_ = bf16[64,512]{1,0:T(8,128)(2,1)S(1)} collective-permute-done((bf16[64,512]{1,0:T(8,128)(2,1)S(1)}, bf16[64,512]{1,0:T(8,128)(2,1)S(1)}, u32[]{:S(2)}, u32[]{:S(2)}) %collective-permute-start.12) | collective-permute-done | bytes 65568 | tf_op jit(solution)/shard_map/ppermute | solution.py:33
  37.3 2.0 %collective-permute-start.13 = (bf16[64,512]{1,0:T(8,128)(2,1)S(1)}, bf16[64,512]{1,0:T(8,128)(2,1)S(1)}, u32[]{:S(2)}, u32[]{:S(2)}) collective-permute-start(bf16[64,512]{1,0:T(8,128)(2,1)S(1)} %collective-permute-done.12.refs_0_), channel_id=1, source_target_pairs={{0,1},{1,0},{2,3},{3,2},{4,5},{5,4},{6,7},{7,6},{8,9},{9,8},{10,11... | collective-permute-start | bytes 196616 | tf_op jit(solution)/shard_map/ppermute | solution.py:33
  41.1 1.8 %collective-permute-start.17 = (bf16[64,512]{1,0:T(8,128)(2,1)S(1)}, bf16[64,512]{1,0:T(8,128)(2,1)S(1)}, u32[]{:S(2)}, u32[]{:S(2)}) collective-permute-start(bf16[64,512]{1,0:T(8,128)(2,1)S(1)} %collective-permute-done.16.refs_0_.refs_4_), channel_id=1, source_target_pairs={{0,1},{1,0},{2,3},{3,2},{4,5},{5,4},{6,7},{7,6},{8,9},{9,8},{10,11... | collective-permute-start | bytes 196616 | tf_op jit(solution)/shard_map/ppermute | solution.py:33
  46.7 2.2 %hidden.4 = (bf16[128,1792]{1,0:T(8,128)(2,1)S(1)}, bf16[1024,1792]{1,0:T(8,128)(2,1)S(1)}) custom-call(bf16[128,2048]{1,0:T(8,128)(2,1)S(1)} %norm.2.x_ref.refs_0_, bf16[2048,1792]{1,0:T(8,128)(2,1)S(1)} %get-tuple-element.92.gate_ref, bf16[2048,1792]{1,0:T(8,128)(2,1)S(1)} %get-tuple-element.93.up_ref, bf16[1,3,2048,1792]{3,2,1,0:T(8,128)(2,1)} %refs_0_.3), custom_call_target="tpu_custom_call" | custom-call | flops 1000000 | tf_op jit(solution)/shard_map/hidden/pallas_call | solution.py:500
  49.0 2.2 %hidden.5 = (bf16[128,1792]{1,0:T(8,128)(2,1)S(1)}, bf16[1024,1792]{1,0:T(8,128)(2,1)S(1)}) custom-call(bf16[128,2048]{1,0:T(8,128)(2,1)S(1)} %collective-permute-done.20.x_ref, bf16[2048,1792]{1,0:T(8,128)(2,1)S(1)} %get-tuple-element.92.gate_ref, bf16[2048,1792]{1,0:T(8,128)(2,1)S(1)} %get-tuple-element.93.up_ref, bf16[1,3,2048,1792]{3,2,1,0:T(8,128)(2,1)} %refs_0_.3, ...), custom_call_target="tpu_custom_call" | custom-call | flops 1000000 | tf_op jit(solution)/shard_map/hidden/pallas_call | solution.py:500
  51.2 2.1 %down.2 = (f32[128,2048]{1,0:T(8,128)S(1)}, bf16[128,2048]{1,0:T(8,128)(2,1)S(1)}) custom-call(bf16[128,1792]{1,0:T(8,128)(2,1)S(1)} %get-tuple-element.94.refs_1_.hidden_own_ref, bf16[128,1792]{1,0:T(8,128)(2,1)S(1)} %get-tuple-element.95.hidden_other_ref, bf16[1024,1792]{1,0:T(8,128)(2,1)S(1)} %get-tuple-element.96.low_ref, ...), custom_call_target="tpu_custom_call" | custom-call | flops 1000000 | tf_op jit(solution)/shard_map/down/pallas_call | solution.py:535
  54.2 2.2 %hidden.6.refs_0_.hidden_own_ref = bf16[128,1792]{1,0:T(8,128)(2,1)S(1)} custom-call(bf16[128,2048]{1,0:T(8,128)(2,1)S(1)} %norm.3.x_ref, bf16[2048,1792]{1,0:T(8,128)(2,1)S(1)} %get-tuple-element.92.gate_ref, bf16[2048,1792]{1,0:T(8,128)(2,1)S(1)} %get-tuple-element.93.up_ref), custom_call_target="tpu_custom_call" | custom-call | flops 1000000 | tf_op jit(solution)/shard_map/hidden/pallas_call | solution.py:500
  56.5 1.7 %collective-permute-start.24 = (bf16[128,512]{1,0:T(8,128)(2,1)S(1)}, bf16[128,512]{1,0:T(8,128)(2,1)S(1)}, u32[]{:S(2)}, u32[]{:S(2)}) collective-permute-start(bf16[128,512]{1,0:T(8,128)(2,1)S(1)} %get-tuple-element.103), channel_id=1, source_target_pairs={{0,1},{1,0},{2,3},{3,2},{4,5},{5,4},{6,7},{7,6},{8,9},{9,8},{10,11... | collective-permute-start | bytes 393224 | tf_op jit(solution)/shard_map/ppermute | solution.py:33
  60.1 2.4 %hidden.7.hidden_other_ref = bf16[128,1792]{1,0:T(8,128)(2,1)S(1)} custom-call(bf16[128,2048]{1,0:T(8,128)(2,1)S(1)} %collective-permute-done.21.x_ref, bf16[2048,1792]{1,0:T(8,128)(2,1)S(1)} %get-tuple-element.92.gate_ref, bf16[2048,1792]{1,0:T(8,128)(2,1)S(1)} %get-tuple-element.93.up_ref, f32[128,512]{1,0:T(8,128)S(1)} %get-tuple-element.100.refs_0_), custom_call_target="tpu_custom_call" | custom-call | flops 1000000 | tf_op jit(solution)/shard_map/hidden/pallas_call | solution.py:500
  62.5 2.1 %down.3 = (f32[128,2048]{1,0:T(8,128)S(1)}, bf16[128,2048]{1,0:T(8,128)(2,1)S(1)}) custom-call(bf16[128,1792]{1,0:T(8,128)(2,1)S(1)} %hidden.6.refs_0_.hidden_own_ref, bf16[128,1792]{1,0:T(8,128)(2,1)S(1)} %hidden.7.hidden_other_ref, bf16[1024,1792]{1,0:T(8,128)(2,1)S(1)} %get-tuple-element.96.low_ref, bf16[1024,1792]{1,0:T(8,128)(2,1)S(1)} %get-tuple-element.97.high_ref), custom_call_target="tpu_custom_call" | custom-call | flops 1000000 | tf_op jit(solution)/shard_map/down/pallas_call | solution.py:535
  64.7 1.9 %collective-permute-done.25.refs_2_ = bf16[128,512]{1,0:T(8,128)(2,1)S(1)} collective-permute-done((bf16[128,512]{1,0:T(8,128)(2,1)S(1)}, bf16[128,512]{1,0:T(8,128)(2,1)S(1)}, u32[]{:S(2)}, u32[]{:S(2)}) %collective-permute-start.25) | collective-permute-done | bytes 131104 | tf_op jit(solution)/shard_map/ppermute | solution.py:33
  70.5 1.8 %collective-permute-start.31 = (bf16[64,512]{1,0:T(8,128)(2,1)S(1)}, bf16[64,512]{1,0:T(8,128)(2,1)S(1)}, u32[]{:S(2)}, u32[]{:S(2)}) collective-permute-start(bf16[64,512]{1,0:T(8,128)(2,1)S(1)} %get-tuple-element.106.refs_1_), channel_id=1, source_target_pairs={{0,8},{4,12},{8,0},{12,4},{1,9},{5,13},{9,1},{13,5},{2,10},{6,14},... | collective-permute-start | bytes 196616 | tf_op jit(solution)/shard_map/ppermute | solution.py:33
  72.3 3.0 %collective-permute-start.32 = (bf16[64,512]{1,0:T(8,128)(2,1)S(1)}, bf16[64,512]{1,0:T(8,128)(2,1)S(1)}, u32[]{:S(2)}, u32[]{:S(2)}) collective-permute-start(bf16[64,512]{1,0:T(8,128)(2,1)S(1)} %get-tuple-element.113), channel_id=1, source_target_pairs={{0,12},{4,8},{8,4},{12,0},{1,13},{5,9},{9,5},{13,1},{2,14},{6,10},... | collective-permute-start | bytes 196616 | tf_op jit(solution)/shard_map/ppermute | solution.py:33
  76.6 2.0 %collective-permute-start.30 = (bf16[64,512]{1,0:T(8,128)(2,1)S(1)}, bf16[64,512]{1,0:T(8,128)(2,1)S(1)}, u32[]{:S(2)}, u32[]{:S(2)}) collective-permute-start(bf16[64,512]{1,0:T(8,128)(2,1)S(1)} %get-tuple-element.112), channel_id=1, source_target_pairs={{0,4},{4,0},{8,12},{12,8},{1,5},{5,1},{9,13},{13,9},{2,6},{6,2},{1... | collective-permute-start | bytes 196616 | tf_op jit(solution)/shard_map/ppermute | solution.py:33
  78.6 2.3 %collective-permute-done.30.refs_1_ = bf16[64,512]{1,0:T(8,128)(2,1)S(1)} collective-permute-done((bf16[64,512]{1,0:T(8,128)(2,1)S(1)}, bf16[64,512]{1,0:T(8,128)(2,1)S(1)}, u32[]{:S(2)}, u32[]{:S(2)}) %collective-permute-start.30) | collective-permute-done | bytes 65568 | tf_op jit(solution)/shard_map/ppermute | solution.py:33
  (71 shorter events, 25.1 us)
Async XLA Ops:
  4.3 6.7 %collective-permute-start.3 = (bf16[144,256]{1,0:T(8,128)(2,1)S(1)}, bf16[144,256]{1,0:T(8,128)(2,1)S(1)}, u32[]{:S(2)}, u32[]{:S(2)}) collective-permute-start(bf16[144,256]{1,0:T(8,128)(2,1)S(1)} %get-tuple-element.65.refs_0_), channel_id=1, source_target_pairs={{0,1},{1,0},{2,3},{3,2},{4,5},{5,4},{6,7},{7,6},{8,9},{9,8},{10,11... | collective-permute-start | bytes 221192 | tf_op jit(solution)/shard_map/ppermute | solution.py:33
  19.6 6.7 %collective-permute-start.5 = (bf16[128,512]{1,0:T(8,128)(2,1)S(1)}, bf16[128,512]{1,0:T(8,128)(2,1)S(1)}, u32[]{:S(2)}, u32[]{:S(2)}) collective-permute-start(bf16[128,512]{1,0:T(8,128)(2,1)S(1)} %get-tuple-element.83), channel_id=1, source_target_pairs={{0,1},{1,0},{2,3},{3,2},{4,5},{5,4},{6,7},{7,6},{8,9},{9,8},{10,11... | collective-permute-start | bytes 393224 | tf_op jit(solution)/shard_map/ppermute | solution.py:33
  20.2 6.1 %collective-permute-start.6 = (bf16[128,512]{1,0:T(8,128)(2,1)S(1)}, bf16[128,512]{1,0:T(8,128)(2,1)S(1)}, u32[]{:S(2)}, u32[]{:S(2)}) collective-permute-start(bf16[128,512]{1,0:T(8,128)(2,1)S(1)} %get-tuple-element.84), channel_id=1, source_target_pairs={{0,2},{1,3},{2,0},{3,1},{4,6},{5,7},{6,4},{7,5},{8,10},{9,11},{10,... | collective-permute-start | bytes 393224 | tf_op jit(solution)/shard_map/ppermute | solution.py:33
  20.9 7.4 %collective-permute-start.7 = (bf16[128,512]{1,0:T(8,128)(2,1)S(1)}, bf16[128,512]{1,0:T(8,128)(2,1)S(1)}, u32[]{:S(2)}, u32[]{:S(2)}) collective-permute-start(bf16[128,512]{1,0:T(8,128)(2,1)S(1)} %get-tuple-element.85), channel_id=1, source_target_pairs={{0,3},{1,2},{2,1},{3,0},{4,7},{5,6},{6,5},{7,4},{8,11},{9,10},{10,... | collective-permute-start | bytes 393224 | tf_op jit(solution)/shard_map/ppermute | solution.py:33
  28.6 7.3 %collective-permute-start.12 = (bf16[64,512]{1,0:T(8,128)(2,1)S(1)}, bf16[64,512]{1,0:T(8,128)(2,1)S(1)}, u32[]{:S(2)}, u32[]{:S(2)}) collective-permute-start(bf16[64,512]{1,0:T(8,128)(2,1)S(1)} %get-tuple-element.90), channel_id=1, source_target_pairs={{0,8},{4,12},{8,0},{12,4},{1,9},{5,13},{9,1},{13,5},{2,10},{6,14},... | collective-permute-start | bytes 196616 | tf_op jit(solution)/shard_map/ppermute | solution.py:33
  31.2 8.1 %collective-permute-start.16 = (bf16[64,512]{1,0:T(8,128)(2,1)S(1)}, bf16[64,512]{1,0:T(8,128)(2,1)S(1)}, u32[]{:S(2)}, u32[]{:S(2)}) collective-permute-start(bf16[64,512]{1,0:T(8,128)(2,1)S(1)} %get-tuple-element.91), channel_id=1, source_target_pairs={{0,12},{4,8},{8,4},{12,0},{1,13},{5,9},{9,5},{13,1},{2,14},{6,10},... | collective-permute-start | bytes 196616 | tf_op jit(solution)/shard_map/ppermute | solution.py:33
  32.6 8.2 %collective-permute-start.8 = (bf16[64,512]{1,0:T(8,128)(2,1)S(1)}, bf16[64,512]{1,0:T(8,128)(2,1)S(1)}, u32[]{:S(2)}, u32[]{:S(2)}) collective-permute-start(bf16[64,512]{1,0:T(8,128)(2,1)S(1)} %get-tuple-element.88), channel_id=1, source_target_pairs={{0,4},{4,0},{8,12},{12,8},{1,5},{5,1},{9,13},{13,9},{2,6},{6,2},{1... | collective-permute-start | bytes 196616 | tf_op jit(solution)/shard_map/ppermute | solution.py:33
  35.8 5.3 %collective-permute-start.15 = (bf16[64,512]{1,0:T(8,128)(2,1)S(1)}, bf16[64,512]{1,0:T(8,128)(2,1)S(1)}, u32[]{:S(2)}, u32[]{:S(2)}) collective-permute-start(bf16[64,512]{1,0:T(8,128)(2,1)S(1)} %collective-permute-done.12.refs_0_), channel_id=1, source_target_pairs={{0,3},{1,2},{2,1},{3,0},{4,7},{5,6},{6,5},{7,4},{8,11},{9,10},{10,... | collective-permute-start | bytes 196616 | tf_op jit(solution)/shard_map/ppermute | solution.py:33
  37.3 5.6 %collective-permute-start.14 = (bf16[64,512]{1,0:T(8,128)(2,1)S(1)}, bf16[64,512]{1,0:T(8,128)(2,1)S(1)}, u32[]{:S(2)}, u32[]{:S(2)}) collective-permute-start(bf16[64,512]{1,0:T(8,128)(2,1)S(1)} %collective-permute-done.12.refs_0_), channel_id=1, source_target_pairs={{0,2},{1,3},{2,0},{3,1},{4,6},{5,7},{6,4},{7,5},{8,10},{9,11},{10,... | collective-permute-start | bytes 196616 | tf_op jit(solution)/shard_map/ppermute | solution.py:33
  37.3 7.1 %collective-permute-start.13 = (bf16[64,512]{1,0:T(8,128)(2,1)S(1)}, bf16[64,512]{1,0:T(8,128)(2,1)S(1)}, u32[]{:S(2)}, u32[]{:S(2)}) collective-permute-start(bf16[64,512]{1,0:T(8,128)(2,1)S(1)} %collective-permute-done.12.refs_0_), channel_id=1, source_target_pairs={{0,1},{1,0},{2,3},{3,2},{4,5},{5,4},{6,7},{7,6},{8,9},{9,8},{10,11... | collective-permute-start | bytes 196616 | tf_op jit(solution)/shard_map/ppermute | solution.py:33
  39.3 5.8 %collective-permute-start.19 = (bf16[64,512]{1,0:T(8,128)(2,1)S(1)}, bf16[64,512]{1,0:T(8,128)(2,1)S(1)}, u32[]{:S(2)}, u32[]{:S(2)}) collective-permute-start(bf16[64,512]{1,0:T(8,128)(2,1)S(1)} %collective-permute-done.16.refs_0_.refs_4_), channel_id=1, source_target_pairs={{0,3},{1,2},{2,1},{3,0},{4,7},{5,6},{6,5},{7,4},{8,11},{9,10},{10,... | collective-permute-start | bytes 196616 | tf_op jit(solution)/shard_map/ppermute | solution.py:33
  40.8 5.6 %collective-permute-start.18 = (bf16[64,512]{1,0:T(8,128)(2,1)S(1)}, bf16[64,512]{1,0:T(8,128)(2,1)S(1)}, u32[]{:S(2)}, u32[]{:S(2)}) collective-permute-start(bf16[64,512]{1,0:T(8,128)(2,1)S(1)} %collective-permute-done.16.refs_0_.refs_4_), channel_id=1, source_target_pairs={{0,2},{1,3},{2,0},{3,1},{4,6},{5,7},{6,4},{7,5},{8,10},{9,11},{10,... | collective-permute-start | bytes 196616 | tf_op jit(solution)/shard_map/ppermute | solution.py:33
  42.9 10.9 %collective-permute-start.11 = (bf16[128,512]{1,0:T(8,128)(2,1)S(1)}, bf16[128,512]{1,0:T(8,128)(2,1)S(1)}, u32[]{:S(2)}, u32[]{:S(2)}) collective-permute-start(bf16[128,512]{1,0:T(8,128)(2,1)S(1)} %stack.1.refs_1_.refs_0_), channel_id=1, source_target_pairs={{0,3},{1,2},{2,1},{3,0},{4,7},{5,6},{6,5},{7,4},{8,11},{9,10},{10,... | collective-permute-start | bytes 393224 | tf_op jit(solution)/shard_map/ppermute | solution.py:33
  44.4 9.5 %collective-permute-start.10 = (bf16[128,512]{1,0:T(8,128)(2,1)S(1)}, bf16[128,512]{1,0:T(8,128)(2,1)S(1)}, u32[]{:S(2)}, u32[]{:S(2)}) collective-permute-start(bf16[128,512]{1,0:T(8,128)(2,1)S(1)} %stack.1.refs_1_.refs_0_), channel_id=1, source_target_pairs={{0,2},{1,3},{2,0},{3,1},{4,6},{5,7},{6,4},{7,5},{8,10},{9,11},{10,... | collective-permute-start | bytes 393224 | tf_op jit(solution)/shard_map/ppermute | solution.py:33
  45.1 8.7 %collective-permute-start.9 = (bf16[128,512]{1,0:T(8,128)(2,1)S(1)}, bf16[128,512]{1,0:T(8,128)(2,1)S(1)}, u32[]{:S(2)}, u32[]{:S(2)}) collective-permute-start(bf16[128,512]{1,0:T(8,128)(2,1)S(1)} %stack.1.refs_1_.refs_0_), channel_id=1, source_target_pairs={{0,1},{1,0},{2,3},{3,2},{4,5},{5,4},{6,7},{7,6},{8,9},{9,8},{10,11... | collective-permute-start | bytes 393224 | tf_op jit(solution)/shard_map/ppermute | solution.py:33
  54.1 6.0 %collective-permute-start.21 = (bf16[128,2048]{1,0:T(8,128)(2,1)S(1)}, bf16[128,2048]{1,0:T(8,128)(2,1)S(1)}, u32[]{:S(2)}, u32[]{:S(2)}) collective-permute-start(bf16[128,2048]{1,0:T(8,128)(2,1)S(1)} %norm.3.x_ref), channel_id=1, source_target_pairs={{0,16},{16,0},{1,17},{17,1},{2,18},{18,2},{3,19},{19,3},{4,20},{20... | collective-permute-start | bytes 1572872 | tf_op jit(solution)/shard_map/ppermute | solution.py:33
  56.5 8.2 %collective-permute-start.24 = (bf16[128,512]{1,0:T(8,128)(2,1)S(1)}, bf16[128,512]{1,0:T(8,128)(2,1)S(1)}, u32[]{:S(2)}, u32[]{:S(2)}) collective-permute-start(bf16[128,512]{1,0:T(8,128)(2,1)S(1)} %get-tuple-element.103), channel_id=1, source_target_pairs={{0,1},{1,0},{2,3},{3,2},{4,5},{5,4},{6,7},{7,6},{8,9},{9,8},{10,11... | collective-permute-start | bytes 393224 | tf_op jit(solution)/shard_map/ppermute | solution.py:33
  58.3 8.4 %collective-permute-start.25 = (bf16[128,512]{1,0:T(8,128)(2,1)S(1)}, bf16[128,512]{1,0:T(8,128)(2,1)S(1)}, u32[]{:S(2)}, u32[]{:S(2)}) collective-permute-start(bf16[128,512]{1,0:T(8,128)(2,1)S(1)} %get-tuple-element.104), channel_id=1, source_target_pairs={{0,2},{1,3},{2,0},{3,1},{4,6},{5,7},{6,4},{7,5},{8,10},{9,11},{10,... | collective-permute-start | bytes 393224 | tf_op jit(solution)/shard_map/ppermute | solution.py:33
  58.8 7.9 %collective-permute-start.26 = (bf16[128,512]{1,0:T(8,128)(2,1)S(1)}, bf16[128,512]{1,0:T(8,128)(2,1)S(1)}, u32[]{:S(2)}, u32[]{:S(2)}) collective-permute-start(bf16[128,512]{1,0:T(8,128)(2,1)S(1)} %get-tuple-element.105), channel_id=1, source_target_pairs={{0,3},{1,2},{2,1},{3,0},{4,7},{5,6},{6,5},{7,4},{8,11},{9,10},{10,... | collective-permute-start | bytes 393224 | tf_op jit(solution)/shard_map/ppermute | solution.py:33
  66.9 8.4 %collective-permute-start.27 = (bf16[128,512]{1,0:T(8,128)(2,1)S(1)}, bf16[128,512]{1,0:T(8,128)(2,1)S(1)}, u32[]{:S(2)}, u32[]{:S(2)}) collective-permute-start(bf16[128,512]{1,0:T(8,128)(2,1)S(1)} %get-tuple-element.108), channel_id=1, source_target_pairs={{0,1},{1,0},{2,3},{3,2},{4,5},{5,4},{6,7},{7,6},{8,9},{9,8},{10,11... | collective-permute-start | bytes 393224 | tf_op jit(solution)/shard_map/ppermute | solution.py:33
  68.5 8.1 %collective-permute-start.28 = (bf16[128,512]{1,0:T(8,128)(2,1)S(1)}, bf16[128,512]{1,0:T(8,128)(2,1)S(1)}, u32[]{:S(2)}, u32[]{:S(2)}) collective-permute-start(bf16[128,512]{1,0:T(8,128)(2,1)S(1)} %get-tuple-element.109), channel_id=1, source_target_pairs={{0,2},{1,3},{2,0},{3,1},{4,6},{5,7},{6,4},{7,5},{8,10},{9,11},{10,... | collective-permute-start | bytes 393224 | tf_op jit(solution)/shard_map/ppermute | solution.py:33
  69.0 7.5 %collective-permute-start.29 = (bf16[128,512]{1,0:T(8,128)(2,1)S(1)}, bf16[128,512]{1,0:T(8,128)(2,1)S(1)}, u32[]{:S(2)}, u32[]{:S(2)}) collective-permute-start(bf16[128,512]{1,0:T(8,128)(2,1)S(1)} %get-tuple-element.110), channel_id=1, source_target_pairs={{0,3},{1,2},{2,1},{3,0},{4,7},{5,6},{6,5},{7,4},{8,11},{9,10},{10,... | collective-permute-start | bytes 393224 | tf_op jit(solution)/shard_map/ppermute | solution.py:33
  70.5 8.2 %collective-permute-start.31 = (bf16[64,512]{1,0:T(8,128)(2,1)S(1)}, bf16[64,512]{1,0:T(8,128)(2,1)S(1)}, u32[]{:S(2)}, u32[]{:S(2)}) collective-permute-start(bf16[64,512]{1,0:T(8,128)(2,1)S(1)} %get-tuple-element.106.refs_1_), channel_id=1, source_target_pairs={{0,8},{4,12},{8,0},{12,4},{1,9},{5,13},{9,1},{13,5},{2,10},{6,14},... | collective-permute-start | bytes 196616 | tf_op jit(solution)/shard_map/ppermute | solution.py:33
  72.3 6.3 %collective-permute-start.32 = (bf16[64,512]{1,0:T(8,128)(2,1)S(1)}, bf16[64,512]{1,0:T(8,128)(2,1)S(1)}, u32[]{:S(2)}, u32[]{:S(2)}) collective-permute-start(bf16[64,512]{1,0:T(8,128)(2,1)S(1)} %get-tuple-element.113), channel_id=1, source_target_pairs={{0,12},{4,8},{8,4},{12,0},{1,13},{5,9},{9,5},{13,1},{2,14},{6,10},... | collective-permute-start | bytes 196616 | tf_op jit(solution)/shard_map/ppermute | solution.py:33
  (11 other events, 50.8 us)
